TPU v7x, 32 devices: a whole 2x2x4 slice. The times are simulated.
32 devices in a mesh: harm: 4 (over x, core), space: 2 (over y), samp: 4 (over z).
Axes of the slice: x: 2, y: 2, z: 4, core: 2. Of those that a mesh axis runs over, the one named last changes fastest.
Arguments:
- coeffs: bfloat16 [32, 4096], P(('harm', 'samp'), 'space'), may hold values from -1.5 to 1.5
- curl_tiles: bfloat16 [32, 4, 128, 384], P('space'), may hold values from -0.25 to 0.25
- pattern: int32 [32, 4], P('space'), may hold values from 0 to 17, as said below
- region_ids: int32 [32], P('space'), may hold values from 0 to 3
- material_law: float32 [3, 4], replicated, may hold values from 0.3 to 3
- source: float32 [32, 4096], P(('harm', 'samp'), 'space'), may hold values from -6 to 6
Outputs:
- residual: float32 [32, 4096], P(('harm', 'samp'), 'space')
Inputs may be any that keep to these rules, and one draw needn't show every extreme that they name: `pattern`: entries index a space shard's window of 18 edge tiles: 0 is the last tile of the previous shard, 17 the first of the next, cyclically over the sector; the first entry of every row is the element tile's own position in its shard plus one.
All inputs are finite; a program needn't handle non-finite values.
Results may differ from a plain program's by a relative error of at most 0.0015.
Values may be sent and summed in bfloat16 or wider, within the bound.
No kernel may reach another device: no remote copies, remote signals or barrier semaphores. Data moves between devices by JAX's collectives and lax.ppermute only.
A program may use at most 64 MiB of HBM per device.

v0:
```python
import math

import jax
import jax.numpy as jnp
from jax import lax
from jax.sharding import PartitionSpec as P

SAMPLES = 64
PARTS_SIZE = 32


def padded(block, sides, width):
    for axis, dim in sides:
        count = lax.axis_size(axis)
        forward = [(i, i + 1) for i in range(count - 1)]
        forward.append((count - 1, 0))
        backward = [(target, source) for source, target in forward]
        low = lax.ppermute(
            lax.slice_in_dim(block, block.shape[dim] - width, None, axis=dim), axis, forward
        )
        high = lax.ppermute(lax.slice_in_dim(block, 0, width, axis=dim), axis, backward)
        block = jnp.concatenate([low, block, high], axis=dim)
    return block


def passed_along(array, axis, by):
    devices = lax.axis_size(axis)
    return lax.ppermute(array, axis, [(i, (i + by) % devices) for i in range(devices)])


def transform_table():
    sample_ids = jnp.arange(SAMPLES, dtype=jnp.int32)[:, None]
    part_ids = jnp.arange(PARTS_SIZE, dtype=jnp.int32)[None, :]
    orders = 2 * (part_ids // 2) + 1
    phase = (orders * sample_ids % SAMPLES).astype(jnp.float32) * (2.0 * math.pi / SAMPLES)
    return jnp.where(part_ids % 2 == 0, jnp.cos(phase), jnp.sin(phase))


def sample_order(group_size):
    samples_here = SAMPLES // group_size
    half_here = samples_here // 2
    slots = jnp.arange(SAMPLES, dtype=jnp.int32)
    owner = slots // samples_here
    within = slots % samples_here
    return owner * half_here + within % half_here + within // half_here * (SAMPLES // 2)


def apply_reluctivity(density, region_ids, material_law, tile_count, tile_width):
    samples_here = density.shape[0]
    shaped = density.reshape(samples_here, tile_count, 3, tile_width)
    magnitude = jnp.sum(shaped * shaped, axis=2)
    region_hits = (
        region_ids[:, None] == jnp.arange(material_law.shape[1], dtype=jnp.int32)[None, :]
    ).astype(jnp.float32)
    region_law = jnp.dot(
        region_hits,
        material_law.T,
        precision=lax.Precision.HIGHEST,
        preferred_element_type=jnp.float32,
    )
    base_value = region_law[:, 0][None, :, None]
    knee_value = region_law[:, 1][None, :, None]
    rise_value = region_law[:, 2][None, :, None]
    reluct = base_value + rise_value * magnitude / (magnitude + knee_value)
    return (reluct[:, :, None, :] * shaped).reshape(samples_here, tile_count * 3 * tile_width)


def window_totals(contrib, pattern, tile_count):
    placement_hits = (
        pattern[:, :, None] == jnp.arange(tile_count + 2, dtype=jnp.int32)[None, None, :]
    ).astype(jnp.float32)
    return jnp.einsum("pgki,gkw->pwi", contrib, placement_hits, precision=lax.Precision.HIGHEST)


def per_device(coeffs, curl_tiles, pattern, region_ids, material_law, source):
    parts_here = coeffs.shape[0]
    tile_count, links, tile_width, comp_width = curl_tiles.shape
    group_size = lax.axis_size(("harm", "samp"))
    rank = lax.axis_index(("harm", "samp"))
    samples_here = SAMPLES // group_size
    window = padded(coeffs, (("space", 1),), tile_width)
    transform = transform_table()
    ordered = jnp.take(transform, sample_order(group_size), axis=0)
    window_tiles = window.reshape(parts_here, tile_count + 2, tile_width)
    picked = jnp.take(window_tiles, pattern.reshape(-1), axis=1).reshape(
        parts_here, tile_count, links, tile_width
    )
    flux_rows = jnp.einsum("pgki,gkij->pgj", picked, curl_tiles, preferred_element_type=jnp.float32)
    flux_rows = flux_rows.reshape(parts_here, tile_count * comp_width)
    own_samples = lax.dynamic_slice_in_dim(ordered, rank * samples_here, samples_here, 0)
    own_parts = lax.dynamic_slice_in_dim(ordered, rank * parts_here, parts_here, 1)
    row_block = own_parts
    density = lax.psum_scatter(
        jnp.dot(
            row_block,
            flux_rows,
            precision=lax.Precision.HIGHEST,
            preferred_element_type=jnp.float32,
        ),
        ("harm", "samp"),
        scatter_dimension=0,
        tiled=True,
    )
    field = apply_reluctivity(density, region_ids, material_law, tile_count, tile_width)
    row_block = own_samples
    harm_field = lax.psum_scatter(
        2.0
        / SAMPLES
        * jnp.dot(
            row_block.T, field, precision=lax.Precision.HIGHEST, preferred_element_type=jnp.float32
        ),
        ("harm", "samp"),
        scatter_dimension=0,
        tiled=True,
    )
    field_half = harm_field.astype(jnp.bfloat16).reshape(parts_here, tile_count, comp_width)
    contrib = jnp.einsum(
        "pgj,gkij->pgki", field_half, curl_tiles, preferred_element_type=jnp.float32
    )
    window_sum = window_totals(contrib, pattern, tile_count)
    from_right = passed_along(window_sum[:, 0], "space", -1)
    from_left = passed_along(window_sum[:, tile_count + 1], "space", 1)
    owned_sum = window_sum[:, 1 : tile_count + 1]
    owned_sum = owned_sum.at[:, 0].add(from_left)
    owned_sum = owned_sum.at[:, tile_count - 1].add(from_right)
    return owned_sum.reshape(parts_here, tile_count * tile_width) - source


def solution(mesh):
    placed = (
        P(("harm", "samp"), "space"),
        P("space", None, None, None),
        P("space", None),
        P("space"),
        P(),
        P(("harm", "samp"), "space"),
    )
    return jax.shard_map(
        per_device,
        mesh=mesh,
        in_specs=placed,
        out_specs=P(("harm", "samp"), "space"),
        check_vma=False,
    )
```

profile of v0, /device:TPU:0, one launch (start us, length us, event | category | flops | bytes accessed | tf_op | source)
XLA Modules:
  0.0 213.3 jit_solution(138028066748298494)
XLA Ops:
  6.5 0.0 copy-start
  6.5 0.0 all-reduce.5.cloned.1.call-start
  6.5 0.7 fusion.37
  7.2 3.0 %collective-permute-start = (bf16[2,128]{1,0:T(2,128)(2,1)S(1)}, bf16[2,128]{1,0:T(2,128)(2,1)S(1)}, u32[]{:S(2)}, u32[]{:S(2)}) collective-permute-start(bf16[2,128]{1,0:T(2,128)(2,1)S(1)} %get-tuple-element.32), channel_id=1, source_target_pairs={{0,4},{4,0},{1,5},{5,1},{2,6},{6,2},{3,7},{7,3},{8,12},{12,8},{9,1... | collective-permute-start | bytes 1544 | tf_op jit(solution)/shard_map/ppermute | solution.py:18
  10.2 0.0 collective-permute-start.1
  10.2 0.8 copy.20
  11.0 0.7 compare_and_fusion
  11.7 0.1 reshape.327
  11.9 0.1 sine_select_fusion
  12.0 0.6 gather_fusion
  12.6 0.1 broadcast_select_fusion.2
  12.7 0.1 copy.19
  12.8 0.0 collective-permute-done
  12.8 0.9 collective-permute-done.1
  13.7 0.7 maximum_bitcast_fusion
  14.4 0.6 gather_fusion.1
  15.1 0.0 copy-start.4
  15.1 0.0 copy-start.3
  15.1 3.8 %fusion.6 = f32[16,2,384,1]{2,1,3,0:T(2,128)S(1)} fusion(bf16[16,4,128,384]{3,2,1,0:T(8,128)(2,1)} %param.11, bf16[2,16,4,128]{3,0,2,1:T(2,128)(2,1)S(1)} %bitcast.56, pred[16,4]{1,0:T(8,128)(4,1)S(1)} %copy.19), kind=kOutput, calls=%fused_computation.17 | convolution fusion | flops 12599296 | bytes 6373440 | tf_op jit(solution)/shard_map/pgki,gkij->pgj/dot_general | solution.py:88
  18.9 0.0 copy-start.1
  18.9 0.0 copy-start.2
  18.9 2.6 %fusion.7 = f32[64,6144]{1,0:T(8,128)} fusion(f32[2,6144]{1,0:T(2,128)S(1)} %bitcast.55, f32[64,32]{1,0:T(8,128)S(1)} %broadcast_select_fusion.2, s32[]{:T(128)S(6)} %select_n.156), kind=kOutput, calls=%fused_computation.19 | convolution fusion | flops 9437184 | bytes 1630212 | tf_op jit(solution)/shard_map/dot_general | solution.py:94
  21.5 0.0 all-reduce.5.cloned.1.call-update
  21.5 0.0 copy-done.4
  21.5 0.6 dynamic-slice.16
  23.4 0.0 copy-done
  23.4 0.0 copy-done.3
  23.4 0.2 fusion.16
  23.6 94.2 %all-reduce.5.cloned.1.call-done = f32[64,6144]{1,0:T(8,128)} async-done(((f32[64,6144]{1,0:T(8,128)}), f32[64,6144]{1,0:T(8,128)}) %all-reduce.5.cloned.1.call-update) | async-done | bytes 1572880
  117.9 0.9 dynamic-slice_multiply_fusion
  118.8 0.1 mul.126
  118.9 0.1 reduce_sum.9
  119.0 0.1 divide_add_fusion
  119.1 0.1 mul.129
  119.2 1.8 convolution_multiply_fusion
  121.0 75.3 %all-reduce.6 = bf16[32,6144]{1,0:T(8,128)(2,1)S(1)} all-reduce(f32[32,6144]{1,0:T(8,128)S(1)} %convolution_multiply_fusion), channel_id=3, replica_groups=mesh['harm'=4,'space'=2,'samp'=4] {'harm','samp'}, use_global_device_ids=true, to_apply=%region_2.3.clone | all-reduce | flops 196608 | bytes 1179648
  196.4 4.5 %convolution_bitcast_fusion = f32[2,16,4,128]{3,0,2,1:T(2,128)S(1)} fusion(bf16[2,16,384,1]{2,0,3,1:T(2,128)(2,1)S(1)} %bitcast.57, bf16[16,4,128,384]{3,2,1,0:T(8,128)(2,1)} %param.11), kind=kOutput, calls=%fused_computation.3 | convolution fusion | flops 12582912 | bytes 6381568 | tf_op jit(solution)/shard_map/pgj,gkij->pgki/dot_general | solution.py:117
  200.9 0.0 copy-done.1
  200.9 0.3 convolution_bitcast_fusion.1
  201.2 0.9 collective-permute-start.2
  202.1 1.2 collective-permute-start.3
  203.4 1.5 collective-permute-done.2
  204.8 0.9 collective-permute-done.3
  205.8 0.0 copy-done.2
  205.8 0.6 bitcast_subtract_fusion
  (15 shorter events, 0.2 us)
Async XLA Ops:
  6.5 16.9 %copy-start = (f32[3,4]{1,0:T(4,128)S(1)}, f32[3,4]{1,0:T(4,128)}, u32[]{:S(2)}) copy-start(f32[3,4]{1,0:T(4,128)} %param.14) | copy-start | bytes 148
  6.5 111.3 %all-reduce.5.cloned.1.call-start = ((), (), s32[]{:S(2)}) async-start(), calls=%async_computation | async-start | bytes 3145728
  7.2 5.6 %collective-permute-start = (bf16[2,128]{1,0:T(2,128)(2,1)S(1)}, bf16[2,128]{1,0:T(2,128)(2,1)S(1)}, u32[]{:S(2)}, u32[]{:S(2)}) collective-permute-start(bf16[2,128]{1,0:T(2,128)(2,1)S(1)} %get-tuple-element.32), channel_id=1, source_target_pairs={{0,4},{4,0},{1,5},{5,1},{2,6},{6,2},{3,7},{7,3},{8,12},{12,8},{9,1... | collective-permute-start | bytes 1544 | tf_op jit(solution)/shard_map/ppermute | solution.py:18
  10.2 3.5 %collective-permute-start.1 = (bf16[2,128]{1,0:T(2,128)(2,1)S(1)}, bf16[2,128]{1,0:T(2,128)(2,1)S(1)}, u32[]{:S(2)}, u32[]{:S(2)}) collective-permute-start(bf16[2,128]{1,0:T(2,128)(2,1)S(1)} %get-tuple-element.33), channel_id=1, source_target_pairs={{4,0},{0,4},{5,1},{1,5},{6,2},{2,6},{7,3},{3,7},{12,8},{8,12},{13,... | collective-permute-start | bytes 1544 | tf_op jit(solution)/shard_map/ppermute | solution.py:21
  15.1 6.4 %copy-start.4 = (u32[32]{0:T(128)S(1)}, u32[32]{0:T(128)}, u32[]{:S(2)}) copy-start(u32[32]{0:T(128)} %constant.196) | copy-start | bytes 388
  15.1 8.3 %copy-start.3 = (s32[16]{0:T(128)S(1)}, s32[16]{0:T(128)}, u32[]{:S(2)}) copy-start(s32[16]{0:T(128)} %param.13) | copy-start | bytes 196
  18.9 182.0 %copy-start.1 = (s32[16,4]{0,1:T(4,128)S(1)}, s32[16,4]{0,1:T(4,128)}, u32[]{:S(2)}) copy-start(s32[16,4]{0,1:T(4,128)} %param.12) | copy-start | bytes 772
  18.9 186.9 %copy-start.2 = (f32[2,2048]{1,0:T(2,128)S(1)}, f32[2,2048]{1,0:T(2,128)}, u32[]{:S(2)}) copy-start(f32[2,2048]{1,0:T(2,128)} %param.15) | copy-start | bytes 49156
  201.2 3.6 %collective-permute-start.2 = (f32[2,128]{1,0:T(2,128)S(1)}, f32[2,128]{1,0:T(2,128)S(1)}, u32[]{:S(2)}, u32[]{:S(2)}) collective-permute-start(f32[2,128]{1,0:T(2,128)S(1)} %bitcast.60), channel_id=1, source_target_pairs={{0,4},{4,0},{1,5},{5,1},{2,6},{6,2},{3,7},{7,3},{8,12},{12,8},{9,1... | collective-permute-start | bytes 3080 | tf_op jit(solution)/shard_map/ppermute | solution.py:28
  202.1 3.6 %collective-permute-start.3 = (f32[2,128]{1,0:T(2,128)S(1)}, f32[2,128]{1,0:T(2,128)S(1)}, u32[]{:S(2)}, u32[]{:S(2)}) collective-permute-start(f32[2,128]{1,0:T(2,128)S(1)} %bitcast.59), channel_id=1, source_target_pairs={{0,4},{4,0},{1,5},{5,1},{2,6},{6,2},{3,7},{7,3},{8,12},{12,8},{9,1... | collective-permute-start | bytes 3080 | tf_op jit(solution)/shard_map/ppermute | solution.py:28
Sparse Core Ops, SparseCore 0:
  21.6 96.1 all-reduce.4
where the time goes:
time: 214 us; the launch traced here: 213 us
  waiting for transfers between devices  97.6 us (46%)
  blocking collectives  75.3 us (35%)
  between operations  14.9 us (7%)
  matrix products  13.2 us (6%)
  starting transfers between devices  5.16 us (2%)
  local copies, waits for them, and re-layouts  3.74 us (2%)
  other arithmetic  3.42 us (2%)
    unnamed x2, waiting for transfers between devices  94.2 us
    unnamed x1, blocking collectives  75.3 us
    dot_general x1, matrix products, per_device(): jnp.einsum('pgj,gkij->pgki', field_half, curl_tiles, preferred_element_ty...  4.5 us
  transfers between devices with their start and end apart: 5, of which 4 were waited for; matrix products, arithmetic and copies ran while one was open for 2% of the time, Pallas kernels for 0%

commit v1 on v0

v1 whole, which is shorter than its diff:
```python
import math

import jax
import jax.numpy as jnp
import ml_dtypes
import numpy as np
from jax import lax
from jax.experimental import pallas as pl
from jax.experimental.pallas import tpu as pltpu
from jax.sharding import PartitionSpec as P

SAMPLES = 64
HALF = SAMPLES // 2
GROUP = ("harm", "samp")


def half_table(parts):
    sample_ids = np.arange(HALF)[:, None]
    part_ids = np.arange(parts)[None, :]
    phase = ((2 * (part_ids // 2) + 1) * sample_ids % SAMPLES) * (2.0 * math.pi / SAMPLES)
    return np.where(part_ids % 2 == 0, np.cos(phase), np.sin(phase))


def bf16_pieces(table):
    rest = table
    pieces = []
    for _ in range(3):
        piece = rest.astype(ml_dtypes.bfloat16)
        pieces.append(piece)
        rest = rest - piece.astype(np.float64)
    return np.concatenate(pieces, axis=1)


def ring(axis, by):
    count = lax.axis_size(axis)
    return [(i, (i + by) % count) for i in range(count)]


def exchange(to_left, to_right, axis):
    if lax.axis_size(axis) == 2:
        width = to_left.shape[1]
        both = lax.ppermute(jnp.concatenate([to_left, to_right], axis=1), axis, ring(axis, 1))
        return both[:, :width], both[:, width:]
    return lax.ppermute(to_left, axis, ring(axis, -1)), lax.ppermute(to_right, axis, ring(axis, 1))


def shard_kernel(
    pattern, region_ids, law, window, pieces, table, curl, source, out, halo, timed, sums
):
    tile_count, links, tile, comps = curl.shape
    parts_here = out.shape[0]
    rank = lax.axis_index(GROUP)
    stacked = jnp.concatenate([window[...]] * 3, axis=0)
    samples = jnp.dot(pieces[...], stacked, preferred_element_type=jnp.float32)
    high = samples.astype(jnp.bfloat16)
    timed[:HALF, :] = high
    timed[HALF:, :] = (samples - high.astype(jnp.float32)).astype(jnp.bfloat16)
    sums[...] = jnp.zeros_like(sums)
    lanes = lax.broadcasted_iota(jnp.int32, table.shape, 1)
    columns = [
        jnp.sum(
            jnp.where(lanes == rank * parts_here + part, table[...], 0.0), axis=1, keepdims=True
        )
        for part in range(parts_here)
    ]
    for elem in range(tile_count):
        places = [pattern[elem, link] for link in range(links)]
        picked = jnp.concatenate(
            [timed[:, pl.ds(pl.multiple_of(place * tile, tile), tile)] for place in places], axis=1
        )
        blocks = curl[elem].reshape(links * tile, comps)
        split = jnp.dot(picked, blocks, preferred_element_type=jnp.float32)
        density = split[:HALF] + split[HALF:]
        comp = [density[:, c * tile : (c + 1) * tile] for c in range(comps // tile)]
        square = comp[0] * comp[0]
        for c in comp[1:]:
            square = square + c * c
        region = region_ids[elem]
        reluct = law[0, region] + law[2, region] * square / (square + law[1, region])
        field = jnp.concatenate([reluct * c for c in comp], axis=1)
        projected = jnp.concatenate(
            [jnp.sum(column * field, axis=0, keepdims=True) for column in columns], axis=0
        )
        projected = (projected * (4.0 / SAMPLES)).astype(jnp.bfloat16)
        contrib = lax.dot_general(
            projected, blocks, (((1,), (1,)), ((), ())), preferred_element_type=jnp.float32
        )
        for link, place in enumerate(places):
            sums[place] += contrib[:, link * tile : (link + 1) * tile]
    for w in range(tile_count):
        at = slice(w * tile, (w + 1) * tile)
        out[:, at] = sums[w + 1] - source[:, at]
    halo[:, :tile] = sums[0]
    halo[:, tile:] = sums[tile_count + 1]


def per_device(coeffs, curl_tiles, pattern, region_ids, material_law, source):
    parts_here = coeffs.shape[0]
    tile_count, links, tile, comps = curl_tiles.shape
    parts = parts_here * lax.axis_size(GROUP)
    high, low = exchange(coeffs[:, :tile], coeffs[:, -tile:], "space")
    window = lax.all_gather(
        jnp.concatenate([low, coeffs, high], axis=1), GROUP, axis=0, tiled=True
    )
    table = half_table(parts)
    vmem, smem = pl.BlockSpec(memory_space=pltpu.VMEM), pl.BlockSpec(memory_space=pltpu.SMEM)
    own, halo = pl.pallas_call(
        shard_kernel,
        out_shape=(
            jax.ShapeDtypeStruct(source.shape, jnp.float32),
            jax.ShapeDtypeStruct((parts_here, 2 * tile), jnp.float32),
        ),
        in_specs=[smem] * 3 + [vmem] * 5,
        out_specs=(vmem, vmem),
        scratch_shapes=[
            pltpu.VMEM((SAMPLES, (tile_count + 2) * tile), jnp.bfloat16),
            pltpu.VMEM((tile_count + 2, parts_here, tile), jnp.float32),
        ],
        compiler_params=pltpu.CompilerParams(vmem_limit_bytes=32 * 1024 * 1024),
        cost_estimate=pl.CostEstimate(
            flops=4 * SAMPLES * tile_count * links * tile * comps,
            bytes_accessed=2 * curl_tiles.size,
            transcendentals=0,
        ),
        name="shard_residual",
    )(
        pattern,
        region_ids,
        material_law,
        window,
        jnp.asarray(bf16_pieces(table)),
        jnp.asarray(table.astype(np.float32)),
        curl_tiles,
        source,
    )
    from_right, from_left = exchange(halo[:, :tile], halo[:, tile:], "space")
    return own.at[:, :tile].add(from_left).at[:, -tile:].add(from_right)


def solution(mesh):
    placed = (
        P(GROUP, "space"),
        P("space", None, None, None),
        P("space", None),
        P("space"),
        P(),
        P(GROUP, "space"),
    )
    return jax.shard_map(
        per_device,
        mesh=mesh,
        in_specs=placed,
        out_specs=P(GROUP, "space"),
        check_vma=False,
    )
```

time: 214 us -> 58.4 us (0.27)
  waiting for transfers between devices: 97.6 us -> 2.15 us
  blocking collectives: 75.3 us -> 32.9 us
  between operations: 14.9 us -> 0.03 us
  matrix products: 13.2 us -> 0 us
  Pallas kernels: 0 us -> 5.9 us
  local copies, waits for them, and re-layouts: 3.74 us -> 7.74 us
    unnamed x2 -> x0, waiting for transfers between devices: 94.2 us -> none
    unnamed x1 -> x0, blocking collectives: 75.3 us -> none
    all_gather x0 -> x1, blocking collectives: none -> 32.9 us  [per_device(): lax.all_gather(jnp.concatenate([low, coeffs, high], axis=1), GROUP, axis=...]
    dot_general x6 -> x0, matrix products: 13.2 us -> none  [the longest x1 4.5 us: per_device(): jnp.einsum('pgj,gkij->pgki', field_half, curl_tiles, preferred_element_ty...]
    pallas_call x0 -> x1, Pallas kernels: none -> 5.9 us  [per_device(): pl.pallas_call(shard_kernel, out_shape=(jax.ShapeDtypeStruct(source.shape...]
    unnamed x13 -> x14, local copies, waits for them, and re-layouts: 1.38 us -> 7.06 us
    scatter-add x2, other arithmetic: 0.02 us -> 3.17 us  [per_device(): return own.at[:, :tile].add(from_left).at[:, -tile:].add(from_right)]
    ppermute x4 -> x2, starting transfers between devices: 5.16 us -> 4.54 us  [exchange(): lax.ppermute(jnp.concatenate([to_left, to_right], axis=1), axis, ring(axi...]
  transfers between devices with their start and end apart: 5 -> 2, of which waited for: 4 -> 2; matrix products, arithmetic and copies ran while one was open for 2% -> 3% of each run, Pallas kernels for 0% -> 0%
where the time goes in v1:
time: 58.4 us; the launch traced here: 57.8 us
  blocking collectives  32.9 us (56%)
  local copies, waits for them, and re-layouts  7.74 us (13%)
  Pallas kernels  5.9 us (10%)
  other arithmetic  4.59 us (8%)
  starting transfers between devices  4.54 us (8%)
  waiting for transfers between devices  2.15 us (4%)
    all_gather x1, blocking collectives, per_device(): lax.all_gather(jnp.concatenate([low, coeffs, high], axis=1), GROUP, axis=...  32.9 us
    unnamed x14, local copies, waits for them, and re-layouts  7.06 us
    pallas_call x1, Pallas kernels, per_device(): pl.pallas_call(shard_kernel, out_shape=(jax.ShapeDtypeStruct(source.shape...  5.9 us
    ppermute x2, starting transfers between devices, exchange(): lax.ppermute(jnp.concatenate([to_left, to_right], axis=1), axis, ring(axi...  4.54 us
    scatter-add x2, other arithmetic, per_device(): return own.at[:, :tile].add(from_left).at[:, -tile:].add(from_right)  3.17 us
    ppermute x2, waiting for transfers between devices, exchange(): lax.ppermute(jnp.concatenate([to_left, to_right], axis=1), axis, ring(axi...  2.15 us
  transfers between devices with their start and end apart: 2, of which 2 were waited for; matrix products, arithmetic and copies ran while one was open for 3% of the time, Pallas kernels for 0%

profile of v1, /device:TPU:0, one launch (start us, length us, event | category | flops | bytes accessed | tf_op | source)
XLA Modules:
  0.0 57.8 jit_solution(17277471390968103752)
XLA Ops:
  0.0 0.7 %fusion.2 = (bf16[2,128]{1,0:T(2,128)(2,1)S(1)}, bf16[2,128]{1,0:T(2,128)(2,1)S(1)}) fusion(bf16[2,2048]{1,0:T(2,128)(2,1)} %param.12), kind=kLoop, calls=%fused_computation.7 | loop fusion | bytes 2048 | tf_op jit(solution)/shard_map/slice | solution.py:101
  0.7 3.0 %collective-permute-start = (bf16[2,256]{1,0:T(2,128)(2,1)S(1)}, bf16[2,256]{1,0:T(2,128)(2,1)S(1)}, u32[]{:S(2)}, u32[]{:S(2)}) collective-permute-start(bf16[2,256]{1,0:T(2,128)(2,1)S(1)} %pad_maximum_fusion), channel_id=1, source_target_pairs={{0,4},{4,0},{1,5},{5,1},{2,6},{6,2},{3,7},{7,3},{8,12},{12,8},{9,1... | collective-permute-start | bytes 3080 | tf_op jit(solution)/shard_map/ppermute | solution.py:42
  3.7 0.8 %copy.10.pattern = s32[16,4]{1,0:T(8,128)S(1)} copy(s32[16,4]{0,1:T(4,128)} %param.14) | data formatting | bytes 512 | tf_op args[2]
  4.5 0.8 %collective-permute-done = bf16[2,256]{1,0:T(2,128)(2,1)S(1)} collective-permute-done((bf16[2,256]{1,0:T(2,128)(2,1)S(1)}, bf16[2,256]{1,0:T(2,128)(2,1)S(1)}, u32[]{:S(2)}, u32[]{:S(2)}) %collective-permute-start) | collective-permute-done | bytes 1056 | tf_op jit(solution)/shard_map/ppermute | solution.py:42
  5.3 0.7 %maximum_bitcast_fusion = bf16[1,2,2304]{2,1,0:T(2,128)(2,1)S(1)} fusion(bf16[2,128]{1,0:T(2,128)(2,1)S(1)} %get-tuple-element.36, bf16[2,2048]{1,0:T(2,128)(2,1)} %param.12, bf16[2,128]{1,0:T(2,128)(2,1)S(1)} %get-tuple-element.35), kind=kLoop, calls=%fused_computation | loop fusion | flops 27648 | bytes 18432
  6.0 32.9 %all-gather = bf16[16,2,2304]{2,1,0:T(2,128)(2,1)S(1)} all-gather(bf16[1,2,2304]{2,1,0:T(2,128)(2,1)S(1)} %maximum_bitcast_fusion), channel_id=1, replica_groups=mesh['harm'=4,'space'=2,'samp'=4] {'harm','samp'}, dimensions={0}, use_global_device_ids=true | all-gather | bytes 156672 | tf_op jit(solution)/shard_map/all_gather | solution.py:102
  38.8 0.1 reshape.50.window
  38.9 0.0 copy-start
  38.9 2.8 %copy-done = bf16[16,4,128,384]{3,2,1,0:T(8,128)(2,1)S(1)} copy-done((bf16[16,4,128,384]{3,2,1,0:T(8,128)(2,1)S(1)}, bf16[16,4,128,384]{3,2,1,0:T(8,128)(2,1)}, u32[]{:S(2)}) %copy-start) | copy-done | bytes 6291480
  41.7 0.0 copy-start.1
  41.7 0.7 %copy-done.1 = f32[2,2048]{1,0:T(2,128)S(1)} copy-done((f32[2,2048]{1,0:T(2,128)S(1)}, f32[2,2048]{1,0:T(2,128)}, u32[]{:S(2)}) %copy-start.1) | copy-done | bytes 16408
  42.4 0.0 copy-start.2
  42.4 0.7 %copy-done.2 = f32[32,32]{1,0:T(8,128)S(1)} copy-done((f32[32,32]{1,0:T(8,128)S(1)}, f32[32,32]{1,0:T(8,128)}, u32[]{:S(2)}) %copy-start.2) | copy-done | bytes 4120
  43.1 0.0 copy-start.3
  43.1 0.7 %copy-done.3 = bf16[32,96]{1,0:T(8,128)(2,1)S(1)} copy-done((bf16[32,96]{1,0:T(8,128)(2,1)S(1)}, bf16[32,96]{1,0:T(8,128)(2,1)}, u32[]{:S(2)}) %copy-start.3) | copy-done | bytes 6168
  43.8 0.0 copy-start.4
  43.8 0.7 %copy-done.4 = f32[3,4]{1,0:T(4,128)S(1)} copy-done((f32[3,4]{1,0:T(4,128)S(1)}, f32[3,4]{1,0:T(4,128)}, u32[]{:S(2)}) %copy-start.4) | copy-done | bytes 72
  44.5 0.0 copy-start.5
  44.5 0.7 %copy-done.5 = s32[16]{0:T(128)S(1)} copy-done((s32[16]{0:T(128)S(1)}, s32[16]{0:T(128)}, u32[]{:S(2)}) %copy-start.5) | copy-done | bytes 88
  45.2 5.9 %shard_residual.1 = (f32[2,2048]{1,0:T(2,128)}, f32[2,256]{1,0:T(2,128)S(1)}) custom-call(s32[16,4]{1,0:T(8,128)S(1)} %copy.10.pattern, s32[16]{0:T(128)S(1)} %copy-done.5, f32[3,4]{1,0:T(4,128)S(1)} %copy-done.4, bf16[32,2304]{1,0:T(8,128)(2,1)S(1)} %reshape.50.window, bf16[32,96]{1,0:T(8,128)(2,1)S(1)} %copy-done.3, f32[32,32]{1,0:T(8,128)S(1)} %copy-done.2, ...), custom_call_target="tpu_custom_call" | custom-call | flops 805306368 | bytes 6291456 | tf_op jit(solution)/shard_map/shard_residual/pallas_call | solution.py:107
  51.1 1.5 %collective-permute-start.1 = (f32[2,256]{1,0:T(2,128)S(1)}, f32[2,256]{1,0:T(2,128)S(1)}, u32[]{:S(2)}, u32[]{:S(2)}) collective-permute-start(f32[2,256]{1,0:T(2,128)S(1)} %get-tuple-element.32), channel_id=1, source_target_pairs={{0,4},{4,0},{1,5},{5,1},{2,6},{6,2},{3,7},{7,3},{8,12},{12,8},{9,1... | collective-permute-start | bytes 6152 | tf_op jit(solution)/shard_map/ppermute | solution.py:42
  52.6 0.7 %compare_reduce_fusion = pred[]{:T(512)} fusion(), kind=kLoop, calls=%fused_computation.1 | loop fusion | flops 5 | bytes 1 | tf_op jit(solution)/shard_map/reduce.2
  53.3 1.4 %collective-permute-done.1 = f32[2,256]{1,0:T(2,128)S(1)} collective-permute-done((f32[2,256]{1,0:T(2,128)S(1)}, f32[2,256]{1,0:T(2,128)S(1)}, u32[]{:S(2)}, u32[]{:S(2)}) %collective-permute-start.1) | collective-permute-done | bytes 2080 | tf_op jit(solution)/shard_map/ppermute | solution.py:42
  54.6 1.9 %fusion = f32[2,2048]{1,0:T(2,128)} fusion(f32[2,2048]{1,0:T(2,128)} %get-tuple-element.31, f32[2,256]{1,0:T(2,128)S(1)} %collective-permute-done.1, pred[]{:T(512)} %compare_reduce_fusion), kind=kLoop, calls=%fused_computation.3 | loop fusion | flops 512 | bytes 3584 | tf_op jit(solution)/shard_map/scatter-add | solution.py:137
  56.6 1.2 %fusion.1 = f32[2,2048]{1,0:T(2,128)} fusion(f32[2,2048]{1,0:T(2,128)} %fusion, f32[2,256]{1,0:T(2,128)S(1)} %collective-permute-done.1), kind=kLoop, calls=%fused_computation.5 | loop fusion | flops 256 | bytes 3072 | tf_op jit(solution)/shard_map/scatter-add | solution.py:137
  (2 shorter events, 0.0 us)
Async XLA Ops:
  0.7 4.6 %collective-permute-start = (bf16[2,256]{1,0:T(2,128)(2,1)S(1)}, bf16[2,256]{1,0:T(2,128)(2,1)S(1)}, u32[]{:S(2)}, u32[]{:S(2)}) collective-permute-start(bf16[2,256]{1,0:T(2,128)(2,1)S(1)} %pad_maximum_fusion), channel_id=1, source_target_pairs={{0,4},{4,0},{1,5},{5,1},{2,6},{6,2},{3,7},{7,3},{8,12},{12,8},{9,1... | collective-permute-start | bytes 3080 | tf_op jit(solution)/shard_map/ppermute | solution.py:42
  38.9 2.8 %copy-start = (bf16[16,4,128,384]{3,2,1,0:T(8,128)(2,1)S(1)}, bf16[16,4,128,384]{3,2,1,0:T(8,128)(2,1)}, u32[]{:S(2)}) copy-start(bf16[16,4,128,384]{3,2,1,0:T(8,128)(2,1)} %curl.1) | copy-start | bytes 18874372
  41.7 0.7 %copy-start.1 = (f32[2,2048]{1,0:T(2,128)S(1)}, f32[2,2048]{1,0:T(2,128)}, u32[]{:S(2)}) copy-start(f32[2,2048]{1,0:T(2,128)} %source.1) | copy-start | bytes 49156
  42.4 0.7 %copy-start.2 = (f32[32,32]{1,0:T(8,128)S(1)}, f32[32,32]{1,0:T(8,128)}, u32[]{:S(2)}) copy-start(f32[32,32]{1,0:T(8,128)} %constant.61.clone.table) | copy-start | bytes 12292
  43.1 0.7 %copy-start.3 = (bf16[32,96]{1,0:T(8,128)(2,1)S(1)}, bf16[32,96]{1,0:T(8,128)(2,1)}, u32[]{:S(2)}) copy-start(bf16[32,96]{1,0:T(8,128)(2,1)} %constant.60.clone.pieces) | copy-start | bytes 18436
  43.8 0.7 %copy-start.4 = (f32[3,4]{1,0:T(4,128)S(1)}, f32[3,4]{1,0:T(4,128)}, u32[]{:S(2)}) copy-start(f32[3,4]{1,0:T(4,128)} %law.1) | copy-start | bytes 148
  44.5 0.7 %copy-start.5 = (s32[16]{0:T(128)S(1)}, s32[16]{0:T(128)}, u32[]{:S(2)}) copy-start(s32[16]{0:T(128)} %region_ids.1) | copy-start | bytes 196
  51.1 3.6 %collective-permute-start.1 = (f32[2,256]{1,0:T(2,128)S(1)}, f32[2,256]{1,0:T(2,128)S(1)}, u32[]{:S(2)}, u32[]{:S(2)}) collective-permute-start(f32[2,256]{1,0:T(2,128)S(1)} %get-tuple-element.32), channel_id=1, source_target_pairs={{0,4},{4,0},{1,5},{5,1},{2,6},{6,2},{3,7},{7,3},{8,12},{12,8},{9,1... | collective-permute-start | bytes 6152 | tf_op jit(solution)/shard_map/ppermute | solution.py:42

commit v2 on v1

--- a/solution.py
+++ b/solution.py
@@ -45,17 +45,57 @@
 
 
 def shard_kernel(
-    pattern, region_ids, law, window, pieces, table, curl, source, out, halo, timed, sums
+    window,
+    pattern_hbm,
+    region_hbm,
+    law_hbm,
+    pieces_hbm,
+    table_hbm,
+    source_hbm,
+    curl_hbm,
+    out,
+    halo,
+    pattern,
+    region_ids,
+    law,
+    pieces,
+    table,
+    source,
+    curl,
+    timed,
+    sums,
+    small_sems,
+    curl_sems,
 ):
     tile_count, links, tile, comps = curl.shape
     parts_here = out.shape[0]
+    fetched = [
+        (pieces_hbm, pieces),
+        (table_hbm, table),
+        (pattern_hbm, pattern),
+        (region_hbm, region_ids),
+        (law_hbm, law),
+        (source_hbm, source),
+    ]
+    small = [
+        pltpu.make_async_copy(src, dst, small_sems.at[i]) for i, (src, dst) in enumerate(fetched)
+    ]
+    blocks_in = [
+        pltpu.make_async_copy(curl_hbm.at[elem], curl.at[elem], curl_sems.at[elem])
+        for elem in range(tile_count)
+    ]
+    for copy in small + blocks_in:
+        copy.start()
     rank = lax.axis_index(GROUP)
+    sums[...] = jnp.zeros_like(sums)
+    small[0].wait()
     stacked = jnp.concatenate([window[...]] * 3, axis=0)
     samples = jnp.dot(pieces[...], stacked, preferred_element_type=jnp.float32)
     high = samples.astype(jnp.bfloat16)
     timed[:HALF, :] = high
     timed[HALF:, :] = (samples - high.astype(jnp.float32)).astype(jnp.bfloat16)
-    sums[...] = jnp.zeros_like(sums)
+    for copy in small[1:]:
+        copy.wait()
     lanes = lax.broadcasted_iota(jnp.int32, table.shape, 1)
     columns = [
         jnp.sum(
@@ -64,10 +104,11 @@
         for part in range(parts_here)
     ]
     for elem in range(tile_count):
-        places = [pattern[elem, link] for link in range(links)]
+        places = [pattern[link, elem] for link in range(links)]
         picked = jnp.concatenate(
             [timed[:, pl.ds(pl.multiple_of(place * tile, tile), tile)] for place in places], axis=1
         )
+        blocks_in[elem].wait()
         blocks = curl[elem].reshape(links * tile, comps)
         split = jnp.dot(picked, blocks, preferred_element_type=jnp.float32)
         density = split[:HALF] + split[HALF:]
@@ -94,27 +135,46 @@
     halo[:, tile:] = sums[tile_count + 1]
 
 
+def halo_kernel(own, from_right, from_left, out):
+    tile = from_left.shape[1]
+    out[...] = own[...]
+    out[:, :tile] += from_left[...]
+    out[:, -tile:] += from_right[...]
+
+
 def per_device(coeffs, curl_tiles, pattern, region_ids, material_law, source):
     parts_here = coeffs.shape[0]
     tile_count, links, tile, comps = curl_tiles.shape
-    parts = parts_here * lax.axis_size(GROUP)
+    group_size = lax.axis_size(GROUP)
+    parts = parts_here * group_size
     high, low = exchange(coeffs[:, :tile], coeffs[:, -tile:], "space")
-    window = lax.all_gather(
-        jnp.concatenate([low, coeffs, high], axis=1), GROUP, axis=0, tiled=True
-    )
+    block = jnp.concatenate([low, coeffs, high], axis=1)
+    window = lax.all_to_all(
+        jnp.broadcast_to(block[None], (group_size,) + block.shape), GROUP, 0, 0
+    ).reshape(parts, block.shape[1])
     table = half_table(parts)
-    vmem, smem = pl.BlockSpec(memory_space=pltpu.VMEM), pl.BlockSpec(memory_space=pltpu.SMEM)
+    pieces = bf16_pieces(table)
+    vmem, hbm = pl.BlockSpec(memory_space=pltpu.VMEM), pl.BlockSpec(memory_space=pltpu.HBM)
     own, halo = pl.pallas_call(
         shard_kernel,
         out_shape=(
             jax.ShapeDtypeStruct(source.shape, jnp.float32),
             jax.ShapeDtypeStruct((parts_here, 2 * tile), jnp.float32),
         ),
-        in_specs=[smem] * 3 + [vmem] * 5,
+        in_specs=[vmem] + [hbm] * 7,
         out_specs=(vmem, vmem),
         scratch_shapes=[
+            pltpu.SMEM((links, tile_count), jnp.int32),
+            pltpu.SMEM(region_ids.shape, jnp.int32),
+            pltpu.SMEM(material_law.shape, jnp.float32),
+            pltpu.VMEM(pieces.shape, jnp.bfloat16),
+            pltpu.VMEM(table.shape, jnp.float32),
+            pltpu.VMEM(source.shape, jnp.float32),
+            pltpu.VMEM(curl_tiles.shape, jnp.bfloat16),
             pltpu.VMEM((SAMPLES, (tile_count + 2) * tile), jnp.bfloat16),
             pltpu.VMEM((tile_count + 2, parts_here, tile), jnp.float32),
+            pltpu.SemaphoreType.DMA((6,)),
+            pltpu.SemaphoreType.DMA((tile_count,)),
         ],
         compiler_params=pltpu.CompilerParams(vmem_limit_bytes=32 * 1024 * 1024),
         cost_estimate=pl.CostEstimate(
@@ -124,17 +184,28 @@
         ),
         name="shard_residual",
     )(
-        pattern,
-        region_ids,
-        material_law,
         window,
-        jnp.asarray(bf16_pieces(table)),
-        jnp.asarray(table.astype(np.float32)),
-        curl_tiles,
-        source,
+        *[
+            pltpu.with_memory_space_constraint(operand, pltpu.HBM)
+            for operand in (
+                pattern.T,
+                region_ids,
+                material_law,
+                jnp.asarray(pieces),
+                jnp.asarray(table.astype(np.float32)),
+                source,
+                curl_tiles,
+            )
+        ],
     )
     from_right, from_left = exchange(halo[:, :tile], halo[:, tile:], "space")
-    return own.at[:, :tile].add(from_left).at[:, -tile:].add(from_right)
+    return pl.pallas_call(
+        halo_kernel,
+        out_shape=jax.ShapeDtypeStruct(source.shape, jnp.float32),
+        in_specs=[vmem] * 3,
+        out_specs=vmem,
+        name="halo_sum",
+    )(own, from_right, from_left)
 
 
 def solution(mesh):

time: 58.4 us -> 35.6 us (0.61)
  blocking collectives: 32.9 us -> 13.7 us
  local copies, waits for them, and re-layouts: 7.74 us -> 2 us
  Pallas kernels: 5.9 us -> 10.8 us
  other arithmetic: 4.59 us -> 0.72 us
  waiting for transfers between devices: 2.15 us -> 3.62 us
    all_gather x1 -> x0, blocking collectives: 32.9 us -> none  [per_device(): lax.all_gather(jnp.concatenate([low, coeffs, high], axis=1), GROUP, axis=...]
    all_to_all x0 -> x1, blocking collectives: none -> 13.7 us  [per_device(): lax.all_to_all(jnp.broadcast_to(block[None], (group_size,) + block.shape)...]
    unnamed x14 -> x2, local copies, waits for them, and re-layouts: 7.06 us -> 0.59 us
    pallas_call x1, Pallas kernels: 5.9 us -> 9.46 us  [per_device(): pl.pallas_call(shard_kernel, out_shape=(jax.ShapeDtypeStruct(source.shape...]
    scatter-add x2 -> x0, other arithmetic: 3.17 us -> none  [per_device(): return own.at[:, :tile].add(from_left).at[:, -tile:].add(from_right)]
    ppermute x2, waiting for transfers between devices: 2.15 us -> 3.62 us  [exchange(): lax.ppermute(jnp.concatenate([to_left, to_right], axis=1), axis, ring(axi...]
    pallas_call x0 -> x1, Pallas kernels: none -> 1.34 us  [per_device(): pl.pallas_call(halo_kernel, out_shape=jax.ShapeDtypeStruct(source.shape,...]
    concatenate x0 -> x1, other arithmetic: none -> 0.71 us  [per_device(): block = jnp.concatenate([low, coeffs, high], axis=1)]
  transfers between devices with their start and end apart: 2 -> 2, of which waited for: 2 -> 2; matrix products, arithmetic and copies ran while one was open for 3% -> 0% of each run, Pallas kernels for 0% -> 0%
where the time goes in v2:
time: 35.6 us; the launch traced here: 35.4 us
  blocking collectives  13.7 us (38%)
  Pallas kernels  10.8 us (30%)
  starting transfers between devices  4.54 us (13%)
  waiting for transfers between devices  3.62 us (10%)
  local copies, waits for them, and re-layouts  2 us (6%)
  other arithmetic  0.72 us (2%)
    all_to_all x1, blocking collectives, per_device(): lax.all_to_all(jnp.broadcast_to(block[None], (group_size,) + block.shape)...  13.7 us
    pallas_call x1, Pallas kernels, per_device(): pl.pallas_call(shard_kernel, out_shape=(jax.ShapeDtypeStruct(source.shape...  9.46 us
    ppermute x2, starting transfers between devices, exchange(): lax.ppermute(jnp.concatenate([to_left, to_right], axis=1), axis, ring(axi...  4.54 us
    ppermute x2, waiting for transfers between devices, exchange(): lax.ppermute(jnp.concatenate([to_left, to_right], axis=1), axis, ring(axi...  3.62 us
    pallas_call x1, Pallas kernels, per_device(): pl.pallas_call(halo_kernel, out_shape=jax.ShapeDtypeStruct(source.shape,...  1.34 us
  transfers between devices with their start and end apart: 2, of which 2 were waited for; matrix products, arithmetic and copies ran while one was open for 0% of the time, Pallas kernels for 0%

profile of v2, /device:TPU:0, one launch (start us, length us, event | category | flops | bytes accessed | tf_op | source)
XLA Modules:
  0.0 35.4 jit_solution(3639823645917279410)
XLA Ops:
  0.0 0.7 %fusion = (bf16[2,128]{1,0:T(2,128)(2,1)S(1)}, bf16[2,128]{1,0:T(2,128)(2,1)S(1)}) fusion(bf16[2,2048]{1,0:T(2,128)(2,1)} %param.8), kind=kLoop, calls=%fused_computation.2 | loop fusion | bytes 2048 | tf_op jit(solution)/shard_map/slice | solution.py:150
  0.7 3.0 %collective-permute-start = (bf16[2,256]{1,0:T(2,128)(2,1)S(1)}, bf16[2,256]{1,0:T(2,128)(2,1)S(1)}, u32[]{:S(2)}, u32[]{:S(2)}) collective-permute-start(bf16[2,256]{1,0:T(2,128)(2,1)S(1)} %pad_maximum_fusion.1), channel_id=1, source_target_pairs={{0,4},{4,0},{1,5},{5,1},{2,6},{6,2},{3,7},{7,3},{8,12},{12,8},{9,1... | collective-permute-start | bytes 3080 | tf_op jit(solution)/shard_map/ppermute | solution.py:42
  3.7 1.5 %collective-permute-done = bf16[2,256]{1,0:T(2,128)(2,1)S(1)} collective-permute-done((bf16[2,256]{1,0:T(2,128)(2,1)S(1)}, bf16[2,256]{1,0:T(2,128)(2,1)S(1)}, u32[]{:S(2)}, u32[]{:S(2)}) %collective-permute-start) | collective-permute-done | bytes 1056 | tf_op jit(solution)/shard_map/ppermute | solution.py:42
  5.3 0.7 %pad_maximum_fusion = bf16[2,2304]{1,0:T(2,128)(2,1)S(1)} fusion(bf16[2,128]{1,0:T(2,128)(2,1)S(1)} %get-tuple-element.14, bf16[2,2048]{1,0:T(2,128)(2,1)} %param.8, bf16[2,128]{1,0:T(2,128)(2,1)S(1)} %get-tuple-element.13), kind=kLoop, calls=%fused_computation | loop fusion | flops 27648 | bytes 18432 | tf_op jit(solution)/shard_map/concatenate | solution.py:151
  6.0 0.1 broadcast_in_dim.2
  6.1 13.7 %all_to_all.5 = bf16[16,2,2304]{2,1,0:T(2,128)(2,1)S(1)} all-to-all(bf16[16,2,2304]{2,1,0:T(2,128)(2,1)S(1)} %broadcast_in_dim.2), channel_id=1, replica_groups=mesh['harm'=4,'space'=2,'samp'=4] {'harm','samp'}, dimensions={0} | all-to-all | bytes 294912 | tf_op jit(solution)/shard_map/all_to_all | solution.py:152
  19.8 0.1 reshape.4.window
  19.8 9.5 %shard_residual.1 = (f32[2,2048]{1,0:T(2,128)S(1)}, f32[2,256]{1,0:T(2,128)S(1)}) custom-call(bf16[32,2304]{1,0:T(8,128)(2,1)S(1)} %reshape.4.window, s32[4,16]{1,0:T(4,128)} %bitcast.1, s32[16]{0:T(128)} %region_hbm.1, f32[3,4]{1,0:T(4,128)} %law_hbm.1, bf16[32,96]{1,0:T(8,128)(2,1)} %constant.4.clone.pieces_hbm, f32[32,32]{1,0:T(8,128)} %constant.5.clone.table_hbm, ...), custom_call_target="tpu_custom_call" | custom-call | flops 805306368 | bytes 6291456 | tf_op jit(solution)/shard_map/shard_residual/pallas_call | solution.py:158
  29.3 0.0 copy-start
  29.3 0.6 %copy-done = f32[2,2048]{1,0:T(2,128)} copy-done((f32[2,2048]{1,0:T(2,128)}, f32[2,2048]{1,0:T(2,128)S(1)}, u32[]{:S(2)}) %copy-start) | copy-done | bytes 16408
  29.9 1.5 %collective-permute-start.1 = (f32[2,256]{1,0:T(2,128)S(1)}, f32[2,256]{1,0:T(2,128)S(1)}, u32[]{:S(2)}, u32[]{:S(2)}) collective-permute-start(f32[2,256]{1,0:T(2,128)S(1)} %get-tuple-element.8), channel_id=1, source_target_pairs={{0,4},{4,0},{1,5},{5,1},{2,6},{6,2},{3,7},{7,3},{8,12},{12,8},{9,1... | collective-permute-start | bytes 6152 | tf_op jit(solution)/shard_map/ppermute | solution.py:42
  31.4 2.1 %collective-permute-done.1 = f32[2,256]{1,0:T(2,128)S(1)} collective-permute-done((f32[2,256]{1,0:T(2,128)S(1)}, f32[2,256]{1,0:T(2,128)S(1)}, u32[]{:S(2)}, u32[]{:S(2)}) %collective-permute-start.1) | collective-permute-done | bytes 2080 | tf_op jit(solution)/shard_map/ppermute | solution.py:42
  33.5 0.6 %fusion.1 = (f32[2,128]{1,0:T(2,128)}, f32[2,128]{1,0:T(2,128)}) fusion(f32[2,256]{1,0:T(2,128)S(1)} %collective-permute-done.1), kind=kLoop, calls=%fused_computation.3 | loop fusion | bytes 4096 | tf_op jit(solution)/shard_map/slice | solution.py:43
  34.1 1.3 %halo_sum.1 = f32[2,2048]{1,0:T(2,128)} custom-call(f32[2,2048]{1,0:T(2,128)} %copy-done, f32[2,128]{1,0:T(2,128)} %get-tuple-element.12.from_right, f32[2,128]{1,0:T(2,128)} %get-tuple-element.11.from_left), custom_call_target="tpu_custom_call" | custom-call | tf_op jit(solution)/shard_map/halo_sum/pallas_call | solution.py:202
  (2 shorter events, 0.0 us)
Async XLA Ops:
  0.7 4.6 %collective-permute-start = (bf16[2,256]{1,0:T(2,128)(2,1)S(1)}, bf16[2,256]{1,0:T(2,128)(2,1)S(1)}, u32[]{:S(2)}, u32[]{:S(2)}) collective-permute-start(bf16[2,256]{1,0:T(2,128)(2,1)S(1)} %pad_maximum_fusion.1), channel_id=1, source_target_pairs={{0,4},{4,0},{1,5},{5,1},{2,6},{6,2},{3,7},{7,3},{8,12},{12,8},{9,1... | collective-permute-start | bytes 3080 | tf_op jit(solution)/shard_map/ppermute | solution.py:42
  29.3 0.6 %copy-start = (f32[2,2048]{1,0:T(2,128)}, f32[2,2048]{1,0:T(2,128)S(1)}, u32[]{:S(2)}) copy-start(f32[2,2048]{1,0:T(2,128)S(1)} %get-tuple-element.7.own) | copy-start | bytes 49156
  29.9 3.6 %collective-permute-start.1 = (f32[2,256]{1,0:T(2,128)S(1)}, f32[2,256]{1,0:T(2,128)S(1)}, u32[]{:S(2)}, u32[]{:S(2)}) collective-permute-start(f32[2,256]{1,0:T(2,128)S(1)} %get-tuple-element.8), channel_id=1, source_target_pairs={{0,4},{4,0},{1,5},{5,1},{2,6},{6,2},{3,7},{7,3},{8,12},{12,8},{9,1... | collective-permute-start | bytes 6152 | tf_op jit(solution)/shard_map/ppermute | solution.py:42

commit v3 on v2

v3 whole, which is shorter than its diff:
```python
import math

import jax
import jax.numpy as jnp
import ml_dtypes
import numpy as np
from jax import lax
from jax.experimental import pallas as pl
from jax.experimental.pallas import tpu as pltpu
from jax.sharding import PartitionSpec as P

SAMPLES = 64
HALF = SAMPLES // 2
GROUP = ("harm", "samp")


def half_table(parts):
    sample_ids = np.arange(HALF)[:, None]
    part_ids = np.arange(parts)[None, :]
    phase = ((2 * (part_ids // 2) + 1) * sample_ids % SAMPLES) * (2.0 * math.pi / SAMPLES)
    return np.where(part_ids % 2 == 0, np.cos(phase), np.sin(phase))


def bf16_pieces(table):
    rest = table
    pieces = []
    for _ in range(3):
        piece = rest.astype(ml_dtypes.bfloat16)
        pieces.append(piece)
        rest = rest - piece.astype(np.float64)
    return np.concatenate(pieces, axis=-1)


def arrival_order(harm, samp, parts_here):
    order = np.empty((harm * samp, harm * samp * parts_here), np.int32)
    for h in range(harm):
        for s in range(samp):
            ranks = [
                (h - j) % harm * samp + (s - k) % samp for j in range(harm) for k in range(samp)
            ]
            order[h * samp + s] = (
                np.array(ranks)[:, None] * parts_here + np.arange(parts_here)
            ).reshape(-1)
    return order


def shifted(array, axes, by):
    sizes = [lax.axis_size(axis) for axis in axes]
    places = list(np.ndindex(*sizes))
    pairs = []
    for place in places:
        target = tuple((p + step) % size for p, step, size in zip(place, by, sizes))
        pairs.append((places.index(place), places.index(target)))
    return lax.ppermute(array, axes, pairs)


def from_neighbours(edges, samp_step):
    axes, tile = ("space", "samp"), edges.shape[1] // 2
    if lax.axis_size("space") == 2:
        return shifted(edges, axes, (1, samp_step))
    return jnp.concatenate(
        [
            shifted(edges[:, :tile], axes, (-1, samp_step)),
            shifted(edges[:, tile:], axes, (1, samp_step)),
        ],
        axis=1,
    )


def fetch_kernel(curl_hbm, curl, sem):
    copy = pltpu.make_async_copy(curl_hbm.at[: curl.shape[0]], curl, sem)
    copy.start()
    copy.wait()


def shard_kernel(
    window,
    first_curl,
    curl_hbm,
    pattern_hbm,
    region_hbm,
    law_hbm,
    pieces_hbm,
    table_hbm,
    source_hbm,
    out,
    halo,
    pattern,
    region_ids,
    law,
    pieces,
    table,
    source,
    later_curl,
    timed,
    sums,
    small_sems,
    curl_sem,
):
    tile_count, links, tile, comps = curl_hbm.shape
    early = first_curl.shape[0]
    parts_here = out.shape[0]
    rank = lax.axis_index(GROUP)
    fetched = [
        (pieces_hbm.at[rank], pieces),
        (table_hbm.at[rank], table),
        (pattern_hbm, pattern),
        (region_hbm, region_ids),
        (law_hbm, law),
        (source_hbm, source),
    ]
    small = [
        pltpu.make_async_copy(src, dst, small_sems.at[i]) for i, (src, dst) in enumerate(fetched)
    ]
    rest = pltpu.make_async_copy(curl_hbm.at[early:], later_curl, curl_sem)
    for copy in small + [rest]:
        copy.start()
    sums[...] = jnp.zeros_like(sums)
    for copy in small:
        copy.wait()
    stacked = jnp.concatenate([window[...]] * 3, axis=0)
    samples = jnp.dot(pieces[...], stacked, preferred_element_type=jnp.float32)
    high = samples.astype(jnp.bfloat16)
    timed[:HALF, :] = high
    timed[HALF:, :] = (samples - high.astype(jnp.float32)).astype(jnp.bfloat16)
    columns = [
        jnp.broadcast_to(table[:, part : part + 1], (HALF, comps)) for part in range(parts_here)
    ]
    for elem in range(tile_count):
        places = [pattern[link, elem] for link in range(links)]
        picked = jnp.concatenate(
            [timed[:, pl.ds(pl.multiple_of(place * tile, tile), tile)] for place in places], axis=1
        )
        if elem == early:
            rest.wait()
        curl = first_curl[elem] if elem < early else later_curl[elem - early]
        blocks = curl.reshape(links * tile, comps)
        split = jnp.dot(picked, blocks, preferred_element_type=jnp.float32)
        density = split[:HALF] + split[HALF:]
        comp = [density[:, c * tile : (c + 1) * tile] for c in range(comps // tile)]
        square = comp[0] * comp[0]
        for c in comp[1:]:
            square = square + c * c
        region = region_ids[elem]
        reluct = law[0, region] + law[2, region] * square / (square + law[1, region])
        field = jnp.concatenate([reluct * c for c in comp], axis=1)
        projected = jnp.concatenate(
            [jnp.sum(column * field, axis=0, keepdims=True) for column in columns], axis=0
        )
        projected = (projected * (4.0 / SAMPLES)).astype(jnp.bfloat16)
        contrib = lax.dot_general(
            projected, blocks, (((1,), (1,)), ((), ())), preferred_element_type=jnp.float32
        )
        for link, place in enumerate(places):
            sums[place] += contrib[:, link * tile : (link + 1) * tile]
    for w in range(tile_count):
        at = slice(w * tile, (w + 1) * tile)
        out[:, at] = sums[w + 1] - source[:, at]
    halo[:, :tile] = sums[0]
    halo[:, tile:] = sums[tile_count + 1]


def halo_kernel(own, received, out):
    tile = received.shape[1] // 2
    out[...] = own[...]
    out[:, :tile] += received[:, tile:]
    out[:, -tile:] += received[:, :tile]


def per_device(coeffs, curl_tiles, pattern, region_ids, material_law, source):
    parts_here = coeffs.shape[0]
    tile_count, links, tile, comps = curl_tiles.shape
    harm, samp = lax.axis_size("harm"), lax.axis_size("samp")
    parts = parts_here * harm * samp
    order = arrival_order(harm, samp, parts_here)
    table = half_table(parts)[:, order].transpose(1, 0, 2)
    pieces = bf16_pieces(table)
    own_columns = table[:, :, :parts_here].astype(np.float32)
    vmem, hbm = pl.BlockSpec(memory_space=pltpu.VMEM), pl.BlockSpec(memory_space=pltpu.HBM)

    edges = jnp.concatenate([coeffs[:, :tile], coeffs[:, -tile:]], axis=1)
    blocks = []
    for k in range(samp):
        beside = from_neighbours(edges, k)
        block = shifted(coeffs, ("samp",), (k,)) if k else coeffs
        blocks.append(jnp.concatenate([beside[:, tile:], block, beside[:, :tile]], axis=1))
    curl_hbm = pltpu.with_memory_space_constraint(curl_tiles, pltpu.HBM)
    early = 3 * tile_count // 8
    first_curl = pl.pallas_call(
        fetch_kernel,
        out_shape=pltpu.VMEM((early,) + curl_tiles.shape[1:], curl_tiles.dtype),
        in_specs=[hbm],
        out_specs=vmem,
        scratch_shapes=[pltpu.SemaphoreType.DMA],
        compiler_params=pltpu.CompilerParams(vmem_limit_bytes=16 * 1024 * 1024),
        cost_estimate=pl.CostEstimate(
            flops=0, bytes_accessed=4 * early * links * tile * comps, transcendentals=0
        ),
        name="fetch_curl",
    )(curl_hbm)
    near = jnp.stack(blocks)
    far = [near] + [shifted(near, ("harm",), (j,)) for j in range(1, harm)]
    window = jnp.concatenate(far, axis=0).reshape(parts, near.shape[-1])
    own, halo = pl.pallas_call(
        shard_kernel,
        out_shape=(
            pltpu.VMEM(source.shape, jnp.float32),
            pltpu.VMEM((parts_here, 2 * tile), jnp.float32),
        ),
        in_specs=[vmem] * 2 + [hbm] * 7,
        out_specs=(vmem, vmem),
        scratch_shapes=[
            pltpu.SMEM((links, tile_count), jnp.int32),
            pltpu.SMEM(region_ids.shape, jnp.int32),
            pltpu.SMEM(material_law.shape, jnp.float32),
            pltpu.VMEM(pieces.shape[1:], jnp.bfloat16),
            pltpu.VMEM(own_columns.shape[1:], jnp.float32),
            pltpu.VMEM(source.shape, jnp.float32),
            pltpu.VMEM((tile_count - early,) + curl_tiles.shape[1:], curl_tiles.dtype),
            pltpu.VMEM((SAMPLES, (tile_count + 2) * tile), jnp.bfloat16),
            pltpu.VMEM((tile_count + 2, parts_here, tile), jnp.float32),
            pltpu.SemaphoreType.DMA((6,)),
            pltpu.SemaphoreType.DMA,
        ],
        compiler_params=pltpu.CompilerParams(vmem_limit_bytes=32 * 1024 * 1024),
        cost_estimate=pl.CostEstimate(
            flops=4 * SAMPLES * tile_count * links * tile * comps,
            bytes_accessed=2 * curl_tiles.size,
            transcendentals=0,
        ),
        name="shard_residual",
    )(
        window,
        pltpu.with_memory_space_constraint(first_curl, pltpu.VMEM),
        curl_hbm,
        *[
            pltpu.with_memory_space_constraint(operand, pltpu.HBM)
            for operand in (
                pattern.T,
                region_ids,
                material_law,
                jnp.asarray(pieces),
                jnp.asarray(own_columns),
                source,
            )
        ],
    )
    return pl.pallas_call(
        halo_kernel,
        out_shape=jax.ShapeDtypeStruct(source.shape, jnp.float32),
        in_specs=[vmem] * 2,
        out_specs=vmem,
        compiler_params=pltpu.CompilerParams(vmem_limit_bytes=16 * 1024 * 1024),
        name="halo_sum",
    )(pltpu.with_memory_space_constraint(own, pltpu.VMEM), from_neighbours(halo, 0))


def solution(mesh):
    placed = (
        P(GROUP, "space"),
        P("space", None, None, None),
        P("space", None),
        P("space"),
        P(),
        P(GROUP, "space"),
    )
    return jax.shard_map(
        per_device,
        mesh=mesh,
        in_specs=placed,
        out_specs=P(GROUP, "space"),
        check_vma=False,
    )
```

time: 35.6 us -> 36.1 us (1.014)
  blocking collectives: 13.7 us -> 0 us
  starting transfers between devices: 4.54 us -> 16 us
  waiting for transfers between devices: 3.62 us -> 9.54 us
  Pallas kernels: 10.8 us -> 9.11 us
  local copies, waits for them, and re-layouts: 2 us -> 0.92 us
  other arithmetic: 0.72 us -> 0.19 us
    all_to_all x1 -> x0, blocking collectives: 13.7 us -> none  [per_device(): lax.all_to_all(jnp.broadcast_to(block[None], (group_size,) + block.shape)...]
    ppermute x2 -> x11, starting transfers between devices: 4.54 us -> 16 us  [shifted(): return lax.ppermute(array, axes, pairs)]
    ppermute x2 -> x11, waiting for transfers between devices: 3.62 us -> 9.54 us  [shifted(): return lax.ppermute(array, axes, pairs)]
    pallas_call x1 -> x2, Pallas kernels: 9.46 us -> 8.49 us  [the longest x1 6.82 us: per_device(): pl.pallas_call(shard_kernel, out_shape=(pltpu.VMEM(source.shape, jnp.floa...]
    pallas_call x1, Pallas kernels: 1.34 us -> 0.61 us  [per_device(): pl.pallas_call(halo_kernel, out_shape=jax.ShapeDtypeStruct(source.shape,...]
    concatenate x2 -> x1, other arithmetic: 0.72 us -> 0.01 us  [per_device(): edges = jnp.concatenate([coeffs[:, :tile], coeffs[:, -tile:]], axis=1)]
    unnamed x2 -> x4, local copies, waits for them, and re-layouts: 0.59 us -> 0.08 us
    slice x3 -> x5, local copies, waits for them, and re-layouts: 1.26 us -> 0.75 us  [the longest x1 0.73 us: per_device(): edges = jnp.concatenate([coeffs[:, :tile], coeffs[:, -tile:]], axis=1)]
  transfers between devices with their start and end apart: 2 -> 11, of which waited for: 2 -> 4; matrix products, arithmetic and copies ran while one was open for 0% -> 1% of each run, Pallas kernels for 0% -> 5%
where the time goes in v3:
time: 36.1 us; the launch traced here: 35.9 us
  starting transfers between devices  16 us (44%)
  waiting for transfers between devices  9.54 us (26%)
  Pallas kernels  9.11 us (25%)
  local copies, waits for them, and re-layouts  0.92 us (3%)
    ppermute x11, starting transfers between devices, shifted(): return lax.ppermute(array, axes, pairs)  16 us
    ppermute x11, waiting for transfers between devices, shifted(): return lax.ppermute(array, axes, pairs)  9.54 us
    pallas_call x1, Pallas kernels, per_device(): pl.pallas_call(shard_kernel, out_shape=(pltpu.VMEM(source.shape, jnp.floa...  6.82 us
    pallas_call x1, Pallas kernels, per_device(): pl.pallas_call(fetch_kernel, out_shape=pltpu.VMEM((early,) + curl_tiles.s...  1.67 us
    slice x1, local copies, waits for them, and re-layouts, per_device(): edges = jnp.concatenate([coeffs[:, :tile], coeffs[:, -tile:]], axis=1)  0.73 us
  transfers between devices with their start and end apart: 11, of which 4 were waited for; matrix products, arithmetic and copies ran while one was open for 1% of the time, Pallas kernels for 5%

profile of v3, /device:TPU:0, one launch (start us, length us, event | category | flops | bytes accessed | tf_op | source)
XLA Modules:
  0.0 35.9 jit_solution(9710521193845674500)
XLA Ops:
  0.0 0.0 copy-start
  0.0 0.7 %fusion = (bf16[2,128]{1,0:T(2,128)(2,1)S(1)}, bf16[2,128]{1,0:T(2,128)(2,1)S(1)}) fusion(bf16[2,2048]{1,0:T(2,128)(2,1)} %param.8), kind=kLoop, calls=%fused_computation.13 | loop fusion | bytes 2048 | tf_op jit(solution)/shard_map/slice | solution.py:181
  0.7 3.0 %collective-permute-start = (bf16[2,256]{1,0:T(2,128)(2,1)S(1)}, bf16[2,256]{1,0:T(2,128)(2,1)S(1)}, u32[]{:S(2)}, u32[]{:S(2)}) collective-permute-start(bf16[2,256]{1,0:T(2,128)(2,1)S(1)} %pad_maximum_fusion.1), channel_id=1, source_target_pairs={{0,4},{1,5},{2,6},{3,7},{4,0},{5,1},{6,2},{7,3},{8,12},{9,13},{10,... | collective-permute-start | bytes 3080 | tf_op jit(solution)/shard_map/ppermute | solution.py:54
  3.8 3.5 %collective-permute-start.5 = (bf16[2,256]{1,0:T(2,128)(2,1)S(1)}, bf16[2,256]{1,0:T(2,128)(2,1)S(1)}, u32[]{:S(2)}, u32[]{:S(2)}) collective-permute-start(bf16[2,256]{1,0:T(2,128)(2,1)S(1)} %pad_maximum_fusion.1), channel_id=1, source_target_pairs={{0,7},{1,4},{2,5},{3,6},{4,3},{5,0},{6,1},{7,2},{8,15},{9,12},{10,... | collective-permute-start | bytes 3080 | tf_op jit(solution)/shard_map/ppermute | solution.py:54
  7.3 0.4 %collective-permute-start.3 = (bf16[2,256]{1,0:T(2,128)(2,1)S(1)}, bf16[2,256]{1,0:T(2,128)(2,1)S(1)}, u32[]{:S(2)}, u32[]{:S(2)}) collective-permute-start(bf16[2,256]{1,0:T(2,128)(2,1)S(1)} %pad_maximum_fusion.1), channel_id=1, source_target_pairs={{0,6},{1,7},{2,4},{3,5},{4,2},{5,3},{6,0},{7,1},{8,14},{9,15},{10,... | collective-permute-start | bytes 3080 | tf_op jit(solution)/shard_map/ppermute | solution.py:54
  7.7 1.5 %collective-permute-start.1 = (bf16[2,256]{1,0:T(2,128)(2,1)S(1)}, bf16[2,256]{1,0:T(2,128)(2,1)S(1)}, u32[]{:S(2)}, u32[]{:S(2)}) collective-permute-start(bf16[2,256]{1,0:T(2,128)(2,1)S(1)} %pad_maximum_fusion.1), channel_id=1, source_target_pairs={{0,5},{1,6},{2,7},{3,4},{4,1},{5,2},{6,3},{7,0},{8,13},{9,14},{10,... | collective-permute-start | bytes 3080 | tf_op jit(solution)/shard_map/ppermute | solution.py:54
  9.2 2.5 %collective-permute-start.2 = (bf16[2,2048]{1,0:T(2,128)(2,1)}, bf16[2,2048]{1,0:T(2,128)(2,1)S(1)}, u32[]{:S(2)}, u32[]{:S(2)}) collective-permute-start(bf16[2,2048]{1,0:T(2,128)(2,1)} %param.8), channel_id=1, source_target_pairs={{0,1},{1,2},{2,3},{3,0},{4,5},{5,6},{6,7},{7,4},{8,9},{9,10},{10,1... | collective-permute-start | bytes 24584 | tf_op jit(solution)/shard_map/ppermute | solution.py:54
  11.7 1.7 %fetch_curl.1.first_curl = bf16[6,4,128,384]{3,2,1,0:T(8,128)(2,1)S(1)} custom-call(bf16[16,4,128,384]{3,2,1,0:T(8,128)(2,1)} %curl_hbm.3), custom_call_target="tpu_custom_call" | custom-call | bytes 4718592 | tf_op jit(solution)/shard_map/fetch_curl/pallas_call | solution.py:189
  13.4 0.0 collective-permute-done
  13.4 0.0 copy-done
  13.4 1.4 %collective-permute-start.6 = (bf16[2,2048]{1,0:T(2,128)(2,1)S(1)}, bf16[2,2048]{1,0:T(2,128)(2,1)S(1)}, u32[]{:S(2)}, u32[]{:S(2)}) collective-permute-start(bf16[2,2048]{1,0:T(2,128)(2,1)S(1)} %copy-done), channel_id=1, source_target_pairs={{0,3},{1,0},{2,1},{3,2},{4,7},{5,4},{6,5},{7,6},{8,11},{9,8},{10,9... | collective-permute-start | bytes 24584 | tf_op jit(solution)/shard_map/ppermute | solution.py:54
  14.9 0.0 collective-permute-done.5
  14.9 0.2 collective-permute-start.4
  15.1 0.0 collective-permute-done.3
  15.1 0.0 collective-permute-done.1
  15.1 0.0 collective-permute-done.2
  15.2 1.9 %collective-permute-done.6 = bf16[2,2048]{1,0:T(2,128)(2,1)S(1)} collective-permute-done((bf16[2,2048]{1,0:T(2,128)(2,1)S(1)}, bf16[2,2048]{1,0:T(2,128)(2,1)S(1)}, u32[]{:S(2)}, u32[]{:S(2)}) %collective-permute-start.6) | collective-permute-done | bytes 8224 | tf_op jit(solution)/shard_map/ppermute | solution.py:54
  17.1 2.4 %collective-permute-done.4 = bf16[2,2048]{1,0:T(2,128)(2,1)S(1)} collective-permute-done((bf16[2,2048]{1,0:T(2,128)(2,1)S(1)}, bf16[2,2048]{1,0:T(2,128)(2,1)S(1)}, u32[]{:S(2)}, u32[]{:S(2)}) %collective-permute-start.4) | collective-permute-done | bytes 8224 | tf_op jit(solution)/shard_map/ppermute | solution.py:54
  19.5 0.1 pad_maximum_fusion
  19.6 0.1 collective-permute-start.9
  19.6 1.6 %collective-permute-start.8 = (bf16[4,2,2304]{2,1,0:T(2,128)(2,1)S(1)}, bf16[4,2,2304]{2,1,0:T(2,128)(2,1)S(1)}, u32[]{:S(2)}, u32[]{:S(2)}) collective-permute-start(bf16[4,2,2304]{2,1,0:T(2,128)(2,1)S(1)} %pad_maximum_fusion), channel_id=1, source_target_pairs={{0,16},{8,24},{16,0},{24,8},{1,17},{9,25},{17,1},{25,9},{2,18},{10... | collective-permute-start | bytes 110600 | tf_op jit(solution)/shard_map/ppermute | solution.py:54
  21.2 0.2 collective-permute-start.7
  21.4 3.2 %collective-permute-done.7 = bf16[4,2,2304]{2,1,0:T(2,128)(2,1)S(1)} collective-permute-done((bf16[4,2,2304]{2,1,0:T(2,128)(2,1)S(1)}, bf16[4,2,2304]{2,1,0:T(2,128)(2,1)S(1)}, u32[]{:S(2)}, u32[]{:S(2)}) %collective-permute-start.7) | collective-permute-done | bytes 36896 | tf_op jit(solution)/shard_map/ppermute | solution.py:54
  24.6 0.0 collective-permute-done.8
  24.7 0.0 collective-permute-done.9
  24.7 0.1 reshape.3.window
  24.8 6.8 %shard_residual.1 = (f32[2,2048]{1,0:T(2,128)S(1)}, f32[2,256]{1,0:T(2,128)S(1)}) custom-call(bf16[32,2304]{1,0:T(8,128)(2,1)S(1)} %reshape.3.window, bf16[6,4,128,384]{3,2,1,0:T(8,128)(2,1)S(1)} %fetch_curl.1.first_curl, bf16[16,4,128,384]{3,2,1,0:T(8,128)(2,1)} %curl_hbm.3, s32[4,16]{1,0:T(4,128)} %bitcast.17, s32[16]{0:T(128)} %region_hbm.1, ...), custom_call_target="tpu_custom_call" | custom-call | flops 805306368 | bytes 6291456 | tf_op jit(solution)/shard_map/shard_residual/pallas_call | solution.py:204
  31.6 1.6 %collective-permute-start.10 = (f32[2,256]{1,0:T(2,128)S(1)}, f32[2,256]{1,0:T(2,128)S(1)}, u32[]{:S(2)}, u32[]{:S(2)}) collective-permute-start(f32[2,256]{1,0:T(2,128)S(1)} %get-tuple-element.8), channel_id=1, source_target_pairs={{0,4},{1,5},{2,6},{3,7},{4,0},{5,1},{6,2},{7,3},{8,12},{9,13},{10,... | collective-permute-start | bytes 6152 | tf_op jit(solution)/shard_map/ppermute | solution.py:54
  33.2 2.1 %collective-permute-done.10.received = f32[2,256]{1,0:T(2,128)S(1)} collective-permute-done((f32[2,256]{1,0:T(2,128)S(1)}, f32[2,256]{1,0:T(2,128)S(1)}, u32[]{:S(2)}, u32[]{:S(2)}) %collective-permute-start.10) | collective-permute-done | bytes 2080 | tf_op jit(solution)/shard_map/ppermute | solution.py:54
  35.3 0.6 %halo_sum.1 = f32[2,2048]{1,0:T(2,128)} custom-call(f32[2,2048]{1,0:T(2,128)S(1)} %get-tuple-element.7.own, f32[2,256]{1,0:T(2,128)S(1)} %collective-permute-done.10.received), custom_call_target="tpu_custom_call" | custom-call | tf_op jit(solution)/shard_map/halo_sum/pallas_call | solution.py:248
  (16 shorter events, 0.3 us)
Async XLA Ops:
  0.0 13.4 %copy-start = (bf16[2,2048]{1,0:T(2,128)(2,1)S(1)}, bf16[2,2048]{1,0:T(2,128)(2,1)}, u32[]{:S(2)}) copy-start(bf16[2,2048]{1,0:T(2,128)(2,1)} %param.8) | copy-start | bytes 24580
  0.7 12.6 %collective-permute-start = (bf16[2,256]{1,0:T(2,128)(2,1)S(1)}, bf16[2,256]{1,0:T(2,128)(2,1)S(1)}, u32[]{:S(2)}, u32[]{:S(2)}) collective-permute-start(bf16[2,256]{1,0:T(2,128)(2,1)S(1)} %pad_maximum_fusion.1), channel_id=1, source_target_pairs={{0,4},{1,5},{2,6},{3,7},{4,0},{5,1},{6,2},{7,3},{8,12},{9,13},{10,... | collective-permute-start | bytes 3080 | tf_op jit(solution)/shard_map/ppermute | solution.py:54
  3.8 11.1 %collective-permute-start.5 = (bf16[2,256]{1,0:T(2,128)(2,1)S(1)}, bf16[2,256]{1,0:T(2,128)(2,1)S(1)}, u32[]{:S(2)}, u32[]{:S(2)}) collective-permute-start(bf16[2,256]{1,0:T(2,128)(2,1)S(1)} %pad_maximum_fusion.1), channel_id=1, source_target_pairs={{0,7},{1,4},{2,5},{3,6},{4,3},{5,0},{6,1},{7,2},{8,15},{9,12},{10,... | collective-permute-start | bytes 3080 | tf_op jit(solution)/shard_map/ppermute | solution.py:54
  7.3 7.8 %collective-permute-start.3 = (bf16[2,256]{1,0:T(2,128)(2,1)S(1)}, bf16[2,256]{1,0:T(2,128)(2,1)S(1)}, u32[]{:S(2)}, u32[]{:S(2)}) collective-permute-start(bf16[2,256]{1,0:T(2,128)(2,1)S(1)} %pad_maximum_fusion.1), channel_id=1, source_target_pairs={{0,6},{1,7},{2,4},{3,5},{4,2},{5,3},{6,0},{7,1},{8,14},{9,15},{10,... | collective-permute-start | bytes 3080 | tf_op jit(solution)/shard_map/ppermute | solution.py:54
  7.7 7.4 %collective-permute-start.1 = (bf16[2,256]{1,0:T(2,128)(2,1)S(1)}, bf16[2,256]{1,0:T(2,128)(2,1)S(1)}, u32[]{:S(2)}, u32[]{:S(2)}) collective-permute-start(bf16[2,256]{1,0:T(2,128)(2,1)S(1)} %pad_maximum_fusion.1), channel_id=1, source_target_pairs={{0,5},{1,6},{2,7},{3,4},{4,1},{5,2},{6,3},{7,0},{8,13},{9,14},{10,... | collective-permute-start | bytes 3080 | tf_op jit(solution)/shard_map/ppermute | solution.py:54
  9.2 5.9 %collective-permute-start.2 = (bf16[2,2048]{1,0:T(2,128)(2,1)}, bf16[2,2048]{1,0:T(2,128)(2,1)S(1)}, u32[]{:S(2)}, u32[]{:S(2)}) collective-permute-start(bf16[2,2048]{1,0:T(2,128)(2,1)} %param.8), channel_id=1, source_target_pairs={{0,1},{1,2},{2,3},{3,0},{4,5},{5,6},{6,7},{7,4},{8,9},{9,10},{10,1... | collective-permute-start | bytes 24584 | tf_op jit(solution)/shard_map/ppermute | solution.py:54
  13.4 3.7 %collective-permute-start.6 = (bf16[2,2048]{1,0:T(2,128)(2,1)S(1)}, bf16[2,2048]{1,0:T(2,128)(2,1)S(1)}, u32[]{:S(2)}, u32[]{:S(2)}) collective-permute-start(bf16[2,2048]{1,0:T(2,128)(2,1)S(1)} %copy-done), channel_id=1, source_target_pairs={{0,3},{1,0},{2,1},{3,2},{4,7},{5,4},{6,5},{7,6},{8,11},{9,8},{10,9... | collective-permute-start | bytes 24584 | tf_op jit(solution)/shard_map/ppermute | solution.py:54
  14.9 4.6 %collective-permute-start.4 = (bf16[2,2048]{1,0:T(2,128)(2,1)S(1)}, bf16[2,2048]{1,0:T(2,128)(2,1)S(1)}, u32[]{:S(2)}, u32[]{:S(2)}) collective-permute-start(bf16[2,2048]{1,0:T(2,128)(2,1)S(1)} %copy-done), channel_id=1, source_target_pairs={{0,2},{1,3},{2,0},{3,1},{4,6},{5,7},{6,4},{7,5},{8,10},{9,11},{10,... | collective-permute-start | bytes 24584 | tf_op jit(solution)/shard_map/ppermute | solution.py:54
  19.6 5.1 %collective-permute-start.9 = (bf16[4,2,2304]{2,1,0:T(2,128)(2,1)S(1)}, bf16[4,2,2304]{2,1,0:T(2,128)(2,1)S(1)}, u32[]{:S(2)}, u32[]{:S(2)}) collective-permute-start(bf16[4,2,2304]{2,1,0:T(2,128)(2,1)S(1)} %pad_maximum_fusion), channel_id=1, source_target_pairs={{0,24},{8,0},{16,8},{24,16},{1,25},{9,1},{17,9},{25,17},{2,26},{10... | collective-permute-start | bytes 110600 | tf_op jit(solution)/shard_map/ppermute | solution.py:54
  19.6 5.0 %collective-permute-start.8 = (bf16[4,2,2304]{2,1,0:T(2,128)(2,1)S(1)}, bf16[4,2,2304]{2,1,0:T(2,128)(2,1)S(1)}, u32[]{:S(2)}, u32[]{:S(2)}) collective-permute-start(bf16[4,2,2304]{2,1,0:T(2,128)(2,1)S(1)} %pad_maximum_fusion), channel_id=1, source_target_pairs={{0,16},{8,24},{16,0},{24,8},{1,17},{9,25},{17,1},{25,9},{2,18},{10... | collective-permute-start | bytes 110600 | tf_op jit(solution)/shard_map/ppermute | solution.py:54
  21.2 3.4 %collective-permute-start.7 = (bf16[4,2,2304]{2,1,0:T(2,128)(2,1)S(1)}, bf16[4,2,2304]{2,1,0:T(2,128)(2,1)S(1)}, u32[]{:S(2)}, u32[]{:S(2)}) collective-permute-start(bf16[4,2,2304]{2,1,0:T(2,128)(2,1)S(1)} %pad_maximum_fusion), channel_id=1, source_target_pairs={{0,8},{8,16},{16,24},{24,0},{1,9},{9,17},{17,25},{25,1},{2,10},{10... | collective-permute-start | bytes 110600 | tf_op jit(solution)/shard_map/ppermute | solution.py:54
  31.6 3.7 %collective-permute-start.10 = (f32[2,256]{1,0:T(2,128)S(1)}, f32[2,256]{1,0:T(2,128)S(1)}, u32[]{:S(2)}, u32[]{:S(2)}) collective-permute-start(f32[2,256]{1,0:T(2,128)S(1)} %get-tuple-element.8), channel_id=1, source_target_pairs={{0,4},{1,5},{2,6},{3,7},{4,0},{5,1},{6,2},{7,3},{8,12},{9,13},{10,... | collective-permute-start | bytes 6152 | tf_op jit(solution)/shard_map/ppermute | solution.py:54

commit v4 on v3

--- a/solution.py
+++ b/solution.py
@@ -31,40 +31,23 @@
     return np.concatenate(pieces, axis=-1)
 
 
-def arrival_order(harm, samp, parts_here):
-    order = np.empty((harm * samp, harm * samp * parts_here), np.int32)
-    for h in range(harm):
-        for s in range(samp):
-            ranks = [
-                (h - j) % harm * samp + (s - k) % samp for j in range(harm) for k in range(samp)
-            ]
-            order[h * samp + s] = (
-                np.array(ranks)[:, None] * parts_here + np.arange(parts_here)
-            ).reshape(-1)
-    return order
-
-
-def shifted(array, axes, by):
-    sizes = [lax.axis_size(axis) for axis in axes]
-    places = list(np.ndindex(*sizes))
-    pairs = []
-    for place in places:
-        target = tuple((p + step) % size for p, step, size in zip(place, by, sizes))
-        pairs.append((places.index(place), places.index(target)))
-    return lax.ppermute(array, axes, pairs)
-
-
-def from_neighbours(edges, samp_step):
-    axes, tile = ("space", "samp"), edges.shape[1] // 2
-    if lax.axis_size("space") == 2:
-        return shifted(edges, axes, (1, samp_step))
+def shifted(array, axis, by):
+    count = lax.axis_size(axis)
+    return lax.ppermute(array, axis, [(i, (i + by) % count) for i in range(count)])
+
+
+def from_neighbours(edges, axis):
+    tile = edges.shape[1] // 2
+    if lax.axis_size(axis) == 2:
+        return shifted(edges, axis, 1)
     return jnp.concatenate(
-        [
-            shifted(edges[:, :tile], axes, (-1, samp_step)),
-            shifted(edges[:, tile:], axes, (1, samp_step)),
-        ],
-        axis=1,
-    )
+        [shifted(edges[:, :tile], axis, -1), shifted(edges[:, tile:], axis, 1)], axis=1
+    )
+
+
+def gathered(block, axis):
+    copies = jnp.broadcast_to(block[None], (lax.axis_size(axis),) + block.shape)
+    return lax.all_to_all(copies, axis, 0, 0)
 
 
 def fetch_kernel(curl_hbm, curl, sem):
@@ -102,7 +85,7 @@
     parts_here = out.shape[0]
     rank = lax.axis_index(GROUP)
     fetched = [
-        (pieces_hbm.at[rank], pieces),
+        (pieces_hbm, pieces),
         (table_hbm.at[rank], table),
         (pattern_hbm, pattern),
         (region_hbm, region_ids),
@@ -170,20 +153,15 @@
 def per_device(coeffs, curl_tiles, pattern, region_ids, material_law, source):
     parts_here = coeffs.shape[0]
     tile_count, links, tile, comps = curl_tiles.shape
-    harm, samp = lax.axis_size("harm"), lax.axis_size("samp")
-    parts = parts_here * harm * samp
-    order = arrival_order(harm, samp, parts_here)
-    table = half_table(parts)[:, order].transpose(1, 0, 2)
+    group_size = lax.axis_size(GROUP)
+    parts = parts_here * group_size
+    table = half_table(parts)
     pieces = bf16_pieces(table)
-    own_columns = table[:, :, :parts_here].astype(np.float32)
+    own_columns = table.reshape(HALF, group_size, parts_here).transpose(1, 0, 2)
     vmem, hbm = pl.BlockSpec(memory_space=pltpu.VMEM), pl.BlockSpec(memory_space=pltpu.HBM)
 
     edges = jnp.concatenate([coeffs[:, :tile], coeffs[:, -tile:]], axis=1)
-    blocks = []
-    for k in range(samp):
-        beside = from_neighbours(edges, k)
-        block = shifted(coeffs, ("samp",), (k,)) if k else coeffs
-        blocks.append(jnp.concatenate([beside[:, tile:], block, beside[:, :tile]], axis=1))
+    beside = from_neighbours(edges, "space")
     curl_hbm = pltpu.with_memory_space_constraint(curl_tiles, pltpu.HBM)
     early = 3 * tile_count // 8
     first_curl = pl.pallas_call(
@@ -198,9 +176,8 @@
         ),
         name="fetch_curl",
     )(curl_hbm)
-    near = jnp.stack(blocks)
-    far = [near] + [shifted(near, ("harm",), (j,)) for j in range(1, harm)]
-    window = jnp.concatenate(far, axis=0).reshape(parts, near.shape[-1])
+    block = jnp.concatenate([beside[:, tile:], coeffs, beside[:, :tile]], axis=1)
+    window = gathered(gathered(block, "samp"), "harm").reshape(parts, block.shape[1])
     own, halo = pl.pallas_call(
         shard_kernel,
         out_shape=(
@@ -213,7 +190,7 @@
             pltpu.SMEM((links, tile_count), jnp.int32),
             pltpu.SMEM(region_ids.shape, jnp.int32),
             pltpu.SMEM(material_law.shape, jnp.float32),
-            pltpu.VMEM(pieces.shape[1:], jnp.bfloat16),
+            pltpu.VMEM(pieces.shape, jnp.bfloat16),
             pltpu.VMEM(own_columns.shape[1:], jnp.float32),
             pltpu.VMEM(source.shape, jnp.float32),
             pltpu.VMEM((tile_count - early,) + curl_tiles.shape[1:], curl_tiles.dtype),
@@ -240,7 +217,7 @@
                 region_ids,
                 material_law,
                 jnp.asarray(pieces),
-                jnp.asarray(own_columns),
+                jnp.asarray(own_columns.astype(np.float32)),
                 source,
             )
         ],
@@ -252,7 +229,7 @@
         out_specs=vmem,
         compiler_params=pltpu.CompilerParams(vmem_limit_bytes=16 * 1024 * 1024),
         name="halo_sum",
-    )(pltpu.with_memory_space_constraint(own, pltpu.VMEM), from_neighbours(halo, 0))
+    )(pltpu.with_memory_space_constraint(own, pltpu.VMEM), from_neighbours(halo, "space"))
 
 
 def solution(mesh):

time: 36.1 us -> 37.2 us (1.030)
  blocking collectives: 0 us -> 10.8 us
  starting transfers between devices: 16 us -> 7.94 us
  waiting for transfers between devices: 9.54 us -> 6.7 us
  local copies, waits for them, and re-layouts: 0.92 us -> 1.49 us
  other arithmetic: 0.19 us -> 0.72 us
    ppermute x11 -> x2, starting transfers between devices: 16 us -> 4.6 us  [shifted(): lax.ppermute(array, axis, [(i, (i + by) % count) for i in range(count)])]
    all_to_all x0 -> x1, blocking collectives: none -> 10.8 us  [gathered(): return lax.all_to_all(copies, axis, 0, 0)]
    ppermute x11 -> x2, waiting for transfers between devices: 9.54 us -> 3.61 us  [shifted(): lax.ppermute(array, axis, [(i, (i + by) % count) for i in range(count)])]
    all_to_all x0 -> x1, starting transfers between devices: none -> 3.33 us  [gathered(): return lax.all_to_all(copies, axis, 0, 0)]
    all_to_all x0 -> x1, waiting for transfers between devices: none -> 3.09 us  [gathered(): return lax.all_to_all(copies, axis, 0, 0)]
    broadcast_in_dim x0 -> x2, local copies, waits for them, and re-layouts: none -> 0.76 us  [gathered(): copies = jnp.broadcast_to(block[None], (lax.axis_size(axis),) + block.shape)]
    concatenate x0 -> x1, other arithmetic: none -> 0.71 us  [per_device(): jnp.concatenate([beside[:, tile:], coeffs, beside[:, :tile]], axis=1)]
  transfers between devices with their start and end apart: 11 -> 3, of which waited for: 4 -> 3; matrix products, arithmetic and copies ran while one was open for 1% -> 0% of each run, Pallas kernels for 5% -> 5%
where the time goes in v4:
time: 37.2 us; the launch traced here: 36.9 us
  blocking collectives  10.8 us (29%)
  Pallas kernels  9.12 us (25%)
  starting transfers between devices  7.94 us (21%)
  waiting for transfers between devices  6.7 us (18%)
  local copies, waits for them, and re-layouts  1.49 us (4%)
  other arithmetic  0.72 us (2%)
    all_to_all x1, blocking collectives, gathered(): return lax.all_to_all(copies, axis, 0, 0)  10.8 us
    pallas_call x1, Pallas kernels, per_device(): pl.pallas_call(shard_kernel, out_shape=(pltpu.VMEM(source.shape, jnp.floa...  6.83 us
    ppermute x2, starting transfers between devices, shifted(): lax.ppermute(array, axis, [(i, (i + by) % count) for i in range(count)])  4.6 us
    ppermute x2, waiting for transfers between devices, shifted(): lax.ppermute(array, axis, [(i, (i + by) % count) for i in range(count)])  3.61 us
    all_to_all x1, starting transfers between devices, gathered(): return lax.all_to_all(copies, axis, 0, 0)  3.33 us
    all_to_all x1, waiting for transfers between devices, gathered(): return lax.all_to_all(copies, axis, 0, 0)  3.09 us
    pallas_call x1, Pallas kernels, per_device(): pl.pallas_call(fetch_kernel, out_shape=pltpu.VMEM((early,) + curl_tiles.s...  1.68 us
    broadcast_in_dim x2, local copies, waits for them, and re-layouts, gathered(): copies = jnp.broadcast_to(block[None], (lax.axis_size(axis),) + block.shape)  0.76 us
  transfers between devices with their start and end apart: 3, of which 3 were waited for; matrix products, arithmetic and copies ran while one was open for 0% of the time, Pallas kernels for 5%

profile of v4, /device:TPU:0, one launch (start us, length us, event | category | flops | bytes accessed | tf_op | source)
XLA Modules:
  0.0 36.9 jit_solution(6081201786159121084)
XLA Ops:
  0.0 0.7 %fusion = (bf16[2,128]{1,0:T(2,128)(2,1)S(1)}, bf16[2,128]{1,0:T(2,128)(2,1)S(1)}) fusion(bf16[2,2048]{1,0:T(2,128)(2,1)} %param.8), kind=kLoop, calls=%fused_computation.2 | loop fusion | bytes 2048 | tf_op jit(solution)/shard_map/slice | solution.py:163
  0.7 3.0 %collective-permute-start = (bf16[2,256]{1,0:T(2,128)(2,1)S(1)}, bf16[2,256]{1,0:T(2,128)(2,1)S(1)}, u32[]{:S(2)}, u32[]{:S(2)}) collective-permute-start(bf16[2,256]{1,0:T(2,128)(2,1)S(1)} %pad_maximum_fusion.1), channel_id=1, source_target_pairs={{0,4},{4,0},{1,5},{5,1},{2,6},{6,2},{3,7},{7,3},{8,12},{12,8},{9,1... | collective-permute-start | bytes 3080 | tf_op jit(solution)/shard_map/ppermute | solution.py:36
  3.7 1.5 %collective-permute-done = bf16[2,256]{1,0:T(2,128)(2,1)S(1)} collective-permute-done((bf16[2,256]{1,0:T(2,128)(2,1)S(1)}, bf16[2,256]{1,0:T(2,128)(2,1)S(1)}, u32[]{:S(2)}, u32[]{:S(2)}) %collective-permute-start) | collective-permute-done | bytes 1056 | tf_op jit(solution)/shard_map/ppermute | solution.py:36
  5.3 0.7 %pad_maximum_fusion = bf16[2,2304]{1,0:T(2,128)(2,1)S(1)} fusion(bf16[2,128]{1,0:T(2,128)(2,1)S(1)} %get-tuple-element.12, bf16[2,2048]{1,0:T(2,128)(2,1)} %param.8, bf16[2,128]{1,0:T(2,128)(2,1)S(1)} %get-tuple-element.11), kind=kLoop, calls=%fused_computation | loop fusion | flops 27648 | bytes 18432 | tf_op jit(solution)/shard_map/concatenate | solution.py:179
  6.0 10.8 %all_to_all.10 = bf16[4,2,2304]{2,1,0:T(2,128)(2,1)S(1)} all-to-all(bf16[4,2,2304]{2,1,0:T(2,128)(2,1)S(1)} %broadcast_in_dim.4), channel_id=1, replica_groups=mesh['harm'=4,'space'=2,'samp'=4] {'samp'}, dimensions={0} | all-to-all | bytes 73728 | tf_op jit(solution)/shard_map/all_to_all | solution.py:50
  16.8 0.7 %broadcast_in_dim.5 = bf16[4,4,2,2304]{3,2,1,0:T(2,128)(2,1)} broadcast(bf16[4,2,2304]{2,1,0:T(2,128)(2,1)S(1)} %all_to_all.10), dimensions={1,2,3} | broadcast | bytes 184320 | tf_op jit(solution)/shard_map/broadcast_in_dim | solution.py:49
  17.6 3.3 %all-to-all-start.1 = ((bf16[4,4,2,2304]{3,2,1,0:T(2,128)(2,1)}), bf16[4,4,2,2304]{3,2,1,0:T(2,128)(2,1)S(1)}, u32[]{:S(2)}, u32[]{:S(2)}) async-start(bf16[4,4,2,2304]{3,2,1,0:T(2,128)(2,1)} %broadcast_in_dim.5), calls=%async_computation.1 | async-start | bytes 294912 | tf_op jit(solution)/shard_map/all_to_all | solution.py:50
  20.9 1.7 %fetch_curl.1.first_curl = bf16[6,4,128,384]{3,2,1,0:T(8,128)(2,1)S(1)} custom-call(bf16[16,4,128,384]{3,2,1,0:T(8,128)(2,1)} %curl_hbm.3), custom_call_target="tpu_custom_call" | custom-call | bytes 4718592 | tf_op jit(solution)/shard_map/fetch_curl/pallas_call | solution.py:167
  22.6 3.1 %all-to-all-done.1 = bf16[4,4,2,2304]{3,2,1,0:T(2,128)(2,1)S(1)} async-done(((bf16[4,4,2,2304]{3,2,1,0:T(2,128)(2,1)}), bf16[4,4,2,2304]{3,2,1,0:T(2,128)(2,1)S(1)}, u32[]{:S(2)}, u32[]{:S(2)}) %all-to-all-start.1) | async-done | bytes 147488 | tf_op jit(solution)/shard_map/all_to_all | solution.py:50
  25.7 0.1 reshape.5.window
  25.8 6.8 %shard_residual.1 = (f32[2,2048]{1,0:T(2,128)S(1)}, f32[2,256]{1,0:T(2,128)S(1)}) custom-call(bf16[32,2304]{1,0:T(8,128)(2,1)S(1)} %reshape.5.window, bf16[6,4,128,384]{3,2,1,0:T(8,128)(2,1)S(1)} %fetch_curl.1.first_curl, bf16[16,4,128,384]{3,2,1,0:T(8,128)(2,1)} %curl_hbm.3, s32[4,16]{1,0:T(4,128)} %bitcast.1, s32[16]{0:T(128)} %region_hbm.1, ...), custom_call_target="tpu_custom_call" | custom-call | flops 805306368 | bytes 6291456 | tf_op jit(solution)/shard_map/shard_residual/pallas_call | solution.py:181
  32.6 1.6 %collective-permute-start.1 = (f32[2,256]{1,0:T(2,128)S(1)}, f32[2,256]{1,0:T(2,128)S(1)}, u32[]{:S(2)}, u32[]{:S(2)}) collective-permute-start(f32[2,256]{1,0:T(2,128)S(1)} %get-tuple-element.8), channel_id=1, source_target_pairs={{0,4},{4,0},{1,5},{5,1},{2,6},{6,2},{3,7},{7,3},{8,12},{12,8},{9,1... | collective-permute-start | bytes 6152 | tf_op jit(solution)/shard_map/ppermute | solution.py:36
  34.2 2.1 %collective-permute-done.1.received = f32[2,256]{1,0:T(2,128)S(1)} collective-permute-done((f32[2,256]{1,0:T(2,128)S(1)}, f32[2,256]{1,0:T(2,128)S(1)}, u32[]{:S(2)}, u32[]{:S(2)}) %collective-permute-start.1) | collective-permute-done | bytes 2080 | tf_op jit(solution)/shard_map/ppermute | solution.py:36
  36.2 0.6 %halo_sum.1 = f32[2,2048]{1,0:T(2,128)} custom-call(f32[2,2048]{1,0:T(2,128)S(1)} %get-tuple-element.7.own, f32[2,256]{1,0:T(2,128)S(1)} %collective-permute-done.1.received), custom_call_target="tpu_custom_call" | custom-call | tf_op jit(solution)/shard_map/halo_sum/pallas_call | solution.py:225
  (3 shorter events, 0.0 us)
Async XLA Ops:
  0.7 4.6 %collective-permute-start = (bf16[2,256]{1,0:T(2,128)(2,1)S(1)}, bf16[2,256]{1,0:T(2,128)(2,1)S(1)}, u32[]{:S(2)}, u32[]{:S(2)}) collective-permute-start(bf16[2,256]{1,0:T(2,128)(2,1)S(1)} %pad_maximum_fusion.1), channel_id=1, source_target_pairs={{0,4},{4,0},{1,5},{5,1},{2,6},{6,2},{3,7},{7,3},{8,12},{12,8},{9,1... | collective-permute-start | bytes 3080 | tf_op jit(solution)/shard_map/ppermute | solution.py:36
  17.6 8.1 %all-to-all-start.1 = ((bf16[4,4,2,2304]{3,2,1,0:T(2,128)(2,1)}), bf16[4,4,2,2304]{3,2,1,0:T(2,128)(2,1)S(1)}, u32[]{:S(2)}, u32[]{:S(2)}) async-start(bf16[4,4,2,2304]{3,2,1,0:T(2,128)(2,1)} %broadcast_in_dim.5), calls=%async_computation.1 | async-start | bytes 294912 | tf_op jit(solution)/shard_map/all_to_all | solution.py:50
  32.6 3.7 %collective-permute-start.1 = (f32[2,256]{1,0:T(2,128)S(1)}, f32[2,256]{1,0:T(2,128)S(1)}, u32[]{:S(2)}, u32[]{:S(2)}) collective-permute-start(f32[2,256]{1,0:T(2,128)S(1)} %get-tuple-element.8), channel_id=1, source_target_pairs={{0,4},{4,0},{1,5},{5,1},{2,6},{6,2},{3,7},{7,3},{8,12},{12,8},{9,1... | collective-permute-start | bytes 6152 | tf_op jit(solution)/shard_map/ppermute | solution.py:36

commit v5 on v4

--- a/solution.py
+++ b/solution.py
@@ -31,23 +31,52 @@
     return np.concatenate(pieces, axis=-1)
 
 
-def shifted(array, axis, by):
-    count = lax.axis_size(axis)
-    return lax.ppermute(array, axis, [(i, (i + by) % count) for i in range(count)])
-
-
-def from_neighbours(edges, axis):
-    tile = edges.shape[1] // 2
-    if lax.axis_size(axis) == 2:
-        return shifted(edges, axis, 1)
+def partner(index, step, size):
+    return index ^ step if size & (size - 1) == 0 else (index + step) % size
+
+
+def sender(index, step, size):
+    return index ^ step if size & (size - 1) == 0 else (index - step) % size
+
+
+def send(array, axis, step, along=None, by=0):
+    size = lax.axis_size(axis)
+    if along is None:
+        return lax.ppermute(array, axis, [(i, partner(i, step, size)) for i in range(size)])
+    count = lax.axis_size(along)
+    pairs = [
+        (i * count + n, partner(i, step, size) * count + (n + by) % count)
+        for i in range(size)
+        for n in range(count)
+    ]
+    return lax.ppermute(array, (axis, along), pairs)
+
+
+def from_neighbours(edges, axis, step):
+    tile = edges.shape[-1] // 2
+    if lax.axis_size("space") == 2:
+        return send(edges, axis, step, "space", 1)
     return jnp.concatenate(
-        [shifted(edges[:, :tile], axis, -1), shifted(edges[:, tile:], axis, 1)], axis=1
-    )
-
-
-def gathered(block, axis):
-    copies = jnp.broadcast_to(block[None], (lax.axis_size(axis),) + block.shape)
-    return lax.all_to_all(copies, axis, 0, 0)
+        [
+            send(edges[..., :tile], axis, step, "space", -1),
+            send(edges[..., tile:], axis, step, "space", 1),
+        ],
+        axis=-1,
+    )
+
+
+def arrival_order(harm, samp, parts_here):
+    ranks = [
+        [
+            sender(h, j, harm) * samp + sender(s, k, samp)
+            for j in range(harm)
+            for k in range(samp)
+        ]
+        for h in range(harm)
+        for s in range(samp)
+    ]
+    rows = np.array(ranks)[:, :, None] * parts_here + np.arange(parts_here)
+    return rows.reshape(harm * samp, -1)
 
 
 def fetch_kernel(curl_hbm, curl, sem):
@@ -85,7 +114,7 @@
     parts_here = out.shape[0]
     rank = lax.axis_index(GROUP)
     fetched = [
-        (pieces_hbm, pieces),
+        (pieces_hbm.at[rank], pieces),
         (table_hbm.at[rank], table),
         (pattern_hbm, pattern),
         (region_hbm, region_ids),
@@ -153,15 +182,15 @@
 def per_device(coeffs, curl_tiles, pattern, region_ids, material_law, source):
     parts_here = coeffs.shape[0]
     tile_count, links, tile, comps = curl_tiles.shape
-    group_size = lax.axis_size(GROUP)
-    parts = parts_here * group_size
-    table = half_table(parts)
+    harm, samp = lax.axis_size("harm"), lax.axis_size("samp")
+    parts = parts_here * harm * samp
+    table = half_table(parts)[:, arrival_order(harm, samp, parts_here)].transpose(1, 0, 2)
     pieces = bf16_pieces(table)
-    own_columns = table.reshape(HALF, group_size, parts_here).transpose(1, 0, 2)
+    own_columns = table[:, :, :parts_here]
     vmem, hbm = pl.BlockSpec(memory_space=pltpu.VMEM), pl.BlockSpec(memory_space=pltpu.HBM)
 
-    edges = jnp.concatenate([coeffs[:, :tile], coeffs[:, -tile:]], axis=1)
-    beside = from_neighbours(edges, "space")
+    near = jnp.stack([coeffs] + [send(coeffs, "samp", k) for k in range(1, samp)])
+    edges = jnp.concatenate([near[..., :tile], near[..., -tile:]], axis=-1)
     curl_hbm = pltpu.with_memory_space_constraint(curl_tiles, pltpu.HBM)
     early = 3 * tile_count // 8
     first_curl = pl.pallas_call(
@@ -176,8 +205,12 @@
         ),
         name="fetch_curl",
     )(curl_hbm)
-    block = jnp.concatenate([beside[:, tile:], coeffs, beside[:, :tile]], axis=1)
-    window = gathered(gathered(block, "samp"), "harm").reshape(parts, block.shape[1])
+    rows = []
+    for j in range(harm):
+        block = send(near, "harm", j) if j else near
+        beside = from_neighbours(edges, "harm", j)
+        rows.append(jnp.concatenate([beside[..., tile:], block, beside[..., :tile]], axis=-1))
+    window = jnp.concatenate(rows, axis=0).reshape(parts, -1)
     own, halo = pl.pallas_call(
         shard_kernel,
         out_shape=(
@@ -190,7 +223,7 @@
             pltpu.SMEM((links, tile_count), jnp.int32),
             pltpu.SMEM(region_ids.shape, jnp.int32),
             pltpu.SMEM(material_law.shape, jnp.float32),
-            pltpu.VMEM(pieces.shape, jnp.bfloat16),
+            pltpu.VMEM(pieces.shape[1:], jnp.bfloat16),
             pltpu.VMEM(own_columns.shape[1:], jnp.float32),
             pltpu.VMEM(source.shape, jnp.float32),
             pltpu.VMEM((tile_count - early,) + curl_tiles.shape[1:], curl_tiles.dtype),
@@ -229,7 +262,7 @@
         out_specs=vmem,
         compiler_params=pltpu.CompilerParams(vmem_limit_bytes=16 * 1024 * 1024),
         name="halo_sum",
-    )(pltpu.with_memory_space_constraint(own, pltpu.VMEM), from_neighbours(halo, "space"))
+    )(pltpu.with_memory_space_constraint(own, pltpu.VMEM), from_neighbours(halo, "harm", 0))
 
 
 def solution(mesh):

time: 37.2 us -> 34.4 us (0.925)
  blocking collectives: 10.8 us -> 0 us
  starting transfers between devices: 7.94 us -> 13.9 us
  waiting for transfers between devices: 6.7 us -> 10.1 us
  local copies, waits for them, and re-layouts: 1.49 us -> 0.09 us
    all_to_all x1 -> x0, blocking collectives: 10.8 us -> none  [gathered(): return lax.all_to_all(copies, axis, 0, 0)]
    ppermute x2 -> x11, starting transfers between devices: 4.6 us -> 13.9 us  [the longest x6 7.82 us: send(): lax.ppermute(array, axis, [(i, partner(i, step, size)) for i in range(siz...]
    ppermute x2 -> x11, waiting for transfers between devices: 3.61 us -> 10.1 us  [the longest x6 7.13 us: send(): lax.ppermute(array, axis, [(i, partner(i, step, size)) for i in range(siz...]
    all_to_all x1 -> x0, starting transfers between devices: 3.33 us -> none  [gathered(): return lax.all_to_all(copies, axis, 0, 0)]
    all_to_all x1 -> x0, waiting for transfers between devices: 3.09 us -> none  [gathered(): return lax.all_to_all(copies, axis, 0, 0)]
    broadcast_in_dim x2 -> x0, local copies, waits for them, and re-layouts: 0.76 us -> none  [gathered(): copies = jnp.broadcast_to(block[None], (lax.axis_size(axis),) + block.shape)]
    another operation x0 -> x1, other arithmetic: none -> 0.75 us  [per_device(): jnp.stack([coeffs] + [send(coeffs, 'samp', k) for k in range(1, samp)])]
    slice x2 -> x5, local copies, waits for them, and re-layouts: 0.68 us -> 0.03 us  [the longest x4 0.02 us: per_device(): beside[..., tile:]]
  transfers between devices with their start and end apart: 3 -> 11, of which waited for: 3 -> 6; matrix products, arithmetic and copies ran while one was open for 0% -> 0% of each run, Pallas kernels for 5% -> 5%
where the time goes in v5:
time: 34.4 us; the launch traced here: 34.2 us
  starting transfers between devices  13.9 us (40%)
  waiting for transfers between devices  10.1 us (29%)
  Pallas kernels  9.11 us (26%)
  other arithmetic  0.89 us (3%)
    ppermute x6, starting transfers between devices, send(): lax.ppermute(array, axis, [(i, partner(i, step, size)) for i in range(siz...  7.82 us
    ppermute x6, waiting for transfers between devices, send(): lax.ppermute(array, axis, [(i, partner(i, step, size)) for i in range(siz...  7.13 us
    pallas_call x1, Pallas kernels, per_device(): pl.pallas_call(shard_kernel, out_shape=(pltpu.VMEM(source.shape, jnp.floa...  6.82 us
    ppermute x5, starting transfers between devices, send(): return lax.ppermute(array, (axis, along), pairs)  6.1 us
    ppermute x5, waiting for transfers between devices, send(): return lax.ppermute(array, (axis, along), pairs)  2.93 us
    pallas_call x1, Pallas kernels, per_device(): pl.pallas_call(fetch_kernel, out_shape=pltpu.VMEM((early,) + curl_tiles.s...  1.67 us
    another operation x1, other arithmetic, per_device(): jnp.stack([coeffs] + [send(coeffs, 'samp', k) for k in range(1, samp)])  0.75 us
  transfers between devices with their start and end apart: 11, of which 6 were waited for; matrix products, arithmetic and copies ran while one was open for 0% of the time, Pallas kernels for 5%

profile of v5, /device:TPU:0, one launch (start us, length us, event | category | flops | bytes accessed | tf_op | source)
XLA Modules:
  0.0 34.2 jit_solution(14272212188728588772)
XLA Ops:
  0.0 0.0 copy-start
  0.0 3.0 %collective-permute-start = (bf16[2,2048]{1,0:T(2,128)(2,1)}, bf16[2,2048]{1,0:T(2,128)(2,1)S(1)}, u32[]{:S(2)}, u32[]{:S(2)}) collective-permute-start(bf16[2,2048]{1,0:T(2,128)(2,1)} %param.8), channel_id=1, source_target_pairs={{0,1},{1,0},{2,3},{3,2},{4,5},{5,4},{6,7},{7,6},{8,9},{9,8},{10,11... | collective-permute-start | bytes 24584 | tf_op jit(solution)/shard_map/ppermute | solution.py:45
  3.0 2.5 %collective-permute-start.2 = (bf16[2,2048]{1,0:T(2,128)(2,1)}, bf16[2,2048]{1,0:T(2,128)(2,1)S(1)}, u32[]{:S(2)}, u32[]{:S(2)}) collective-permute-start(bf16[2,2048]{1,0:T(2,128)(2,1)} %param.8), channel_id=1, source_target_pairs={{0,3},{1,2},{2,1},{3,0},{4,7},{5,6},{6,5},{7,4},{8,11},{9,10},{10,... | collective-permute-start | bytes 24584 | tf_op jit(solution)/shard_map/ppermute | solution.py:45
  5.5 0.1 collective-permute-start.1
  5.6 0.0 collective-permute-done
  5.6 3.1 %collective-permute-done.2 = bf16[2,2048]{1,0:T(2,128)(2,1)S(1)} collective-permute-done((bf16[2,2048]{1,0:T(2,128)(2,1)}, bf16[2,2048]{1,0:T(2,128)(2,1)S(1)}, u32[]{:S(2)}, u32[]{:S(2)}) %collective-permute-start.2) | collective-permute-done | bytes 8224 | tf_op jit(solution)/shard_map/ppermute | solution.py:45
  8.8 1.5 %collective-permute-done.1 = bf16[2,2048]{1,0:T(2,128)(2,1)S(1)} collective-permute-done((bf16[2,2048]{1,0:T(2,128)(2,1)}, bf16[2,2048]{1,0:T(2,128)(2,1)S(1)}, u32[]{:S(2)}, u32[]{:S(2)}) %collective-permute-start.1) | collective-permute-done | bytes 8224 | tf_op jit(solution)/shard_map/ppermute | solution.py:45
  10.3 0.8 %pad_maximum_fusion = bf16[4,2,2048]{2,1,0:T(2,128)(2,1)S(1)} fusion(bf16[1,2,2048]{2,1,0:T(2,128)(2,1)S(1)} %bitcast.9, bf16[1,2,2048]{2,1,0:T(2,128)(2,1)S(1)} %bitcast.11, bf16[1,2,2048]{2,1,0:T(2,128)(2,1)S(1)} %bitcast.7, bf16[1,2,2048]{2,1,0:T(2,128)(2,1)} %bitcast.5), kind=kLoop, calls=%fused_computation.1 | loop fusion | flops 49152 | bytes 65536 | tf_op jit(solution)/shard_map/stack | solution.py:192
  11.0 0.5 %collective-permute-start.8 = (bf16[4,2,256]{2,1,0:T(2,128)(2,1)S(1)}, bf16[4,2,256]{2,1,0:T(2,128)(2,1)S(1)}, u32[]{:S(2)}, u32[]{:S(2)}) collective-permute-start(bf16[4,2,256]{2,1,0:T(2,128)(2,1)S(1)} %pad_maximum_fusion.1), channel_id=1, source_target_pairs={{0,28},{4,24},{8,20},{12,16},{16,12},{20,8},{24,4},{28,0},{1,29},{... | collective-permute-start | bytes 12296 | tf_op jit(solution)/shard_map/ppermute | solution.py:52
  11.6 1.7 %fetch_curl.1.first_curl = bf16[6,4,128,384]{3,2,1,0:T(8,128)(2,1)S(1)} custom-call(bf16[16,4,128,384]{3,2,1,0:T(8,128)(2,1)} %curl_hbm.3), custom_call_target="tpu_custom_call" | custom-call | bytes 4718592 | tf_op jit(solution)/shard_map/fetch_curl/pallas_call | solution.py:196
  13.3 2.1 %collective-permute-start.6 = (bf16[4,2,256]{2,1,0:T(2,128)(2,1)S(1)}, bf16[4,2,256]{2,1,0:T(2,128)(2,1)S(1)}, u32[]{:S(2)}, u32[]{:S(2)}) collective-permute-start(bf16[4,2,256]{2,1,0:T(2,128)(2,1)S(1)} %pad_maximum_fusion.1), channel_id=1, source_target_pairs={{0,20},{4,16},{8,28},{12,24},{16,4},{20,0},{24,12},{28,8},{1,21},{... | collective-permute-start | bytes 12296 | tf_op jit(solution)/shard_map/ppermute | solution.py:52
  15.3 1.4 %collective-permute-start.4 = (bf16[4,2,256]{2,1,0:T(2,128)(2,1)S(1)}, bf16[4,2,256]{2,1,0:T(2,128)(2,1)S(1)}, u32[]{:S(2)}, u32[]{:S(2)}) collective-permute-start(bf16[4,2,256]{2,1,0:T(2,128)(2,1)S(1)} %pad_maximum_fusion.1), channel_id=1, source_target_pairs={{0,12},{4,8},{8,4},{12,0},{16,28},{20,24},{24,20},{28,16},{1,13},{... | collective-permute-start | bytes 12296 | tf_op jit(solution)/shard_map/ppermute | solution.py:52
  16.7 0.5 %collective-permute-start.3 = (bf16[4,2,256]{2,1,0:T(2,128)(2,1)S(1)}, bf16[4,2,256]{2,1,0:T(2,128)(2,1)S(1)}, u32[]{:S(2)}, u32[]{:S(2)}) collective-permute-start(bf16[4,2,256]{2,1,0:T(2,128)(2,1)S(1)} %pad_maximum_fusion.1), channel_id=1, source_target_pairs={{0,4},{4,0},{8,12},{12,8},{16,20},{20,16},{24,28},{28,24},{1,5},{5... | collective-permute-start | bytes 12296 | tf_op jit(solution)/shard_map/ppermute | solution.py:52
  17.3 0.0 collective-permute-start.5
  17.3 0.0 collective-permute-done.8
  17.3 1.6 %collective-permute-start.9 = (bf16[4,2,2048]{2,1,0:T(2,128)(2,1)S(1)}, bf16[4,2,2048]{2,1,0:T(2,128)(2,1)S(1)}, u32[]{:S(2)}, u32[]{:S(2)}) collective-permute-start(bf16[4,2,2048]{2,1,0:T(2,128)(2,1)S(1)} %pad_maximum_fusion), channel_id=1, source_target_pairs={{0,24},{8,16},{16,8},{24,0},{1,25},{9,17},{17,9},{25,1},{2,26},{10... | collective-permute-start | bytes 98312 | tf_op jit(solution)/shard_map/ppermute | solution.py:45
  18.9 0.0 collective-permute-done.6
  18.9 0.6 %collective-permute-start.7 = (bf16[4,2,2048]{2,1,0:T(2,128)(2,1)S(1)}, bf16[4,2,2048]{2,1,0:T(2,128)(2,1)S(1)}, u32[]{:S(2)}, u32[]{:S(2)}) collective-permute-start(bf16[4,2,2048]{2,1,0:T(2,128)(2,1)S(1)} %pad_maximum_fusion), channel_id=1, source_target_pairs={{0,16},{8,24},{16,0},{24,8},{1,17},{9,25},{17,1},{25,9},{2,18},{10... | collective-permute-start | bytes 98312 | tf_op jit(solution)/shard_map/ppermute | solution.py:45
  19.5 0.0 collective-permute-done.4
  19.5 0.9 %collective-permute-done.3 = bf16[4,2,256]{2,1,0:T(2,128)(2,1)S(1)} collective-permute-done((bf16[4,2,256]{2,1,0:T(2,128)(2,1)S(1)}, bf16[4,2,256]{2,1,0:T(2,128)(2,1)S(1)}, u32[]{:S(2)}, u32[]{:S(2)}) %collective-permute-start.3) | collective-permute-done | bytes 4128 | tf_op jit(solution)/shard_map/ppermute | solution.py:52
  20.4 0.0 collective-permute-done.5
  20.4 0.2 collective-permute-done.9
  20.6 2.3 %collective-permute-done.7 = bf16[4,2,2048]{2,1,0:T(2,128)(2,1)S(1)} collective-permute-done((bf16[4,2,2048]{2,1,0:T(2,128)(2,1)S(1)}, bf16[4,2,2048]{2,1,0:T(2,128)(2,1)S(1)}, u32[]{:S(2)}, u32[]{:S(2)}) %collective-permute-start.7) | collective-permute-done | bytes 32800 | tf_op jit(solution)/shard_map/ppermute | solution.py:45
  22.9 0.0 copy-done
  22.9 0.1 maximum_maximum_fusion
  23.0 0.1 reshape.3.window
  23.1 6.8 %shard_residual.1 = (f32[2,2048]{1,0:T(2,128)S(1)}, f32[2,256]{1,0:T(2,128)S(1)}) custom-call(bf16[32,2304]{1,0:T(8,128)(2,1)S(1)} %reshape.3.window, bf16[6,4,128,384]{3,2,1,0:T(8,128)(2,1)S(1)} %fetch_curl.1.first_curl, bf16[16,4,128,384]{3,2,1,0:T(8,128)(2,1)} %curl_hbm.3, s32[4,16]{1,0:T(4,128)} %bitcast.13, s32[16]{0:T(128)} %region_hbm.1, ...), custom_call_target="tpu_custom_call" | custom-call | flops 805306368 | bytes 6291456 | tf_op jit(solution)/shard_map/shard_residual/pallas_call | solution.py:214
  29.9 1.6 %collective-permute-start.10 = (f32[2,256]{1,0:T(2,128)S(1)}, f32[2,256]{1,0:T(2,128)S(1)}, u32[]{:S(2)}, u32[]{:S(2)}) collective-permute-start(f32[2,256]{1,0:T(2,128)S(1)} %get-tuple-element.8), channel_id=1, source_target_pairs={{0,4},{4,0},{8,12},{12,8},{16,20},{20,16},{24,28},{28,24},{1,5},{5... | collective-permute-start | bytes 6152 | tf_op jit(solution)/shard_map/ppermute | solution.py:52
  31.5 2.1 %collective-permute-done.10.received = f32[2,256]{1,0:T(2,128)S(1)} collective-permute-done((f32[2,256]{1,0:T(2,128)S(1)}, f32[2,256]{1,0:T(2,128)S(1)}, u32[]{:S(2)}, u32[]{:S(2)}) %collective-permute-start.10) | collective-permute-done | bytes 2080 | tf_op jit(solution)/shard_map/ppermute | solution.py:52
  33.5 0.6 %halo_sum.1 = f32[2,2048]{1,0:T(2,128)} custom-call(f32[2,2048]{1,0:T(2,128)S(1)} %get-tuple-element.7.own, f32[2,256]{1,0:T(2,128)S(1)} %collective-permute-done.10.received), custom_call_target="tpu_custom_call" | custom-call | tf_op jit(solution)/shard_map/halo_sum/pallas_call | solution.py:258
  (6 shorter events, 0.0 us)
Async XLA Ops:
  0.0 22.9 %copy-start = (bf16[2,2048]{1,0:T(2,128)(2,1)S(1)}, bf16[2,2048]{1,0:T(2,128)(2,1)}, u32[]{:S(2)}) copy-start(bf16[2,2048]{1,0:T(2,128)(2,1)} %param.8) | copy-start | bytes 24580
  0.0 5.6 %collective-permute-start = (bf16[2,2048]{1,0:T(2,128)(2,1)}, bf16[2,2048]{1,0:T(2,128)(2,1)S(1)}, u32[]{:S(2)}, u32[]{:S(2)}) collective-permute-start(bf16[2,2048]{1,0:T(2,128)(2,1)} %param.8), channel_id=1, source_target_pairs={{0,1},{1,0},{2,3},{3,2},{4,5},{5,4},{6,7},{7,6},{8,9},{9,8},{10,11... | collective-permute-start | bytes 24584 | tf_op jit(solution)/shard_map/ppermute | solution.py:45
  3.0 5.7 %collective-permute-start.2 = (bf16[2,2048]{1,0:T(2,128)(2,1)}, bf16[2,2048]{1,0:T(2,128)(2,1)S(1)}, u32[]{:S(2)}, u32[]{:S(2)}) collective-permute-start(bf16[2,2048]{1,0:T(2,128)(2,1)} %param.8), channel_id=1, source_target_pairs={{0,3},{1,2},{2,1},{3,0},{4,7},{5,6},{6,5},{7,4},{8,11},{9,10},{10,... | collective-permute-start | bytes 24584 | tf_op jit(solution)/shard_map/ppermute | solution.py:45
  5.5 4.8 %collective-permute-start.1 = (bf16[2,2048]{1,0:T(2,128)(2,1)}, bf16[2,2048]{1,0:T(2,128)(2,1)S(1)}, u32[]{:S(2)}, u32[]{:S(2)}) collective-permute-start(bf16[2,2048]{1,0:T(2,128)(2,1)} %param.8), channel_id=1, source_target_pairs={{0,2},{1,3},{2,0},{3,1},{4,6},{5,7},{6,4},{7,5},{8,10},{9,11},{10,... | collective-permute-start | bytes 24584 | tf_op jit(solution)/shard_map/ppermute | solution.py:45
  11.0 6.2 %collective-permute-start.8 = (bf16[4,2,256]{2,1,0:T(2,128)(2,1)S(1)}, bf16[4,2,256]{2,1,0:T(2,128)(2,1)S(1)}, u32[]{:S(2)}, u32[]{:S(2)}) collective-permute-start(bf16[4,2,256]{2,1,0:T(2,128)(2,1)S(1)} %pad_maximum_fusion.1), channel_id=1, source_target_pairs={{0,28},{4,24},{8,20},{12,16},{16,12},{20,8},{24,4},{28,0},{1,29},{... | collective-permute-start | bytes 12296 | tf_op jit(solution)/shard_map/ppermute | solution.py:52
  13.3 5.6 %collective-permute-start.6 = (bf16[4,2,256]{2,1,0:T(2,128)(2,1)S(1)}, bf16[4,2,256]{2,1,0:T(2,128)(2,1)S(1)}, u32[]{:S(2)}, u32[]{:S(2)}) collective-permute-start(bf16[4,2,256]{2,1,0:T(2,128)(2,1)S(1)} %pad_maximum_fusion.1), channel_id=1, source_target_pairs={{0,20},{4,16},{8,28},{12,24},{16,4},{20,0},{24,12},{28,8},{1,21},{... | collective-permute-start | bytes 12296 | tf_op jit(solution)/shard_map/ppermute | solution.py:52
  15.3 4.2 %collective-permute-start.4 = (bf16[4,2,256]{2,1,0:T(2,128)(2,1)S(1)}, bf16[4,2,256]{2,1,0:T(2,128)(2,1)S(1)}, u32[]{:S(2)}, u32[]{:S(2)}) collective-permute-start(bf16[4,2,256]{2,1,0:T(2,128)(2,1)S(1)} %pad_maximum_fusion.1), channel_id=1, source_target_pairs={{0,12},{4,8},{8,4},{12,0},{16,28},{20,24},{24,20},{28,16},{1,13},{... | collective-permute-start | bytes 12296 | tf_op jit(solution)/shard_map/ppermute | solution.py:52
  16.7 3.6 %collective-permute-start.3 = (bf16[4,2,256]{2,1,0:T(2,128)(2,1)S(1)}, bf16[4,2,256]{2,1,0:T(2,128)(2,1)S(1)}, u32[]{:S(2)}, u32[]{:S(2)}) collective-permute-start(bf16[4,2,256]{2,1,0:T(2,128)(2,1)S(1)} %pad_maximum_fusion.1), channel_id=1, source_target_pairs={{0,4},{4,0},{8,12},{12,8},{16,20},{20,16},{24,28},{28,24},{1,5},{5... | collective-permute-start | bytes 12296 | tf_op jit(solution)/shard_map/ppermute | solution.py:52
  17.3 3.1 %collective-permute-start.5 = (bf16[4,2,2048]{2,1,0:T(2,128)(2,1)S(1)}, bf16[4,2,2048]{2,1,0:T(2,128)(2,1)S(1)}, u32[]{:S(2)}, u32[]{:S(2)}) collective-permute-start(bf16[4,2,2048]{2,1,0:T(2,128)(2,1)S(1)} %pad_maximum_fusion), channel_id=1, source_target_pairs={{0,8},{8,0},{16,24},{24,16},{1,9},{9,1},{17,25},{25,17},{2,10},{10... | collective-permute-start | bytes 98312 | tf_op jit(solution)/shard_map/ppermute | solution.py:45
  17.3 3.3 %collective-permute-start.9 = (bf16[4,2,2048]{2,1,0:T(2,128)(2,1)S(1)}, bf16[4,2,2048]{2,1,0:T(2,128)(2,1)S(1)}, u32[]{:S(2)}, u32[]{:S(2)}) collective-permute-start(bf16[4,2,2048]{2,1,0:T(2,128)(2,1)S(1)} %pad_maximum_fusion), channel_id=1, source_target_pairs={{0,24},{8,16},{16,8},{24,0},{1,25},{9,17},{17,9},{25,1},{2,26},{10... | collective-permute-start | bytes 98312 | tf_op jit(solution)/shard_map/ppermute | solution.py:45
  18.9 4.0 %collective-permute-start.7 = (bf16[4,2,2048]{2,1,0:T(2,128)(2,1)S(1)}, bf16[4,2,2048]{2,1,0:T(2,128)(2,1)S(1)}, u32[]{:S(2)}, u32[]{:S(2)}) collective-permute-start(bf16[4,2,2048]{2,1,0:T(2,128)(2,1)S(1)} %pad_maximum_fusion), channel_id=1, source_target_pairs={{0,16},{8,24},{16,0},{24,8},{1,17},{9,25},{17,1},{25,9},{2,18},{10... | collective-permute-start | bytes 98312 | tf_op jit(solution)/shard_map/ppermute | solution.py:45
  29.9 3.7 %collective-permute-start.10 = (f32[2,256]{1,0:T(2,128)S(1)}, f32[2,256]{1,0:T(2,128)S(1)}, u32[]{:S(2)}, u32[]{:S(2)}) collective-permute-start(f32[2,256]{1,0:T(2,128)S(1)} %get-tuple-element.8), channel_id=1, source_target_pairs={{0,4},{4,0},{8,12},{12,8},{16,20},{20,16},{24,28},{28,24},{1,5},{5... | collective-permute-start | bytes 6152 | tf_op jit(solution)/shard_map/ppermute | solution.py:52

commit v6 on v4

v6 whole, which is shorter than its diff:
```python
import math

import jax
import jax.numpy as jnp
import ml_dtypes
import numpy as np
from jax import lax
from jax.experimental import pallas as pl
from jax.experimental.pallas import tpu as pltpu
from jax.sharding import PartitionSpec as P

SAMPLES = 64
HALF = SAMPLES // 2
GROUP = ("harm", "samp")
MIB = 1024 * 1024


def half_table(parts):
    sample_ids = np.arange(HALF)[:, None]
    part_ids = np.arange(parts)[None, :]
    phase = ((2 * (part_ids // 2) + 1) * sample_ids % SAMPLES) * (2.0 * math.pi / SAMPLES)
    return np.where(part_ids % 2 == 0, np.cos(phase), np.sin(phase))


def bf16_pieces(table):
    rest = table
    pieces = []
    for _ in range(3):
        piece = rest.astype(ml_dtypes.bfloat16)
        pieces.append(piece)
        rest = rest - piece.astype(np.float64)
    return np.concatenate(pieces, axis=-1)


def shifted(array, axis, by):
    count = lax.axis_size(axis)
    return lax.ppermute(array, axis, [(i, (i + by) % count) for i in range(count)])


def from_neighbours(array, tile):
    if lax.axis_size("space") == 2:
        other = shifted(array, "space", 1)
        return other[:, :tile], other[:, -tile:]
    return shifted(array[:, :tile], "space", -1), shifted(array[:, -tile:], "space", 1)


def fetch_kernel(*refs):
    count = (len(refs) - 1) // 2
    sources, targets, sems = refs[:count], refs[count : 2 * count], refs[-1]
    rank = lax.axis_index(GROUP)
    sources = (sources[0].at[: targets[0].shape[0]], sources[1].at[rank]) + sources[2:]
    copies = [
        pltpu.make_async_copy(source, target, sems.at[i])
        for i, (source, target) in enumerate(zip(sources, targets))
    ]
    for copy in copies:
        copy.start()
    for copy in copies:
        copy.wait()


def shard_kernel(
    window,
    first_curl,
    table,
    pieces,
    source,
    pattern_in,
    region_in,
    law_in,
    curl_hbm,
    out,
    halo,
    pattern,
    region_ids,
    law,
    later_curl,
    timed,
    densities,
    small_sems,
    curl_sem,
    *sums,
):
    tile_count, links, tile, comps = curl_hbm.shape
    early = first_curl.shape[0]
    parts_here = out.shape[0]
    fetched = [(pattern_in, pattern), (region_in, region_ids), (law_in, law)]
    small = [
        pltpu.make_async_copy(src, dst, small_sems.at[i]) for i, (src, dst) in enumerate(fetched)
    ]
    rest = pltpu.make_async_copy(curl_hbm.at[early:], later_curl, curl_sem)
    for copy in small + [rest]:
        copy.start()
    for total in sums:
        total[...] = jnp.zeros_like(total)
    stacked = jnp.concatenate([window[...]] * 3, axis=0)
    samples = jnp.dot(pieces[...], stacked, preferred_element_type=jnp.float32)
    high = samples.astype(jnp.bfloat16)
    timed[:HALF, :] = high
    timed[HALF:, :] = (samples - high.astype(jnp.float32)).astype(jnp.bfloat16)
    columns = [
        jnp.broadcast_to(table[:, part : part + 1], (HALF, comps)) for part in range(parts_here)
    ]
    for copy in small:
        copy.wait()
    places = [[pattern[link, elem] for link in range(links)] for elem in range(tile_count)]

    def blocks(elem):
        curl = first_curl[elem] if elem < early else later_curl[elem - early]
        return curl.reshape(links * tile, comps)

    def find_density(elem):
        picked = jnp.concatenate(
            [timed[:, pl.ds(pl.multiple_of(at * tile, tile), tile)] for at in places[elem]], axis=1
        )
        split = jnp.dot(picked, blocks(elem), preferred_element_type=jnp.float32)
        densities[elem] = split[:HALF] + split[HALF:]

    def project(elem):
        density = densities[elem]
        comp = [density[:, c * tile : (c + 1) * tile] for c in range(comps // tile)]
        square = comp[0] * comp[0]
        for c in comp[1:]:
            square = square + c * c
        region = region_ids[elem]
        reluct = law[0, region] + law[2, region] * square / (square + law[1, region])
        field = jnp.concatenate([reluct * c for c in comp], axis=1)
        rows = [jnp.sum(column * field, axis=0, keepdims=True) for column in columns]
        return (jnp.concatenate(rows, axis=0) * (4.0 / SAMPLES)).astype(jnp.bfloat16)

    def contribute(elem, projected):
        contrib = lax.dot_general(
            projected, blocks(elem), (((1,), (1,)), ((), ())), preferred_element_type=jnp.float32
        )
        for link, at in enumerate(places[elem]):
            sums[link][at] += contrib[:, link * tile : (link + 1) * tile]

    step = 2
    chunks = [range(at, min(at + step, tile_count)) for at in range(0, tile_count, step)]
    projected = {}
    for turn in range(len(chunks) + 2):
        if turn < len(chunks):
            if early in chunks[turn]:
                rest.wait()
            for elem in chunks[turn]:
                find_density(elem)
        if 0 <= turn - 1 < len(chunks):
            for elem in chunks[turn - 1]:
                projected[elem] = project(elem)
        if 0 <= turn - 2:
            for elem in chunks[turn - 2]:
                contribute(elem, projected[elem])

    def window_sum(w):
        total = sums[0][w]
        for other in sums[1:]:
            total = total + other[w]
        return total

    for w in range(tile_count):
        at = slice(w * tile, (w + 1) * tile)
        out[:, at] = window_sum(w + 1) - source[:, at]
    halo[:, :tile] = window_sum(0)
    halo[:, tile:] = window_sum(tile_count + 1)


def halo_kernel(own, from_right, from_left, out):
    tile = from_left.shape[1] // 2
    out[...] = own[...]
    out[:, :tile] += from_left[:, tile:]
    out[:, -tile:] += from_right[:, :tile]


def per_device(coeffs, curl_tiles, pattern, region_ids, material_law, source):
    parts_here = coeffs.shape[0]
    tile_count, links, tile, comps = curl_tiles.shape
    group_size = lax.axis_size(GROUP)
    parts = parts_here * group_size
    table = half_table(parts)
    pieces = jnp.asarray(bf16_pieces(table))
    own_columns = jnp.asarray(
        table.reshape(HALF, group_size, parts_here).transpose(1, 0, 2).astype(np.float32)
    )
    vmem, hbm = pl.BlockSpec(memory_space=pltpu.VMEM), pl.BlockSpec(memory_space=pltpu.HBM)

    def in_vmem(array):
        return pltpu.with_memory_space_constraint(array, pltpu.VMEM)

    def in_hbm(array):
        return pltpu.with_memory_space_constraint(array, pltpu.HBM)

    early = 3 * tile_count // 8
    operands = [
        curl_tiles,
        own_columns,
        coeffs,
        pieces,
        source,
        pattern.T,
        region_ids,
        material_law,
    ]
    shapes = [
        (early,) + curl_tiles.shape[1:],
        own_columns.shape[1:],
    ] + [operand.shape for operand in operands[2:]]
    fetched = pl.pallas_call(
        fetch_kernel,
        out_shape=[pltpu.VMEM(shape, o.dtype) for shape, o in zip(shapes, operands)],
        in_specs=[hbm] * len(operands),
        out_specs=[vmem] * len(operands),
        scratch_shapes=[pltpu.SemaphoreType.DMA((len(operands),))],
        compiler_params=pltpu.CompilerParams(vmem_limit_bytes=16 * MIB),
        cost_estimate=pl.CostEstimate(
            flops=0, bytes_accessed=4 * early * links * tile * comps, transcendentals=0
        ),
        name="fetch_operands",
    )(*[in_hbm(operand) for operand in operands])
    first_curl, columns_here, coeffs_here, pieces_here, *others = fetched

    right, left = from_neighbours(coeffs, tile)
    block = jnp.concatenate([left, coeffs_here, right], axis=1)
    copies = jnp.broadcast_to(block[None], (group_size,) + block.shape)
    window = lax.all_to_all(copies, GROUP, 0, 0).reshape(parts, block.shape[1])
    own, halo = pl.pallas_call(
        shard_kernel,
        out_shape=(
            pltpu.VMEM(source.shape, jnp.float32),
            pltpu.VMEM((parts_here, 2 * tile), jnp.float32),
        ),
        in_specs=[vmem] * 8 + [hbm],
        out_specs=(vmem, vmem),
        scratch_shapes=[
            pltpu.SMEM((links, tile_count), jnp.int32),
            pltpu.SMEM(region_ids.shape, jnp.int32),
            pltpu.SMEM(material_law.shape, jnp.float32),
            pltpu.VMEM((tile_count - early,) + curl_tiles.shape[1:], curl_tiles.dtype),
            pltpu.VMEM((SAMPLES, (tile_count + 2) * tile), jnp.bfloat16),
            pltpu.VMEM((tile_count, HALF, comps), jnp.float32),
            pltpu.SemaphoreType.DMA((3,)),
            pltpu.SemaphoreType.DMA,
        ]
        + [pltpu.VMEM((tile_count + 2, parts_here, tile), jnp.float32)] * links,
        compiler_params=pltpu.CompilerParams(vmem_limit_bytes=32 * MIB),
        cost_estimate=pl.CostEstimate(
            flops=4 * SAMPLES * tile_count * links * tile * comps,
            bytes_accessed=2 * curl_tiles.size,
            transcendentals=0,
        ),
        name="shard_residual",
    )(
        in_vmem(window),
        *[in_vmem(array) for array in (first_curl, columns_here, pieces_here, *others)],
        in_hbm(curl_tiles),
    )
    if lax.axis_size("space") == 2:
        beside = [shifted(halo, "space", 1)] * 2
    else:
        beside = [shifted(halo, "space", -1), shifted(halo, "space", 1)]
    return pl.pallas_call(
        halo_kernel,
        out_shape=jax.ShapeDtypeStruct(source.shape, jnp.float32),
        in_specs=[vmem] * 3,
        out_specs=vmem,
        compiler_params=pltpu.CompilerParams(vmem_limit_bytes=16 * MIB),
        name="halo_sum",
    )(in_vmem(own), *beside)


def solution(mesh):
    placed = (
        P(GROUP, "space"),
        P("space", None, None, None),
        P("space", None),
        P("space"),
        P(),
        P(GROUP, "space"),
    )
    return jax.shard_map(
        per_device,
        mesh=mesh,
        in_specs=placed,
        out_specs=P(GROUP, "space"),
        check_vma=False,
    )
```

time: 37.2 us -> 27.6 us (0.74)
  waiting for transfers between devices: 6.7 us -> 2.15 us
  starting transfers between devices: 7.94 us -> 4.55 us
  blocking collectives: 10.8 us -> 13.7 us
  Pallas kernels: 9.12 us -> 6.76 us
  local copies, waits for them, and re-layouts: 1.49 us -> 0.14 us
  other arithmetic: 0.72 us -> 0.01 us
    all_to_all x1 -> x0, starting transfers between devices: 3.33 us -> none  [gathered(): return lax.all_to_all(copies, axis, 0, 0)]
    all_to_all x1 -> x0, waiting for transfers between devices: 3.09 us -> none  [gathered(): return lax.all_to_all(copies, axis, 0, 0)]
    all_to_all x1, blocking collectives: 10.8 us -> 13.7 us  [per_device(): window = lax.all_to_all(copies, GROUP, 0, 0).reshape(parts, block.shape[1])]
    pallas_call x1, Pallas kernels: 6.83 us -> 4.4 us  [per_device(): pl.pallas_call(shard_kernel, out_shape=(pltpu.VMEM(source.shape, jnp.floa...]
    ppermute x2, waiting for transfers between devices: 3.61 us -> 2.15 us  [shifted(): lax.ppermute(array, axis, [(i, (i + by) % count) for i in range(count)])]
    concatenate x2 -> x1, other arithmetic: 0.72 us -> 0.01 us  [per_device(): block = jnp.concatenate([left, coeffs_here, right], axis=1)]
    broadcast_in_dim x2 -> x1, local copies, waits for them, and re-layouts: 0.76 us -> 0.08 us  [per_device(): copies = jnp.broadcast_to(block[None], (group_size,) + block.shape)]
    slice x2 -> x1, local copies, waits for them, and re-layouts: 0.68 us -> 0.01 us  [from_neighbours(): return (other[:, :tile], other[:, -tile:])]
  transfers between devices with their start and end apart: 3 -> 2, of which waited for: 3 -> 2; matrix products, arithmetic and copies ran while one was open for 0% -> 0% of each run, Pallas kernels for 5% -> 6%
where the time goes in v6:
time: 27.6 us; the launch traced here: 27.3 us
  blocking collectives  13.7 us (50%)
  Pallas kernels  6.76 us (24%)
  starting transfers between devices  4.55 us (16%)
  waiting for transfers between devices  2.15 us (8%)
    all_to_all x1, blocking collectives, per_device(): window = lax.all_to_all(copies, GROUP, 0, 0).reshape(parts, block.shape[1])  13.7 us
    ppermute x2, starting transfers between devices, shifted(): lax.ppermute(array, axis, [(i, (i + by) % count) for i in range(count)])  4.55 us
    pallas_call x1, Pallas kernels, per_device(): pl.pallas_call(shard_kernel, out_shape=(pltpu.VMEM(source.shape, jnp.floa...  4.4 us
    ppermute x2, waiting for transfers between devices, shifted(): lax.ppermute(array, axis, [(i, (i + by) % count) for i in range(count)])  2.15 us
    pallas_call x1, Pallas kernels, per_device(): pl.pallas_call(fetch_kernel, out_shape=[pltpu.VMEM(shape, o.dtype) for sh...  1.75 us
    pallas_call x1, Pallas kernels, per_device(): pl.pallas_call(halo_kernel, out_shape=jax.ShapeDtypeStruct(source.shape,...  0.61 us
  transfers between devices with their start and end apart: 2, of which 2 were waited for; matrix products, arithmetic and copies ran while one was open for 0% of the time, Pallas kernels for 6%

profile of v6, /device:TPU:0, one launch (start us, length us, event | category | flops | bytes accessed | tf_op | source)
XLA Modules:
  0.0 27.3 jit_solution(17141130380763076312)
XLA Ops:
  0.0 3.0 %collective-permute-start = (bf16[2,2048]{1,0:T(2,128)(2,1)}, bf16[2,2048]{1,0:T(2,128)(2,1)S(1)}, u32[]{:S(2)}, u32[]{:S(2)}) collective-permute-start(bf16[2,2048]{1,0:T(2,128)(2,1)} %refs_2_.1), channel_id=1, source_target_pairs={{0,4},{4,0},{1,5},{5,1},{2,6},{6,2},{3,7},{7,3},{8,12},{12,8},{9,1... | collective-permute-start | bytes 24584 | tf_op jit(solution)/shard_map/ppermute | solution.py:37
  3.0 1.7 %fetch_operands.1 = (bf16[6,4,128,384]{3,2,1,0:T(8,128)(2,1)S(1)}, f32[32,2]{1,0:T(8,128)S(1)}, bf16[2,2048]{1,0:T(2,128)(2,1)S(1)}, bf16[32,96]{1,0:T(8,128)(2,...) custom-call(bf16[16,4,128,384]{3,2,1,0:T(8,128)(2,1)} %curl_hbm.1, ...), custom_call_target="tpu_custom_call" | custom-call | bytes 4718592 | tf_op jit(solution)/shard_map/fetch_operands/pallas_call | solution.py:207
  4.7 0.1 collective-permute-done
  4.8 0.1 broadcast_in_dim.2
  4.9 13.7 %all_to_all.5 = bf16[16,2,2304]{2,1,0:T(2,128)(2,1)S(1)} all-to-all(bf16[16,2,2304]{2,1,0:T(2,128)(2,1)S(1)} %broadcast_in_dim.2), channel_id=1, replica_groups=mesh['harm'=4,'space'=2,'samp'=4] {'harm','samp'}, dimensions={0} | all-to-all | bytes 294912 | tf_op jit(solution)/shard_map/all_to_all | solution.py:224
  18.6 0.1 reshape.4.window
  18.7 4.4 %shard_residual.1 = (f32[2,2048]{1,0:T(2,128)S(1)}, f32[2,256]{1,0:T(2,128)S(1)}) custom-call(bf16[32,2304]{1,0:T(8,128)(2,1)S(1)} %reshape.4.window, bf16[6,4,128,384]{3,2,1,0:T(8,128)(2,1)S(1)} %get-tuple-element.16.first_curl, f32[32,2]{1,0:T(8,128)S(1)} %get-tuple-element.17.table, bf16[32,96]{1,0:T(8,128)(2,1)S(1)} %get-tuple-element.18.pieces, ...), custom_call_target="tpu_custom_call" | custom-call | flops 805306368 | bytes 6291456 | tf_op jit(solution)/shard_map/shard_residual/pallas_call | solution.py:225
  23.1 1.6 %collective-permute-start.1 = (f32[2,256]{1,0:T(2,128)S(1)}, f32[2,256]{1,0:T(2,128)S(1)}, u32[]{:S(2)}, u32[]{:S(2)}) collective-permute-start(f32[2,256]{1,0:T(2,128)S(1)} %get-tuple-element.24), channel_id=1, source_target_pairs={{0,4},{4,0},{1,5},{5,1},{2,6},{6,2},{3,7},{7,3},{8,12},{12,8},{9,1... | collective-permute-start | bytes 6152 | tf_op jit(solution)/shard_map/ppermute | solution.py:37
  24.7 2.1 %collective-permute-done.1.from_right.from_left = f32[2,256]{1,0:T(2,128)S(1)} collective-permute-done((f32[2,256]{1,0:T(2,128)S(1)}, f32[2,256]{1,0:T(2,128)S(1)}, u32[]{:S(2)}, u32[]{:S(2)}) %collective-permute-start.1) | collective-permute-done | bytes 2080 | tf_op jit(solution)/shard_map/ppermute | solution.py:37
  26.7 0.6 %halo_sum.1 = f32[2,2048]{1,0:T(2,128)} custom-call(f32[2,2048]{1,0:T(2,128)S(1)} %get-tuple-element.23.own, f32[2,256]{1,0:T(2,128)S(1)} %collective-permute-done.1.from_right.from_left, f32[2,256]{1,0:T(2,128)S(1)} %collective-permute-done.1.from_right.from_left), custom_call_target="tpu_custom_call" | custom-call | tf_op jit(solution)/shard_map/halo_sum/pallas_call | solution.py:260
  (2 shorter events, 0.0 us)
Async XLA Ops:
  0.0 4.8 %collective-permute-start = (bf16[2,2048]{1,0:T(2,128)(2,1)}, bf16[2,2048]{1,0:T(2,128)(2,1)S(1)}, u32[]{:S(2)}, u32[]{:S(2)}) collective-permute-start(bf16[2,2048]{1,0:T(2,128)(2,1)} %refs_2_.1), channel_id=1, source_target_pairs={{0,4},{4,0},{1,5},{5,1},{2,6},{6,2},{3,7},{7,3},{8,12},{12,8},{9,1... | collective-permute-start | bytes 24584 | tf_op jit(solution)/shard_map/ppermute | solution.py:37
  23.1 3.7 %collective-permute-start.1 = (f32[2,256]{1,0:T(2,128)S(1)}, f32[2,256]{1,0:T(2,128)S(1)}, u32[]{:S(2)}, u32[]{:S(2)}) collective-permute-start(f32[2,256]{1,0:T(2,128)S(1)} %get-tuple-element.24), channel_id=1, source_target_pairs={{0,4},{4,0},{1,5},{5,1},{2,6},{6,2},{3,7},{7,3},{8,12},{12,8},{9,1... | collective-permute-start | bytes 6152 | tf_op jit(solution)/shard_map/ppermute | solution.py:37

commit v7 on v6

--- a/solution.py
+++ b/solution.py
@@ -44,11 +44,43 @@
     return shifted(array[:, :tile], "space", -1), shifted(array[:, -tile:], "space", 1)
 
 
+def partner(index, step, size):
+    return index ^ step if size & (size - 1) == 0 else (index + step) % size
+
+
+def sender(index, step, size):
+    return index ^ step if size & (size - 1) == 0 else (index - step) % size
+
+
+def gathered(block, axis):
+    size = lax.axis_size(axis)
+    blocks = [block]
+    for step in range(1, size):
+        pairs = [(i, partner(i, step, size)) for i in range(size)]
+        blocks.append(lax.ppermute(block, axis, pairs))
+    return jnp.concatenate(blocks, axis=0)
+
+
+def arrival_order(harm, samp, parts_here):
+    ranks = [
+        [
+            sender(h, j, harm) * samp + sender(s, k, samp)
+            for j in range(harm)
+            for k in range(samp)
+        ]
+        for h in range(harm)
+        for s in range(samp)
+    ]
+    rows = np.array(ranks)[:, :, None] * parts_here + np.arange(parts_here)
+    return rows.reshape(harm * samp, -1)
+
+
 def fetch_kernel(*refs):
     count = (len(refs) - 1) // 2
     sources, targets, sems = refs[:count], refs[count : 2 * count], refs[-1]
     rank = lax.axis_index(GROUP)
-    sources = (sources[0].at[: targets[0].shape[0]], sources[1].at[rank]) + sources[2:]
+    first = sources[0].at[: targets[0].shape[0]]
+    sources = (first, sources[1].at[rank], sources[2].at[rank]) + sources[3:]
     copies = [
         pltpu.make_async_copy(source, target, sems.at[i])
         for i, (source, target) in enumerate(zip(sources, targets))
@@ -174,13 +206,11 @@
 def per_device(coeffs, curl_tiles, pattern, region_ids, material_law, source):
     parts_here = coeffs.shape[0]
     tile_count, links, tile, comps = curl_tiles.shape
-    group_size = lax.axis_size(GROUP)
-    parts = parts_here * group_size
-    table = half_table(parts)
+    harm, samp = lax.axis_size("harm"), lax.axis_size("samp")
+    parts = parts_here * harm * samp
+    table = half_table(parts)[:, arrival_order(harm, samp, parts_here)].transpose(1, 0, 2)
     pieces = jnp.asarray(bf16_pieces(table))
-    own_columns = jnp.asarray(
-        table.reshape(HALF, group_size, parts_here).transpose(1, 0, 2).astype(np.float32)
-    )
+    own_columns = jnp.asarray(table[:, :, :parts_here].astype(np.float32))
     vmem, hbm = pl.BlockSpec(memory_space=pltpu.VMEM), pl.BlockSpec(memory_space=pltpu.HBM)
 
     def in_vmem(array):
@@ -193,8 +223,8 @@
     operands = [
         curl_tiles,
         own_columns,
+        pieces,
         coeffs,
-        pieces,
         source,
         pattern.T,
         region_ids,
@@ -203,7 +233,8 @@
     shapes = [
         (early,) + curl_tiles.shape[1:],
         own_columns.shape[1:],
-    ] + [operand.shape for operand in operands[2:]]
+        pieces.shape[1:],
+    ] + [operand.shape for operand in operands[3:]]
     fetched = pl.pallas_call(
         fetch_kernel,
         out_shape=[pltpu.VMEM(shape, o.dtype) for shape, o in zip(shapes, operands)],
@@ -216,12 +247,11 @@
         ),
         name="fetch_operands",
     )(*[in_hbm(operand) for operand in operands])
-    first_curl, columns_here, coeffs_here, pieces_here, *others = fetched
+    first_curl, columns_here, pieces_here, coeffs_here, *others = fetched
 
     right, left = from_neighbours(coeffs, tile)
     block = jnp.concatenate([left, coeffs_here, right], axis=1)
-    copies = jnp.broadcast_to(block[None], (group_size,) + block.shape)
-    window = lax.all_to_all(copies, GROUP, 0, 0).reshape(parts, block.shape[1])
+    window = gathered(gathered(block[None], "samp"), "harm").reshape(parts, block.shape[1])
     own, halo = pl.pallas_call(
         shard_kernel,
         out_shape=(

time: 27.6 us -> 29.1 us (1.054)
  blocking collectives: 13.7 us -> 0 us
  waiting for transfers between devices: 2.15 us -> 10.6 us
  starting transfers between devices: 4.55 us -> 11.2 us
    all_to_all x1 -> x0, blocking collectives: 13.7 us -> none  [per_device(): window = lax.all_to_all(copies, GROUP, 0, 0).reshape(parts, block.shape[1])]
    ppermute x0 -> x6, waiting for transfers between devices: none -> 8.42 us  [gathered(): blocks.append(lax.ppermute(block, axis, pairs))]
    ppermute x0 -> x6, starting transfers between devices: none -> 6.67 us  [gathered(): blocks.append(lax.ppermute(block, axis, pairs))]
  transfers between devices with their start and end apart: 2 -> 8, of which waited for: 2 -> 6; matrix products, arithmetic and copies ran while one was open for 0% -> 0% of each run, Pallas kernels for 6% -> 6%
where the time goes in v7:
time: 29.1 us; the launch traced here: 28.9 us
  starting transfers between devices  11.2 us (38%)
  waiting for transfers between devices  10.6 us (36%)
  Pallas kernels  6.75 us (23%)
    ppermute x6, waiting for transfers between devices, gathered(): blocks.append(lax.ppermute(block, axis, pairs))  8.42 us
    ppermute x6, starting transfers between devices, gathered(): blocks.append(lax.ppermute(block, axis, pairs))  6.67 us
    ppermute x2, starting transfers between devices, shifted(): lax.ppermute(array, axis, [(i, (i + by) % count) for i in range(count)])  4.55 us
    pallas_call x1, Pallas kernels, per_device(): pl.pallas_call(shard_kernel, out_shape=(pltpu.VMEM(source.shape, jnp.floa...  4.39 us
    ppermute x2, waiting for transfers between devices, shifted(): lax.ppermute(array, axis, [(i, (i + by) % count) for i in range(count)])  2.15 us
    pallas_call x1, Pallas kernels, per_device(): pl.pallas_call(fetch_kernel, out_shape=[pltpu.VMEM(shape, o.dtype) for sh...  1.75 us
    pallas_call x1, Pallas kernels, per_device(): pl.pallas_call(halo_kernel, out_shape=jax.ShapeDtypeStruct(source.shape,...  0.61 us
  transfers between devices with their start and end apart: 8, of which 6 were waited for; matrix products, arithmetic and copies ran while one was open for 0% of the time, Pallas kernels for 6%

profile of v7, /device:TPU:0, one launch (start us, length us, event | category | flops | bytes accessed | tf_op | source)
XLA Modules:
  0.0 28.9 jit_solution(3075431285380056063)
XLA Ops:
  0.0 3.0 %collective-permute-start = (bf16[2,2048]{1,0:T(2,128)(2,1)}, bf16[2,2048]{1,0:T(2,128)(2,1)S(1)}, u32[]{:S(2)}, u32[]{:S(2)}) collective-permute-start(bf16[2,2048]{1,0:T(2,128)(2,1)} %refs_3_.1), channel_id=1, source_target_pairs={{0,4},{4,0},{1,5},{5,1},{2,6},{6,2},{3,7},{7,3},{8,12},{12,8},{9,1... | collective-permute-start | bytes 24584 | tf_op jit(solution)/shard_map/ppermute | solution.py:37
  3.0 1.7 %fetch_operands.1 = (bf16[6,4,128,384]{3,2,1,0:T(8,128)(2,1)S(1)}, f32[32,2]{1,0:T(8,128)S(1)}, bf16[32,96]{1,0:T(8,128)(2,1)S(1)}, bf16[2,2048]{1,0:T(2,128)(2,...) custom-call(bf16[16,4,128,384]{3,2,1,0:T(8,128)(2,1)} %curl_hbm.1, ...), custom_call_target="tpu_custom_call" | custom-call | bytes 4718592 | tf_op jit(solution)/shard_map/fetch_operands/pallas_call | solution.py:238
  4.7 0.1 collective-permute-done
  4.8 2.1 %collective-permute-start.1 = (bf16[1,2,2304]{2,1,0:T(2,128)(2,1)S(1)}, bf16[1,2,2304]{2,1,0:T(2,128)(2,1)S(1)}, u32[]{:S(2)}, u32[]{:S(2)}) collective-permute-start(bf16[1,2,2304]{2,1,0:T(2,128)(2,1)S(1)} %maximum_bitcast_fusion), channel_id=1, source_target_pairs={{0,1},{1,0},{2,3},{3,2},{4,5},{5,4},{6,7},{7,6},{8,9},{9,8},{10,11... | collective-permute-start | bytes 27656 | tf_op jit(solution)/shard_map/ppermute | solution.py:60
  7.0 2.6 %collective-permute-start.2 = (bf16[1,2,2304]{2,1,0:T(2,128)(2,1)S(1)}, bf16[1,2,2304]{2,1,0:T(2,128)(2,1)S(1)}, u32[]{:S(2)}, u32[]{:S(2)}) collective-permute-start(bf16[1,2,2304]{2,1,0:T(2,128)(2,1)S(1)} %maximum_bitcast_fusion), channel_id=1, source_target_pairs={{0,2},{1,3},{2,0},{3,1},{4,6},{5,7},{6,4},{7,5},{8,10},{9,11},{10,... | collective-permute-start | bytes 27656 | tf_op jit(solution)/shard_map/ppermute | solution.py:60
  9.6 0.0 collective-permute-start.3
  9.6 0.0 collective-permute-done.1
  9.6 1.9 %collective-permute-done.2 = bf16[1,2,2304]{2,1,0:T(2,128)(2,1)S(1)} collective-permute-done((bf16[1,2,2304]{2,1,0:T(2,128)(2,1)S(1)}, bf16[1,2,2304]{2,1,0:T(2,128)(2,1)S(1)}, u32[]{:S(2)}, u32[]{:S(2)}) %collective-permute-start.2) | collective-permute-done | bytes 9248 | tf_op jit(solution)/shard_map/ppermute | solution.py:60
  11.5 3.5 %collective-permute-done.3 = bf16[1,2,2304]{2,1,0:T(2,128)(2,1)S(1)} collective-permute-done((bf16[1,2,2304]{2,1,0:T(2,128)(2,1)S(1)}, bf16[1,2,2304]{2,1,0:T(2,128)(2,1)S(1)}, u32[]{:S(2)}, u32[]{:S(2)}) %collective-permute-start.3) | collective-permute-done | bytes 9248 | tf_op jit(solution)/shard_map/ppermute | solution.py:60
  15.0 0.1 pad_maximum_fusion
  15.1 0.1 collective-permute-start.4
  15.2 1.6 %collective-permute-start.5 = (bf16[4,2,2304]{2,1,0:T(2,128)(2,1)S(1)}, bf16[4,2,2304]{2,1,0:T(2,128)(2,1)S(1)}, u32[]{:S(2)}, u32[]{:S(2)}) collective-permute-start(bf16[4,2,2304]{2,1,0:T(2,128)(2,1)S(1)} %pad_maximum_fusion), channel_id=1, source_target_pairs={{0,16},{8,24},{16,0},{24,8},{1,17},{9,25},{17,1},{25,9},{2,18},{10... | collective-permute-start | bytes 110600 | tf_op jit(solution)/shard_map/ppermute | solution.py:60
  16.7 0.3 %collective-permute-start.6 = (bf16[4,2,2304]{2,1,0:T(2,128)(2,1)S(1)}, bf16[4,2,2304]{2,1,0:T(2,128)(2,1)S(1)}, u32[]{:S(2)}, u32[]{:S(2)}) collective-permute-start(bf16[4,2,2304]{2,1,0:T(2,128)(2,1)S(1)} %pad_maximum_fusion), channel_id=1, source_target_pairs={{0,24},{8,16},{16,8},{24,0},{1,25},{9,17},{17,9},{25,1},{2,26},{10... | collective-permute-start | bytes 110600 | tf_op jit(solution)/shard_map/ppermute | solution.py:60
  17.1 0.0 collective-permute-done.4
  17.1 2.1 %collective-permute-done.5 = bf16[4,2,2304]{2,1,0:T(2,128)(2,1)S(1)} collective-permute-done((bf16[4,2,2304]{2,1,0:T(2,128)(2,1)S(1)}, bf16[4,2,2304]{2,1,0:T(2,128)(2,1)S(1)}, u32[]{:S(2)}, u32[]{:S(2)}) %collective-permute-start.5) | collective-permute-done | bytes 36896 | tf_op jit(solution)/shard_map/ppermute | solution.py:60
  19.2 0.9 %collective-permute-done.6 = bf16[4,2,2304]{2,1,0:T(2,128)(2,1)S(1)} collective-permute-done((bf16[4,2,2304]{2,1,0:T(2,128)(2,1)S(1)}, bf16[4,2,2304]{2,1,0:T(2,128)(2,1)S(1)}, u32[]{:S(2)}, u32[]{:S(2)}) %collective-permute-start.6) | collective-permute-done | bytes 36896 | tf_op jit(solution)/shard_map/ppermute | solution.py:60
  20.2 0.1 reshape.3.window
  20.3 4.4 %shard_residual.1 = (f32[2,2048]{1,0:T(2,128)S(1)}, f32[2,256]{1,0:T(2,128)S(1)}) custom-call(bf16[32,2304]{1,0:T(8,128)(2,1)S(1)} %reshape.3.window, bf16[6,4,128,384]{3,2,1,0:T(8,128)(2,1)S(1)} %get-tuple-element.16.first_curl, f32[32,2]{1,0:T(8,128)S(1)} %get-tuple-element.17.table, bf16[32,96]{1,0:T(8,128)(2,1)S(1)} %get-tuple-element.18.pieces, ...), custom_call_target="tpu_custom_call" | custom-call | flops 805306368 | bytes 6291456 | tf_op jit(solution)/shard_map/shard_residual/pallas_call | solution.py:255
  24.7 1.6 %collective-permute-start.7 = (f32[2,256]{1,0:T(2,128)S(1)}, f32[2,256]{1,0:T(2,128)S(1)}, u32[]{:S(2)}, u32[]{:S(2)}) collective-permute-start(f32[2,256]{1,0:T(2,128)S(1)} %get-tuple-element.24), channel_id=1, source_target_pairs={{0,4},{4,0},{1,5},{5,1},{2,6},{6,2},{3,7},{7,3},{8,12},{12,8},{9,1... | collective-permute-start | bytes 6152 | tf_op jit(solution)/shard_map/ppermute | solution.py:37
  26.2 2.1 %collective-permute-done.7.from_right.from_left = f32[2,256]{1,0:T(2,128)S(1)} collective-permute-done((f32[2,256]{1,0:T(2,128)S(1)}, f32[2,256]{1,0:T(2,128)S(1)}, u32[]{:S(2)}, u32[]{:S(2)}) %collective-permute-start.7) | collective-permute-done | bytes 2080 | tf_op jit(solution)/shard_map/ppermute | solution.py:37
  28.3 0.6 %halo_sum.1 = f32[2,2048]{1,0:T(2,128)} custom-call(f32[2,2048]{1,0:T(2,128)S(1)} %get-tuple-element.23.own, f32[2,256]{1,0:T(2,128)S(1)} %collective-permute-done.7.from_right.from_left, f32[2,256]{1,0:T(2,128)S(1)} %collective-permute-done.7.from_right.from_left), custom_call_target="tpu_custom_call" | custom-call | tf_op jit(solution)/shard_map/halo_sum/pallas_call | solution.py:290
  (9 shorter events, 0.2 us)
Async XLA Ops:
  0.0 4.8 %collective-permute-start = (bf16[2,2048]{1,0:T(2,128)(2,1)}, bf16[2,2048]{1,0:T(2,128)(2,1)S(1)}, u32[]{:S(2)}, u32[]{:S(2)}) collective-permute-start(bf16[2,2048]{1,0:T(2,128)(2,1)} %refs_3_.1), channel_id=1, source_target_pairs={{0,4},{4,0},{1,5},{5,1},{2,6},{6,2},{3,7},{7,3},{8,12},{12,8},{9,1... | collective-permute-start | bytes 24584 | tf_op jit(solution)/shard_map/ppermute | solution.py:37
  4.8 4.8 %collective-permute-start.1 = (bf16[1,2,2304]{2,1,0:T(2,128)(2,1)S(1)}, bf16[1,2,2304]{2,1,0:T(2,128)(2,1)S(1)}, u32[]{:S(2)}, u32[]{:S(2)}) collective-permute-start(bf16[1,2,2304]{2,1,0:T(2,128)(2,1)S(1)} %maximum_bitcast_fusion), channel_id=1, source_target_pairs={{0,1},{1,0},{2,3},{3,2},{4,5},{5,4},{6,7},{7,6},{8,9},{9,8},{10,11... | collective-permute-start | bytes 27656 | tf_op jit(solution)/shard_map/ppermute | solution.py:60
  7.0 4.6 %collective-permute-start.2 = (bf16[1,2,2304]{2,1,0:T(2,128)(2,1)S(1)}, bf16[1,2,2304]{2,1,0:T(2,128)(2,1)S(1)}, u32[]{:S(2)}, u32[]{:S(2)}) collective-permute-start(bf16[1,2,2304]{2,1,0:T(2,128)(2,1)S(1)} %maximum_bitcast_fusion), channel_id=1, source_target_pairs={{0,2},{1,3},{2,0},{3,1},{4,6},{5,7},{6,4},{7,5},{8,10},{9,11},{10,... | collective-permute-start | bytes 27656 | tf_op jit(solution)/shard_map/ppermute | solution.py:60
  9.6 5.5 %collective-permute-start.3 = (bf16[1,2,2304]{2,1,0:T(2,128)(2,1)S(1)}, bf16[1,2,2304]{2,1,0:T(2,128)(2,1)S(1)}, u32[]{:S(2)}, u32[]{:S(2)}) collective-permute-start(bf16[1,2,2304]{2,1,0:T(2,128)(2,1)S(1)} %maximum_bitcast_fusion), channel_id=1, source_target_pairs={{0,3},{1,2},{2,1},{3,0},{4,7},{5,6},{6,5},{7,4},{8,11},{9,10},{10,... | collective-permute-start | bytes 27656 | tf_op jit(solution)/shard_map/ppermute | solution.py:60
  15.1 2.0 %collective-permute-start.4 = (bf16[4,2,2304]{2,1,0:T(2,128)(2,1)S(1)}, bf16[4,2,2304]{2,1,0:T(2,128)(2,1)S(1)}, u32[]{:S(2)}, u32[]{:S(2)}) collective-permute-start(bf16[4,2,2304]{2,1,0:T(2,128)(2,1)S(1)} %pad_maximum_fusion), channel_id=1, source_target_pairs={{0,8},{8,0},{16,24},{24,16},{1,9},{9,1},{17,25},{25,17},{2,10},{10... | collective-permute-start | bytes 110600 | tf_op jit(solution)/shard_map/ppermute | solution.py:60
  15.2 4.0 %collective-permute-start.5 = (bf16[4,2,2304]{2,1,0:T(2,128)(2,1)S(1)}, bf16[4,2,2304]{2,1,0:T(2,128)(2,1)S(1)}, u32[]{:S(2)}, u32[]{:S(2)}) collective-permute-start(bf16[4,2,2304]{2,1,0:T(2,128)(2,1)S(1)} %pad_maximum_fusion), channel_id=1, source_target_pairs={{0,16},{8,24},{16,0},{24,8},{1,17},{9,25},{17,1},{25,9},{2,18},{10... | collective-permute-start | bytes 110600 | tf_op jit(solution)/shard_map/ppermute | solution.py:60
  16.7 3.4 %collective-permute-start.6 = (bf16[4,2,2304]{2,1,0:T(2,128)(2,1)S(1)}, bf16[4,2,2304]{2,1,0:T(2,128)(2,1)S(1)}, u32[]{:S(2)}, u32[]{:S(2)}) collective-permute-start(bf16[4,2,2304]{2,1,0:T(2,128)(2,1)S(1)} %pad_maximum_fusion), channel_id=1, source_target_pairs={{0,24},{8,16},{16,8},{24,0},{1,25},{9,17},{17,9},{25,1},{2,26},{10... | collective-permute-start | bytes 110600 | tf_op jit(solution)/shard_map/ppermute | solution.py:60
  24.7 3.7 %collective-permute-start.7 = (f32[2,256]{1,0:T(2,128)S(1)}, f32[2,256]{1,0:T(2,128)S(1)}, u32[]{:S(2)}, u32[]{:S(2)}) collective-permute-start(f32[2,256]{1,0:T(2,128)S(1)} %get-tuple-element.24), channel_id=1, source_target_pairs={{0,4},{4,0},{1,5},{5,1},{2,6},{6,2},{3,7},{7,3},{8,12},{12,8},{9,1... | collective-permute-start | bytes 6152 | tf_op jit(solution)/shard_map/ppermute | solution.py:37

commit v8 on v6

--- a/solution.py
+++ b/solution.py
@@ -11,7 +11,7 @@
 
 SAMPLES = 64
 HALF = SAMPLES // 2
-GROUP = ("harm", "samp")
+GROUP = ("chip", "core", "samp")
 MIB = 1024 * 1024
 
 
@@ -32,23 +32,43 @@
     return np.concatenate(pieces, axis=-1)
 
 
-def shifted(array, axis, by):
-    count = lax.axis_size(axis)
-    return lax.ppermute(array, axis, [(i, (i + by) % count) for i in range(count)])
-
-
-def from_neighbours(array, tile):
+def across(array, core_step, space_step):
+    cores, shards = lax.axis_size("core"), lax.axis_size("space")
+    pairs = [
+        (c * shards + s, (c + core_step) % cores * shards + (s + space_step) % shards)
+        for c in range(cores)
+        for s in range(shards)
+    ]
+    return lax.ppermute(array, ("core", "space"), pairs)
+
+
+def from_neighbours(array, tile, core_step):
     if lax.axis_size("space") == 2:
-        other = shifted(array, "space", 1)
+        other = across(array, core_step, 1)
         return other[:, :tile], other[:, -tile:]
-    return shifted(array[:, :tile], "space", -1), shifted(array[:, -tile:], "space", 1)
+    return across(array[:, :tile], core_step, -1), across(array[:, -tile:], core_step, 1)
+
+
+def arrival_order(chips, cores, samp, parts_here):
+    ranks = [
+        [
+            (chip * cores + (c - step) % cores) * samp + s
+            for chip in range(chips)
+            for s in range(samp)
+            for step in range(cores)
+        ]
+        for c in range(cores)
+    ]
+    rows = np.array(ranks)[:, :, None] * parts_here + np.arange(parts_here)
+    return rows.reshape(cores, -1)
 
 
 def fetch_kernel(*refs):
     count = (len(refs) - 1) // 2
     sources, targets, sems = refs[:count], refs[count : 2 * count], refs[-1]
-    rank = lax.axis_index(GROUP)
-    sources = (sources[0].at[: targets[0].shape[0]], sources[1].at[rank]) + sources[2:]
+    first = sources[0].at[: targets[0].shape[0]]
+    own_columns = sources[1].at[lax.axis_index(GROUP)]
+    sources = (first, own_columns, sources[2].at[lax.axis_index("core")]) + sources[3:]
     copies = [
         pltpu.make_async_copy(source, target, sems.at[i])
         for i, (source, target) in enumerate(zip(sources, targets))
@@ -174,10 +194,12 @@
 def per_device(coeffs, curl_tiles, pattern, region_ids, material_law, source):
     parts_here = coeffs.shape[0]
     tile_count, links, tile, comps = curl_tiles.shape
-    group_size = lax.axis_size(GROUP)
+    chips, cores, samp = (lax.axis_size(axis) for axis in GROUP)
+    group_size = chips * cores * samp
     parts = parts_here * group_size
     table = half_table(parts)
-    pieces = jnp.asarray(bf16_pieces(table))
+    order = arrival_order(chips, cores, samp, parts_here)
+    pieces = jnp.asarray(bf16_pieces(table[:, order].transpose(1, 0, 2)))
     own_columns = jnp.asarray(
         table.reshape(HALF, group_size, parts_here).transpose(1, 0, 2).astype(np.float32)
     )
@@ -193,8 +215,8 @@
     operands = [
         curl_tiles,
         own_columns,
+        pieces,
         coeffs,
-        pieces,
         source,
         pattern.T,
         region_ids,
@@ -203,7 +225,8 @@
     shapes = [
         (early,) + curl_tiles.shape[1:],
         own_columns.shape[1:],
-    ] + [operand.shape for operand in operands[2:]]
+        pieces.shape[1:],
+    ] + [operand.shape for operand in operands[3:]]
     fetched = pl.pallas_call(
         fetch_kernel,
         out_shape=[pltpu.VMEM(shape, o.dtype) for shape, o in zip(shapes, operands)],
@@ -216,12 +239,16 @@
         ),
         name="fetch_operands",
     )(*[in_hbm(operand) for operand in operands])
-    first_curl, columns_here, coeffs_here, pieces_here, *others = fetched
-
-    right, left = from_neighbours(coeffs, tile)
-    block = jnp.concatenate([left, coeffs_here, right], axis=1)
-    copies = jnp.broadcast_to(block[None], (group_size,) + block.shape)
-    window = lax.all_to_all(copies, GROUP, 0, 0).reshape(parts, block.shape[1])
+    first_curl, columns_here, pieces_here, coeffs_here, *others = fetched
+
+    blocks = []
+    for step in range(cores):
+        right, left = from_neighbours(coeffs, tile, step)
+        middle = across(coeffs, step, 0) if step else coeffs_here
+        blocks.append(jnp.concatenate([left, middle, right], axis=1))
+    block = jnp.stack(blocks)
+    copies = jnp.broadcast_to(block[None], (chips * samp,) + block.shape)
+    window = lax.all_to_all(copies, ("chip", "samp"), 0, 0).reshape(parts, block.shape[-1])
     own, halo = pl.pallas_call(
         shard_kernel,
         out_shape=(
@@ -254,9 +281,9 @@
         in_hbm(curl_tiles),
     )
     if lax.axis_size("space") == 2:
-        beside = [shifted(halo, "space", 1)] * 2
+        beside = [across(halo, 0, 1)] * 2
     else:
-        beside = [shifted(halo, "space", -1), shifted(halo, "space", 1)]
+        beside = [across(halo, 0, -1), across(halo, 0, 1)]
     return pl.pallas_call(
         halo_kernel,
         out_shape=jax.ShapeDtypeStruct(source.shape, jnp.float32),
@@ -268,6 +295,14 @@
 
 
 def solution(mesh):
+    at = mesh.axis_names.index("harm")
+    harm = mesh.shape["harm"]
+    cores = 2 if harm % 2 == 0 else 1
+    sizes = mesh.devices.shape
+    split = jax.sharding.Mesh(
+        mesh.devices.reshape(sizes[:at] + (harm // cores, cores) + sizes[at + 1 :]),
+        mesh.axis_names[:at] + ("chip", "core") + mesh.axis_names[at + 1 :],
+    )
     placed = (
         P(GROUP, "space"),
         P("space", None, None, None),
@@ -278,7 +313,7 @@
     )
     return jax.shard_map(
         per_device,
-        mesh=mesh,
+        mesh=split,
         in_specs=placed,
         out_specs=P(GROUP, "space"),
         check_vma=False,

time: 27.6 us -> 29 us (1.051)
  waiting for transfers between devices: 2.15 us -> 4.44 us
  starting transfers between devices: 4.55 us -> 3.67 us
    ppermute x2 -> x4, waiting for transfers between devices: 2.15 us -> 4.44 us  [across(): return lax.ppermute(array, ('core', 'space'), pairs)]
    ppermute x2 -> x4, starting transfers between devices: 4.55 us -> 3.67 us  [across(): return lax.ppermute(array, ('core', 'space'), pairs)]
  transfers between devices with their start and end apart: 2 -> 4, of which waited for: 2 -> 2; matrix products, arithmetic and copies ran while one was open for 0% -> 0% of each run, Pallas kernels for 6% -> 6%
where the time goes in v8:
time: 29 us; the launch traced here: 28.8 us
  blocking collectives  13.7 us (47%)
  Pallas kernels  6.76 us (23%)
  waiting for transfers between devices  4.44 us (15%)
  starting transfers between devices  3.67 us (13%)
    all_to_all x1, blocking collectives, per_device(): lax.all_to_all(copies, ('chip', 'samp'), 0, 0)  13.7 us
    ppermute x4, waiting for transfers between devices, across(): return lax.ppermute(array, ('core', 'space'), pairs)  4.44 us
    pallas_call x1, Pallas kernels, per_device(): pl.pallas_call(shard_kernel, out_shape=(pltpu.VMEM(source.shape, jnp.floa...  4.4 us
    ppermute x4, starting transfers between devices, across(): return lax.ppermute(array, ('core', 'space'), pairs)  3.67 us
    pallas_call x1, Pallas kernels, per_device(): pl.pallas_call(fetch_kernel, out_shape=[pltpu.VMEM(shape, o.dtype) for sh...  1.75 us
    pallas_call x1, Pallas kernels, per_device(): pl.pallas_call(halo_kernel, out_shape=jax.ShapeDtypeStruct(source.shape,...  0.61 us
  transfers between devices with their start and end apart: 4, of which 2 were waited for; matrix products, arithmetic and copies ran while one was open for 0% of the time, Pallas kernels for 6%

profile of v8, /device:TPU:0, one launch (start us, length us, event | category | flops | bytes accessed | tf_op | source)
XLA Modules:
  0.0 28.8 jit_solution(2870990090992803562)
XLA Ops:
  0.0 3.0 %collective-permute-start = (bf16[2,2048]{1,0:T(2,128)(2,1)}, bf16[2,2048]{1,0:T(2,128)(2,1)S(1)}, u32[]{:S(2)}, u32[]{:S(2)}) collective-permute-start(bf16[2,2048]{1,0:T(2,128)(2,1)} %refs_3_.1), channel_id=1, source_target_pairs={{0,4},{4,0},{8,12},{12,8},{1,5},{5,1},{9,13},{13,9},{2,6},{6,2},{1... | collective-permute-start | bytes 24584 | tf_op jit(solution)/shard_map/ppermute | solution.py:42
  3.0 0.0 collective-permute-start.2
  3.0 0.1 collective-permute-start.1
  3.1 1.7 %fetch_operands.1 = (bf16[6,4,128,384]{3,2,1,0:T(8,128)(2,1)S(1)}, f32[32,2]{1,0:T(8,128)S(1)}, bf16[32,96]{1,0:T(8,128)(2,1)S(1)}, bf16[2,2048]{1,0:T(2,128)(2,...) custom-call(bf16[16,4,128,384]{3,2,1,0:T(8,128)(2,1)} %curl_hbm.1, ...), custom_call_target="tpu_custom_call" | custom-call | bytes 4718592 | tf_op jit(solution)/shard_map/fetch_operands/pallas_call | solution.py:230
  4.8 0.0 collective-permute-done
  4.9 1.4 %collective-permute-done.1 = bf16[2,2048]{1,0:T(2,128)(2,1)S(1)} collective-permute-done((bf16[2,2048]{1,0:T(2,128)(2,1)}, bf16[2,2048]{1,0:T(2,128)(2,1)S(1)}, u32[]{:S(2)}, u32[]{:S(2)}) %collective-permute-start.1) | collective-permute-done | bytes 8224 | tf_op jit(solution)/shard_map/ppermute | solution.py:42
  6.3 0.0 collective-permute-done.2
  6.3 0.1 broadcast_in_dim.2
  6.4 13.7 %all_to_all.5 = bf16[8,2,2,2304]{3,2,1,0:T(2,128)(2,1)S(1)} all-to-all(bf16[8,2,2,2304]{3,2,1,0:T(2,128)(2,1)S(1)} %broadcast_in_dim.2), channel_id=1, replica_groups=mesh['chip'=2,'core'=2,'space'=2,'samp'=4] {'chip','samp'}, dimensions={0} | all-to-all | bytes 294912 | tf_op jit(solution)/shard_map/all_to_all | solution.py:251
  20.1 0.1 reshape.4.window
  20.2 4.4 %shard_residual.1 = (f32[2,2048]{1,0:T(2,128)S(1)}, f32[2,256]{1,0:T(2,128)S(1)}) custom-call(bf16[32,2304]{1,0:T(8,128)(2,1)S(1)} %reshape.4.window, bf16[6,4,128,384]{3,2,1,0:T(8,128)(2,1)S(1)} %get-tuple-element.16.first_curl, f32[32,2]{1,0:T(8,128)S(1)} %get-tuple-element.17.table, bf16[32,96]{1,0:T(8,128)(2,1)S(1)} %get-tuple-element.18.pieces, ...), custom_call_target="tpu_custom_call" | custom-call | flops 805306368 | bytes 6291456 | tf_op jit(solution)/shard_map/shard_residual/pallas_call | solution.py:252
  24.6 0.6 %collective-permute-start.3 = (f32[2,256]{1,0:T(2,128)S(1)}, f32[2,256]{1,0:T(2,128)S(1)}, u32[]{:S(2)}, u32[]{:S(2)}) collective-permute-start(f32[2,256]{1,0:T(2,128)S(1)} %get-tuple-element.24), channel_id=1, source_target_pairs={{0,4},{4,0},{8,12},{12,8},{1,5},{5,1},{9,13},{13,9},{2,6},{6,2},{1... | collective-permute-start | bytes 6152 | tf_op jit(solution)/shard_map/ppermute | solution.py:42
  25.2 3.1 %collective-permute-done.3.from_right.from_left = f32[2,256]{1,0:T(2,128)S(1)} collective-permute-done((f32[2,256]{1,0:T(2,128)S(1)}, f32[2,256]{1,0:T(2,128)S(1)}, u32[]{:S(2)}, u32[]{:S(2)}) %collective-permute-start.3) | collective-permute-done | bytes 2080 | tf_op jit(solution)/shard_map/ppermute | solution.py:42
  28.2 0.6 %halo_sum.1 = f32[2,2048]{1,0:T(2,128)} custom-call(f32[2,2048]{1,0:T(2,128)S(1)} %get-tuple-element.23.own, f32[2,256]{1,0:T(2,128)S(1)} %collective-permute-done.3.from_right.from_left, f32[2,256]{1,0:T(2,128)S(1)} %collective-permute-done.3.from_right.from_left), custom_call_target="tpu_custom_call" | custom-call | tf_op jit(solution)/shard_map/halo_sum/pallas_call | solution.py:287
  (5 shorter events, 0.1 us)
Async XLA Ops:
  0.0 4.8 %collective-permute-start = (bf16[2,2048]{1,0:T(2,128)(2,1)}, bf16[2,2048]{1,0:T(2,128)(2,1)S(1)}, u32[]{:S(2)}, u32[]{:S(2)}) collective-permute-start(bf16[2,2048]{1,0:T(2,128)(2,1)} %refs_3_.1), channel_id=1, source_target_pairs={{0,4},{4,0},{8,12},{12,8},{1,5},{5,1},{9,13},{13,9},{2,6},{6,2},{1... | collective-permute-start | bytes 24584 | tf_op jit(solution)/shard_map/ppermute | solution.py:42
  3.0 3.3 %collective-permute-start.2 = (bf16[2,2048]{1,0:T(2,128)(2,1)}, bf16[2,2048]{1,0:T(2,128)(2,1)S(1)}, u32[]{:S(2)}, u32[]{:S(2)}) collective-permute-start(bf16[2,2048]{1,0:T(2,128)(2,1)} %refs_3_.1), channel_id=1, source_target_pairs={{0,8},{4,12},{8,0},{12,4},{1,9},{5,13},{9,1},{13,5},{2,10},{6,14},... | collective-permute-start | bytes 24584 | tf_op jit(solution)/shard_map/ppermute | solution.py:42
  3.0 3.3 %collective-permute-start.1 = (bf16[2,2048]{1,0:T(2,128)(2,1)}, bf16[2,2048]{1,0:T(2,128)(2,1)S(1)}, u32[]{:S(2)}, u32[]{:S(2)}) collective-permute-start(bf16[2,2048]{1,0:T(2,128)(2,1)} %refs_3_.1), channel_id=1, source_target_pairs={{0,12},{4,8},{8,4},{12,0},{1,13},{5,9},{9,5},{13,1},{2,14},{6,10},... | collective-permute-start | bytes 24584 | tf_op jit(solution)/shard_map/ppermute | solution.py:42
  24.6 3.7 %collective-permute-start.3 = (f32[2,256]{1,0:T(2,128)S(1)}, f32[2,256]{1,0:T(2,128)S(1)}, u32[]{:S(2)}, u32[]{:S(2)}) collective-permute-start(f32[2,256]{1,0:T(2,128)S(1)} %get-tuple-element.24), channel_id=1, source_target_pairs={{0,4},{4,0},{8,12},{12,8},{1,5},{5,1},{9,13},{13,9},{2,6},{6,2},{1... | collective-permute-start | bytes 6152 | tf_op jit(solution)/shard_map/ppermute | solution.py:42

commit v9 on v6

--- a/solution.py
+++ b/solution.py
@@ -135,7 +135,7 @@
         for link, at in enumerate(places[elem]):
             sums[link][at] += contrib[:, link * tile : (link + 1) * tile]
 
-    step = 2
+    step = 4
     chunks = [range(at, min(at + step, tile_count)) for at in range(0, tile_count, step)]
     projected = {}
     for turn in range(len(chunks) + 2):
@@ -220,8 +220,8 @@
 
     right, left = from_neighbours(coeffs, tile)
     block = jnp.concatenate([left, coeffs_here, right], axis=1)
-    copies = jnp.broadcast_to(block[None], (group_size,) + block.shape)
-    window = lax.all_to_all(copies, GROUP, 0, 0).reshape(parts, block.shape[1])
+    near = lax.all_gather(block, "samp", axis=0, tiled=True)
+    window = lax.all_gather(near, "harm", axis=0, tiled=True)
     own, halo = pl.pallas_call(
         shard_kernel,
         out_shape=(

time: 27.6 us -> 33.4 us (1.21)
  blocking collectives: 13.7 us -> 19.3 us
    all_gather x0 -> x2, blocking collectives: none -> 19.3 us  [the longest x1 13.9 us: per_device(): near = lax.all_gather(block, 'samp', axis=0, tiled=True)]
    all_to_all x1 -> x0, blocking collectives: 13.7 us -> none  [per_device(): window = lax.all_to_all(copies, GROUP, 0, 0).reshape(parts, block.shape[1])]
  transfers between devices with their start and end apart: 2 -> 2, of which waited for: 2 -> 2; matrix products, arithmetic and copies ran while one was open for 0% -> 0% of each run, Pallas kernels for 6% -> 5%
where the time goes in v9:
time: 33.4 us; the launch traced here: 33.2 us
  blocking collectives  19.3 us (58%)
  Pallas kernels  7.07 us (21%)
  starting transfers between devices  4.55 us (14%)
  waiting for transfers between devices  2.15 us (6%)
    all_gather x1, blocking collectives, per_device(): near = lax.all_gather(block, 'samp', axis=0, tiled=True)  13.9 us
    all_gather x1, blocking collectives, per_device(): window = lax.all_gather(near, 'harm', axis=0, tiled=True)  5.47 us
    pallas_call x1, Pallas kernels, per_device(): pl.pallas_call(shard_kernel, out_shape=(pltpu.VMEM(source.shape, jnp.floa...  4.71 us
    ppermute x2, starting transfers between devices, shifted(): lax.ppermute(array, axis, [(i, (i + by) % count) for i in range(count)])  4.55 us
    ppermute x2, waiting for transfers between devices, shifted(): lax.ppermute(array, axis, [(i, (i + by) % count) for i in range(count)])  2.15 us
    pallas_call x1, Pallas kernels, per_device(): pl.pallas_call(fetch_kernel, out_shape=[pltpu.VMEM(shape, o.dtype) for sh...  1.75 us
  transfers between devices with their start and end apart: 2, of which 2 were waited for; matrix products, arithmetic and copies ran while one was open for 0% of the time, Pallas kernels for 5%

profile of v9, /device:TPU:0, one launch (start us, length us, event | category | flops | bytes accessed | tf_op | source)
XLA Modules:
  0.0 33.2 jit_solution(4337319832382513452)
XLA Ops:
  0.0 3.0 %collective-permute-start = (bf16[2,2048]{1,0:T(2,128)(2,1)}, bf16[2,2048]{1,0:T(2,128)(2,1)S(1)}, u32[]{:S(2)}, u32[]{:S(2)}) collective-permute-start(bf16[2,2048]{1,0:T(2,128)(2,1)} %refs_2_.1), channel_id=1, source_target_pairs={{0,4},{4,0},{1,5},{5,1},{2,6},{6,2},{3,7},{7,3},{8,12},{12,8},{9,1... | collective-permute-start | bytes 24584 | tf_op jit(solution)/shard_map/ppermute | solution.py:37
  3.0 1.7 %fetch_operands.1 = (bf16[6,4,128,384]{3,2,1,0:T(8,128)(2,1)S(1)}, f32[32,2]{1,0:T(8,128)S(1)}, bf16[2,2048]{1,0:T(2,128)(2,1)S(1)}, bf16[32,96]{1,0:T(8,128)(2,...) custom-call(bf16[16,4,128,384]{3,2,1,0:T(8,128)(2,1)} %curl_hbm.1, ...), custom_call_target="tpu_custom_call" | custom-call | bytes 4718592 | tf_op jit(solution)/shard_map/fetch_operands/pallas_call | solution.py:207
  4.7 0.1 collective-permute-done
  4.8 13.9 %all-gather = bf16[4,2,2304]{2,1,0:T(2,128)(2,1)S(1)} all-gather(bf16[1,2,2304]{2,1,0:T(2,128)(2,1)S(1)} %maximum_bitcast_fusion), channel_id=1, replica_groups=mesh['harm'=4,'space'=2,'samp'=4] {'samp'}, dimensions={0}, use_global_device_ids=true | all-gather | bytes 46080 | tf_op jit(solution)/shard_map/all_gather | solution.py:223
  18.7 5.5 %all_gather.7.window = bf16[32,2304]{1,0:T(8,128)(2,1)S(1)} all-gather(bf16[8,2304]{1,0:T(8,128)(2,1)S(1)} %reshape.1), channel_id=1, replica_groups=mesh['harm'=4,'space'=2,'samp'=4] {'harm'}, dimensions={0}, use_global_device_ids=true | all-gather | bytes 184320 | tf_op jit(solution)/shard_map/all_gather | solution.py:224
  24.2 4.7 %shard_residual.1 = (f32[2,2048]{1,0:T(2,128)S(1)}, f32[2,256]{1,0:T(2,128)S(1)}) custom-call(bf16[32,2304]{1,0:T(8,128)(2,1)S(1)} %all_gather.7.window, bf16[6,4,128,384]{3,2,1,0:T(8,128)(2,1)S(1)} %get-tuple-element.16.first_curl, f32[32,2]{1,0:T(8,128)S(1)} %get-tuple-element.17.table, bf16[32,96]{1,0:T(8,128)(2,1)S(1)} %get-tuple-element.18.pieces, ...), custom_call_target="tpu_custom_call" | custom-call | flops 805306368 | bytes 6291456 | tf_op jit(solution)/shard_map/shard_residual/pallas_call | solution.py:225
  28.9 1.6 %collective-permute-start.1 = (f32[2,256]{1,0:T(2,128)S(1)}, f32[2,256]{1,0:T(2,128)S(1)}, u32[]{:S(2)}, u32[]{:S(2)}) collective-permute-start(f32[2,256]{1,0:T(2,128)S(1)} %get-tuple-element.24), channel_id=1, source_target_pairs={{0,4},{4,0},{1,5},{5,1},{2,6},{6,2},{3,7},{7,3},{8,12},{12,8},{9,1... | collective-permute-start | bytes 6152 | tf_op jit(solution)/shard_map/ppermute | solution.py:37
  30.5 2.1 %collective-permute-done.1.from_right.from_left = f32[2,256]{1,0:T(2,128)S(1)} collective-permute-done((f32[2,256]{1,0:T(2,128)S(1)}, f32[2,256]{1,0:T(2,128)S(1)}, u32[]{:S(2)}, u32[]{:S(2)}) %collective-permute-start.1) | collective-permute-done | bytes 2080 | tf_op jit(solution)/shard_map/ppermute | solution.py:37
  32.6 0.6 %halo_sum.1 = f32[2,2048]{1,0:T(2,128)} custom-call(f32[2,2048]{1,0:T(2,128)S(1)} %get-tuple-element.23.own, f32[2,256]{1,0:T(2,128)S(1)} %collective-permute-done.1.from_right.from_left, f32[2,256]{1,0:T(2,128)S(1)} %collective-permute-done.1.from_right.from_left), custom_call_target="tpu_custom_call" | custom-call | tf_op jit(solution)/shard_map/halo_sum/pallas_call | solution.py:260
  (3 shorter events, 0.0 us)
Async XLA Ops:
  0.0 4.8 %collective-permute-start = (bf16[2,2048]{1,0:T(2,128)(2,1)}, bf16[2,2048]{1,0:T(2,128)(2,1)S(1)}, u32[]{:S(2)}, u32[]{:S(2)}) collective-permute-start(bf16[2,2048]{1,0:T(2,128)(2,1)} %refs_2_.1), channel_id=1, source_target_pairs={{0,4},{4,0},{1,5},{5,1},{2,6},{6,2},{3,7},{7,3},{8,12},{12,8},{9,1... | collective-permute-start | bytes 24584 | tf_op jit(solution)/shard_map/ppermute | solution.py:37
  28.9 3.7 %collective-permute-start.1 = (f32[2,256]{1,0:T(2,128)S(1)}, f32[2,256]{1,0:T(2,128)S(1)}, u32[]{:S(2)}, u32[]{:S(2)}) collective-permute-start(f32[2,256]{1,0:T(2,128)S(1)} %get-tuple-element.24), channel_id=1, source_target_pairs={{0,4},{4,0},{1,5},{5,1},{2,6},{6,2},{3,7},{7,3},{8,12},{12,8},{9,1... | collective-permute-start | bytes 6152 | tf_op jit(solution)/shard_map/ppermute | solution.py:37

commit v10 on v8

--- a/solution.py
+++ b/solution.py
@@ -45,17 +45,17 @@
 def from_neighbours(array, tile, core_step):
     if lax.axis_size("space") == 2:
         other = across(array, core_step, 1)
-        return other[:, :tile], other[:, -tile:]
-    return across(array[:, :tile], core_step, -1), across(array[:, -tile:], core_step, 1)
+        return other[..., :tile], other[..., -tile:]
+    return across(array[..., :tile], core_step, -1), across(array[..., -tile:], core_step, 1)
 
 
 def arrival_order(chips, cores, samp, parts_here):
     ranks = [
         [
             (chip * cores + (c - step) % cores) * samp + s
+            for step in range(cores)
             for chip in range(chips)
             for s in range(samp)
-            for step in range(cores)
         ]
         for c in range(cores)
     ]
@@ -155,7 +155,7 @@
         for link, at in enumerate(places[elem]):
             sums[link][at] += contrib[:, link * tile : (link + 1) * tile]
 
-    step = 2
+    step = 1
     chunks = [range(at, min(at + step, tile_count)) for at in range(0, tile_count, step)]
     projected = {}
     for turn in range(len(chunks) + 2):
@@ -216,7 +216,6 @@
         curl_tiles,
         own_columns,
         pieces,
-        coeffs,
         source,
         pattern.T,
         region_ids,
@@ -239,16 +238,18 @@
         ),
         name="fetch_operands",
     )(*[in_hbm(operand) for operand in operands])
-    first_curl, columns_here, pieces_here, coeffs_here, *others = fetched
-
+    first_curl, columns_here, pieces_here, *others = fetched
+
+    copies = jnp.broadcast_to(coeffs[None], (chips * samp,) + coeffs.shape)
+    near = lax.all_to_all(copies, ("chip", "samp"), 0, 0)
+    near, first_curl = lax.optimization_barrier((near, first_curl))
+    edges = jnp.concatenate([near[..., :tile], near[..., -tile:]], axis=-1)
     blocks = []
     for step in range(cores):
-        right, left = from_neighbours(coeffs, tile, step)
-        middle = across(coeffs, step, 0) if step else coeffs_here
-        blocks.append(jnp.concatenate([left, middle, right], axis=1))
-    block = jnp.stack(blocks)
-    copies = jnp.broadcast_to(block[None], (chips * samp,) + block.shape)
-    window = lax.all_to_all(copies, ("chip", "samp"), 0, 0).reshape(parts, block.shape[-1])
+        right, left = from_neighbours(edges, tile, step)
+        middle = across(near, step, 0) if step else near
+        blocks.append(jnp.concatenate([left, middle, right], axis=-1))
+    window = jnp.concatenate(blocks, axis=0).reshape(parts, -1)
     own, halo = pl.pallas_call(
         shard_kernel,
         out_shape=(

time: 29 us -> 28.4 us (0.979)
  blocking collectives: 13.7 us -> 0 us
  starting transfers between devices: 3.67 us -> 10.8 us
  waiting for transfers between devices: 4.44 us -> 9.17 us
  local copies, waits for them, and re-layouts: 0.15 us -> 1.44 us
    all_to_all x1 -> x0, blocking collectives: 13.7 us -> none  [per_device(): lax.all_to_all(copies, ('chip', 'samp'), 0, 0)]
    all_to_all x0 -> x1, starting transfers between devices: none -> 7.25 us  [per_device(): near = lax.all_to_all(copies, ('chip', 'samp'), 0, 0)]
    all_to_all x0 -> x1, waiting for transfers between devices: none -> 5.25 us  [per_device(): near = lax.all_to_all(copies, ('chip', 'samp'), 0, 0)]
    broadcast_in_dim x1, local copies, waits for them, and re-layouts: 0.08 us -> 1.36 us  [per_device(): copies = jnp.broadcast_to(coeffs[None], (chips * samp,) + coeffs.shape)]
    ppermute x4, waiting for transfers between devices: 4.44 us -> 3.92 us  [across(): return lax.ppermute(array, ('core', 'space'), pairs)]
  transfers between devices with their start and end apart: 4 -> 5, of which waited for: 2 -> 4; matrix products, arithmetic and copies ran while one was open for 0% -> 0% of each run, Pallas kernels for 6% -> 6%
where the time goes in v10:
time: 28.4 us; the launch traced here: 28.1 us
  starting transfers between devices  10.8 us (38%)
  waiting for transfers between devices  9.17 us (32%)
  Pallas kernels  6.53 us (23%)
  local copies, waits for them, and re-layouts  1.44 us (5%)
    all_to_all x1, starting transfers between devices, per_device(): near = lax.all_to_all(copies, ('chip', 'samp'), 0, 0)  7.25 us
    all_to_all x1, waiting for transfers between devices, per_device(): near = lax.all_to_all(copies, ('chip', 'samp'), 0, 0)  5.25 us
    pallas_call x1, Pallas kernels, per_device(): pl.pallas_call(shard_kernel, out_shape=(pltpu.VMEM(source.shape, jnp.floa...  4.18 us
    ppermute x4, waiting for transfers between devices, across(): return lax.ppermute(array, ('core', 'space'), pairs)  3.92 us
    ppermute x4, starting transfers between devices, across(): return lax.ppermute(array, ('core', 'space'), pairs)  3.51 us
    pallas_call x1, Pallas kernels, per_device(): pl.pallas_call(fetch_kernel, out_shape=[pltpu.VMEM(shape, o.dtype) for sh...  1.74 us
    broadcast_in_dim x1, local copies, waits for them, and re-layouts, per_device(): copies = jnp.broadcast_to(coeffs[None], (chips * samp,) + coeffs.shape)  1.36 us
    pallas_call x1, Pallas kernels, per_device(): pl.pallas_call(halo_kernel, out_shape=jax.ShapeDtypeStruct(source.shape,...  0.61 us
  transfers between devices with their start and end apart: 5, of which 4 were waited for; matrix products, arithmetic and copies ran while one was open for 0% of the time, Pallas kernels for 6%

profile of v10, /device:TPU:0, one launch (start us, length us, event | category | flops | bytes accessed | tf_op | source)
XLA Modules:
  0.0 28.1 jit_solution(2217055717040084628)
XLA Ops:
  0.0 1.4 %broadcast_in_dim.2 = bf16[8,2,2048]{2,1,0:T(2,128)(2,1)} broadcast(bf16[2,2048]{1,0:T(2,128)(2,1)} %param.8), dimensions={1,2} | broadcast | bytes 73728 | tf_op jit(solution)/shard_map/broadcast_in_dim | solution.py:243
  1.4 7.3 %all-to-all-start = ((bf16[8,2,2048]{2,1,0:T(2,128)(2,1)}), bf16[8,2,2048]{2,1,0:T(2,128)(2,1)S(1)}, u32[]{:S(2)}, u32[]{:S(2)}) async-start(bf16[8,2,2048]{2,1,0:T(2,128)(2,1)} %broadcast_in_dim.2), calls=%async_computation | async-start | bytes 131072 | tf_op jit(solution)/shard_map/all_to_all | solution.py:244
  8.6 1.7 %fetch_operands.1 = (bf16[6,4,128,384]{3,2,1,0:T(8,128)(2,1)S(1)}, f32[32,2]{1,0:T(8,128)S(1)}, bf16[32,96]{1,0:T(8,128)(2,1)S(1)}, f32[2,2048]{1,0:T(2,128)S(1)...) custom-call(bf16[16,4,128,384]{3,2,1,0:T(8,128)(2,1)} %curl_hbm.1, f32[16,32,2]{2,1,0:T(8,128)} %constant.5.clone.refs_1_, ...), custom_call_target="tpu_custom_call" | custom-call | bytes 4718592 | tf_op jit(solution)/shard_map/fetch_operands/pallas_call | solution.py:229
  10.4 5.2 %all-to-all-done = bf16[8,2,2048]{2,1,0:T(2,128)(2,1)S(1)} async-done(((bf16[8,2,2048]{2,1,0:T(2,128)(2,1)}), bf16[8,2,2048]{2,1,0:T(2,128)(2,1)S(1)}, u32[]{:S(2)}, u32[]{:S(2)}) %all-to-all-start) | async-done | bytes 65568 | tf_op jit(solution)/shard_map/all_to_all | solution.py:244
  15.6 0.1 collective-permute-start.1
  15.7 1.6 %collective-permute-start = (bf16[8,2,256]{2,1,0:T(2,128)(2,1)S(1)}, bf16[8,2,256]{2,1,0:T(2,128)(2,1)S(1)}, u32[]{:S(2)}, u32[]{:S(2)}) collective-permute-start(bf16[8,2,256]{2,1,0:T(2,128)(2,1)S(1)} %pad_maximum_fusion), channel_id=1, source_target_pairs={{0,4},{4,0},{8,12},{12,8},{1,5},{5,1},{9,13},{13,9},{2,6},{6,2},{1... | collective-permute-start | bytes 24584 | tf_op jit(solution)/shard_map/ppermute | solution.py:42
  17.3 0.3 collective-permute-start.2
  17.6 1.2 %collective-permute-done.1 = bf16[8,2,256]{2,1,0:T(2,128)(2,1)S(1)} collective-permute-done((bf16[8,2,256]{2,1,0:T(2,128)(2,1)S(1)}, bf16[8,2,256]{2,1,0:T(2,128)(2,1)S(1)}, u32[]{:S(2)}, u32[]{:S(2)}) %collective-permute-start.1) | collective-permute-done | bytes 8224 | tf_op jit(solution)/shard_map/ppermute | solution.py:42
  18.8 0.6 %collective-permute-done = bf16[8,2,256]{2,1,0:T(2,128)(2,1)S(1)} collective-permute-done((bf16[8,2,256]{2,1,0:T(2,128)(2,1)S(1)}, bf16[8,2,256]{2,1,0:T(2,128)(2,1)S(1)}, u32[]{:S(2)}, u32[]{:S(2)}) %collective-permute-start) | collective-permute-done | bytes 8224 | tf_op jit(solution)/shard_map/ppermute | solution.py:42
  19.4 0.0 collective-permute-done.2
  19.5 0.1 maximum_maximum_fusion
  19.6 0.1 reshape.4.window
  19.7 4.2 %shard_residual.1 = (f32[2,2048]{1,0:T(2,128)S(1)}, f32[2,256]{1,0:T(2,128)S(1)}) custom-call(bf16[32,2304]{1,0:T(8,128)(2,1)S(1)} %reshape.4.window, bf16[6,4,128,384]{3,2,1,0:T(8,128)(2,1)S(1)} %get-tuple-element.18.first_curl, f32[32,2]{1,0:T(8,128)S(1)} %get-tuple-element.19.table, bf16[32,96]{1,0:T(8,128)(2,1)S(1)} %get-tuple-element.20.pieces, ...), custom_call_target="tpu_custom_call" | custom-call | flops 805306368 | bytes 6291456 | tf_op jit(solution)/shard_map/shard_residual/pallas_call | solution.py:253
  23.9 1.6 %collective-permute-start.3 = (f32[2,256]{1,0:T(2,128)S(1)}, f32[2,256]{1,0:T(2,128)S(1)}, u32[]{:S(2)}, u32[]{:S(2)}) collective-permute-start(f32[2,256]{1,0:T(2,128)S(1)} %get-tuple-element.26), channel_id=1, source_target_pairs={{0,4},{4,0},{8,12},{12,8},{1,5},{5,1},{9,13},{13,9},{2,6},{6,2},{1... | collective-permute-start | bytes 6152 | tf_op jit(solution)/shard_map/ppermute | solution.py:42
  25.4 2.1 %collective-permute-done.3.from_right.from_left = f32[2,256]{1,0:T(2,128)S(1)} collective-permute-done((f32[2,256]{1,0:T(2,128)S(1)}, f32[2,256]{1,0:T(2,128)S(1)}, u32[]{:S(2)}, u32[]{:S(2)}) %collective-permute-start.3) | collective-permute-done | bytes 2080 | tf_op jit(solution)/shard_map/ppermute | solution.py:42
  27.5 0.6 %halo_sum.1 = f32[2,2048]{1,0:T(2,128)} custom-call(f32[2,2048]{1,0:T(2,128)S(1)} %get-tuple-element.25.own, f32[2,256]{1,0:T(2,128)S(1)} %collective-permute-done.3.from_right.from_left, f32[2,256]{1,0:T(2,128)S(1)} %collective-permute-done.3.from_right.from_left), custom_call_target="tpu_custom_call" | custom-call | tf_op jit(solution)/shard_map/halo_sum/pallas_call | solution.py:288
  (4 shorter events, 0.0 us)
Async XLA Ops:
  1.4 14.2 %all-to-all-start = ((bf16[8,2,2048]{2,1,0:T(2,128)(2,1)}), bf16[8,2,2048]{2,1,0:T(2,128)(2,1)S(1)}, u32[]{:S(2)}, u32[]{:S(2)}) async-start(bf16[8,2,2048]{2,1,0:T(2,128)(2,1)} %broadcast_in_dim.2), calls=%async_computation | async-start | bytes 131072 | tf_op jit(solution)/shard_map/all_to_all | solution.py:244
  15.6 3.2 %collective-permute-start.1 = (bf16[8,2,256]{2,1,0:T(2,128)(2,1)S(1)}, bf16[8,2,256]{2,1,0:T(2,128)(2,1)S(1)}, u32[]{:S(2)}, u32[]{:S(2)}) collective-permute-start(bf16[8,2,256]{2,1,0:T(2,128)(2,1)S(1)} %pad_maximum_fusion), channel_id=1, source_target_pairs={{0,12},{4,8},{8,4},{12,0},{1,13},{5,9},{9,5},{13,1},{2,14},{6,10},... | collective-permute-start | bytes 24584 | tf_op jit(solution)/shard_map/ppermute | solution.py:42
  15.7 3.7 %collective-permute-start = (bf16[8,2,256]{2,1,0:T(2,128)(2,1)S(1)}, bf16[8,2,256]{2,1,0:T(2,128)(2,1)S(1)}, u32[]{:S(2)}, u32[]{:S(2)}) collective-permute-start(bf16[8,2,256]{2,1,0:T(2,128)(2,1)S(1)} %pad_maximum_fusion), channel_id=1, source_target_pairs={{0,4},{4,0},{8,12},{12,8},{1,5},{5,1},{9,13},{13,9},{2,6},{6,2},{1... | collective-permute-start | bytes 24584 | tf_op jit(solution)/shard_map/ppermute | solution.py:42
  17.3 2.1 %collective-permute-start.2 = (bf16[8,2,2048]{2,1,0:T(2,128)(2,1)S(1)}, bf16[8,2,2048]{2,1,0:T(2,128)(2,1)S(1)}, u32[]{:S(2)}, u32[]{:S(2)}) collective-permute-start(bf16[8,2,2048]{2,1,0:T(2,128)(2,1)S(1)} %all-to-all-done), channel_id=1, source_target_pairs={{0,8},{4,12},{8,0},{12,4},{1,9},{5,13},{9,1},{13,5},{2,10},{6,14},... | collective-permute-start | bytes 196616 | tf_op jit(solution)/shard_map/ppermute | solution.py:42
  23.9 3.7 %collective-permute-start.3 = (f32[2,256]{1,0:T(2,128)S(1)}, f32[2,256]{1,0:T(2,128)S(1)}, u32[]{:S(2)}, u32[]{:S(2)}) collective-permute-start(f32[2,256]{1,0:T(2,128)S(1)} %get-tuple-element.26), channel_id=1, source_target_pairs={{0,4},{4,0},{8,12},{12,8},{1,5},{5,1},{9,13},{13,9},{2,6},{6,2},{1... | collective-permute-start | bytes 6152 | tf_op jit(solution)/shard_map/ppermute | solution.py:42

commit v11 on v6

--- a/solution.py
+++ b/solution.py
@@ -77,13 +77,14 @@
     later_curl,
     timed,
     densities,
+    totals,
     small_sems,
     curl_sem,
-    *sums,
 ):
     tile_count, links, tile, comps = curl_hbm.shape
     early = first_curl.shape[0]
     parts_here = out.shape[0]
+    slots = links * parts_here
     fetched = [(pattern_in, pattern), (region_in, region_ids), (law_in, law)]
     small = [
         pltpu.make_async_copy(src, dst, small_sems.at[i]) for i, (src, dst) in enumerate(fetched)
@@ -91,8 +92,6 @@
     rest = pltpu.make_async_copy(curl_hbm.at[early:], later_curl, curl_sem)
     for copy in small + [rest]:
         copy.start()
-    for total in sums:
-        total[...] = jnp.zeros_like(total)
     stacked = jnp.concatenate([window[...]] * 3, axis=0)
     samples = jnp.dot(pieces[...], stacked, preferred_element_type=jnp.float32)
     high = samples.astype(jnp.bfloat16)
@@ -126,16 +125,21 @@
         reluct = law[0, region] + law[2, region] * square / (square + law[1, region])
         field = jnp.concatenate([reluct * c for c in comp], axis=1)
         rows = [jnp.sum(column * field, axis=0, keepdims=True) for column in columns]
-        return (jnp.concatenate(rows, axis=0) * (4.0 / SAMPLES)).astype(jnp.bfloat16)
+        return jnp.concatenate(rows * links, axis=0) * (4.0 / SAMPLES)
 
     def contribute(elem, projected):
+        empty = jnp.zeros_like(projected)
+        spread = [projected if other == elem else empty for other in range(tile_count)]
+        spread = jnp.concatenate(spread, axis=0).astype(jnp.bfloat16)
         contrib = lax.dot_general(
-            projected, blocks(elem), (((1,), (1,)), ((), ())), preferred_element_type=jnp.float32
+            blocks(elem), spread, (((1,), (1,)), ((), ())), preferred_element_type=jnp.float32
         )
-        for link, at in enumerate(places[elem]):
-            sums[link][at] += contrib[:, link * tile : (link + 1) * tile]
-
-    step = 2
+        if elem:
+            totals[...] += contrib
+        else:
+            totals[...] = contrib
+
+    step = 1
     chunks = [range(at, min(at + step, tile_count)) for at in range(0, tile_count, step)]
     projected = {}
     for turn in range(len(chunks) + 2):
@@ -151,11 +155,35 @@
             for elem in chunks[turn - 2]:
                 contribute(elem, projected[elem])
 
+    width = tile_count * slots
+    column = lax.broadcasted_iota(jnp.int32, (tile, width), 1)
+    kept = jnp.zeros((tile, width), jnp.float32)
+    for link in range(links):
+        block = totals[link * tile : (link + 1) * tile, :]
+        kept = jnp.where(column % slots // parts_here == link, block, kept)
+    kept_pieces = []
+    for _ in range(3):
+        piece = kept.astype(jnp.bfloat16)
+        kept_pieces.append(piece)
+        kept = kept - piece.astype(jnp.float32)
+    rows_out = (tile_count + 2) * parts_here
+    row = lax.broadcasted_iota(jnp.int32, (rows_out, width), 0)
+    column = lax.broadcasted_iota(jnp.int32, (rows_out, width), 1)
+    target = jnp.full((1, width), -1, jnp.int32)
+    lane = lax.broadcasted_iota(jnp.int32, (1, width), 1) // parts_here
+    for elem in range(tile_count):
+        for link in range(links):
+            target = jnp.where(lane == elem * links + link, places[elem][link], target)
+    hits = (target * parts_here + column % parts_here == row).astype(jnp.bfloat16)
+    sums = lax.dot_general(
+        jnp.concatenate([hits] * 3, axis=1),
+        jnp.concatenate(kept_pieces, axis=1),
+        (((1,), (1,)), ((), ())),
+        preferred_element_type=jnp.float32,
+    )
+
     def window_sum(w):
-        total = sums[0][w]
-        for other in sums[1:]:
-            total = total + other[w]
-        return total
+        return sums[w * parts_here : (w + 1) * parts_here]
 
     for w in range(tile_count):
         at = slice(w * tile, (w + 1) * tile)
@@ -237,10 +265,10 @@
             pltpu.VMEM((tile_count - early,) + curl_tiles.shape[1:], curl_tiles.dtype),
             pltpu.VMEM((SAMPLES, (tile_count + 2) * tile), jnp.bfloat16),
             pltpu.VMEM((tile_count, HALF, comps), jnp.float32),
+            pltpu.VMEM((links * tile, tile_count * links * parts_here), jnp.float32),
             pltpu.SemaphoreType.DMA((3,)),
             pltpu.SemaphoreType.DMA,
-        ]
-        + [pltpu.VMEM((tile_count + 2, parts_here, tile), jnp.float32)] * links,
+        ],
         compiler_params=pltpu.CompilerParams(vmem_limit_bytes=32 * MIB),
         cost_estimate=pl.CostEstimate(
             flops=4 * SAMPLES * tile_count * links * tile * comps,

time: 27.6 us -> 27.5 us (level)
  no operation moved by 1% of the time
where the time goes in v11:
time: 27.5 us; the launch traced here: 27.2 us
  blocking collectives  13.7 us (50%)
  Pallas kernels  6.65 us (24%)
  starting transfers between devices  4.54 us (17%)
  waiting for transfers between devices  2.16 us (8%)
    all_to_all x1, blocking collectives, per_device(): window = lax.all_to_all(copies, GROUP, 0, 0).reshape(parts, block.shape[1])  13.7 us
    ppermute x2, starting transfers between devices, shifted(): lax.ppermute(array, axis, [(i, (i + by) % count) for i in range(count)])  4.54 us
    pallas_call x1, Pallas kernels, per_device(): pl.pallas_call(shard_kernel, out_shape=(pltpu.VMEM(source.shape, jnp.floa...  4.29 us
    ppermute x2, waiting for transfers between devices, shifted(): lax.ppermute(array, axis, [(i, (i + by) % count) for i in range(count)])  2.16 us
    pallas_call x1, Pallas kernels, per_device(): pl.pallas_call(fetch_kernel, out_shape=[pltpu.VMEM(shape, o.dtype) for sh...  1.75 us
    pallas_call x1, Pallas kernels, per_device(): pl.pallas_call(halo_kernel, out_shape=jax.ShapeDtypeStruct(source.shape,...  0.61 us
  transfers between devices with their start and end apart: 2, of which 2 were waited for; matrix products, arithmetic and copies ran while one was open for 0% of the time, Pallas kernels for 6%

profile of v11, /device:TPU:0, one launch (start us, length us, event | category | flops | bytes accessed | tf_op | source)
XLA Modules:
  0.0 27.2 jit_solution(12281968489910740288)
XLA Ops:
  0.0 3.0 %collective-permute-start = (bf16[2,2048]{1,0:T(2,128)(2,1)}, bf16[2,2048]{1,0:T(2,128)(2,1)S(1)}, u32[]{:S(2)}, u32[]{:S(2)}) collective-permute-start(bf16[2,2048]{1,0:T(2,128)(2,1)} %refs_2_.1), channel_id=1, source_target_pairs={{0,4},{4,0},{1,5},{5,1},{2,6},{6,2},{3,7},{7,3},{8,12},{12,8},{9,1... | collective-permute-start | bytes 24584 | tf_op jit(solution)/shard_map/ppermute | solution.py:37
  3.0 1.7 %fetch_operands.1 = (bf16[6,4,128,384]{3,2,1,0:T(8,128)(2,1)S(1)}, f32[32,2]{1,0:T(8,128)S(1)}, bf16[2,2048]{1,0:T(2,128)(2,1)S(1)}, bf16[32,96]{1,0:T(8,128)(2,...) custom-call(bf16[16,4,128,384]{3,2,1,0:T(8,128)(2,1)} %curl_hbm.1, ...), custom_call_target="tpu_custom_call" | custom-call | bytes 4718592 | tf_op jit(solution)/shard_map/fetch_operands/pallas_call | solution.py:235
  4.7 0.1 collective-permute-done
  4.8 0.1 broadcast_in_dim.2
  4.9 13.7 %all_to_all.5 = bf16[16,2,2304]{2,1,0:T(2,128)(2,1)S(1)} all-to-all(bf16[16,2,2304]{2,1,0:T(2,128)(2,1)S(1)} %broadcast_in_dim.2), channel_id=1, replica_groups=mesh['harm'=4,'space'=2,'samp'=4] {'harm','samp'}, dimensions={0} | all-to-all | bytes 294912 | tf_op jit(solution)/shard_map/all_to_all | solution.py:252
  18.6 0.1 reshape.4.window
  18.7 4.3 %shard_residual.1 = (f32[2,2048]{1,0:T(2,128)S(1)}, f32[2,256]{1,0:T(2,128)S(1)}) custom-call(bf16[32,2304]{1,0:T(8,128)(2,1)S(1)} %reshape.4.window, bf16[6,4,128,384]{3,2,1,0:T(8,128)(2,1)S(1)} %get-tuple-element.16.first_curl, f32[32,2]{1,0:T(8,128)S(1)} %get-tuple-element.17.table, bf16[32,96]{1,0:T(8,128)(2,1)S(1)} %get-tuple-element.18.pieces, ...), custom_call_target="tpu_custom_call" | custom-call | flops 805306368 | bytes 6291456 | tf_op jit(solution)/shard_map/shard_residual/pallas_call | solution.py:253
  23.0 1.6 %collective-permute-start.1 = (f32[2,256]{1,0:T(2,128)S(1)}, f32[2,256]{1,0:T(2,128)S(1)}, u32[]{:S(2)}, u32[]{:S(2)}) collective-permute-start(f32[2,256]{1,0:T(2,128)S(1)} %get-tuple-element.24), channel_id=1, source_target_pairs={{0,4},{4,0},{1,5},{5,1},{2,6},{6,2},{3,7},{7,3},{8,12},{12,8},{9,1... | collective-permute-start | bytes 6152 | tf_op jit(solution)/shard_map/ppermute | solution.py:37
  24.6 2.1 %collective-permute-done.1.from_right.from_left = f32[2,256]{1,0:T(2,128)S(1)} collective-permute-done((f32[2,256]{1,0:T(2,128)S(1)}, f32[2,256]{1,0:T(2,128)S(1)}, u32[]{:S(2)}, u32[]{:S(2)}) %collective-permute-start.1) | collective-permute-done | bytes 2080 | tf_op jit(solution)/shard_map/ppermute | solution.py:37
  26.6 0.6 %halo_sum.1 = f32[2,2048]{1,0:T(2,128)} custom-call(f32[2,2048]{1,0:T(2,128)S(1)} %get-tuple-element.23.own, f32[2,256]{1,0:T(2,128)S(1)} %collective-permute-done.1.from_right.from_left, f32[2,256]{1,0:T(2,128)S(1)} %collective-permute-done.1.from_right.from_left), custom_call_target="tpu_custom_call" | custom-call | tf_op jit(solution)/shard_map/halo_sum/pallas_call | solution.py:288
  (2 shorter events, 0.0 us)
Async XLA Ops:
  0.0 4.8 %collective-permute-start = (bf16[2,2048]{1,0:T(2,128)(2,1)}, bf16[2,2048]{1,0:T(2,128)(2,1)S(1)}, u32[]{:S(2)}, u32[]{:S(2)}) collective-permute-start(bf16[2,2048]{1,0:T(2,128)(2,1)} %refs_2_.1), channel_id=1, source_target_pairs={{0,4},{4,0},{1,5},{5,1},{2,6},{6,2},{3,7},{7,3},{8,12},{12,8},{9,1... | collective-permute-start | bytes 24584 | tf_op jit(solution)/shard_map/ppermute | solution.py:37
  23.0 3.7 %collective-permute-start.1 = (f32[2,256]{1,0:T(2,128)S(1)}, f32[2,256]{1,0:T(2,128)S(1)}, u32[]{:S(2)}, u32[]{:S(2)}) collective-permute-start(f32[2,256]{1,0:T(2,128)S(1)} %get-tuple-element.24), channel_id=1, source_target_pairs={{0,4},{4,0},{1,5},{5,1},{2,6},{6,2},{3,7},{7,3},{8,12},{12,8},{9,1... | collective-permute-start | bytes 6152 | tf_op jit(solution)/shard_map/ppermute | solution.py:37

commit v12 on v11

--- a/solution.py
+++ b/solution.py
@@ -13,6 +13,7 @@
 HALF = SAMPLES // 2
 GROUP = ("harm", "samp")
 MIB = 1024 * 1024
+CHUNK = 2
 
 
 def half_table(parts):
@@ -79,7 +80,7 @@
     densities,
     totals,
     small_sems,
-    curl_sem,
+    curl_sems,
 ):
     tile_count, links, tile, comps = curl_hbm.shape
     early = first_curl.shape[0]
@@ -89,8 +90,15 @@
     small = [
         pltpu.make_async_copy(src, dst, small_sems.at[i]) for i, (src, dst) in enumerate(fetched)
     ]
-    rest = pltpu.make_async_copy(curl_hbm.at[early:], later_curl, curl_sem)
-    for copy in small + [rest]:
+    later = {
+        elem: pltpu.make_async_copy(
+            curl_hbm.at[elem : min(elem + CHUNK, tile_count)],
+            later_curl.at[elem - early : min(elem + CHUNK, tile_count) - early],
+            curl_sems.at[(elem - early) // CHUNK],
+        )
+        for elem in range(early, tile_count, CHUNK)
+    }
+    for copy in small + list(later.values()):
         copy.start()
     stacked = jnp.concatenate([window[...]] * 3, axis=0)
     samples = jnp.dot(pieces[...], stacked, preferred_element_type=jnp.float32)
@@ -144,9 +152,9 @@
     projected = {}
     for turn in range(len(chunks) + 2):
         if turn < len(chunks):
-            if early in chunks[turn]:
-                rest.wait()
             for elem in chunks[turn]:
+                if elem in later:
+                    later[elem].wait()
                 find_density(elem)
         if 0 <= turn - 1 < len(chunks):
             for elem in chunks[turn - 1]:
@@ -217,7 +225,7 @@
     def in_hbm(array):
         return pltpu.with_memory_space_constraint(array, pltpu.HBM)
 
-    early = 3 * tile_count // 8
+    early = 7 * tile_count // 16
     operands = [
         curl_tiles,
         own_columns,
@@ -267,7 +275,7 @@
             pltpu.VMEM((tile_count, HALF, comps), jnp.float32),
             pltpu.VMEM((links * tile, tile_count * links * parts_here), jnp.float32),
             pltpu.SemaphoreType.DMA((3,)),
-            pltpu.SemaphoreType.DMA,
+            pltpu.SemaphoreType.DMA((-((early - tile_count) // CHUNK),)),
         ],
         compiler_params=pltpu.CompilerParams(vmem_limit_bytes=32 * MIB),
         cost_estimate=pl.CostEstimate(

time: 27.5 us -> 27.5 us (level)
  transfers between devices with their start and end apart: 2 -> 2, of which waited for: 2 -> 1; matrix products, arithmetic and copies ran while one was open for 0% -> 0% of each run, Pallas kernels for 6% -> 7%
where the time goes in v12:
time: 27.5 us; the launch traced here: 27.4 us
  blocking collectives  13.7 us (50%)
  Pallas kernels  6.9 us (25%)
  starting transfers between devices  4.56 us (17%)
  waiting for transfers between devices  2.06 us (7%)
    all_to_all x1, blocking collectives, per_device(): window = lax.all_to_all(copies, GROUP, 0, 0).reshape(parts, block.shape[1])  13.7 us
    ppermute x2, starting transfers between devices, shifted(): lax.ppermute(array, axis, [(i, (i + by) % count) for i in range(count)])  4.56 us
    pallas_call x1, Pallas kernels, per_device(): pl.pallas_call(shard_kernel, out_shape=(pltpu.VMEM(source.shape, jnp.floa...  4.42 us
    ppermute x2, waiting for transfers between devices, shifted(): lax.ppermute(array, axis, [(i, (i + by) % count) for i in range(count)])  2.06 us
    pallas_call x1, Pallas kernels, per_device(): pl.pallas_call(fetch_kernel, out_shape=[pltpu.VMEM(shape, o.dtype) for sh...  1.86 us
    pallas_call x1, Pallas kernels, per_device(): pl.pallas_call(halo_kernel, out_shape=jax.ShapeDtypeStruct(source.shape,...  0.61 us
  transfers between devices with their start and end apart: 2, of which 1 were waited for; matrix products, arithmetic and copies ran while one was open for 0% of the time, Pallas kernels for 7%

profile of v12, /device:TPU:0, one launch (start us, length us, event | category | flops | bytes accessed | tf_op | source)
XLA Modules:
  0.0 27.4 jit_solution(1038907850157726160)
XLA Ops:
  0.0 3.0 %collective-permute-start = (bf16[2,2048]{1,0:T(2,128)(2,1)}, bf16[2,2048]{1,0:T(2,128)(2,1)S(1)}, u32[]{:S(2)}, u32[]{:S(2)}) collective-permute-start(bf16[2,2048]{1,0:T(2,128)(2,1)} %refs_2_.1), channel_id=1, source_target_pairs={{0,4},{4,0},{1,5},{5,1},{2,6},{6,2},{3,7},{7,3},{8,12},{12,8},{9,1... | collective-permute-start | bytes 24584 | tf_op jit(solution)/shard_map/ppermute | solution.py:38
  3.0 1.9 %fetch_operands.1 = (bf16[7,4,128,384]{3,2,1,0:T(8,128)(2,1)S(1)}, f32[32,2]{1,0:T(8,128)S(1)}, bf16[2,2048]{1,0:T(2,128)(2,1)S(1)}, bf16[32,96]{1,0:T(8,128)(2,...) custom-call(bf16[16,4,128,384]{3,2,1,0:T(8,128)(2,1)} %curl_hbm.1, ...), custom_call_target="tpu_custom_call" | custom-call | bytes 5505024 | tf_op jit(solution)/shard_map/fetch_operands/pallas_call | solution.py:243
  4.8 0.0 collective-permute-done
  4.9 0.1 broadcast_in_dim.2
  5.0 13.7 %all_to_all.5 = bf16[16,2,2304]{2,1,0:T(2,128)(2,1)S(1)} all-to-all(bf16[16,2,2304]{2,1,0:T(2,128)(2,1)S(1)} %broadcast_in_dim.2), channel_id=1, replica_groups=mesh['harm'=4,'space'=2,'samp'=4] {'harm','samp'}, dimensions={0} | all-to-all | bytes 294912 | tf_op jit(solution)/shard_map/all_to_all | solution.py:260
  18.6 0.1 reshape.4.window
  18.7 4.4 %shard_residual.1 = (f32[2,2048]{1,0:T(2,128)S(1)}, f32[2,256]{1,0:T(2,128)S(1)}) custom-call(bf16[32,2304]{1,0:T(8,128)(2,1)S(1)} %reshape.4.window, bf16[7,4,128,384]{3,2,1,0:T(8,128)(2,1)S(1)} %get-tuple-element.16.first_curl, f32[32,2]{1,0:T(8,128)S(1)} %get-tuple-element.17.table, bf16[32,96]{1,0:T(8,128)(2,1)S(1)} %get-tuple-element.18.pieces, ...), custom_call_target="tpu_custom_call" | custom-call | flops 805306368 | bytes 6291456 | tf_op jit(solution)/shard_map/shard_residual/pallas_call | solution.py:261
  23.1 1.6 %collective-permute-start.1 = (f32[2,256]{1,0:T(2,128)S(1)}, f32[2,256]{1,0:T(2,128)S(1)}, u32[]{:S(2)}, u32[]{:S(2)}) collective-permute-start(f32[2,256]{1,0:T(2,128)S(1)} %get-tuple-element.24), channel_id=1, source_target_pairs={{0,4},{4,0},{1,5},{5,1},{2,6},{6,2},{3,7},{7,3},{8,12},{12,8},{9,1... | collective-permute-start | bytes 6152 | tf_op jit(solution)/shard_map/ppermute | solution.py:38
  24.7 2.1 %collective-permute-done.1.from_right.from_left = f32[2,256]{1,0:T(2,128)S(1)} collective-permute-done((f32[2,256]{1,0:T(2,128)S(1)}, f32[2,256]{1,0:T(2,128)S(1)}, u32[]{:S(2)}, u32[]{:S(2)}) %collective-permute-start.1) | collective-permute-done | bytes 2080 | tf_op jit(solution)/shard_map/ppermute | solution.py:38
  26.8 0.6 %halo_sum.1 = f32[2,2048]{1,0:T(2,128)} custom-call(f32[2,2048]{1,0:T(2,128)S(1)} %get-tuple-element.23.own, f32[2,256]{1,0:T(2,128)S(1)} %collective-permute-done.1.from_right.from_left, f32[2,256]{1,0:T(2,128)S(1)} %collective-permute-done.1.from_right.from_left), custom_call_target="tpu_custom_call" | custom-call | tf_op jit(solution)/shard_map/halo_sum/pallas_call | solution.py:296
  (2 shorter events, 0.0 us)
Async XLA Ops:
  0.0 4.8 %collective-permute-start = (bf16[2,2048]{1,0:T(2,128)(2,1)}, bf16[2,2048]{1,0:T(2,128)(2,1)S(1)}, u32[]{:S(2)}, u32[]{:S(2)}) collective-permute-start(bf16[2,2048]{1,0:T(2,128)(2,1)} %refs_2_.1), channel_id=1, source_target_pairs={{0,4},{4,0},{1,5},{5,1},{2,6},{6,2},{3,7},{7,3},{8,12},{12,8},{9,1... | collective-permute-start | bytes 24584 | tf_op jit(solution)/shard_map/ppermute | solution.py:38
  23.1 3.7 %collective-permute-start.1 = (f32[2,256]{1,0:T(2,128)S(1)}, f32[2,256]{1,0:T(2,128)S(1)}, u32[]{:S(2)}, u32[]{:S(2)}) collective-permute-start(f32[2,256]{1,0:T(2,128)S(1)} %get-tuple-element.24), channel_id=1, source_target_pairs={{0,4},{4,0},{1,5},{5,1},{2,6},{6,2},{3,7},{7,3},{8,12},{12,8},{9,1... | collective-permute-start | bytes 6152 | tf_op jit(solution)/shard_map/ppermute | solution.py:38

commit v13 on v11

--- a/solution.py
+++ b/solution.py
@@ -11,7 +11,7 @@
 
 SAMPLES = 64
 HALF = SAMPLES // 2
-GROUP = ("harm", "samp")
+GROUP = ("chip", "core", "samp")
 MIB = 1024 * 1024
 
 
@@ -44,11 +44,26 @@
     return shifted(array[:, :tile], "space", -1), shifted(array[:, -tile:], "space", 1)
 
 
+def arrival_order(chips, cores, samp, parts_here):
+    ranks = [
+        [
+            (chip * cores + (c - step) % cores) * samp + s
+            for step in range(cores)
+            for chip in range(chips)
+            for s in range(samp)
+        ]
+        for c in range(cores)
+    ]
+    rows = np.array(ranks)[:, :, None] * parts_here + np.arange(parts_here)
+    return rows.reshape(cores, -1)
+
+
 def fetch_kernel(*refs):
     count = (len(refs) - 1) // 2
     sources, targets, sems = refs[:count], refs[count : 2 * count], refs[-1]
-    rank = lax.axis_index(GROUP)
-    sources = (sources[0].at[: targets[0].shape[0]], sources[1].at[rank]) + sources[2:]
+    first = sources[0].at[: targets[0].shape[0]]
+    own_columns = sources[1].at[lax.axis_index(GROUP)]
+    sources = (first, own_columns, sources[2].at[lax.axis_index("core")]) + sources[3:]
     copies = [
         pltpu.make_async_copy(source, target, sems.at[i])
         for i, (source, target) in enumerate(zip(sources, targets))
@@ -108,12 +123,28 @@
         curl = first_curl[elem] if elem < early else later_curl[elem - early]
         return curl.reshape(links * tile, comps)
 
-    def find_density(elem):
-        picked = jnp.concatenate(
+    def picked(elem):
+        return jnp.concatenate(
             [timed[:, pl.ds(pl.multiple_of(at * tile, tile), tile)] for at in places[elem]], axis=1
         )
-        split = jnp.dot(picked, blocks(elem), preferred_element_type=jnp.float32)
-        densities[elem] = split[:HALF] + split[HALF:]
+
+    def product(left, right):
+        return jnp.dot(left, right, preferred_element_type=jnp.float32)
+
+    def find_densities(one, two):
+        cut, rest = 2 * tile, comps - 2 * tile
+        samples_one, samples_two = picked(one), picked(two)
+        curl_one, curl_two = blocks(one), blocks(two)
+        shared = product(
+            jnp.concatenate([samples_one, samples_two], axis=0),
+            jnp.concatenate([curl_one[:, cut:], curl_two[:, :rest]], axis=1),
+        )
+        split_one = product(samples_one, curl_one[:, :cut])
+        split_two = product(samples_two, curl_two[:, rest:])
+        densities[one, :, :cut] = split_one[:HALF] + split_one[HALF:]
+        densities[one, :, cut:] = shared[:HALF, :rest] + shared[HALF : 2 * HALF, :rest]
+        densities[two, :, :rest] = shared[2 * HALF : 3 * HALF, rest:] + shared[3 * HALF :, rest:]
+        densities[two, :, rest:] = split_two[:HALF] + split_two[HALF:]
 
     def project(elem):
         density = densities[elem]
@@ -127,33 +158,34 @@
         rows = [jnp.sum(column * field, axis=0, keepdims=True) for column in columns]
         return jnp.concatenate(rows * links, axis=0) * (4.0 / SAMPLES)
 
-    def contribute(elem, projected):
-        empty = jnp.zeros_like(projected)
-        spread = [projected if other == elem else empty for other in range(tile_count)]
-        spread = jnp.concatenate(spread, axis=0).astype(jnp.bfloat16)
+    def contribute(one, two, rows_one, rows_two):
+        empty = jnp.zeros_like(rows_one)
+        spread = [
+            jnp.concatenate([rows_one if e == one else empty, rows_two if e == two else empty], 1)
+            for e in range(tile_count)
+        ]
         contrib = lax.dot_general(
-            blocks(elem), spread, (((1,), (1,)), ((), ())), preferred_element_type=jnp.float32
+            jnp.concatenate([blocks(one), blocks(two)], axis=1),
+            jnp.concatenate(spread, axis=0).astype(jnp.bfloat16),
+            (((1,), (1,)), ((), ())),
+            preferred_element_type=jnp.float32,
         )
-        if elem:
+        if one:
             totals[...] += contrib
         else:
             totals[...] = contrib
 
-    step = 1
-    chunks = [range(at, min(at + step, tile_count)) for at in range(0, tile_count, step)]
+    pairs = [(at, at + 1) for at in range(0, tile_count, 2)]
     projected = {}
-    for turn in range(len(chunks) + 2):
-        if turn < len(chunks):
-            if early in chunks[turn]:
+    for turn in range(len(pairs) + 2):
+        if turn < len(pairs):
+            if early in pairs[turn]:
                 rest.wait()
-            for elem in chunks[turn]:
-                find_density(elem)
-        if 0 <= turn - 1 < len(chunks):
-            for elem in chunks[turn - 1]:
-                projected[elem] = project(elem)
+            find_densities(*pairs[turn])
+        if 0 <= turn - 1 < len(pairs):
+            projected[turn - 1] = [project(elem) for elem in pairs[turn - 1]]
         if 0 <= turn - 2:
-            for elem in chunks[turn - 2]:
-                contribute(elem, projected[elem])
+            contribute(*pairs[turn - 2], *projected[turn - 2])
 
     width = tile_count * slots
     column = lax.broadcasted_iota(jnp.int32, (tile, width), 1)
@@ -202,10 +234,12 @@
 def per_device(coeffs, curl_tiles, pattern, region_ids, material_law, source):
     parts_here = coeffs.shape[0]
     tile_count, links, tile, comps = curl_tiles.shape
-    group_size = lax.axis_size(GROUP)
+    chips, cores, samp = (lax.axis_size(axis) for axis in GROUP)
+    group_size = chips * cores * samp
     parts = parts_here * group_size
     table = half_table(parts)
-    pieces = jnp.asarray(bf16_pieces(table))
+    order = arrival_order(chips, cores, samp, parts_here)
+    pieces = jnp.asarray(bf16_pieces(table[:, order].transpose(1, 0, 2)))
     own_columns = jnp.asarray(
         table.reshape(HALF, group_size, parts_here).transpose(1, 0, 2).astype(np.float32)
     )
@@ -221,8 +255,8 @@
     operands = [
         curl_tiles,
         own_columns,
+        pieces,
         coeffs,
-        pieces,
         source,
         pattern.T,
         region_ids,
@@ -231,7 +265,8 @@
     shapes = [
         (early,) + curl_tiles.shape[1:],
         own_columns.shape[1:],
-    ] + [operand.shape for operand in operands[2:]]
+        pieces.shape[1:],
+    ] + [operand.shape for operand in operands[3:]]
     fetched = pl.pallas_call(
         fetch_kernel,
         out_shape=[pltpu.VMEM(shape, o.dtype) for shape, o in zip(shapes, operands)],
@@ -244,12 +279,14 @@
         ),
         name="fetch_operands",
     )(*[in_hbm(operand) for operand in operands])
-    first_curl, columns_here, coeffs_here, pieces_here, *others = fetched
+    first_curl, columns_here, pieces_here, coeffs_here, *others = fetched
 
     right, left = from_neighbours(coeffs, tile)
     block = jnp.concatenate([left, coeffs_here, right], axis=1)
-    copies = jnp.broadcast_to(block[None], (group_size,) + block.shape)
-    window = lax.all_to_all(copies, GROUP, 0, 0).reshape(parts, block.shape[1])
+    copies = jnp.broadcast_to(block[None], (chips * samp,) + block.shape)
+    near = lax.all_to_all(copies, ("chip", "samp"), 0, 0)
+    rows = [near] + [shifted(near, "core", step) for step in range(1, cores)]
+    window = jnp.concatenate(rows, axis=0).reshape(parts, block.shape[1])
     own, halo = pl.pallas_call(
         shard_kernel,
         out_shape=(
@@ -296,6 +333,14 @@
 
 
 def solution(mesh):
+    at = mesh.axis_names.index("harm")
+    harm = mesh.shape["harm"]
+    cores = 2 if harm % 2 == 0 else 1
+    sizes = mesh.devices.shape
+    split = jax.sharding.Mesh(
+        mesh.devices.reshape(sizes[:at] + (harm // cores, cores) + sizes[at + 1 :]),
+        mesh.axis_names[:at] + ("chip", "core") + mesh.axis_names[at + 1 :],
+    )
     placed = (
         P(GROUP, "space"),
         P("space", None, None, None),
@@ -306,7 +351,7 @@
     )
     return jax.shard_map(
         per_device,
-        mesh=mesh,
+        mesh=split,
         in_specs=placed,
         out_specs=P(GROUP, "space"),
         check_vma=False,

time: 27.5 us -> 29.2 us (1.062)
  waiting for transfers between devices: 2.16 us -> 3.42 us
  Pallas kernels: 6.65 us -> 7.46 us
  blocking collectives: 13.7 us -> 13.2 us
    ppermute x2 -> x3, waiting for transfers between devices: 2.16 us -> 3.42 us  [shifted(): lax.ppermute(array, axis, [(i, (i + by) % count) for i in range(count)])]
    pallas_call x1, Pallas kernels: 4.29 us -> 5.1 us  [per_device(): pl.pallas_call(shard_kernel, out_shape=(pltpu.VMEM(source.shape, jnp.floa...]
    all_to_all x1, blocking collectives: 13.7 us -> 13.2 us  [per_device(): near = lax.all_to_all(copies, ('chip', 'samp'), 0, 0)]
    ppermute x2 -> x3, starting transfers between devices: 4.54 us -> 4.55 us  [shifted(): lax.ppermute(array, axis, [(i, (i + by) % count) for i in range(count)])]
  transfers between devices with their start and end apart: 2 -> 3, of which waited for: 2 -> 3; matrix products, arithmetic and copies ran while one was open for 0% -> 0% of each run, Pallas kernels for 6% -> 6%
where the time goes in v13:
time: 29.2 us; the launch traced here: 28.9 us
  blocking collectives  13.2 us (45%)
  Pallas kernels  7.46 us (26%)
  starting transfers between devices  4.55 us (16%)
  waiting for transfers between devices  3.42 us (12%)
    all_to_all x1, blocking collectives, per_device(): near = lax.all_to_all(copies, ('chip', 'samp'), 0, 0)  13.2 us
    pallas_call x1, Pallas kernels, per_device(): pl.pallas_call(shard_kernel, out_shape=(pltpu.VMEM(source.shape, jnp.floa...  5.1 us
    ppermute x3, starting transfers between devices, shifted(): lax.ppermute(array, axis, [(i, (i + by) % count) for i in range(count)])  4.55 us
    ppermute x3, waiting for transfers between devices, shifted(): lax.ppermute(array, axis, [(i, (i + by) % count) for i in range(count)])  3.42 us
    pallas_call x1, Pallas kernels, per_device(): pl.pallas_call(fetch_kernel, out_shape=[pltpu.VMEM(shape, o.dtype) for sh...  1.75 us
    pallas_call x1, Pallas kernels, per_device(): pl.pallas_call(halo_kernel, out_shape=jax.ShapeDtypeStruct(source.shape,...  0.61 us
  transfers between devices with their start and end apart: 3, of which 3 were waited for; matrix products, arithmetic and copies ran while one was open for 0% of the time, Pallas kernels for 6%

profile of v13, /device:TPU:0, one launch (start us, length us, event | category | flops | bytes accessed | tf_op | source)
XLA Modules:
  0.0 28.9 jit_solution(15409761704845765000)
XLA Ops:
  0.0 3.0 %collective-permute-start = (bf16[2,2048]{1,0:T(2,128)(2,1)}, bf16[2,2048]{1,0:T(2,128)(2,1)S(1)}, u32[]{:S(2)}, u32[]{:S(2)}) collective-permute-start(bf16[2,2048]{1,0:T(2,128)(2,1)} %refs_3_.1), channel_id=1, source_target_pairs={{0,4},{4,0},{1,5},{5,1},{2,6},{6,2},{3,7},{7,3},{8,12},{12,8},{9,1... | collective-permute-start | bytes 24584 | tf_op jit(solution)/shard_map/ppermute | solution.py:37
  3.0 1.7 %fetch_operands.1 = (bf16[6,4,128,384]{3,2,1,0:T(8,128)(2,1)S(1)}, f32[32,2]{1,0:T(8,128)S(1)}, bf16[32,96]{1,0:T(8,128)(2,1)S(1)}, bf16[2,2048]{1,0:T(2,128)(2,...) custom-call(bf16[16,4,128,384]{3,2,1,0:T(8,128)(2,1)} %curl_hbm.1, ...), custom_call_target="tpu_custom_call" | custom-call | bytes 4718592 | tf_op jit(solution)/shard_map/fetch_operands/pallas_call | solution.py:270
  4.7 0.1 collective-permute-done
  4.9 13.2 %all_to_all.5 = bf16[8,2,2304]{2,1,0:T(2,128)(2,1)S(1)} all-to-all(bf16[8,2,2304]{2,1,0:T(2,128)(2,1)S(1)} %broadcast_in_dim.2), channel_id=1, replica_groups=mesh['chip'=2,'core'=2,'space'=2,'samp'=4] {'chip','samp'}, dimensions={0} | all-to-all | bytes 147456 | tf_op jit(solution)/shard_map/all_to_all | solution.py:287
  18.0 0.0 collective-permute-start.1
  18.0 1.3 %collective-permute-done.1 = bf16[8,2,2304]{2,1,0:T(2,128)(2,1)S(1)} collective-permute-done((bf16[8,2,2304]{2,1,0:T(2,128)(2,1)S(1)}, bf16[8,2,2304]{2,1,0:T(2,128)(2,1)S(1)}, u32[]{:S(2)}, u32[]{:S(2)}) %collective-permute-start.1) | collective-permute-done | bytes 73760 | tf_op jit(solution)/shard_map/ppermute | solution.py:37
  19.3 0.2 pad_maximum_fusion
  19.5 0.1 reshape.4.window
  19.6 5.1 %shard_residual.1 = (f32[2,2048]{1,0:T(2,128)S(1)}, f32[2,256]{1,0:T(2,128)S(1)}) custom-call(bf16[32,2304]{1,0:T(8,128)(2,1)S(1)} %reshape.4.window, bf16[6,4,128,384]{3,2,1,0:T(8,128)(2,1)S(1)} %get-tuple-element.16.first_curl, f32[32,2]{1,0:T(8,128)S(1)} %get-tuple-element.17.table, bf16[32,96]{1,0:T(8,128)(2,1)S(1)} %get-tuple-element.18.pieces, ...), custom_call_target="tpu_custom_call" | custom-call | flops 805306368 | bytes 6291456 | tf_op jit(solution)/shard_map/shard_residual/pallas_call | solution.py:290
  24.7 1.6 %collective-permute-start.2 = (f32[2,256]{1,0:T(2,128)S(1)}, f32[2,256]{1,0:T(2,128)S(1)}, u32[]{:S(2)}, u32[]{:S(2)}) collective-permute-start(f32[2,256]{1,0:T(2,128)S(1)} %get-tuple-element.24), channel_id=1, source_target_pairs={{0,4},{4,0},{1,5},{5,1},{2,6},{6,2},{3,7},{7,3},{8,12},{12,8},{9,1... | collective-permute-start | bytes 6152 | tf_op jit(solution)/shard_map/ppermute | solution.py:37
  26.3 2.1 %collective-permute-done.2.from_right.from_left = f32[2,256]{1,0:T(2,128)S(1)} collective-permute-done((f32[2,256]{1,0:T(2,128)S(1)}, f32[2,256]{1,0:T(2,128)S(1)}, u32[]{:S(2)}, u32[]{:S(2)}) %collective-permute-start.2) | collective-permute-done | bytes 2080 | tf_op jit(solution)/shard_map/ppermute | solution.py:37
  28.3 0.6 %halo_sum.1 = f32[2,2048]{1,0:T(2,128)} custom-call(f32[2,2048]{1,0:T(2,128)S(1)} %get-tuple-element.23.own, f32[2,256]{1,0:T(2,128)S(1)} %collective-permute-done.2.from_right.from_left, f32[2,256]{1,0:T(2,128)S(1)} %collective-permute-done.2.from_right.from_left), custom_call_target="tpu_custom_call" | custom-call | tf_op jit(solution)/shard_map/halo_sum/pallas_call | solution.py:325
  (3 shorter events, 0.1 us)
Async XLA Ops:
  0.0 4.8 %collective-permute-start = (bf16[2,2048]{1,0:T(2,128)(2,1)}, bf16[2,2048]{1,0:T(2,128)(2,1)S(1)}, u32[]{:S(2)}, u32[]{:S(2)}) collective-permute-start(bf16[2,2048]{1,0:T(2,128)(2,1)} %refs_3_.1), channel_id=1, source_target_pairs={{0,4},{4,0},{1,5},{5,1},{2,6},{6,2},{3,7},{7,3},{8,12},{12,8},{9,1... | collective-permute-start | bytes 24584 | tf_op jit(solution)/shard_map/ppermute | solution.py:37
  18.0 1.3 %collective-permute-start.1 = (bf16[8,2,2304]{2,1,0:T(2,128)(2,1)S(1)}, bf16[8,2,2304]{2,1,0:T(2,128)(2,1)S(1)}, u32[]{:S(2)}, u32[]{:S(2)}) collective-permute-start(bf16[8,2,2304]{2,1,0:T(2,128)(2,1)S(1)} %all_to_all.5), channel_id=1, source_target_pairs={{0,8},{8,0},{1,9},{9,1},{2,10},{10,2},{3,11},{11,3},{4,12},{12,4},... | collective-permute-start | bytes 221192 | tf_op jit(solution)/shard_map/ppermute | solution.py:37
  24.7 3.7 %collective-permute-start.2 = (f32[2,256]{1,0:T(2,128)S(1)}, f32[2,256]{1,0:T(2,128)S(1)}, u32[]{:S(2)}, u32[]{:S(2)}) collective-permute-start(f32[2,256]{1,0:T(2,128)S(1)} %get-tuple-element.24), channel_id=1, source_target_pairs={{0,4},{4,0},{1,5},{5,1},{2,6},{6,2},{3,7},{7,3},{8,12},{12,8},{9,1... | collective-permute-start | bytes 6152 | tf_op jit(solution)/shard_map/ppermute | solution.py:37

commit v14 on v6

--- a/solution.py
+++ b/solution.py
@@ -48,7 +48,7 @@
     count = (len(refs) - 1) // 2
     sources, targets, sems = refs[:count], refs[count : 2 * count], refs[-1]
     rank = lax.axis_index(GROUP)
-    sources = (sources[0].at[: targets[0].shape[0]], sources[1].at[rank]) + sources[2:]
+    sources = (sources[0].at[rank],) + sources[1:]
     copies = [
         pltpu.make_async_copy(source, target, sems.at[i])
         for i, (source, target) in enumerate(zip(sources, targets))
@@ -61,7 +61,6 @@
 
 def shard_kernel(
     window,
-    first_curl,
     table,
     pieces,
     source,
@@ -74,22 +73,23 @@
     pattern,
     region_ids,
     law,
-    later_curl,
+    curl,
     timed,
-    densities,
     small_sems,
-    curl_sem,
+    curl_sems,
     *sums,
 ):
-    tile_count, links, tile, comps = curl_hbm.shape
-    early = first_curl.shape[0]
+    tile_count, links, tile, comps = curl.shape
     parts_here = out.shape[0]
     fetched = [(pattern_in, pattern), (region_in, region_ids), (law_in, law)]
     small = [
         pltpu.make_async_copy(src, dst, small_sems.at[i]) for i, (src, dst) in enumerate(fetched)
     ]
-    rest = pltpu.make_async_copy(curl_hbm.at[early:], later_curl, curl_sem)
-    for copy in small + [rest]:
+
+    def curl_copy(elem):
+        return pltpu.make_async_copy(curl_hbm.at[elem], curl.at[elem], curl_sems.at[elem])
+
+    for copy in small + [curl_copy(elem) for elem in range(tile_count)]:
         copy.start()
     for total in sums:
         total[...] = jnp.zeros_like(total)
@@ -99,57 +99,60 @@
     timed[:HALF, :] = high
     timed[HALF:, :] = (samples - high.astype(jnp.float32)).astype(jnp.bfloat16)
     columns = [
-        jnp.broadcast_to(table[:, part : part + 1], (HALF, comps)) for part in range(parts_here)
+        jnp.broadcast_to(table[:, part : part + 1], (HALF, tile)) for part in range(parts_here)
     ]
     for copy in small:
         copy.wait()
-    places = [[pattern[link, elem] for link in range(links)] for elem in range(tile_count)]
 
     def blocks(elem):
-        curl = first_curl[elem] if elem < early else later_curl[elem - early]
-        return curl.reshape(links * tile, comps)
+        return curl[elem].reshape(links * tile, comps)
 
     def find_density(elem):
+        curl_copy(elem).wait()
         picked = jnp.concatenate(
-            [timed[:, pl.ds(pl.multiple_of(at * tile, tile), tile)] for at in places[elem]], axis=1
+            [
+                timed[:, pl.ds(pl.multiple_of(pattern[link, elem] * tile, tile), tile)]
+                for link in range(links)
+            ],
+            axis=1,
         )
         split = jnp.dot(picked, blocks(elem), preferred_element_type=jnp.float32)
-        densities[elem] = split[:HALF] + split[HALF:]
-
-    def project(elem):
-        density = densities[elem]
+        return split[:HALF] + split[HALF:]
+
+    def project(elem, density):
         comp = [density[:, c * tile : (c + 1) * tile] for c in range(comps // tile)]
         square = comp[0] * comp[0]
         for c in comp[1:]:
             square = square + c * c
         region = region_ids[elem]
         reluct = law[0, region] + law[2, region] * square / (square + law[1, region])
-        field = jnp.concatenate([reluct * c for c in comp], axis=1)
-        rows = [jnp.sum(column * field, axis=0, keepdims=True) for column in columns]
+        rows = [
+            jnp.concatenate(
+                [jnp.sum(column * reluct * c, axis=0, keepdims=True) for c in comp], axis=1
+            )
+            for column in columns
+        ]
         return (jnp.concatenate(rows, axis=0) * (4.0 / SAMPLES)).astype(jnp.bfloat16)
 
     def contribute(elem, projected):
         contrib = lax.dot_general(
             projected, blocks(elem), (((1,), (1,)), ((), ())), preferred_element_type=jnp.float32
         )
-        for link, at in enumerate(places[elem]):
-            sums[link][at] += contrib[:, link * tile : (link + 1) * tile]
-
-    step = 2
-    chunks = [range(at, min(at + step, tile_count)) for at in range(0, tile_count, step)]
-    projected = {}
-    for turn in range(len(chunks) + 2):
-        if turn < len(chunks):
-            if early in chunks[turn]:
-                rest.wait()
-            for elem in chunks[turn]:
-                find_density(elem)
-        if 0 <= turn - 1 < len(chunks):
-            for elem in chunks[turn - 1]:
-                projected[elem] = project(elem)
-        if 0 <= turn - 2:
-            for elem in chunks[turn - 2]:
-                contribute(elem, projected[elem])
+        for link in range(links):
+            sums[link][pattern[link, elem]] += contrib[:, link * tile : (link + 1) * tile]
+
+    def turn(elem, carry):
+        density, projected = carry
+        contribute(elem - 2, projected)
+        projected = project(elem - 1, density)
+        return find_density(elem), projected
+
+    density = find_density(0)
+    projected = project(0, density)
+    density = find_density(1)
+    density, projected = lax.fori_loop(2, tile_count, turn, (density, projected))
+    contribute(tile_count - 2, projected)
+    contribute(tile_count - 1, project(tile_count - 1, density))
 
     def window_sum(w):
         total = sums[0][w]
@@ -189,9 +192,7 @@
     def in_hbm(array):
         return pltpu.with_memory_space_constraint(array, pltpu.HBM)
 
-    early = 3 * tile_count // 8
     operands = [
-        curl_tiles,
         own_columns,
         coeffs,
         pieces,
@@ -200,10 +201,7 @@
         region_ids,
         material_law,
     ]
-    shapes = [
-        (early,) + curl_tiles.shape[1:],
-        own_columns.shape[1:],
-    ] + [operand.shape for operand in operands[2:]]
+    shapes = [own_columns.shape[1:]] + [operand.shape for operand in operands[1:]]
     fetched = pl.pallas_call(
         fetch_kernel,
         out_shape=[pltpu.VMEM(shape, o.dtype) for shape, o in zip(shapes, operands)],
@@ -212,11 +210,11 @@
         scratch_shapes=[pltpu.SemaphoreType.DMA((len(operands),))],
         compiler_params=pltpu.CompilerParams(vmem_limit_bytes=16 * MIB),
         cost_estimate=pl.CostEstimate(
-            flops=0, bytes_accessed=4 * early * links * tile * comps, transcendentals=0
+            flops=0, bytes_accessed=1024 * 1024, transcendentals=0
         ),
         name="fetch_operands",
     )(*[in_hbm(operand) for operand in operands])
-    first_curl, columns_here, coeffs_here, pieces_here, *others = fetched
+    columns_here, coeffs_here, pieces_here, *others = fetched
 
     right, left = from_neighbours(coeffs, tile)
     block = jnp.concatenate([left, coeffs_here, right], axis=1)
@@ -228,17 +226,16 @@
             pltpu.VMEM(source.shape, jnp.float32),
             pltpu.VMEM((parts_here, 2 * tile), jnp.float32),
         ),
-        in_specs=[vmem] * 8 + [hbm],
+        in_specs=[vmem] * 7 + [hbm],
         out_specs=(vmem, vmem),
         scratch_shapes=[
             pltpu.SMEM((links, tile_count), jnp.int32),
             pltpu.SMEM(region_ids.shape, jnp.int32),
             pltpu.SMEM(material_law.shape, jnp.float32),
-            pltpu.VMEM((tile_count - early,) + curl_tiles.shape[1:], curl_tiles.dtype),
+            pltpu.VMEM(curl_tiles.shape, curl_tiles.dtype),
             pltpu.VMEM((SAMPLES, (tile_count + 2) * tile), jnp.bfloat16),
-            pltpu.VMEM((tile_count, HALF, comps), jnp.float32),
             pltpu.SemaphoreType.DMA((3,)),
-            pltpu.SemaphoreType.DMA,
+            pltpu.SemaphoreType.DMA((tile_count,)),
         ]
         + [pltpu.VMEM((tile_count + 2, parts_here, tile), jnp.float32)] * links,
         compiler_params=pltpu.CompilerParams(vmem_limit_bytes=32 * MIB),
@@ -250,7 +247,7 @@
         name="shard_residual",
     )(
         in_vmem(window),
-        *[in_vmem(array) for array in (first_curl, columns_here, pieces_here, *others)],
+        *[in_vmem(array) for array in (columns_here, pieces_here, *others)],
         in_hbm(curl_tiles),
     )
     if lax.axis_size("space") == 2:

time: 27.6 us -> 31.2 us (1.13)
  Pallas kernels: 6.76 us -> 9.45 us
  waiting for transfers between devices: 2.15 us -> 3.07 us
    pallas_call x1, Pallas kernels: 4.4 us -> 7.99 us  [per_device(): pl.pallas_call(shard_kernel, out_shape=(pltpu.VMEM(source.shape, jnp.floa...]
    ppermute x2, waiting for transfers between devices: 2.15 us -> 3.07 us  [shifted(): lax.ppermute(array, axis, [(i, (i + by) % count) for i in range(count)])]
    pallas_call x1, Pallas kernels: 1.75 us -> 0.84 us  [per_device(): pl.pallas_call(fetch_kernel, out_shape=[pltpu.VMEM(shape, o.dtype) for sh...]
  transfers between devices with their start and end apart: 2 -> 2, of which waited for: 2 -> 2; matrix products, arithmetic and copies ran while one was open for 0% -> 0% of each run, Pallas kernels for 6% -> 3%
where the time goes in v14:
time: 31.2 us; the launch traced here: 30.9 us
  blocking collectives  13.7 us (44%)
  Pallas kernels  9.45 us (30%)
  starting transfers between devices  4.54 us (15%)
  waiting for transfers between devices  3.07 us (10%)
    all_to_all x1, blocking collectives, per_device(): window = lax.all_to_all(copies, GROUP, 0, 0).reshape(parts, block.shape[1])  13.7 us
    pallas_call x1, Pallas kernels, per_device(): pl.pallas_call(shard_kernel, out_shape=(pltpu.VMEM(source.shape, jnp.floa...  7.99 us
    ppermute x2, starting transfers between devices, shifted(): lax.ppermute(array, axis, [(i, (i + by) % count) for i in range(count)])  4.54 us
    ppermute x2, waiting for transfers between devices, shifted(): lax.ppermute(array, axis, [(i, (i + by) % count) for i in range(count)])  3.07 us
    pallas_call x1, Pallas kernels, per_device(): pl.pallas_call(fetch_kernel, out_shape=[pltpu.VMEM(shape, o.dtype) for sh...  0.84 us
  transfers between devices with their start and end apart: 2, of which 2 were waited for; matrix products, arithmetic and copies ran while one was open for 0% of the time, Pallas kernels for 3%

profile of v14, /device:TPU:0, one launch (start us, length us, event | category | flops | bytes accessed | tf_op | source)
XLA Modules:
  0.0 30.9 jit_solution(2083628499986478195)
XLA Ops:
  0.0 3.0 %collective-permute-start = (bf16[2,2048]{1,0:T(2,128)(2,1)}, bf16[2,2048]{1,0:T(2,128)(2,1)S(1)}, u32[]{:S(2)}, u32[]{:S(2)}) collective-permute-start(bf16[2,2048]{1,0:T(2,128)(2,1)} %refs_1_.1), channel_id=1, source_target_pairs={{0,4},{4,0},{1,5},{5,1},{2,6},{6,2},{3,7},{7,3},{8,12},{12,8},{9,1... | collective-permute-start | bytes 24584 | tf_op jit(solution)/shard_map/ppermute | solution.py:37
  3.0 0.8 %fetch_operands.1 = (f32[32,2]{1,0:T(8,128)S(1)}, bf16[2,2048]{1,0:T(2,128)(2,1)S(1)}, bf16[32,96]{1,0:T(8,128)(2,1)S(1)}, f32[2,2048]{1,0:T(2,128)S(1)}, s32[4,...) custom-call(f32[16,32,2]{2,1,0:T(8,128)} %constant.5.clone.refs_0_, bf16[2,2048]{1,0:T(2,128)(2,1)} %refs_1_.1, ...), custom_call_target="tpu_custom_call" | custom-call | bytes 1048576 | tf_op jit(solution)/shard_map/fetch_operands/pallas_call | solution.py:205
  3.8 1.0 %collective-permute-done = bf16[2,2048]{1,0:T(2,128)(2,1)S(1)} collective-permute-done((bf16[2,2048]{1,0:T(2,128)(2,1)}, bf16[2,2048]{1,0:T(2,128)(2,1)S(1)}, u32[]{:S(2)}, u32[]{:S(2)}) %collective-permute-start) | collective-permute-done | bytes 8224 | tf_op jit(solution)/shard_map/ppermute | solution.py:37
  4.8 0.1 broadcast_in_dim.2
  4.9 13.7 %all_to_all.5 = bf16[16,2,2304]{2,1,0:T(2,128)(2,1)S(1)} all-to-all(bf16[16,2,2304]{2,1,0:T(2,128)(2,1)S(1)} %broadcast_in_dim.2), channel_id=1, replica_groups=mesh['harm'=4,'space'=2,'samp'=4] {'harm','samp'}, dimensions={0} | all-to-all | bytes 294912 | tf_op jit(solution)/shard_map/all_to_all | solution.py:222
  18.6 0.1 reshape.4.window
  18.7 8.0 %shard_residual.1 = (f32[2,2048]{1,0:T(2,128)S(1)}, f32[2,256]{1,0:T(2,128)S(1)}) custom-call(bf16[32,2304]{1,0:T(8,128)(2,1)S(1)} %reshape.4.window, f32[32,2]{1,0:T(8,128)S(1)} %get-tuple-element.15.table, bf16[32,96]{1,0:T(8,128)(2,1)S(1)} %get-tuple-element.16.pieces, f32[2,2048]{1,0:T(2,128)S(1)} %get-tuple-element.17.source, ...), custom_call_target="tpu_custom_call" | custom-call | flops 805306368 | bytes 6291456 | tf_op jit(solution)/shard_map/shard_residual/pallas_call | solution.py:223
  26.7 1.6 %collective-permute-start.1 = (f32[2,256]{1,0:T(2,128)S(1)}, f32[2,256]{1,0:T(2,128)S(1)}, u32[]{:S(2)}, u32[]{:S(2)}) collective-permute-start(f32[2,256]{1,0:T(2,128)S(1)} %get-tuple-element.22), channel_id=1, source_target_pairs={{0,4},{4,0},{1,5},{5,1},{2,6},{6,2},{3,7},{7,3},{8,12},{12,8},{9,1... | collective-permute-start | bytes 6152 | tf_op jit(solution)/shard_map/ppermute | solution.py:37
  28.3 2.1 %collective-permute-done.1.from_right.from_left = f32[2,256]{1,0:T(2,128)S(1)} collective-permute-done((f32[2,256]{1,0:T(2,128)S(1)}, f32[2,256]{1,0:T(2,128)S(1)}, u32[]{:S(2)}, u32[]{:S(2)}) %collective-permute-start.1) | collective-permute-done | bytes 2080 | tf_op jit(solution)/shard_map/ppermute | solution.py:37
  30.3 0.6 %halo_sum.1 = f32[2,2048]{1,0:T(2,128)} custom-call(f32[2,2048]{1,0:T(2,128)S(1)} %get-tuple-element.21.own, f32[2,256]{1,0:T(2,128)S(1)} %collective-permute-done.1.from_right.from_left, f32[2,256]{1,0:T(2,128)S(1)} %collective-permute-done.1.from_right.from_left), custom_call_target="tpu_custom_call" | custom-call | tf_op jit(solution)/shard_map/halo_sum/pallas_call | solution.py:257
  (2 shorter events, 0.0 us)
Async XLA Ops:
  0.0 4.8 %collective-permute-start = (bf16[2,2048]{1,0:T(2,128)(2,1)}, bf16[2,2048]{1,0:T(2,128)(2,1)S(1)}, u32[]{:S(2)}, u32[]{:S(2)}) collective-permute-start(bf16[2,2048]{1,0:T(2,128)(2,1)} %refs_1_.1), channel_id=1, source_target_pairs={{0,4},{4,0},{1,5},{5,1},{2,6},{6,2},{3,7},{7,3},{8,12},{12,8},{9,1... | collective-permute-start | bytes 24584 | tf_op jit(solution)/shard_map/ppermute | solution.py:37
  26.7 3.7 %collective-permute-start.1 = (f32[2,256]{1,0:T(2,128)S(1)}, f32[2,256]{1,0:T(2,128)S(1)}, u32[]{:S(2)}, u32[]{:S(2)}) collective-permute-start(f32[2,256]{1,0:T(2,128)S(1)} %get-tuple-element.22), channel_id=1, source_target_pairs={{0,4},{4,0},{1,5},{5,1},{2,6},{6,2},{3,7},{7,3},{8,12},{12,8},{9,1... | collective-permute-start | bytes 6152 | tf_op jit(solution)/shard_map/ppermute | solution.py:37

commit v15 on v7

--- a/solution.py
+++ b/solution.py
@@ -52,7 +52,7 @@
     return index ^ step if size & (size - 1) == 0 else (index - step) % size
 
 
-def gathered(block, axis):
+def exchanged(block, axis):
     size = lax.axis_size(axis)
     blocks = [block]
     for step in range(1, size):
@@ -61,10 +61,26 @@
     return jnp.concatenate(blocks, axis=0)
 
 
+def gathered_along(block, axis):
+    size = lax.axis_size(axis)
+    places = [block] + [None] * (size - 1)
+    for step in range(size - 1, 0, -1):
+        places[step] = lax.ppermute(block, axis, [(i, i - step) for i in range(step, size)])
+    below = [None] * size
+    for hop in range(1, size):
+        carried = jnp.concatenate(below[size - hop + 1 :] + [block], axis=0)
+        arrived = jnp.split(lax.ppermute(carried, axis, [(hop - 1, hop)]), hop, axis=0)
+        for place, part in zip(range(size - hop, size), arrived):
+            below[place] = part if below[place] is None else below[place] + part
+    for step in range(1, size):
+        places[step] = places[step] + below[step]
+    return jnp.concatenate(places, axis=0)
+
+
 def arrival_order(harm, samp, parts_here):
     ranks = [
         [
-            sender(h, j, harm) * samp + sender(s, k, samp)
+            sender(h, j, harm) * samp + (s + k) % samp
             for j in range(harm)
             for k in range(samp)
         ]
@@ -167,7 +183,7 @@
         for link, at in enumerate(places[elem]):
             sums[link][at] += contrib[:, link * tile : (link + 1) * tile]
 
-    step = 2
+    step = 1
     chunks = [range(at, min(at + step, tile_count)) for at in range(0, tile_count, step)]
     projected = {}
     for turn in range(len(chunks) + 2):
@@ -251,7 +267,7 @@
 
     right, left = from_neighbours(coeffs, tile)
     block = jnp.concatenate([left, coeffs_here, right], axis=1)
-    window = gathered(gathered(block[None], "samp"), "harm").reshape(parts, block.shape[1])
+    window = exchanged(gathered_along(block[None], "samp"), "harm").reshape(parts, block.shape[1])
     own, halo = pl.pallas_call(
         shard_kernel,
         out_shape=(

time: 29.1 us -> 37.7 us (1.30)
  starting transfers between devices: 11.2 us -> 15.7 us
  waiting for transfers between devices: 10.6 us -> 14.6 us
    ppermute x6 -> x9, starting transfers between devices: 6.67 us -> 11.1 us  [the longest x3 5.31 us: gathered_along(): lax.ppermute(carried, axis, [(hop - 1, hop)])]
    ppermute x6 -> x9, waiting for transfers between devices: 8.42 us -> 12.5 us  [the longest x3 8.08 us: gathered_along(): lax.ppermute(block, axis, [(i, i - step) for i in range(step, size)])]
  transfers between devices with their start and end apart: 8 -> 11, of which waited for: 6 -> 8; matrix products, arithmetic and copies ran while one was open for 0% -> 1% of each run, Pallas kernels for 6% -> 5%
where the time goes in v15:
time: 37.7 us; the launch traced here: 37.4 us
  starting transfers between devices  15.7 us (42%)
  waiting for transfers between devices  14.6 us (39%)
  Pallas kernels  6.54 us (17%)
    ppermute x3, waiting for transfers between devices, gathered_along(): lax.ppermute(block, axis, [(i, i - step) for i in range(step, size)])  8.08 us
    ppermute x3, starting transfers between devices, gathered_along(): lax.ppermute(carried, axis, [(hop - 1, hop)])  5.31 us
    ppermute x2, starting transfers between devices, shifted(): lax.ppermute(array, axis, [(i, (i + by) % count) for i in range(count)])  4.55 us
    pallas_call x1, Pallas kernels, per_device(): pl.pallas_call(shard_kernel, out_shape=(pltpu.VMEM(source.shape, jnp.floa...  4.18 us
    ppermute x3, starting transfers between devices, gathered_along(): lax.ppermute(block, axis, [(i, i - step) for i in range(step, size)])  3.88 us
    ppermute x3, waiting for transfers between devices, exchanged(): blocks.append(lax.ppermute(block, axis, pairs))  3.05 us
    ppermute x2, waiting for transfers between devices, shifted(): lax.ppermute(array, axis, [(i, (i + by) % count) for i in range(count)])  2.15 us
    ppermute x3, starting transfers between devices, exchanged(): blocks.append(lax.ppermute(block, axis, pairs))  1.93 us
  transfers between devices with their start and end apart: 11, of which 8 were waited for; matrix products, arithmetic and copies ran while one was open for 1% of the time, Pallas kernels for 5%

profile of v15, /device:TPU:0, one launch (start us, length us, event | category | flops | bytes accessed | tf_op | source)
XLA Modules:
  0.0 37.4 jit_solution(10989944023144411780)
XLA Ops:
  0.0 3.0 %collective-permute-start = (bf16[2,2048]{1,0:T(2,128)(2,1)}, bf16[2,2048]{1,0:T(2,128)(2,1)S(1)}, u32[]{:S(2)}, u32[]{:S(2)}) collective-permute-start(bf16[2,2048]{1,0:T(2,128)(2,1)} %refs_3_.1), channel_id=1, source_target_pairs={{0,4},{4,0},{1,5},{5,1},{2,6},{6,2},{3,7},{7,3},{8,12},{12,8},{9,1... | collective-permute-start | bytes 24584 | tf_op jit(solution)/shard_map/ppermute | solution.py:37
  3.0 1.7 %fetch_operands.1 = (bf16[6,4,128,384]{3,2,1,0:T(8,128)(2,1)S(1)}, f32[32,2]{1,0:T(8,128)S(1)}, bf16[32,96]{1,0:T(8,128)(2,1)S(1)}, bf16[2,2048]{1,0:T(2,128)(2,...) custom-call(bf16[16,4,128,384]{3,2,1,0:T(8,128)(2,1)} %curl_hbm.1, ...), custom_call_target="tpu_custom_call" | custom-call | bytes 4718592 | tf_op jit(solution)/shard_map/fetch_operands/pallas_call | solution.py:254
  4.7 0.1 collective-permute-done
  4.8 4.0 %collective-permute-start.2 = (bf16[1,2,2304]{2,1,0:T(2,128)(2,1)S(1)}, bf16[1,2,2304]{2,1,0:T(2,128)(2,1)S(1)}, u32[]{:S(2)}, u32[]{:S(2)}) collective-permute-start(bf16[1,2,2304]{2,1,0:T(2,128)(2,1)S(1)} %maximum_bitcast_fusion), channel_id=1, source_target_pairs={{0,1},{4,5},{8,9},{12,13},{16,17},{20,21},{24,25},{28,29}} | collective-permute-start | bytes 27656 | tf_op jit(solution)/shard_map/ppermute | solution.py:72
  8.8 1.4 %collective-permute-done.2 = bf16[1,2,2304]{2,1,0:T(2,128)(2,1)S(1)} collective-permute-done((bf16[1,2,2304]{2,1,0:T(2,128)(2,1)S(1)}, bf16[1,2,2304]{2,1,0:T(2,128)(2,1)S(1)}, u32[]{:S(2)}, u32[]{:S(2)}) %collective-permute-start.2) | collective-permute-done | bytes 9248 | tf_op jit(solution)/shard_map/ppermute | solution.py:72
  10.2 0.7 %collective-permute-start.3 = (bf16[2,2,2304]{2,1,0:T(2,128)(2,1)S(1)}, bf16[2,2,2304]{2,1,0:T(2,128)(2,1)S(1)}, u32[]{:S(2)}, u32[]{:S(2)}) collective-permute-start(bf16[2,2,2304]{2,1,0:T(2,128)(2,1)S(1)} %pad_maximum_fusion.2), channel_id=1, source_target_pairs={{1,2},{5,6},{9,10},{13,14},{17,18},{21,22},{25,26},{29,30}} | collective-permute-start | bytes 55304 | tf_op jit(solution)/shard_map/ppermute | solution.py:72
  10.9 1.3 %collective-permute-start.1 = (bf16[1,2,2304]{2,1,0:T(2,128)(2,1)S(1)}, bf16[1,2,2304]{2,1,0:T(2,128)(2,1)S(1)}, u32[]{:S(2)}, u32[]{:S(2)}) collective-permute-start(bf16[1,2,2304]{2,1,0:T(2,128)(2,1)S(1)} %maximum_bitcast_fusion), channel_id=1, source_target_pairs={{1,0},{2,1},{3,2},{5,4},{6,5},{7,6},{9,8},{10,9},{11,10},{13,12},{... | collective-permute-start | bytes 27656 | tf_op jit(solution)/shard_map/ppermute | solution.py:68
  12.2 0.0 collective-permute-done.3
  12.3 0.7 %collective-permute-start.4 = (bf16[3,2,2304]{2,1,0:T(2,128)(2,1)S(1)}, bf16[3,2,2304]{2,1,0:T(2,128)(2,1)S(1)}, u32[]{:S(2)}, u32[]{:S(2)}) collective-permute-start(bf16[3,2,2304]{2,1,0:T(2,128)(2,1)S(1)} %pad_maximum_fusion.1), channel_id=1, source_target_pairs={{2,3},{6,7},{10,11},{14,15},{18,19},{22,23},{26,27},{30,31}} | collective-permute-start | bytes 82952 | tf_op jit(solution)/shard_map/ppermute | solution.py:72
  13.0 1.3 %collective-permute-start.5 = (bf16[1,2,2304]{2,1,0:T(2,128)(2,1)S(1)}, bf16[1,2,2304]{2,1,0:T(2,128)(2,1)S(1)}, u32[]{:S(2)}, u32[]{:S(2)}) collective-permute-start(bf16[1,2,2304]{2,1,0:T(2,128)(2,1)S(1)} %maximum_bitcast_fusion), channel_id=1, source_target_pairs={{2,0},{3,1},{6,4},{7,5},{10,8},{11,9},{14,12},{15,13},{18,16},{19,... | collective-permute-start | bytes 27656 | tf_op jit(solution)/shard_map/ppermute | solution.py:68
  14.3 1.3 %collective-permute-start.6 = (bf16[1,2,2304]{2,1,0:T(2,128)(2,1)S(1)}, bf16[1,2,2304]{2,1,0:T(2,128)(2,1)S(1)}, u32[]{:S(2)}, u32[]{:S(2)}) collective-permute-start(bf16[1,2,2304]{2,1,0:T(2,128)(2,1)S(1)} %maximum_bitcast_fusion), channel_id=1, source_target_pairs={{3,0},{7,4},{11,8},{15,12},{19,16},{23,20},{27,24},{31,28}} | collective-permute-start | bytes 27656 | tf_op jit(solution)/shard_map/ppermute | solution.py:68
  15.6 1.8 %collective-permute-done.1 = bf16[1,2,2304]{2,1,0:T(2,128)(2,1)S(1)} collective-permute-done((bf16[1,2,2304]{2,1,0:T(2,128)(2,1)S(1)}, bf16[1,2,2304]{2,1,0:T(2,128)(2,1)S(1)}, u32[]{:S(2)}, u32[]{:S(2)}) %collective-permute-start.1) | collective-permute-done | bytes 9248 | tf_op jit(solution)/shard_map/ppermute | solution.py:68
  17.3 0.0 collective-permute-done.4
  17.4 4.1 %collective-permute-done.5 = bf16[1,2,2304]{2,1,0:T(2,128)(2,1)S(1)} collective-permute-done((bf16[1,2,2304]{2,1,0:T(2,128)(2,1)S(1)}, bf16[1,2,2304]{2,1,0:T(2,128)(2,1)S(1)}, u32[]{:S(2)}, u32[]{:S(2)}) %collective-permute-start.5) | collective-permute-done | bytes 9248 | tf_op jit(solution)/shard_map/ppermute | solution.py:68
  21.5 2.2 %collective-permute-done.6 = bf16[1,2,2304]{2,1,0:T(2,128)(2,1)S(1)} collective-permute-done((bf16[1,2,2304]{2,1,0:T(2,128)(2,1)S(1)}, bf16[1,2,2304]{2,1,0:T(2,128)(2,1)S(1)}, u32[]{:S(2)}, u32[]{:S(2)}) %collective-permute-start.6) | collective-permute-done | bytes 9248 | tf_op jit(solution)/shard_map/ppermute | solution.py:68
  23.7 0.1 pad_maximum_fusion
  23.8 0.1 collective-permute-start.7
  23.9 1.6 %collective-permute-start.8 = (bf16[4,2,2304]{2,1,0:T(2,128)(2,1)S(1)}, bf16[4,2,2304]{2,1,0:T(2,128)(2,1)S(1)}, u32[]{:S(2)}, u32[]{:S(2)}) collective-permute-start(bf16[4,2,2304]{2,1,0:T(2,128)(2,1)S(1)} %pad_maximum_fusion), channel_id=1, source_target_pairs={{0,16},{8,24},{16,0},{24,8},{1,17},{9,25},{17,1},{25,9},{2,18},{10... | collective-permute-start | bytes 110600 | tf_op jit(solution)/shard_map/ppermute | solution.py:60
  25.4 0.3 collective-permute-start.9
  25.7 0.0 collective-permute-done.7
  25.8 2.1 %collective-permute-done.8 = bf16[4,2,2304]{2,1,0:T(2,128)(2,1)S(1)} collective-permute-done((bf16[4,2,2304]{2,1,0:T(2,128)(2,1)S(1)}, bf16[4,2,2304]{2,1,0:T(2,128)(2,1)S(1)}, u32[]{:S(2)}, u32[]{:S(2)}) %collective-permute-start.8) | collective-permute-done | bytes 36896 | tf_op jit(solution)/shard_map/ppermute | solution.py:60
  27.9 0.9 %collective-permute-done.9 = bf16[4,2,2304]{2,1,0:T(2,128)(2,1)S(1)} collective-permute-done((bf16[4,2,2304]{2,1,0:T(2,128)(2,1)S(1)}, bf16[4,2,2304]{2,1,0:T(2,128)(2,1)S(1)}, u32[]{:S(2)}, u32[]{:S(2)}) %collective-permute-start.9) | collective-permute-done | bytes 36896 | tf_op jit(solution)/shard_map/ppermute | solution.py:60
  28.9 0.1 reshape.3.window
  29.0 4.2 %shard_residual.1 = (f32[2,2048]{1,0:T(2,128)S(1)}, f32[2,256]{1,0:T(2,128)S(1)}) custom-call(bf16[32,2304]{1,0:T(8,128)(2,1)S(1)} %reshape.3.window, bf16[6,4,128,384]{3,2,1,0:T(8,128)(2,1)S(1)} %get-tuple-element.16.first_curl, f32[32,2]{1,0:T(8,128)S(1)} %get-tuple-element.17.table, bf16[32,96]{1,0:T(8,128)(2,1)S(1)} %get-tuple-element.18.pieces, ...), custom_call_target="tpu_custom_call" | custom-call | flops 805306368 | bytes 6291456 | tf_op jit(solution)/shard_map/shard_residual/pallas_call | solution.py:271
  33.2 1.6 %collective-permute-start.10 = (f32[2,256]{1,0:T(2,128)S(1)}, f32[2,256]{1,0:T(2,128)S(1)}, u32[]{:S(2)}, u32[]{:S(2)}) collective-permute-start(f32[2,256]{1,0:T(2,128)S(1)} %get-tuple-element.24), channel_id=1, source_target_pairs={{0,4},{4,0},{1,5},{5,1},{2,6},{6,2},{3,7},{7,3},{8,12},{12,8},{9,1... | collective-permute-start | bytes 6152 | tf_op jit(solution)/shard_map/ppermute | solution.py:37
  34.7 2.1 %collective-permute-done.10.from_right.from_left = f32[2,256]{1,0:T(2,128)S(1)} collective-permute-done((f32[2,256]{1,0:T(2,128)S(1)}, f32[2,256]{1,0:T(2,128)S(1)}, u32[]{:S(2)}, u32[]{:S(2)}) %collective-permute-start.10) | collective-permute-done | bytes 2080 | tf_op jit(solution)/shard_map/ppermute | solution.py:37
  36.8 0.6 %halo_sum.1 = f32[2,2048]{1,0:T(2,128)} custom-call(f32[2,2048]{1,0:T(2,128)S(1)} %get-tuple-element.23.own, f32[2,256]{1,0:T(2,128)S(1)} %collective-permute-done.10.from_right.from_left, f32[2,256]{1,0:T(2,128)S(1)} %collective-permute-done.10.from_right.from_left), custom_call_target="tpu_custom_call" | custom-call | tf_op jit(solution)/shard_map/halo_sum/pallas_call | solution.py:306
  (12 shorter events, 0.3 us)
Async XLA Ops:
  0.0 4.8 %collective-permute-start = (bf16[2,2048]{1,0:T(2,128)(2,1)}, bf16[2,2048]{1,0:T(2,128)(2,1)S(1)}, u32[]{:S(2)}, u32[]{:S(2)}) collective-permute-start(bf16[2,2048]{1,0:T(2,128)(2,1)} %refs_3_.1), channel_id=1, source_target_pairs={{0,4},{4,0},{1,5},{5,1},{2,6},{6,2},{3,7},{7,3},{8,12},{12,8},{9,1... | collective-permute-start | bytes 24584 | tf_op jit(solution)/shard_map/ppermute | solution.py:37
  4.8 5.4 %collective-permute-start.2 = (bf16[1,2,2304]{2,1,0:T(2,128)(2,1)S(1)}, bf16[1,2,2304]{2,1,0:T(2,128)(2,1)S(1)}, u32[]{:S(2)}, u32[]{:S(2)}) collective-permute-start(bf16[1,2,2304]{2,1,0:T(2,128)(2,1)S(1)} %maximum_bitcast_fusion), channel_id=1, source_target_pairs={{0,1},{4,5},{8,9},{12,13},{16,17},{20,21},{24,25},{28,29}} | collective-permute-start | bytes 27656 | tf_op jit(solution)/shard_map/ppermute | solution.py:72
  10.2 2.0 %collective-permute-start.3 = (bf16[2,2,2304]{2,1,0:T(2,128)(2,1)S(1)}, bf16[2,2,2304]{2,1,0:T(2,128)(2,1)S(1)}, u32[]{:S(2)}, u32[]{:S(2)}) collective-permute-start(bf16[2,2,2304]{2,1,0:T(2,128)(2,1)S(1)} %pad_maximum_fusion.2), channel_id=1, source_target_pairs={{1,2},{5,6},{9,10},{13,14},{17,18},{21,22},{25,26},{29,30}} | collective-permute-start | bytes 55304 | tf_op jit(solution)/shard_map/ppermute | solution.py:72
  10.9 6.5 %collective-permute-start.1 = (bf16[1,2,2304]{2,1,0:T(2,128)(2,1)S(1)}, bf16[1,2,2304]{2,1,0:T(2,128)(2,1)S(1)}, u32[]{:S(2)}, u32[]{:S(2)}) collective-permute-start(bf16[1,2,2304]{2,1,0:T(2,128)(2,1)S(1)} %maximum_bitcast_fusion), channel_id=1, source_target_pairs={{1,0},{2,1},{3,2},{5,4},{6,5},{7,6},{9,8},{10,9},{11,10},{13,12},{... | collective-permute-start | bytes 27656 | tf_op jit(solution)/shard_map/ppermute | solution.py:68
  12.3 5.1 %collective-permute-start.4 = (bf16[3,2,2304]{2,1,0:T(2,128)(2,1)S(1)}, bf16[3,2,2304]{2,1,0:T(2,128)(2,1)S(1)}, u32[]{:S(2)}, u32[]{:S(2)}) collective-permute-start(bf16[3,2,2304]{2,1,0:T(2,128)(2,1)S(1)} %pad_maximum_fusion.1), channel_id=1, source_target_pairs={{2,3},{6,7},{10,11},{14,15},{18,19},{22,23},{26,27},{30,31}} | collective-permute-start | bytes 82952 | tf_op jit(solution)/shard_map/ppermute | solution.py:72
  13.0 8.5 %collective-permute-start.5 = (bf16[1,2,2304]{2,1,0:T(2,128)(2,1)S(1)}, bf16[1,2,2304]{2,1,0:T(2,128)(2,1)S(1)}, u32[]{:S(2)}, u32[]{:S(2)}) collective-permute-start(bf16[1,2,2304]{2,1,0:T(2,128)(2,1)S(1)} %maximum_bitcast_fusion), channel_id=1, source_target_pairs={{2,0},{3,1},{6,4},{7,5},{10,8},{11,9},{14,12},{15,13},{18,16},{19,... | collective-permute-start | bytes 27656 | tf_op jit(solution)/shard_map/ppermute | solution.py:68
  14.3 9.4 %collective-permute-start.6 = (bf16[1,2,2304]{2,1,0:T(2,128)(2,1)S(1)}, bf16[1,2,2304]{2,1,0:T(2,128)(2,1)S(1)}, u32[]{:S(2)}, u32[]{:S(2)}) collective-permute-start(bf16[1,2,2304]{2,1,0:T(2,128)(2,1)S(1)} %maximum_bitcast_fusion), channel_id=1, source_target_pairs={{3,0},{7,4},{11,8},{15,12},{19,16},{23,20},{27,24},{31,28}} | collective-permute-start | bytes 27656 | tf_op jit(solution)/shard_map/ppermute | solution.py:68
  23.8 1.9 %collective-permute-start.7 = (bf16[4,2,2304]{2,1,0:T(2,128)(2,1)S(1)}, bf16[4,2,2304]{2,1,0:T(2,128)(2,1)S(1)}, u32[]{:S(2)}, u32[]{:S(2)}) collective-permute-start(bf16[4,2,2304]{2,1,0:T(2,128)(2,1)S(1)} %pad_maximum_fusion), channel_id=1, source_target_pairs={{0,8},{8,0},{16,24},{24,16},{1,9},{9,1},{17,25},{25,17},{2,10},{10... | collective-permute-start | bytes 110600 | tf_op jit(solution)/shard_map/ppermute | solution.py:60
  23.9 4.0 %collective-permute-start.8 = (bf16[4,2,2304]{2,1,0:T(2,128)(2,1)S(1)}, bf16[4,2,2304]{2,1,0:T(2,128)(2,1)S(1)}, u32[]{:S(2)}, u32[]{:S(2)}) collective-permute-start(bf16[4,2,2304]{2,1,0:T(2,128)(2,1)S(1)} %pad_maximum_fusion), channel_id=1, source_target_pairs={{0,16},{8,24},{16,0},{24,8},{1,17},{9,25},{17,1},{25,9},{2,18},{10... | collective-permute-start | bytes 110600 | tf_op jit(solution)/shard_map/ppermute | solution.py:60
  25.4 3.4 %collective-permute-start.9 = (bf16[4,2,2304]{2,1,0:T(2,128)(2,1)S(1)}, bf16[4,2,2304]{2,1,0:T(2,128)(2,1)S(1)}, u32[]{:S(2)}, u32[]{:S(2)}) collective-permute-start(bf16[4,2,2304]{2,1,0:T(2,128)(2,1)S(1)} %pad_maximum_fusion), channel_id=1, source_target_pairs={{0,24},{8,16},{16,8},{24,0},{1,25},{9,17},{17,9},{25,1},{2,26},{10... | collective-permute-start | bytes 110600 | tf_op jit(solution)/shard_map/ppermute | solution.py:60
  33.2 3.7 %collective-permute-start.10 = (f32[2,256]{1,0:T(2,128)S(1)}, f32[2,256]{1,0:T(2,128)S(1)}, u32[]{:S(2)}, u32[]{:S(2)}) collective-permute-start(f32[2,256]{1,0:T(2,128)S(1)} %get-tuple-element.24), channel_id=1, source_target_pairs={{0,4},{4,0},{1,5},{5,1},{2,6},{6,2},{3,7},{7,3},{8,12},{12,8},{9,1... | collective-permute-start | bytes 6152 | tf_op jit(solution)/shard_map/ppermute | solution.py:37

commit v16 on v6

--- a/solution.py
+++ b/solution.py
@@ -13,6 +13,7 @@
 HALF = SAMPLES // 2
 GROUP = ("harm", "samp")
 MIB = 1024 * 1024
+LISTED = 4
 
 
 def half_table(parts):
@@ -59,40 +60,60 @@
         copy.wait()
 
 
-def shard_kernel(
+def curl_copies(curl_hbm, first_curl, later_curl, sem):
+    early = first_curl.shape[0]
+    links, tile, comps = curl_hbm.shape[1:]
+    rest = pltpu.make_async_copy(curl_hbm.at[early:], later_curl, sem)
+
+    def blocks(elem):
+        curl = first_curl[elem] if elem < early else later_curl[elem - early]
+        return curl.reshape(links * tile, comps)
+
+    return rest, blocks
+
+
+def weighted(projected, blocks):
+    return lax.dot_general(
+        projected.astype(jnp.bfloat16),
+        blocks,
+        (((1,), (1,)), ((), ())),
+        preferred_element_type=jnp.float32,
+    )
+
+
+def field_kernel(
     window,
     first_curl,
     table,
     pieces,
-    source,
     pattern_in,
     region_in,
     law_in,
     curl_hbm,
-    out,
+    projected,
     halo,
     pattern,
     region_ids,
     law,
+    outer,
     later_curl,
     timed,
     densities,
+    edge_sums,
     small_sems,
     curl_sem,
-    *sums,
 ):
     tile_count, links, tile, comps = curl_hbm.shape
     early = first_curl.shape[0]
-    parts_here = out.shape[0]
+    parts_here = halo.shape[0]
     fetched = [(pattern_in, pattern), (region_in, region_ids), (law_in, law)]
     small = [
         pltpu.make_async_copy(src, dst, small_sems.at[i]) for i, (src, dst) in enumerate(fetched)
     ]
-    rest = pltpu.make_async_copy(curl_hbm.at[early:], later_curl, curl_sem)
+    rest, blocks = curl_copies(curl_hbm, first_curl, later_curl, curl_sem)
     for copy in small + [rest]:
         copy.start()
-    for total in sums:
-        total[...] = jnp.zeros_like(total)
+    edge_sums[...] = jnp.zeros_like(edge_sums)
     stacked = jnp.concatenate([window[...]] * 3, axis=0)
     samples = jnp.dot(pieces[...], stacked, preferred_element_type=jnp.float32)
     high = samples.astype(jnp.bfloat16)
@@ -104,10 +125,11 @@
     for copy in small:
         copy.wait()
     places = [[pattern[link, elem] for link in range(links)] for elem in range(tile_count)]
-
-    def blocks(elem):
-        curl = first_curl[elem] if elem < early else later_curl[elem - early]
-        return curl.reshape(links * tile, comps)
+    count = jnp.int32(0)
+    for elem in range(tile_count):
+        for link, at in enumerate(places[elem]):
+            outer[count] = elem * links + link
+            count += jnp.where((at == 0) | (at == tile_count + 1), 1, 0)
 
     def find_density(elem):
         picked = jnp.concatenate(
@@ -126,42 +148,73 @@
         reluct = law[0, region] + law[2, region] * square / (square + law[1, region])
         field = jnp.concatenate([reluct * c for c in comp], axis=1)
         rows = [jnp.sum(column * field, axis=0, keepdims=True) for column in columns]
-        return (jnp.concatenate(rows, axis=0) * (4.0 / SAMPLES)).astype(jnp.bfloat16)
-
-    def contribute(elem, projected):
-        contrib = lax.dot_general(
-            projected, blocks(elem), (((1,), (1,)), ((), ())), preferred_element_type=jnp.float32
-        )
-        for link, at in enumerate(places[elem]):
-            sums[link][at] += contrib[:, link * tile : (link + 1) * tile]
-
-    step = 2
-    chunks = [range(at, min(at + step, tile_count)) for at in range(0, tile_count, step)]
-    projected = {}
-    for turn in range(len(chunks) + 2):
-        if turn < len(chunks):
-            if early in chunks[turn]:
+        projected[elem] = jnp.concatenate(rows, axis=0) * (4.0 / SAMPLES)
+
+    for turn in range(tile_count + 1):
+        if turn < tile_count:
+            if turn == early:
                 rest.wait()
-            for elem in chunks[turn]:
-                find_density(elem)
-        if 0 <= turn - 1 < len(chunks):
-            for elem in chunks[turn - 1]:
-                projected[elem] = project(elem)
-        if 0 <= turn - 2:
-            for elem in chunks[turn - 2]:
-                contribute(elem, projected[elem])
-
-    def window_sum(w):
-        total = sums[0][w]
-        for other in sums[1:]:
-            total = total + other[w]
-        return total
-
+            find_density(turn)
+        if turn:
+            project(turn - 1)
+
+    def add_outer(turn, carry):
+        for slot in range(LISTED):
+            spot = turn * LISTED + slot
+            code = jnp.where(spot < count, outer[jnp.minimum(spot, count - 1)], 0)
+            elem, link = code // links, code % links
+            block = jnp.where(
+                elem < early,
+                first_curl[jnp.minimum(elem, early - 1), link],
+                later_curl[jnp.maximum(elem - early, 0), link],
+            )
+            contrib = weighted(projected[elem], block)
+            side = jnp.where(pattern[link, elem] == 0, 0, 1)
+            edge_sums[slot, side] += jnp.where(spot < count, contrib, 0.0)
+        return carry
+
+    lax.fori_loop(0, (count + LISTED - 1) // LISTED, add_outer, 0)
+    total = edge_sums[0]
+    for slot in range(1, LISTED):
+        total = total + edge_sums[slot]
+    halo[:, :tile] = total[0]
+    halo[:, tile:] = total[1]
+
+
+def sum_kernel(
+    projected,
+    first_curl,
+    source,
+    pattern_in,
+    curl_hbm,
+    out,
+    pattern,
+    later_curl,
+    small_sem,
+    curl_sem,
+    *sums,
+):
+    tile_count, links, tile, _ = curl_hbm.shape
+    early = first_curl.shape[0]
+    small = pltpu.make_async_copy(pattern_in, pattern, small_sem)
+    rest, blocks = curl_copies(curl_hbm, first_curl, later_curl, curl_sem)
+    small.start()
+    rest.start()
+    for total in sums:
+        total[...] = jnp.zeros_like(total)
+    small.wait()
+    for elem in range(tile_count):
+        if elem == early:
+            rest.wait()
+        contrib = weighted(projected[elem], blocks(elem))
+        for link in range(links):
+            sums[link][pattern[link, elem]] += contrib[:, link * tile : (link + 1) * tile]
     for w in range(tile_count):
         at = slice(w * tile, (w + 1) * tile)
-        out[:, at] = window_sum(w + 1) - source[:, at]
-    halo[:, :tile] = window_sum(0)
-    halo[:, tile:] = window_sum(tile_count + 1)
+        total = sums[0][w + 1]
+        for other in sums[1:]:
+            total = total + other[w + 1]
+        out[:, at] = total - source[:, at]
 
 
 def halo_kernel(own, from_right, from_left, out):
@@ -216,47 +269,74 @@
         ),
         name="fetch_operands",
     )(*[in_hbm(operand) for operand in operands])
-    first_curl, columns_here, coeffs_here, pieces_here, *others = fetched
+    first_curl, columns_here, coeffs_here, pieces_here, source_here, *others = fetched
+    pattern_here = others[0]
 
     right, left = from_neighbours(coeffs, tile)
     block = jnp.concatenate([left, coeffs_here, right], axis=1)
     copies = jnp.broadcast_to(block[None], (group_size,) + block.shape)
     window = lax.all_to_all(copies, GROUP, 0, 0).reshape(parts, block.shape[1])
-    own, halo = pl.pallas_call(
-        shard_kernel,
+    later_tiles = pltpu.VMEM((tile_count - early,) + curl_tiles.shape[1:], curl_tiles.dtype)
+    pattern_words = pltpu.SMEM((links, tile_count), jnp.int32)
+    projected, halo = pl.pallas_call(
+        field_kernel,
         out_shape=(
-            pltpu.VMEM(source.shape, jnp.float32),
+            pltpu.VMEM((tile_count, parts_here, comps), jnp.float32),
             pltpu.VMEM((parts_here, 2 * tile), jnp.float32),
         ),
-        in_specs=[vmem] * 8 + [hbm],
+        in_specs=[vmem] * 7 + [hbm],
         out_specs=(vmem, vmem),
         scratch_shapes=[
-            pltpu.SMEM((links, tile_count), jnp.int32),
+            pattern_words,
             pltpu.SMEM(region_ids.shape, jnp.int32),
             pltpu.SMEM(material_law.shape, jnp.float32),
-            pltpu.VMEM((tile_count - early,) + curl_tiles.shape[1:], curl_tiles.dtype),
+            pltpu.SMEM((links * tile_count + 1,), jnp.int32),
+            later_tiles,
             pltpu.VMEM((SAMPLES, (tile_count + 2) * tile), jnp.bfloat16),
             pltpu.VMEM((tile_count, HALF, comps), jnp.float32),
+            pltpu.VMEM((LISTED, 2, parts_here, tile), jnp.float32),
             pltpu.SemaphoreType.DMA((3,)),
+            pltpu.SemaphoreType.DMA,
+        ],
+        compiler_params=pltpu.CompilerParams(vmem_limit_bytes=32 * MIB),
+        cost_estimate=pl.CostEstimate(
+            flops=2 * SAMPLES * tile_count * links * tile * comps,
+            bytes_accessed=2 * curl_tiles.size,
+            transcendentals=0,
+        ),
+        name="shard_fields",
+    )(
+        in_vmem(window),
+        *[in_vmem(array) for array in (first_curl, columns_here, pieces_here, *others)],
+        in_hbm(curl_tiles),
+    )
+    if lax.axis_size("space") == 2:
+        beside = [shifted(halo, "space", 1)] * 2
+    else:
+        beside = [shifted(halo, "space", -1), shifted(halo, "space", 1)]
+    own = pl.pallas_call(
+        sum_kernel,
+        out_shape=pltpu.VMEM(source.shape, jnp.float32),
+        in_specs=[vmem] * 4 + [hbm],
+        out_specs=vmem,
+        scratch_shapes=[
+            pattern_words,
+            later_tiles,
+            pltpu.SemaphoreType.DMA,
             pltpu.SemaphoreType.DMA,
         ]
         + [pltpu.VMEM((tile_count + 2, parts_here, tile), jnp.float32)] * links,
         compiler_params=pltpu.CompilerParams(vmem_limit_bytes=32 * MIB),
         cost_estimate=pl.CostEstimate(
-            flops=4 * SAMPLES * tile_count * links * tile * comps,
+            flops=2 * SAMPLES * tile_count * links * tile * comps,
             bytes_accessed=2 * curl_tiles.size,
             transcendentals=0,
         ),
-        name="shard_residual",
+        name="shard_sums",
     )(
-        in_vmem(window),
-        *[in_vmem(array) for array in (first_curl, columns_here, pieces_here, *others)],
+        *[in_vmem(array) for array in (projected, first_curl, source_here, pattern_here)],
         in_hbm(curl_tiles),
     )
-    if lax.axis_size("space") == 2:
-        beside = [shifted(halo, "space", 1)] * 2
-    else:
-        beside = [shifted(halo, "space", -1), shifted(halo, "space", 1)]
     return pl.pallas_call(
         halo_kernel,
         out_shape=jax.ShapeDtypeStruct(source.shape, jnp.float32),

time: 27.6 us -> 27.7 us (level)
  Pallas kernels: 6.76 us -> 8.89 us
  waiting for transfers between devices: 2.15 us -> 0.09 us
    pallas_call x1 -> x2, Pallas kernels: 4.4 us -> 6.53 us  [the longest x1 3.28 us: per_device(): pl.pallas_call(sum_kernel, out_shape=pltpu.VMEM(source.shape, jnp.float32...]
    ppermute x2, waiting for transfers between devices: 2.15 us -> 0.09 us  [shifted(): lax.ppermute(array, axis, [(i, (i + by) % count) for i in range(count)])]
  transfers between devices with their start and end apart: 2 -> 2, of which waited for: 2 -> 1; matrix products, arithmetic and copies ran while one was open for 0% -> 0% of each run, Pallas kernels for 6% -> 18%
where the time goes in v16:
time: 27.7 us; the launch traced here: 27.4 us
  blocking collectives  13.7 us (49%)
  Pallas kernels  8.89 us (32%)
  starting transfers between devices  4.55 us (16%)
    all_to_all x1, blocking collectives, per_device(): window = lax.all_to_all(copies, GROUP, 0, 0).reshape(parts, block.shape[1])  13.7 us
    ppermute x2, starting transfers between devices, shifted(): lax.ppermute(array, axis, [(i, (i + by) % count) for i in range(count)])  4.55 us
    pallas_call x1, Pallas kernels, per_device(): pl.pallas_call(sum_kernel, out_shape=pltpu.VMEM(source.shape, jnp.float32...  3.28 us
    pallas_call x1, Pallas kernels, per_device(): pl.pallas_call(field_kernel, out_shape=(pltpu.VMEM((tile_count, parts_her...  3.25 us
    pallas_call x1, Pallas kernels, per_device(): pl.pallas_call(fetch_kernel, out_shape=[pltpu.VMEM(shape, o.dtype) for sh...  1.75 us
    pallas_call x1, Pallas kernels, per_device(): pl.pallas_call(halo_kernel, out_shape=jax.ShapeDtypeStruct(source.shape,...  0.61 us
  transfers between devices with their start and end apart: 2, of which 1 were waited for; matrix products, arithmetic and copies ran while one was open for 0% of the time, Pallas kernels for 18%

profile of v16, /device:TPU:0, one launch (start us, length us, event | category | flops | bytes accessed | tf_op | source)
XLA Modules:
  0.0 27.4 jit_solution(7660718830649973791)
XLA Ops:
  0.0 3.0 %collective-permute-start = (bf16[2,2048]{1,0:T(2,128)(2,1)}, bf16[2,2048]{1,0:T(2,128)(2,1)S(1)}, u32[]{:S(2)}, u32[]{:S(2)}) collective-permute-start(bf16[2,2048]{1,0:T(2,128)(2,1)} %refs_2_.1), channel_id=1, source_target_pairs={{0,4},{4,0},{1,5},{5,1},{2,6},{6,2},{3,7},{7,3},{8,12},{12,8},{9,1... | collective-permute-start | bytes 24584 | tf_op jit(solution)/shard_map/ppermute | solution.py:38
  3.0 1.7 %fetch_operands.1 = (bf16[6,4,128,384]{3,2,1,0:T(8,128)(2,1)S(1)}, f32[32,2]{1,0:T(8,128)S(1)}, bf16[2,2048]{1,0:T(2,128)(2,1)S(1)}, bf16[32,96]{1,0:T(8,128)(2,...) custom-call(bf16[16,4,128,384]{3,2,1,0:T(8,128)(2,1)} %curl_hbm.3, ...), custom_call_target="tpu_custom_call" | custom-call | bytes 4718592 | tf_op jit(solution)/shard_map/fetch_operands/pallas_call | solution.py:260
  4.7 0.1 collective-permute-done
  4.8 0.1 broadcast_in_dim.2
  4.9 13.7 %all_to_all.5 = bf16[16,2,2304]{2,1,0:T(2,128)(2,1)S(1)} all-to-all(bf16[16,2,2304]{2,1,0:T(2,128)(2,1)S(1)} %broadcast_in_dim.2), channel_id=1, replica_groups=mesh['harm'=4,'space'=2,'samp'=4] {'harm','samp'}, dimensions={0} | all-to-all | bytes 294912 | tf_op jit(solution)/shard_map/all_to_all | solution.py:278
  18.6 0.1 reshape.4.window
  18.7 3.2 %shard_fields.1 = (f32[16,2,384]{2,1,0:T(2,128)S(1)}, f32[2,256]{1,0:T(2,128)S(1)}) custom-call(bf16[32,2304]{1,0:T(8,128)(2,1)S(1)} %reshape.4.window, bf16[6,4,128,384]{3,2,1,0:T(8,128)(2,1)S(1)} %get-tuple-element.16.first_curl, f32[32,2]{1,0:T(8,128)S(1)} %get-tuple-element.17.table, bf16[32,96]{1,0:T(8,128)(2,1)S(1)} %get-tuple-element.18.pieces, ...), custom_call_target="tpu_custom_call" | custom-call | flops 402653184 | bytes 6291456 | tf_op jit(solution)/shard_map/shard_fields/pallas_call | solution.py:281
  21.9 1.6 %collective-permute-start.1 = (f32[2,256]{1,0:T(2,128)S(1)}, f32[2,256]{1,0:T(2,128)S(1)}, u32[]{:S(2)}, u32[]{:S(2)}) collective-permute-start(f32[2,256]{1,0:T(2,128)S(1)} %get-tuple-element.24), channel_id=1, source_target_pairs={{0,4},{4,0},{1,5},{5,1},{2,6},{6,2},{3,7},{7,3},{8,12},{12,8},{9,1... | collective-permute-start | bytes 6152 | tf_op jit(solution)/shard_map/ppermute | solution.py:38
  23.5 3.3 %shard_sums.1.own = f32[2,2048]{1,0:T(2,128)S(1)} custom-call(f32[16,2,384]{2,1,0:T(2,128)S(1)} %get-tuple-element.22.projected, bf16[6,4,128,384]{3,2,1,0:T(8,128)(2,1)S(1)} %get-tuple-element.16.first_curl, f32[2,2048]{1,0:T(2,128)S(1)} %get-tuple-element.23.source, s32[4,16]{1,0:T(4,128)S(1)} %get-tuple-element.19.pattern_in, ...), custom_call_target="tpu_custom_call" | custom-call | flops 402653184 | bytes 6291456 | tf_op jit(solution)/shard_map/shard_sums/pallas_call | solution.py:317
  26.8 0.0 collective-permute-done.1.from_right.from_left
  26.8 0.6 %halo_sum.1 = f32[2,2048]{1,0:T(2,128)} custom-call(f32[2,2048]{1,0:T(2,128)S(1)} %shard_sums.1.own, f32[2,256]{1,0:T(2,128)S(1)} %collective-permute-done.1.from_right.from_left, f32[2,256]{1,0:T(2,128)S(1)} %collective-permute-done.1.from_right.from_left), custom_call_target="tpu_custom_call" | custom-call | tf_op jit(solution)/shard_map/halo_sum/pallas_call | solution.py:340
  (2 shorter events, 0.0 us)
Async XLA Ops:
  0.0 4.8 %collective-permute-start = (bf16[2,2048]{1,0:T(2,128)(2,1)}, bf16[2,2048]{1,0:T(2,128)(2,1)S(1)}, u32[]{:S(2)}, u32[]{:S(2)}) collective-permute-start(bf16[2,2048]{1,0:T(2,128)(2,1)} %refs_2_.1), channel_id=1, source_target_pairs={{0,4},{4,0},{1,5},{5,1},{2,6},{6,2},{3,7},{7,3},{8,12},{12,8},{9,1... | collective-permute-start | bytes 24584 | tf_op jit(solution)/shard_map/ppermute | solution.py:38
  21.9 4.9 %collective-permute-start.1 = (f32[2,256]{1,0:T(2,128)S(1)}, f32[2,256]{1,0:T(2,128)S(1)}, u32[]{:S(2)}, u32[]{:S(2)}) collective-permute-start(f32[2,256]{1,0:T(2,128)S(1)} %get-tuple-element.24), channel_id=1, source_target_pairs={{0,4},{4,0},{1,5},{5,1},{2,6},{6,2},{3,7},{7,3},{8,12},{12,8},{9,1... | collective-permute-start | bytes 6152 | tf_op jit(solution)/shard_map/ppermute | solution.py:38

commit v17 on v16

--- a/solution.py
+++ b/solution.py
@@ -92,11 +92,11 @@
     curl_hbm,
     projected,
     halo,
+    later_curl,
     pattern,
     region_ids,
     law,
     outer,
-    later_curl,
     timed,
     densities,
     edge_sums,
@@ -184,29 +184,25 @@
 def sum_kernel(
     projected,
     first_curl,
+    later_curl,
     source,
     pattern_in,
-    curl_hbm,
     out,
     pattern,
-    later_curl,
     small_sem,
-    curl_sem,
     *sums,
 ):
-    tile_count, links, tile, _ = curl_hbm.shape
+    links, tile, comps = first_curl.shape[1:]
     early = first_curl.shape[0]
+    tile_count = early + later_curl.shape[0]
     small = pltpu.make_async_copy(pattern_in, pattern, small_sem)
-    rest, blocks = curl_copies(curl_hbm, first_curl, later_curl, curl_sem)
     small.start()
-    rest.start()
     for total in sums:
         total[...] = jnp.zeros_like(total)
     small.wait()
     for elem in range(tile_count):
-        if elem == early:
-            rest.wait()
-        contrib = weighted(projected[elem], blocks(elem))
+        curl = first_curl[elem] if elem < early else later_curl[elem - early]
+        contrib = weighted(projected[elem], curl.reshape(links * tile, comps))
         for link in range(links):
             sums[link][pattern[link, elem]] += contrib[:, link * tile : (link + 1) * tile]
     for w in range(tile_count):
@@ -276,22 +272,21 @@
     block = jnp.concatenate([left, coeffs_here, right], axis=1)
     copies = jnp.broadcast_to(block[None], (group_size,) + block.shape)
     window = lax.all_to_all(copies, GROUP, 0, 0).reshape(parts, block.shape[1])
-    later_tiles = pltpu.VMEM((tile_count - early,) + curl_tiles.shape[1:], curl_tiles.dtype)
     pattern_words = pltpu.SMEM((links, tile_count), jnp.int32)
-    projected, halo = pl.pallas_call(
+    projected, halo, later_curl = pl.pallas_call(
         field_kernel,
         out_shape=(
             pltpu.VMEM((tile_count, parts_here, comps), jnp.float32),
             pltpu.VMEM((parts_here, 2 * tile), jnp.float32),
+            pltpu.VMEM((tile_count - early,) + curl_tiles.shape[1:], curl_tiles.dtype),
         ),
         in_specs=[vmem] * 7 + [hbm],
-        out_specs=(vmem, vmem),
+        out_specs=(vmem, vmem, vmem),
         scratch_shapes=[
             pattern_words,
             pltpu.SMEM(region_ids.shape, jnp.int32),
             pltpu.SMEM(material_law.shape, jnp.float32),
             pltpu.SMEM((links * tile_count + 1,), jnp.int32),
-            later_tiles,
             pltpu.VMEM((SAMPLES, (tile_count + 2) * tile), jnp.bfloat16),
             pltpu.VMEM((tile_count, HALF, comps), jnp.float32),
             pltpu.VMEM((LISTED, 2, parts_here, tile), jnp.float32),
@@ -317,12 +312,10 @@
     own = pl.pallas_call(
         sum_kernel,
         out_shape=pltpu.VMEM(source.shape, jnp.float32),
-        in_specs=[vmem] * 4 + [hbm],
+        in_specs=[vmem] * 5,
         out_specs=vmem,
         scratch_shapes=[
             pattern_words,
-            later_tiles,
-            pltpu.SemaphoreType.DMA,
             pltpu.SemaphoreType.DMA,
         ]
         + [pltpu.VMEM((tile_count + 2, parts_here, tile), jnp.float32)] * links,
@@ -334,8 +327,7 @@
         ),
         name="shard_sums",
     )(
-        *[in_vmem(array) for array in (projected, first_curl, source_here, pattern_here)],
-        in_hbm(curl_tiles),
+        *[in_vmem(a) for a in (projected, first_curl, later_curl, source_here, pattern_here)],
     )
     return pl.pallas_call(
         halo_kernel,

time: 27.7 us -> 26.8 us (0.968)
  Pallas kernels: 8.89 us -> 7.94 us
  starting transfers between devices: 4.55 us -> 4.84 us
    pallas_call x1, Pallas kernels: 3.28 us -> 2.34 us  [per_device(): pl.pallas_call(sum_kernel, out_shape=pltpu.VMEM(source.shape, jnp.float32...]
    ppermute x2, starting transfers between devices: 4.55 us -> 4.84 us  [shifted(): lax.ppermute(array, axis, [(i, (i + by) % count) for i in range(count)])]
  transfers between devices with their start and end apart: 2 -> 2, of which waited for: 1 -> 1; matrix products, arithmetic and copies ran while one was open for 0% -> 0% of each run, Pallas kernels for 18% -> 15%
where the time goes in v17:
time: 26.8 us
  blocking collectives  13.7 us (51%)
  Pallas kernels  7.94 us (30%)
  starting transfers between devices  4.84 us (18%)
    all_to_all x1, blocking collectives, per_device(): window = lax.all_to_all(copies, GROUP, 0, 0).reshape(parts, block.shape[1])  13.7 us
    ppermute x2, starting transfers between devices, shifted(): lax.ppermute(array, axis, [(i, (i + by) % count) for i in range(count)])  4.84 us
    pallas_call x1, Pallas kernels, per_device(): pl.pallas_call(field_kernel, out_shape=(pltpu.VMEM((tile_count, parts_her...  3.24 us
    pallas_call x1, Pallas kernels, per_device(): pl.pallas_call(sum_kernel, out_shape=pltpu.VMEM(source.shape, jnp.float32...  2.34 us
    pallas_call x1, Pallas kernels, per_device(): pl.pallas_call(fetch_kernel, out_shape=[pltpu.VMEM(shape, o.dtype) for sh...  1.75 us
    pallas_call x1, Pallas kernels, per_device(): pl.pallas_call(halo_kernel, out_shape=jax.ShapeDtypeStruct(source.shape,...  0.61 us
  transfers between devices with their start and end apart: 2, of which 1 were waited for; matrix products, arithmetic and copies ran while one was open for 0% of the time, Pallas kernels for 15%

profile of v17, /device:TPU:0, one launch (start us, length us, event | category | flops | bytes accessed | tf_op | source)
XLA Modules:
  0.0 26.8 jit_solution(14000972829959372378)
XLA Ops:
  0.0 3.0 %collective-permute-start = (bf16[2,2048]{1,0:T(2,128)(2,1)}, bf16[2,2048]{1,0:T(2,128)(2,1)S(1)}, u32[]{:S(2)}, u32[]{:S(2)}) collective-permute-start(bf16[2,2048]{1,0:T(2,128)(2,1)} %refs_2_.1), channel_id=1, source_target_pairs={{0,4},{4,0},{1,5},{5,1},{2,6},{6,2},{3,7},{7,3},{8,12},{12,8},{9,1... | collective-permute-start | bytes 24584 | tf_op jit(solution)/shard_map/ppermute | solution.py:38
  3.0 1.7 %fetch_operands.1 = (bf16[6,4,128,384]{3,2,1,0:T(8,128)(2,1)S(1)}, f32[32,2]{1,0:T(8,128)S(1)}, bf16[2,2048]{1,0:T(2,128)(2,1)S(1)}, bf16[32,96]{1,0:T(8,128)(2,...) custom-call(bf16[16,4,128,384]{3,2,1,0:T(8,128)(2,1)} %curl_hbm.1, ...), custom_call_target="tpu_custom_call" | custom-call | bytes 4718592 | tf_op jit(solution)/shard_map/fetch_operands/pallas_call | solution.py:256
  4.7 0.1 collective-permute-done
  4.8 0.1 broadcast_in_dim.2
  4.9 13.7 %all_to_all.5 = bf16[16,2,2304]{2,1,0:T(2,128)(2,1)S(1)} all-to-all(bf16[16,2,2304]{2,1,0:T(2,128)(2,1)S(1)} %broadcast_in_dim.2), channel_id=1, replica_groups=mesh['harm'=4,'space'=2,'samp'=4] {'harm','samp'}, dimensions={0} | all-to-all | bytes 294912 | tf_op jit(solution)/shard_map/all_to_all | solution.py:274
  18.6 0.1 reshape.4.window
  18.7 3.2 %shard_fields.1 = (f32[16,2,384]{2,1,0:T(2,128)S(1)}, f32[2,256]{1,0:T(2,128)S(1)}, bf16[10,4,128,384]{3,2,1,0:T(8,128)(2,1)S(1)}) custom-call(bf16[32,2304]{1,0:T(8,128)(2,1)S(1)} %reshape.4.window, bf16[6,4,128,384]{3,2,1,0:T(8,128)(2,1)S(1)} %get-tuple-element.17.first_curl, f32[32,2]{1,0:T(8,128)S(1)} %get-tuple-element.18.table, ...), custom_call_target="tpu_custom_call" | custom-call | flops 402653184 | bytes 6291456 | tf_op jit(solution)/shard_map/shard_fields/pallas_call | solution.py:276
  21.9 1.9 %collective-permute-start.1 = (f32[2,256]{1,0:T(2,128)S(1)}, f32[2,256]{1,0:T(2,128)S(1)}, u32[]{:S(2)}, u32[]{:S(2)}) collective-permute-start(f32[2,256]{1,0:T(2,128)S(1)} %get-tuple-element.26), channel_id=1, source_target_pairs={{0,4},{4,0},{1,5},{5,1},{2,6},{6,2},{3,7},{7,3},{8,12},{12,8},{9,1... | collective-permute-start | bytes 6152 | tf_op jit(solution)/shard_map/ppermute | solution.py:38
  23.8 2.3 %shard_sums.1.own = f32[2,2048]{1,0:T(2,128)S(1)} custom-call(f32[16,2,384]{2,1,0:T(2,128)S(1)} %get-tuple-element.23.projected, bf16[6,4,128,384]{3,2,1,0:T(8,128)(2,1)S(1)} %get-tuple-element.17.first_curl, bf16[10,4,128,384]{3,2,1,0:T(8,128)(2,1)S(1)} %get-tuple-element.24.later_curl, f32[2,2048]{1,0:T(2,128)S(1)} %get-tuple-element.25.source, ...), custom_call_target="tpu_custom_call" | custom-call | flops 402653184 | bytes 6291456 | tf_op jit(solution)/shard_map/shard_sums/pallas_call | solution.py:312
  26.1 0.0 collective-permute-done.1.from_right.from_left
  26.2 0.6 %halo_sum.1 = f32[2,2048]{1,0:T(2,128)} custom-call(f32[2,2048]{1,0:T(2,128)S(1)} %shard_sums.1.own, f32[2,256]{1,0:T(2,128)S(1)} %collective-permute-done.1.from_right.from_left, f32[2,256]{1,0:T(2,128)S(1)} %collective-permute-done.1.from_right.from_left), custom_call_target="tpu_custom_call" | custom-call | tf_op jit(solution)/shard_map/halo_sum/pallas_call | solution.py:332
  (2 shorter events, 0.0 us)
Async XLA Ops:
  0.0 4.8 %collective-permute-start = (bf16[2,2048]{1,0:T(2,128)(2,1)}, bf16[2,2048]{1,0:T(2,128)(2,1)S(1)}, u32[]{:S(2)}, u32[]{:S(2)}) collective-permute-start(bf16[2,2048]{1,0:T(2,128)(2,1)} %refs_2_.1), channel_id=1, source_target_pairs={{0,4},{4,0},{1,5},{5,1},{2,6},{6,2},{3,7},{7,3},{8,12},{12,8},{9,1... | collective-permute-start | bytes 24584 | tf_op jit(solution)/shard_map/ppermute | solution.py:38
  21.9 4.2 %collective-permute-start.1 = (f32[2,256]{1,0:T(2,128)S(1)}, f32[2,256]{1,0:T(2,128)S(1)}, u32[]{:S(2)}, u32[]{:S(2)}) collective-permute-start(f32[2,256]{1,0:T(2,128)S(1)} %get-tuple-element.26), channel_id=1, source_target_pairs={{0,4},{4,0},{1,5},{5,1},{2,6},{6,2},{3,7},{7,3},{8,12},{12,8},{9,1... | collective-permute-start | bytes 6152 | tf_op jit(solution)/shard_map/ppermute | solution.py:38

commit v18 on v17

--- a/solution.py
+++ b/solution.py
@@ -14,6 +14,7 @@
 GROUP = ("harm", "samp")
 MIB = 1024 * 1024
 LISTED = 4
+CHUNK = 4
 
 
 def half_table(parts):
@@ -58,18 +59,6 @@
         copy.start()
     for copy in copies:
         copy.wait()
-
-
-def curl_copies(curl_hbm, first_curl, later_curl, sem):
-    early = first_curl.shape[0]
-    links, tile, comps = curl_hbm.shape[1:]
-    rest = pltpu.make_async_copy(curl_hbm.at[early:], later_curl, sem)
-
-    def blocks(elem):
-        curl = first_curl[elem] if elem < early else later_curl[elem - early]
-        return curl.reshape(links * tile, comps)
-
-    return rest, blocks
 
 
 def weighted(projected, blocks):
@@ -101,7 +90,7 @@
     densities,
     edge_sums,
     small_sems,
-    curl_sem,
+    curl_sems,
 ):
     tile_count, links, tile, comps = curl_hbm.shape
     early = first_curl.shape[0]
@@ -110,8 +99,15 @@
     small = [
         pltpu.make_async_copy(src, dst, small_sems.at[i]) for i, (src, dst) in enumerate(fetched)
     ]
-    rest, blocks = curl_copies(curl_hbm, first_curl, later_curl, curl_sem)
-    for copy in small + [rest]:
+    later = {
+        elem: pltpu.make_async_copy(
+            curl_hbm.at[elem : min(elem + CHUNK, tile_count)],
+            later_curl.at[elem - early : min(elem + CHUNK, tile_count) - early],
+            curl_sems.at[(elem - early) // CHUNK],
+        )
+        for elem in range(early, tile_count, CHUNK)
+    }
+    for copy in small + list(later.values()):
         copy.start()
     edge_sums[...] = jnp.zeros_like(edge_sums)
     stacked = jnp.concatenate([window[...]] * 3, axis=0)
@@ -131,6 +127,10 @@
             outer[count] = elem * links + link
             count += jnp.where((at == 0) | (at == tile_count + 1), 1, 0)
 
+    def blocks(elem):
+        curl = first_curl[elem] if elem < early else later_curl[elem - early]
+        return curl.reshape(links * tile, comps)
+
     def find_density(elem):
         picked = jnp.concatenate(
             [timed[:, pl.ds(pl.multiple_of(at * tile, tile), tile)] for at in places[elem]], axis=1
@@ -152,8 +152,8 @@
 
     for turn in range(tile_count + 1):
         if turn < tile_count:
-            if turn == early:
-                rest.wait()
+            if turn in later:
+                later[turn].wait()
             find_density(turn)
         if turn:
             project(turn - 1)
@@ -238,7 +238,7 @@
     def in_hbm(array):
         return pltpu.with_memory_space_constraint(array, pltpu.HBM)
 
-    early = 3 * tile_count // 8
+    early = tile_count // 2
     operands = [
         curl_tiles,
         own_columns,
@@ -291,7 +291,7 @@
             pltpu.VMEM((tile_count, HALF, comps), jnp.float32),
             pltpu.VMEM((LISTED, 2, parts_here, tile), jnp.float32),
             pltpu.SemaphoreType.DMA((3,)),
-            pltpu.SemaphoreType.DMA,
+            pltpu.SemaphoreType.DMA((pl.cdiv(tile_count - early, CHUNK),)),
         ],
         compiler_params=pltpu.CompilerParams(vmem_limit_bytes=32 * MIB),
         cost_estimate=pl.CostEstimate(

time: 26.8 us -> 26 us (0.970)
  Pallas kernels: 7.94 us -> 7.57 us
  starting transfers between devices: 4.84 us -> 4.55 us
    pallas_call x1, Pallas kernels: 3.24 us -> 2.64 us  [per_device(): pl.pallas_call(field_kernel, out_shape=(pltpu.VMEM((tile_count, parts_her...]
    ppermute x2, starting transfers between devices: 4.84 us -> 4.55 us  [shifted(): lax.ppermute(array, axis, [(i, (i + by) % count) for i in range(count)])]
  transfers between devices with their start and end apart: 2 -> 2, of which waited for: 1 -> 0; matrix products, arithmetic and copies ran while one was open for 0% -> 0% of each run, Pallas kernels for 15% -> 17%
where the time goes in v18:
time: 26 us; the launch traced here: 25.9 us
  blocking collectives  13.5 us (52%)
  Pallas kernels  7.57 us (29%)
  starting transfers between devices  4.55 us (18%)
    all_to_all x1, blocking collectives, per_device(): window = lax.all_to_all(copies, GROUP, 0, 0).reshape(parts, block.shape[1])  13.5 us
    ppermute x2, starting transfers between devices, shifted(): lax.ppermute(array, axis, [(i, (i + by) % count) for i in range(count)])  4.55 us
    pallas_call x1, Pallas kernels, per_device(): pl.pallas_call(field_kernel, out_shape=(pltpu.VMEM((tile_count, parts_her...  2.64 us
    pallas_call x1, Pallas kernels, per_device(): pl.pallas_call(sum_kernel, out_shape=pltpu.VMEM(source.shape, jnp.float32...  2.34 us
    pallas_call x1, Pallas kernels, per_device(): pl.pallas_call(fetch_kernel, out_shape=[pltpu.VMEM(shape, o.dtype) for sh...  1.97 us
    pallas_call x1, Pallas kernels, per_device(): pl.pallas_call(halo_kernel, out_shape=jax.ShapeDtypeStruct(source.shape,...  0.62 us
  transfers between devices with their start and end apart: 2, of which 0 were waited for; matrix products, arithmetic and copies ran while one was open for 0% of the time, Pallas kernels for 17%

profile of v18, /device:TPU:0, one launch (start us, length us, event | category | flops | bytes accessed | tf_op | source)
XLA Modules:
  0.0 25.9 jit_solution(5794671600473934546)
XLA Ops:
  0.0 3.0 %collective-permute-start = (bf16[2,2048]{1,0:T(2,128)(2,1)}, bf16[2,2048]{1,0:T(2,128)(2,1)S(1)}, u32[]{:S(2)}, u32[]{:S(2)}) collective-permute-start(bf16[2,2048]{1,0:T(2,128)(2,1)} %refs_2_.1), channel_id=1, source_target_pairs={{0,4},{4,0},{1,5},{5,1},{2,6},{6,2},{3,7},{7,3},{8,12},{12,8},{9,1... | collective-permute-start | bytes 24584 | tf_op jit(solution)/shard_map/ppermute | solution.py:39
  3.0 2.0 %fetch_operands.1 = (bf16[8,4,128,384]{3,2,1,0:T(8,128)(2,1)S(1)}, f32[32,2]{1,0:T(8,128)S(1)}, bf16[2,2048]{1,0:T(2,128)(2,1)S(1)}, bf16[32,96]{1,0:T(8,128)(2,...) custom-call(bf16[16,4,128,384]{3,2,1,0:T(8,128)(2,1)} %curl_hbm.1, ...), custom_call_target="tpu_custom_call" | custom-call | bytes 6291456 | tf_op jit(solution)/shard_map/fetch_operands/pallas_call | solution.py:256
  4.9 0.0 collective-permute-done
  5.0 0.1 broadcast_in_dim.2
  5.1 13.5 %all_to_all.5 = bf16[16,2,2304]{2,1,0:T(2,128)(2,1)S(1)} all-to-all(bf16[16,2,2304]{2,1,0:T(2,128)(2,1)S(1)} %broadcast_in_dim.2), channel_id=1, replica_groups=mesh['harm'=4,'space'=2,'samp'=4] {'harm','samp'}, dimensions={0} | all-to-all | bytes 294912 | tf_op jit(solution)/shard_map/all_to_all | solution.py:274
  18.6 0.1 reshape.4.window
  18.7 2.6 %shard_fields.1 = (f32[16,2,384]{2,1,0:T(2,128)S(1)}, f32[2,256]{1,0:T(2,128)S(1)}, bf16[8,4,128,384]{3,2,1,0:T(8,128)(2,1)S(1)}) custom-call(bf16[32,2304]{1,0:T(8,128)(2,1)S(1)} %reshape.4.window, bf16[8,4,128,384]{3,2,1,0:T(8,128)(2,1)S(1)} %get-tuple-element.17.first_curl, f32[32,2]{1,0:T(8,128)S(1)} %get-tuple-element.18.table, ...), custom_call_target="tpu_custom_call" | custom-call | flops 402653184 | bytes 6291456 | tf_op jit(solution)/shard_map/shard_fields/pallas_call | solution.py:276
  21.3 1.6 %collective-permute-start.1 = (f32[2,256]{1,0:T(2,128)S(1)}, f32[2,256]{1,0:T(2,128)S(1)}, u32[]{:S(2)}, u32[]{:S(2)}) collective-permute-start(f32[2,256]{1,0:T(2,128)S(1)} %get-tuple-element.26), channel_id=1, source_target_pairs={{0,4},{4,0},{1,5},{5,1},{2,6},{6,2},{3,7},{7,3},{8,12},{12,8},{9,1... | collective-permute-start | bytes 6152 | tf_op jit(solution)/shard_map/ppermute | solution.py:39
  22.9 2.3 %shard_sums.1.own = f32[2,2048]{1,0:T(2,128)S(1)} custom-call(f32[16,2,384]{2,1,0:T(2,128)S(1)} %get-tuple-element.23.projected, bf16[8,4,128,384]{3,2,1,0:T(8,128)(2,1)S(1)} %get-tuple-element.17.first_curl, bf16[8,4,128,384]{3,2,1,0:T(8,128)(2,1)S(1)} %get-tuple-element.24.later_curl, f32[2,2048]{1,0:T(2,128)S(1)} %get-tuple-element.25.source, ...), custom_call_target="tpu_custom_call" | custom-call | flops 402653184 | bytes 6291456 | tf_op jit(solution)/shard_map/shard_sums/pallas_call | solution.py:312
  25.3 0.0 collective-permute-done.1.from_right.from_left
  25.3 0.6 %halo_sum.1 = f32[2,2048]{1,0:T(2,128)} custom-call(f32[2,2048]{1,0:T(2,128)S(1)} %shard_sums.1.own, f32[2,256]{1,0:T(2,128)S(1)} %collective-permute-done.1.from_right.from_left, f32[2,256]{1,0:T(2,128)S(1)} %collective-permute-done.1.from_right.from_left), custom_call_target="tpu_custom_call" | custom-call | tf_op jit(solution)/shard_map/halo_sum/pallas_call | solution.py:332
  (2 shorter events, 0.0 us)
Async XLA Ops:
  0.0 4.9 %collective-permute-start = (bf16[2,2048]{1,0:T(2,128)(2,1)}, bf16[2,2048]{1,0:T(2,128)(2,1)S(1)}, u32[]{:S(2)}, u32[]{:S(2)}) collective-permute-start(bf16[2,2048]{1,0:T(2,128)(2,1)} %refs_2_.1), channel_id=1, source_target_pairs={{0,4},{4,0},{1,5},{5,1},{2,6},{6,2},{3,7},{7,3},{8,12},{12,8},{9,1... | collective-permute-start | bytes 24584 | tf_op jit(solution)/shard_map/ppermute | solution.py:39
  21.3 3.9 %collective-permute-start.1 = (f32[2,256]{1,0:T(2,128)S(1)}, f32[2,256]{1,0:T(2,128)S(1)}, u32[]{:S(2)}, u32[]{:S(2)}) collective-permute-start(f32[2,256]{1,0:T(2,128)S(1)} %get-tuple-element.26), channel_id=1, source_target_pairs={{0,4},{4,0},{1,5},{5,1},{2,6},{6,2},{3,7},{7,3},{8,12},{12,8},{9,1... | collective-permute-start | bytes 6152 | tf_op jit(solution)/shard_map/ppermute | solution.py:39

commit v19 on v18

--- a/solution.py
+++ b/solution.py
@@ -131,12 +131,27 @@
         curl = first_curl[elem] if elem < early else later_curl[elem - early]
         return curl.reshape(links * tile, comps)
 
-    def find_density(elem):
-        picked = jnp.concatenate(
+    def picked(elem):
+        return jnp.concatenate(
             [timed[:, pl.ds(pl.multiple_of(at * tile, tile), tile)] for at in places[elem]], axis=1
         )
-        split = jnp.dot(picked, blocks(elem), preferred_element_type=jnp.float32)
-        densities[elem] = split[:HALF] + split[HALF:]
+
+    def product(left, right):
+        return jnp.dot(left, right, preferred_element_type=jnp.float32)
+
+    def find_densities(one, two):
+        cut, rest = 2 * tile, comps - 2 * tile
+        samples_one, samples_two = picked(one), picked(two)
+        split_one = product(samples_one, blocks(one)[:, :cut])
+        densities[one, :, :cut] = split_one[:HALF] + split_one[HALF:]
+        shared = product(
+            jnp.concatenate([samples_one, samples_two], axis=0),
+            jnp.concatenate([blocks(one)[:, cut:], blocks(two)[:, :rest]], axis=1),
+        )
+        densities[one, :, cut:] = shared[:HALF, :rest] + shared[HALF : 2 * HALF, :rest]
+        densities[two, :, :rest] = shared[2 * HALF : 3 * HALF, rest:] + shared[3 * HALF :, rest:]
+        split_two = product(samples_two, blocks(two)[:, rest:])
+        densities[two, :, rest:] = split_two[:HALF] + split_two[HALF:]
 
     def project(elem):
         density = densities[elem]
@@ -150,13 +165,14 @@
         rows = [jnp.sum(column * field, axis=0, keepdims=True) for column in columns]
         projected[elem] = jnp.concatenate(rows, axis=0) * (4.0 / SAMPLES)
 
-    for turn in range(tile_count + 1):
-        if turn < tile_count:
-            if turn in later:
-                later[turn].wait()
-            find_density(turn)
-        if turn:
-            project(turn - 1)
+    for elem in range(0, tile_count + 1, 2):
+        if elem < tile_count:
+            if elem in later:
+                later[elem].wait()
+            find_densities(elem, elem + 1)
+        if elem:
+            project(elem - 2)
+            project(elem - 1)
 
     def add_outer(turn, carry):
         for slot in range(LISTED):

time: 26 us -> 26.1 us (level)
  Pallas kernels: 7.57 us -> 7.85 us
  starting transfers between devices: 4.55 us -> 4.28 us
    pallas_call x1, Pallas kernels: 2.64 us -> 2.93 us  [per_device(): pl.pallas_call(field_kernel, out_shape=(pltpu.VMEM((tile_count, parts_her...]
    ppermute x2, starting transfers between devices: 4.55 us -> 4.28 us  [shifted(): lax.ppermute(array, axis, [(i, (i + by) % count) for i in range(count)])]
where the time goes in v19:
time: 26.1 us; the launch traced here: 25.9 us
  blocking collectives  13.5 us (52%)
  Pallas kernels  7.85 us (30%)
  starting transfers between devices  4.28 us (16%)
    all_to_all x1, blocking collectives, per_device(): window = lax.all_to_all(copies, GROUP, 0, 0).reshape(parts, block.shape[1])  13.5 us
    ppermute x2, starting transfers between devices, shifted(): lax.ppermute(array, axis, [(i, (i + by) % count) for i in range(count)])  4.28 us
    pallas_call x1, Pallas kernels, per_device(): pl.pallas_call(field_kernel, out_shape=(pltpu.VMEM((tile_count, parts_her...  2.93 us
    pallas_call x1, Pallas kernels, per_device(): pl.pallas_call(sum_kernel, out_shape=pltpu.VMEM(source.shape, jnp.float32...  2.34 us
    pallas_call x1, Pallas kernels, per_device(): pl.pallas_call(fetch_kernel, out_shape=[pltpu.VMEM(shape, o.dtype) for sh...  1.97 us
    pallas_call x1, Pallas kernels, per_device(): pl.pallas_call(halo_kernel, out_shape=jax.ShapeDtypeStruct(source.shape,...  0.62 us
  transfers between devices with their start and end apart: 2, of which 0 were waited for; matrix products, arithmetic and copies ran while one was open for 0% of the time, Pallas kernels for 17%

profile of v19, /device:TPU:0, one launch (start us, length us, event | category | flops | bytes accessed | tf_op | source)
XLA Modules:
  0.0 25.9 jit_solution(13460559802596526020)
XLA Ops:
  0.0 3.0 %collective-permute-start = (bf16[2,2048]{1,0:T(2,128)(2,1)}, bf16[2,2048]{1,0:T(2,128)(2,1)S(1)}, u32[]{:S(2)}, u32[]{:S(2)}) collective-permute-start(bf16[2,2048]{1,0:T(2,128)(2,1)} %refs_2_.1), channel_id=1, source_target_pairs={{0,4},{4,0},{1,5},{5,1},{2,6},{6,2},{3,7},{7,3},{8,12},{12,8},{9,1... | collective-permute-start | bytes 24584 | tf_op jit(solution)/shard_map/ppermute | solution.py:39
  3.0 2.0 %fetch_operands.1 = (bf16[8,4,128,384]{3,2,1,0:T(8,128)(2,1)S(1)}, f32[32,2]{1,0:T(8,128)S(1)}, bf16[2,2048]{1,0:T(2,128)(2,1)S(1)}, bf16[32,96]{1,0:T(8,128)(2,...) custom-call(bf16[16,4,128,384]{3,2,1,0:T(8,128)(2,1)} %curl_hbm.1, ...), custom_call_target="tpu_custom_call" | custom-call | bytes 6291456 | tf_op jit(solution)/shard_map/fetch_operands/pallas_call | solution.py:272
  4.9 0.0 collective-permute-done
  5.0 0.1 broadcast_in_dim.2
  5.1 13.5 %all_to_all.5 = bf16[16,2,2304]{2,1,0:T(2,128)(2,1)S(1)} all-to-all(bf16[16,2,2304]{2,1,0:T(2,128)(2,1)S(1)} %broadcast_in_dim.2), channel_id=1, replica_groups=mesh['harm'=4,'space'=2,'samp'=4] {'harm','samp'}, dimensions={0} | all-to-all | bytes 294912 | tf_op jit(solution)/shard_map/all_to_all | solution.py:290
  18.6 0.1 reshape.4.window
  18.7 2.9 %shard_fields.1 = (f32[16,2,384]{2,1,0:T(2,128)S(1)}, f32[2,256]{1,0:T(2,128)S(1)}, bf16[8,4,128,384]{3,2,1,0:T(8,128)(2,1)S(1)}) custom-call(bf16[32,2304]{1,0:T(8,128)(2,1)S(1)} %reshape.4.window, bf16[8,4,128,384]{3,2,1,0:T(8,128)(2,1)S(1)} %get-tuple-element.17.first_curl, f32[32,2]{1,0:T(8,128)S(1)} %get-tuple-element.18.table, ...), custom_call_target="tpu_custom_call" | custom-call | flops 402653184 | bytes 6291456 | tf_op jit(solution)/shard_map/shard_fields/pallas_call | solution.py:292
  21.6 1.3 %collective-permute-start.1 = (f32[2,256]{1,0:T(2,128)S(1)}, f32[2,256]{1,0:T(2,128)S(1)}, u32[]{:S(2)}, u32[]{:S(2)}) collective-permute-start(f32[2,256]{1,0:T(2,128)S(1)} %get-tuple-element.26), channel_id=1, source_target_pairs={{0,4},{4,0},{1,5},{5,1},{2,6},{6,2},{3,7},{7,3},{8,12},{12,8},{9,1... | collective-permute-start | bytes 6152 | tf_op jit(solution)/shard_map/ppermute | solution.py:39
  22.9 2.3 %shard_sums.1.own = f32[2,2048]{1,0:T(2,128)S(1)} custom-call(f32[16,2,384]{2,1,0:T(2,128)S(1)} %get-tuple-element.23.projected, bf16[8,4,128,384]{3,2,1,0:T(8,128)(2,1)S(1)} %get-tuple-element.17.first_curl, bf16[8,4,128,384]{3,2,1,0:T(8,128)(2,1)S(1)} %get-tuple-element.24.later_curl, f32[2,2048]{1,0:T(2,128)S(1)} %get-tuple-element.25.source, ...), custom_call_target="tpu_custom_call" | custom-call | flops 402653184 | bytes 6291456 | tf_op jit(solution)/shard_map/shard_sums/pallas_call | solution.py:328
  25.3 0.0 collective-permute-done.1.from_right.from_left
  25.3 0.6 %halo_sum.1 = f32[2,2048]{1,0:T(2,128)} custom-call(f32[2,2048]{1,0:T(2,128)S(1)} %shard_sums.1.own, f32[2,256]{1,0:T(2,128)S(1)} %collective-permute-done.1.from_right.from_left, f32[2,256]{1,0:T(2,128)S(1)} %collective-permute-done.1.from_right.from_left), custom_call_target="tpu_custom_call" | custom-call | tf_op jit(solution)/shard_map/halo_sum/pallas_call | solution.py:348
  (2 shorter events, 0.0 us)
Async XLA Ops:
  0.0 4.9 %collective-permute-start = (bf16[2,2048]{1,0:T(2,128)(2,1)}, bf16[2,2048]{1,0:T(2,128)(2,1)S(1)}, u32[]{:S(2)}, u32[]{:S(2)}) collective-permute-start(bf16[2,2048]{1,0:T(2,128)(2,1)} %refs_2_.1), channel_id=1, source_target_pairs={{0,4},{4,0},{1,5},{5,1},{2,6},{6,2},{3,7},{7,3},{8,12},{12,8},{9,1... | collective-permute-start | bytes 24584 | tf_op jit(solution)/shard_map/ppermute | solution.py:39
  21.6 3.7 %collective-permute-start.1 = (f32[2,256]{1,0:T(2,128)S(1)}, f32[2,256]{1,0:T(2,128)S(1)}, u32[]{:S(2)}, u32[]{:S(2)}) collective-permute-start(f32[2,256]{1,0:T(2,128)S(1)} %get-tuple-element.26), channel_id=1, source_target_pairs={{0,4},{4,0},{1,5},{5,1},{2,6},{6,2},{3,7},{7,3},{8,12},{12,8},{9,1... | collective-permute-start | bytes 6152 | tf_op jit(solution)/shard_map/ppermute | solution.py:39

commit v20 on v19

--- a/solution.py
+++ b/solution.py
@@ -14,7 +14,7 @@
 GROUP = ("harm", "samp")
 MIB = 1024 * 1024
 LISTED = 4
-CHUNK = 4
+CHUNK = 2
 
 
 def half_table(parts):

time: 26.1 us -> 26.2 us (level)
  starting transfers between devices: 4.28 us -> 4.55 us
    ppermute x2, starting transfers between devices: 4.28 us -> 4.55 us  [shifted(): lax.ppermute(array, axis, [(i, (i + by) % count) for i in range(count)])]
where the time goes in v20:
time: 26.2 us; the launch traced here: 26.1 us
  blocking collectives  13.5 us (52%)
  Pallas kernels  7.77 us (30%)
  starting transfers between devices  4.55 us (17%)
    all_to_all x1, blocking collectives, per_device(): window = lax.all_to_all(copies, GROUP, 0, 0).reshape(parts, block.shape[1])  13.5 us
    ppermute x2, starting transfers between devices, shifted(): lax.ppermute(array, axis, [(i, (i + by) % count) for i in range(count)])  4.55 us
    pallas_call x1, Pallas kernels, per_device(): pl.pallas_call(field_kernel, out_shape=(pltpu.VMEM((tile_count, parts_her...  2.84 us
    pallas_call x1, Pallas kernels, per_device(): pl.pallas_call(sum_kernel, out_shape=pltpu.VMEM(source.shape, jnp.float32...  2.34 us
    pallas_call x1, Pallas kernels, per_device(): pl.pallas_call(fetch_kernel, out_shape=[pltpu.VMEM(shape, o.dtype) for sh...  1.97 us
    pallas_call x1, Pallas kernels, per_device(): pl.pallas_call(halo_kernel, out_shape=jax.ShapeDtypeStruct(source.shape,...  0.62 us
  transfers between devices with their start and end apart: 2, of which 0 were waited for; matrix products, arithmetic and copies ran while one was open for 0% of the time, Pallas kernels for 17%

profile of v20, /device:TPU:0, one launch (start us, length us, event | category | flops | bytes accessed | tf_op | source)
XLA Modules:
  0.0 26.1 jit_solution(1840122733685995036)
XLA Ops:
  0.0 3.0 %collective-permute-start = (bf16[2,2048]{1,0:T(2,128)(2,1)}, bf16[2,2048]{1,0:T(2,128)(2,1)S(1)}, u32[]{:S(2)}, u32[]{:S(2)}) collective-permute-start(bf16[2,2048]{1,0:T(2,128)(2,1)} %refs_2_.1), channel_id=1, source_target_pairs={{0,4},{4,0},{1,5},{5,1},{2,6},{6,2},{3,7},{7,3},{8,12},{12,8},{9,1... | collective-permute-start | bytes 24584 | tf_op jit(solution)/shard_map/ppermute | solution.py:39
  3.0 2.0 %fetch_operands.1 = (bf16[8,4,128,384]{3,2,1,0:T(8,128)(2,1)S(1)}, f32[32,2]{1,0:T(8,128)S(1)}, bf16[2,2048]{1,0:T(2,128)(2,1)S(1)}, bf16[32,96]{1,0:T(8,128)(2,...) custom-call(bf16[16,4,128,384]{3,2,1,0:T(8,128)(2,1)} %curl_hbm.1, ...), custom_call_target="tpu_custom_call" | custom-call | bytes 6291456 | tf_op jit(solution)/shard_map/fetch_operands/pallas_call | solution.py:272
  4.9 0.0 collective-permute-done
  5.0 0.1 broadcast_in_dim.2
  5.1 13.5 %all_to_all.5 = bf16[16,2,2304]{2,1,0:T(2,128)(2,1)S(1)} all-to-all(bf16[16,2,2304]{2,1,0:T(2,128)(2,1)S(1)} %broadcast_in_dim.2), channel_id=1, replica_groups=mesh['harm'=4,'space'=2,'samp'=4] {'harm','samp'}, dimensions={0} | all-to-all | bytes 294912 | tf_op jit(solution)/shard_map/all_to_all | solution.py:290
  18.6 0.1 reshape.4.window
  18.7 2.8 %shard_fields.1 = (f32[16,2,384]{2,1,0:T(2,128)S(1)}, f32[2,256]{1,0:T(2,128)S(1)}, bf16[8,4,128,384]{3,2,1,0:T(8,128)(2,1)S(1)}) custom-call(bf16[32,2304]{1,0:T(8,128)(2,1)S(1)} %reshape.4.window, bf16[8,4,128,384]{3,2,1,0:T(8,128)(2,1)S(1)} %get-tuple-element.17.first_curl, f32[32,2]{1,0:T(8,128)S(1)} %get-tuple-element.18.table, ...), custom_call_target="tpu_custom_call" | custom-call | flops 402653184 | bytes 6291456 | tf_op jit(solution)/shard_map/shard_fields/pallas_call | solution.py:292
  21.5 1.6 %collective-permute-start.1 = (f32[2,256]{1,0:T(2,128)S(1)}, f32[2,256]{1,0:T(2,128)S(1)}, u32[]{:S(2)}, u32[]{:S(2)}) collective-permute-start(f32[2,256]{1,0:T(2,128)S(1)} %get-tuple-element.26), channel_id=1, source_target_pairs={{0,4},{4,0},{1,5},{5,1},{2,6},{6,2},{3,7},{7,3},{8,12},{12,8},{9,1... | collective-permute-start | bytes 6152 | tf_op jit(solution)/shard_map/ppermute | solution.py:39
  23.1 2.3 %shard_sums.1.own = f32[2,2048]{1,0:T(2,128)S(1)} custom-call(f32[16,2,384]{2,1,0:T(2,128)S(1)} %get-tuple-element.23.projected, bf16[8,4,128,384]{3,2,1,0:T(8,128)(2,1)S(1)} %get-tuple-element.17.first_curl, bf16[8,4,128,384]{3,2,1,0:T(8,128)(2,1)S(1)} %get-tuple-element.24.later_curl, f32[2,2048]{1,0:T(2,128)S(1)} %get-tuple-element.25.source, ...), custom_call_target="tpu_custom_call" | custom-call | flops 402653184 | bytes 6291456 | tf_op jit(solution)/shard_map/shard_sums/pallas_call | solution.py:328
  25.5 0.0 collective-permute-done.1.from_right.from_left
  25.5 0.6 %halo_sum.1 = f32[2,2048]{1,0:T(2,128)} custom-call(f32[2,2048]{1,0:T(2,128)S(1)} %shard_sums.1.own, f32[2,256]{1,0:T(2,128)S(1)} %collective-permute-done.1.from_right.from_left, f32[2,256]{1,0:T(2,128)S(1)} %collective-permute-done.1.from_right.from_left), custom_call_target="tpu_custom_call" | custom-call | tf_op jit(solution)/shard_map/halo_sum/pallas_call | solution.py:348
  (2 shorter events, 0.0 us)
Async XLA Ops:
  0.0 4.9 %collective-permute-start = (bf16[2,2048]{1,0:T(2,128)(2,1)}, bf16[2,2048]{1,0:T(2,128)(2,1)S(1)}, u32[]{:S(2)}, u32[]{:S(2)}) collective-permute-start(bf16[2,2048]{1,0:T(2,128)(2,1)} %refs_2_.1), channel_id=1, source_target_pairs={{0,4},{4,0},{1,5},{5,1},{2,6},{6,2},{3,7},{7,3},{8,12},{12,8},{9,1... | collective-permute-start | bytes 24584 | tf_op jit(solution)/shard_map/ppermute | solution.py:39
  21.5 3.9 %collective-permute-start.1 = (f32[2,256]{1,0:T(2,128)S(1)}, f32[2,256]{1,0:T(2,128)S(1)}, u32[]{:S(2)}, u32[]{:S(2)}) collective-permute-start(f32[2,256]{1,0:T(2,128)S(1)} %get-tuple-element.26), channel_id=1, source_target_pairs={{0,4},{4,0},{1,5},{5,1},{2,6},{6,2},{3,7},{7,3},{8,12},{12,8},{9,1... | collective-permute-start | bytes 6152 | tf_op jit(solution)/shard_map/ppermute | solution.py:39

commit v21 on v17

v21 whole, which is shorter than its diff:
```python
import math

import jax
import jax.numpy as jnp
import ml_dtypes
import numpy as np
from jax import lax
from jax.experimental import pallas as pl
from jax.experimental.pallas import tpu as pltpu
from jax.sharding import PartitionSpec as P

SAMPLES = 64
HALF = SAMPLES // 2
GROUP = ("harm", "samp")
MIB = 1024 * 1024
LISTED = 4
CHUNK = 4


def half_table(parts):
    sample_ids = np.arange(HALF)[:, None]
    part_ids = np.arange(parts)[None, :]
    phase = ((2 * (part_ids // 2) + 1) * sample_ids % SAMPLES) * (2.0 * math.pi / SAMPLES)
    return np.where(part_ids % 2 == 0, np.cos(phase), np.sin(phase))


def bf16_pieces(table):
    rest = table
    pieces = []
    for _ in range(3):
        piece = rest.astype(ml_dtypes.bfloat16)
        pieces.append(piece)
        rest = rest - piece.astype(np.float64)
    return np.concatenate(pieces, axis=-1)


def shifted(array, axis, by):
    count = lax.axis_size(axis)
    return lax.ppermute(array, axis, [(i, (i + by) % count) for i in range(count)])


def from_neighbours(array, tile):
    first, last = array[..., :tile], array[..., -tile:]
    if lax.axis_size("space") == 2:
        other = shifted(jnp.concatenate([first, last], axis=-1), "space", 1)
        return other[..., :tile], other[..., tile:]
    return shifted(first, "space", -1), shifted(last, "space", 1)


def weighted(projected, blocks):
    return lax.dot_general(
        projected.astype(jnp.bfloat16),
        blocks,
        (((1,), (1,)), ((), ())),
        preferred_element_type=jnp.float32,
    )


def time_samples(pieces, rows):
    stacked = jnp.concatenate([rows] * 3, axis=0)
    samples = jnp.dot(pieces, stacked, preferred_element_type=jnp.float32)
    high = samples.astype(jnp.bfloat16)
    low = (samples - high.astype(jnp.float32)).astype(jnp.bfloat16)
    return jnp.concatenate([high, low], axis=0)


def flux_kernel(
    window,
    curl_hbm,
    pattern_hbm,
    pieces_hbm,
    table_hbm,
    *refs,
):
    others_hbm, refs = refs[:3], refs[3:]
    densities, curl, pieces, table = refs[:4]
    others, (pattern_here, pattern, timed, small_sems, curl_sems) = refs[4:7], refs[7:]
    tile_count, links, tile, comps = curl_hbm.shape
    fetched = [
        (pieces_hbm, pieces),
        (pattern_hbm, pattern),
        (table_hbm.at[lax.axis_index(GROUP)], table),
        (pattern_hbm, pattern_here),
        *zip(others_hbm, others),
    ]
    small = [
        pltpu.make_async_copy(src, dst, small_sems.at[i]) for i, (src, dst) in enumerate(fetched)
    ]
    later = {
        elem: pltpu.make_async_copy(
            curl_hbm.at[elem : min(elem + CHUNK, tile_count)],
            curl.at[elem : min(elem + CHUNK, tile_count)],
            curl_sems.at[elem // CHUNK],
        )
        for elem in range(0, tile_count, CHUNK)
    }
    for copy in small + list(later.values()):
        copy.start()
    outer = jnp.zeros((SAMPLES, tile), jnp.bfloat16)
    timed[:, :tile] = outer
    timed[:, (tile_count + 1) * tile :] = outer
    small[0].wait()
    timed[:, tile : (tile_count + 1) * tile] = time_samples(pieces[...], window[...])
    for copy in small[1:]:
        copy.wait()
    for elem in range(tile_count):
        if elem in later:
            later[elem].wait()
        places = [pattern[link, elem] for link in range(links)]
        picked = jnp.concatenate(
            [timed[:, pl.ds(pl.multiple_of(at * tile, tile), tile)] for at in places], axis=1
        )
        blocks = curl[elem].reshape(links * tile, comps)
        split = jnp.dot(picked, blocks, preferred_element_type=jnp.float32)
        densities[elem] = split[:HALF] + split[HALF:]


def field_kernel(
    partial,
    right,
    left,
    curl,
    pieces,
    table,
    pattern_in,
    region_in,
    law_in,
    projected,
    halo,
    pattern,
    region_ids,
    law,
    outer,
    timed,
    densities,
    edge_sums,
    small_sems,
):
    tile_count, links, tile, comps = curl.shape
    parts_here = halo.shape[0]
    fetched = [(pattern_in, pattern), (region_in, region_ids), (law_in, law)]
    small = [
        pltpu.make_async_copy(src, dst, small_sems.at[i]) for i, (src, dst) in enumerate(fetched)
    ]
    for copy in small:
        copy.start()
    edge_sums[...] = jnp.zeros_like(edge_sums)
    timed[0] = time_samples(pieces[...], left[...])
    timed[1] = time_samples(pieces[...], right[...])
    densities[...] = partial[...]
    columns = [
        jnp.broadcast_to(table[:, part : part + 1], (HALF, comps)) for part in range(parts_here)
    ]
    for copy in small:
        copy.wait()
    count = jnp.int32(0)
    for elem in range(tile_count):
        for link in range(links):
            at = pattern[link, elem]
            outer[count] = elem * links + link
            count += jnp.where((at == 0) | (at == tile_count + 1), 1, 0)

    def entry(turn, slot):
        spot = turn * LISTED + slot
        code = jnp.where(spot < count, outer[jnp.minimum(spot, count - 1)], 0)
        elem, link = code // links, code % links
        side = jnp.where(pattern[link, elem] == 0, 0, 1)
        return spot < count, elem, link, side

    def add_density(turn, carry):
        for slot in range(LISTED):
            listed, elem, link, side = entry(turn, slot)
            split = jnp.dot(timed[side], curl[elem, link], preferred_element_type=jnp.float32)
            densities[elem] += jnp.where(listed, split[:HALF] + split[HALF:], 0.0)
        return carry

    def project(elem):
        density = densities[elem]
        comp = [density[:, c * tile : (c + 1) * tile] for c in range(comps // tile)]
        square = comp[0] * comp[0]
        for c in comp[1:]:
            square = square + c * c
        region = region_ids[elem]
        reluct = law[0, region] + law[2, region] * square / (square + law[1, region])
        field = jnp.concatenate([reluct * c for c in comp], axis=1)
        rows = [jnp.sum(column * field, axis=0, keepdims=True) for column in columns]
        projected[elem] = jnp.concatenate(rows, axis=0) * (4.0 / SAMPLES)

    def add_outer(turn, carry):
        for slot in range(LISTED):
            listed, elem, link, side = entry(turn, slot)
            contrib = weighted(projected[elem], curl[elem, link])
            edge_sums[slot, side] += jnp.where(listed, contrib, 0.0)
        return carry

    turns = (count + LISTED - 1) // LISTED
    lax.fori_loop(0, turns, add_density, 0)
    for elem in range(tile_count):
        project(elem)
    lax.fori_loop(0, turns, add_outer, 0)
    total = edge_sums[0]
    for slot in range(1, LISTED):
        total = total + edge_sums[slot]
    halo[:, :tile] = total[0]
    halo[:, tile:] = total[1]


def sum_kernel(
    projected,
    curl,
    source,
    pattern_in,
    out,
    pattern,
    small_sem,
    *sums,
):
    tile_count, links, tile, comps = curl.shape
    small = pltpu.make_async_copy(pattern_in, pattern, small_sem)
    small.start()
    for total in sums:
        total[...] = jnp.zeros_like(total)
    small.wait()
    for elem in range(tile_count):
        contrib = weighted(projected[elem], curl[elem].reshape(links * tile, comps))
        for link in range(links):
            sums[link][pattern[link, elem]] += contrib[:, link * tile : (link + 1) * tile]
    for w in range(tile_count):
        at = slice(w * tile, (w + 1) * tile)
        total = sums[0][w + 1]
        for other in sums[1:]:
            total = total + other[w + 1]
        out[:, at] = total - source[:, at]


def halo_kernel(own, from_right, from_left, out):
    tile = from_left.shape[1] // 2
    out[...] = own[...]
    out[:, :tile] += from_left[:, tile:]
    out[:, -tile:] += from_right[:, :tile]


def per_device(coeffs, curl_tiles, pattern, region_ids, material_law, source):
    parts_here = coeffs.shape[0]
    tile_count, links, tile, comps = curl_tiles.shape
    group_size = lax.axis_size(GROUP)
    parts = parts_here * group_size
    table = half_table(parts)
    pieces = jnp.asarray(bf16_pieces(table))
    own_columns = jnp.asarray(
        table.reshape(HALF, group_size, parts_here).transpose(1, 0, 2).astype(np.float32)
    )
    vmem, hbm = pl.BlockSpec(memory_space=pltpu.VMEM), pl.BlockSpec(memory_space=pltpu.HBM)

    def in_vmem(array):
        return pltpu.with_memory_space_constraint(array, pltpu.VMEM)

    def in_hbm(array):
        return pltpu.with_memory_space_constraint(array, pltpu.HBM)

    flops = 2 * SAMPLES * tile_count * links * tile * comps
    limits = pltpu.CompilerParams(vmem_limit_bytes=32 * MIB)
    cost = pl.CostEstimate(flops=flops, bytes_accessed=2 * curl_tiles.size, transcendentals=0)
    pattern_words = pltpu.SMEM((links, tile_count), jnp.int32)
    kept = (region_ids, material_law, source)

    copies = jnp.broadcast_to(coeffs[None], (group_size,) + coeffs.shape)
    near = lax.all_to_all(copies, GROUP, 0, 0)
    right, left = from_neighbours(near, tile)
    densities, curl, pieces_here, columns_here, region_here, law_here, source_here, pattern_here = (
        pl.pallas_call(
            flux_kernel,
            out_shape=[
                pltpu.VMEM((tile_count, HALF, comps), jnp.float32),
                pltpu.VMEM(curl_tiles.shape, curl_tiles.dtype),
                pltpu.VMEM(pieces.shape, pieces.dtype),
                pltpu.VMEM(own_columns.shape[1:], jnp.float32),
                *[pltpu.VMEM(operand.shape, operand.dtype) for operand in kept],
                pltpu.VMEM((links, tile_count), jnp.int32),
            ],
            in_specs=[vmem] + [hbm] * 7,
            out_specs=[vmem] * 8,
            scratch_shapes=[
                pattern_words,
                pltpu.VMEM((SAMPLES, (tile_count + 2) * tile), jnp.bfloat16),
                pltpu.SemaphoreType.DMA((7,)),
                pltpu.SemaphoreType.DMA((pl.cdiv(tile_count, CHUNK),)),
            ],
            compiler_params=limits,
            cost_estimate=cost,
            name="shard_flux",
        )(
            in_vmem(near.reshape(parts, -1)),
            *[in_hbm(array) for array in (curl_tiles, pattern.T, pieces, own_columns, *kept)],
        )
    )
    projected, halo = pl.pallas_call(
        field_kernel,
        out_shape=(
            pltpu.VMEM((tile_count, parts_here, comps), jnp.float32),
            pltpu.VMEM((parts_here, 2 * tile), jnp.float32),
        ),
        in_specs=[vmem] * 9,
        out_specs=(vmem, vmem),
        scratch_shapes=[
            pattern_words,
            pltpu.SMEM(region_ids.shape, jnp.int32),
            pltpu.SMEM(material_law.shape, jnp.float32),
            pltpu.SMEM((links * tile_count + 1,), jnp.int32),
            pltpu.VMEM((2, SAMPLES, tile), jnp.bfloat16),
            pltpu.VMEM((tile_count, HALF, comps), jnp.float32),
            pltpu.VMEM((LISTED, 2, parts_here, tile), jnp.float32),
            pltpu.SemaphoreType.DMA((3,)),
        ],
        compiler_params=limits,
        cost_estimate=cost,
        name="shard_fields",
    )(
        *[
            in_vmem(array)
            for array in (
                densities,
                right.reshape(parts, tile),
                left.reshape(parts, tile),
                curl,
                pieces_here,
                columns_here,
                pattern_here,
                region_here,
                law_here,
            )
        ],
    )
    if lax.axis_size("space") == 2:
        beside = [shifted(halo, "space", 1)] * 2
    else:
        beside = [shifted(halo, "space", -1), shifted(halo, "space", 1)]
    own = pl.pallas_call(
        sum_kernel,
        out_shape=pltpu.VMEM(source.shape, jnp.float32),
        in_specs=[vmem] * 4,
        out_specs=vmem,
        scratch_shapes=[
            pattern_words,
            pltpu.SemaphoreType.DMA,
        ]
        + [pltpu.VMEM((tile_count + 2, parts_here, tile), jnp.float32)] * links,
        compiler_params=limits,
        cost_estimate=cost,
        name="shard_sums",
    )(*[in_vmem(array) for array in (projected, curl, source_here, pattern_here)])
    return pl.pallas_call(
        halo_kernel,
        out_shape=jax.ShapeDtypeStruct(source.shape, jnp.float32),
        in_specs=[vmem] * 3,
        out_specs=vmem,
        compiler_params=pltpu.CompilerParams(vmem_limit_bytes=16 * MIB),
        name="halo_sum",
    )(in_vmem(own), *beside)


def solution(mesh):
    placed = (
        P(GROUP, "space"),
        P("space", None, None, None),
        P("space", None),
        P("space"),
        P(),
        P(GROUP, "space"),
    )
    return jax.shard_map(
        per_device,
        mesh=mesh,
        in_specs=placed,
        out_specs=P(GROUP, "space"),
        check_vma=False,
    )
```

time: 26.8 us -> 27 us (level)
  starting transfers between devices: 4.84 us -> 2.18 us
  blocking collectives: 13.7 us -> 14.5 us
  local copies, waits for them, and re-layouts: 0.14 us -> 0.84 us
  waiting for transfers between devices: 0.09 us -> 0.71 us
  Pallas kernels: 7.94 us -> 8.43 us
    ppermute x2, starting transfers between devices: 4.84 us -> 2.18 us  [shifted(): lax.ppermute(array, axis, [(i, (i + by) % count) for i in range(count)])]
    pallas_call x1, Pallas kernels: 1.75 us -> 3.85 us  [per_device(): pl.pallas_call(flux_kernel, out_shape=[pltpu.VMEM((tile_count, HALF, comp...]
    pallas_call x1, Pallas kernels: 3.24 us -> 1.62 us  [per_device(): pl.pallas_call(field_kernel, out_shape=(pltpu.VMEM((tile_count, parts_her...]
    all_to_all x1, blocking collectives: 13.7 us -> 14.5 us  [per_device(): near = lax.all_to_all(copies, GROUP, 0, 0)]
    broadcast_in_dim x1, local copies, waits for them, and re-layouts: 0.08 us -> 0.77 us  [per_device(): copies = jnp.broadcast_to(coeffs[None], (group_size,) + coeffs.shape)]
    ppermute x2, waiting for transfers between devices: 0.09 us -> 0.71 us  [shifted(): lax.ppermute(array, axis, [(i, (i + by) % count) for i in range(count)])]
  transfers between devices with their start and end apart: 2 -> 2, of which waited for: 1 -> 1; matrix products, arithmetic and copies ran while one was open for 0% -> 0% of each run, Pallas kernels for 15% -> 23%
where the time goes in v21:
time: 27 us; the launch traced here: 26.8 us
  blocking collectives  14.5 us (54%)
  Pallas kernels  8.43 us (31%)
  starting transfers between devices  2.18 us (8%)
  local copies, waits for them, and re-layouts  0.84 us (3%)
  waiting for transfers between devices  0.71 us (3%)
    all_to_all x1, blocking collectives, per_device(): near = lax.all_to_all(copies, GROUP, 0, 0)  14.5 us
    pallas_call x1, Pallas kernels, per_device(): pl.pallas_call(flux_kernel, out_shape=[pltpu.VMEM((tile_count, HALF, comp...  3.85 us
    pallas_call x1, Pallas kernels, per_device(): pl.pallas_call(sum_kernel, out_shape=pltpu.VMEM(source.shape, jnp.float32...  2.34 us
    ppermute x2, starting transfers between devices, shifted(): lax.ppermute(array, axis, [(i, (i + by) % count) for i in range(count)])  2.18 us
    pallas_call x1, Pallas kernels, per_device(): pl.pallas_call(field_kernel, out_shape=(pltpu.VMEM((tile_count, parts_her...  1.62 us
    broadcast_in_dim x1, local copies, waits for them, and re-layouts, per_device(): copies = jnp.broadcast_to(coeffs[None], (group_size,) + coeffs.shape)  0.77 us
    ppermute x2, waiting for transfers between devices, shifted(): lax.ppermute(array, axis, [(i, (i + by) % count) for i in range(count)])  0.71 us
    pallas_call x1, Pallas kernels, per_device(): pl.pallas_call(halo_kernel, out_shape=jax.ShapeDtypeStruct(source.shape,...  0.61 us
  transfers between devices with their start and end apart: 2, of which 1 were waited for; matrix products, arithmetic and copies ran while one was open for 0% of the time, Pallas kernels for 23%

profile of v21, /device:TPU:0, one launch (start us, length us, event | category | flops | bytes accessed | tf_op | source)
XLA Modules:
  0.0 26.8 jit_solution(4872500263133256084)
XLA Ops:
  0.0 0.8 %broadcast_in_dim.2 = bf16[16,2,2048]{2,1,0:T(2,128)(2,1)S(1)} broadcast(bf16[2,2048]{1,0:T(2,128)(2,1)} %param.8), dimensions={1,2} | broadcast | bytes 139264 | tf_op jit(solution)/shard_map/broadcast_in_dim | solution.py:267
  0.8 14.5 %all_to_all.5 = bf16[16,2,2048]{2,1,0:T(2,128)(2,1)S(1)} all-to-all(bf16[16,2,2048]{2,1,0:T(2,128)(2,1)S(1)} %broadcast_in_dim.2), channel_id=1, replica_groups=mesh['harm'=4,'space'=2,'samp'=4] {'harm','samp'}, dimensions={0} | all-to-all | bytes 262144 | tf_op jit(solution)/shard_map/all_to_all | solution.py:268
  15.3 1.6 %collective-permute-start = (bf16[16,2,256]{2,1,0:T(2,128)(2,1)S(1)}, bf16[16,2,256]{2,1,0:T(2,128)(2,1)S(1)}, u32[]{:S(2)}, u32[]{:S(2)}) collective-permute-start(bf16[16,2,256]{2,1,0:T(2,128)(2,1)S(1)} %pad_maximum_fusion), channel_id=1, source_target_pairs={{0,4},{4,0},{1,5},{5,1},{2,6},{6,2},{3,7},{7,3},{8,12},{12,8},{9,1... | collective-permute-start | bytes 49160 | tf_op jit(solution)/shard_map/ppermute | solution.py:39
  16.9 0.1 reshape.10.window
  17.0 3.9 %shard_flux.1 = (f32[16,32,384]{2,1,0:T(8,128)S(1)}, bf16[16,4,128,384]{3,2,1,0:T(8,128)(2,1)S(1)}, bf16[32,96]{1,0:T(8,128)(2,1)S(1)}, f32[32,2]{1,0:T(8,128)S(...) custom-call(bf16[32,2048]{1,0:T(8,128)(2,1)S(1)} %reshape.10.window, ...), custom_call_target="tpu_custom_call" | custom-call | flops 402653184 | bytes 6291456 | tf_op jit(solution)/shard_map/shard_flux/pallas_call | solution.py:271
  20.8 0.0 collective-permute-done
  20.9 1.6 %shard_fields.1 = (f32[16,2,384]{2,1,0:T(2,128)S(1)}, f32[2,256]{1,0:T(2,128)S(1)}) custom-call(f32[16,32,384]{2,1,0:T(8,128)S(1)} %get-tuple-element.15.partial, bf16[32,128]{1,0:T(8,128)(2,1)S(1)} %bitcast.4, bf16[32,128]{1,0:T(8,128)(2,1)S(1)} %bitcast.3, bf16[16,4,128,384]{3,2,1,0:T(8,128)(2,1)S(1)} %get-tuple-element.16.curl, ...), custom_call_target="tpu_custom_call" | custom-call | flops 402653184 | bytes 6291456 | tf_op jit(solution)/shard_map/shard_fields/pallas_call | solution.py:297
  22.5 0.6 %collective-permute-start.1 = (f32[2,256]{1,0:T(2,128)S(1)}, f32[2,256]{1,0:T(2,128)S(1)}, u32[]{:S(2)}, u32[]{:S(2)}) collective-permute-start(f32[2,256]{1,0:T(2,128)S(1)} %get-tuple-element.24), channel_id=1, source_target_pairs={{0,4},{4,0},{1,5},{5,1},{2,6},{6,2},{3,7},{7,3},{8,12},{12,8},{9,1... | collective-permute-start | bytes 6152 | tf_op jit(solution)/shard_map/ppermute | solution.py:39
  23.1 2.3 %shard_sums.1.own = f32[2,2048]{1,0:T(2,128)S(1)} custom-call(f32[16,2,384]{2,1,0:T(2,128)S(1)} %get-tuple-element.22.projected, bf16[16,4,128,384]{3,2,1,0:T(8,128)(2,1)S(1)} %get-tuple-element.16.curl, f32[2,2048]{1,0:T(2,128)S(1)} %get-tuple-element.23.source, s32[4,16]{1,0:T(4,128)S(1)} %get-tuple-element.19.pattern_in), custom_call_target="tpu_custom_call" | custom-call | flops 402653184 | bytes 6291456 | tf_op jit(solution)/shard_map/shard_sums/pallas_call | solution.py:338
  25.4 0.7 %collective-permute-done.1.from_right.from_left = f32[2,256]{1,0:T(2,128)S(1)} collective-permute-done((f32[2,256]{1,0:T(2,128)S(1)}, f32[2,256]{1,0:T(2,128)S(1)}, u32[]{:S(2)}, u32[]{:S(2)}) %collective-permute-start.1) | collective-permute-done | bytes 2080 | tf_op jit(solution)/shard_map/ppermute | solution.py:39
  26.1 0.6 %halo_sum.1 = f32[2,2048]{1,0:T(2,128)} custom-call(f32[2,2048]{1,0:T(2,128)S(1)} %shard_sums.1.own, f32[2,256]{1,0:T(2,128)S(1)} %collective-permute-done.1.from_right.from_left, f32[2,256]{1,0:T(2,128)S(1)} %collective-permute-done.1.from_right.from_left), custom_call_target="tpu_custom_call" | custom-call | tf_op jit(solution)/shard_map/halo_sum/pallas_call | solution.py:352
  (3 shorter events, 0.0 us)
Async XLA Ops:
  15.3 5.5 %collective-permute-start = (bf16[16,2,256]{2,1,0:T(2,128)(2,1)S(1)}, bf16[16,2,256]{2,1,0:T(2,128)(2,1)S(1)}, u32[]{:S(2)}, u32[]{:S(2)}) collective-permute-start(bf16[16,2,256]{2,1,0:T(2,128)(2,1)S(1)} %pad_maximum_fusion), channel_id=1, source_target_pairs={{0,4},{4,0},{1,5},{5,1},{2,6},{6,2},{3,7},{7,3},{8,12},{12,8},{9,1... | collective-permute-start | bytes 49160 | tf_op jit(solution)/shard_map/ppermute | solution.py:39
  22.5 3.7 %collective-permute-start.1 = (f32[2,256]{1,0:T(2,128)S(1)}, f32[2,256]{1,0:T(2,128)S(1)}, u32[]{:S(2)}, u32[]{:S(2)}) collective-permute-start(f32[2,256]{1,0:T(2,128)S(1)} %get-tuple-element.24), channel_id=1, source_target_pairs={{0,4},{4,0},{1,5},{5,1},{2,6},{6,2},{3,7},{7,3},{8,12},{12,8},{9,1... | collective-permute-start | bytes 6152 | tf_op jit(solution)/shard_map/ppermute | solution.py:39

commit v22 on v18

--- a/solution.py
+++ b/solution.py
@@ -11,7 +11,7 @@
 
 SAMPLES = 64
 HALF = SAMPLES // 2
-GROUP = ("harm", "samp")
+GROUP = ("chip", "core", "samp")
 MIB = 1024 * 1024
 LISTED = 4
 CHUNK = 4
@@ -34,16 +34,21 @@
     return np.concatenate(pieces, axis=-1)
 
 
-def shifted(array, axis, by):
-    count = lax.axis_size(axis)
-    return lax.ppermute(array, axis, [(i, (i + by) % count) for i in range(count)])
+def across(array, core_step, space_step):
+    cores, shards = lax.axis_size("core"), lax.axis_size("space")
+    pairs = [
+        (c * shards + s, (c + core_step) % cores * shards + (s + space_step) % shards)
+        for c in range(cores)
+        for s in range(shards)
+    ]
+    return lax.ppermute(array, ("core", "space"), pairs)
 
 
 def from_neighbours(array, tile):
     if lax.axis_size("space") == 2:
-        other = shifted(array, "space", 1)
-        return other[:, :tile], other[:, -tile:]
-    return shifted(array[:, :tile], "space", -1), shifted(array[:, -tile:], "space", 1)
+        other = across(array, 1, 1)
+        return other[:, -tile:], other[:, :tile]
+    return across(array[:, -tile:], 1, 1), across(array[:, :tile], 1, -1)
 
 
 def fetch_kernel(*refs):
@@ -59,6 +64,14 @@
         copy.start()
     for copy in copies:
         copy.wait()
+
+
+def time_samples(pieces, rows):
+    stacked = jnp.concatenate([rows] * 3, axis=0)
+    samples = jnp.dot(pieces, stacked, preferred_element_type=jnp.float32)
+    high = samples.astype(jnp.bfloat16)
+    low = (samples - high.astype(jnp.float32)).astype(jnp.bfloat16)
+    return jnp.concatenate([high, low], axis=0)
 
 
 def weighted(projected, blocks):
@@ -110,11 +123,10 @@
     for copy in small + list(later.values()):
         copy.start()
     edge_sums[...] = jnp.zeros_like(edge_sums)
-    stacked = jnp.concatenate([window[...]] * 3, axis=0)
-    samples = jnp.dot(pieces[...], stacked, preferred_element_type=jnp.float32)
-    high = samples.astype(jnp.bfloat16)
-    timed[:HALF, :] = high
-    timed[HALF:, :] = (samples - high.astype(jnp.float32)).astype(jnp.bfloat16)
+    own, outer_tiles = pieces[0], pieces[1]
+    timed[:, tile:-tile] = time_samples(own, window[:, tile:-tile])
+    timed[:, :tile] = time_samples(outer_tiles, window[:, :tile])
+    timed[:, -tile:] = time_samples(outer_tiles, window[:, -tile:])
     columns = [
         jnp.broadcast_to(table[:, part : part + 1], (HALF, comps)) for part in range(parts_here)
     ]
@@ -223,10 +235,12 @@
 def per_device(coeffs, curl_tiles, pattern, region_ids, material_law, source):
     parts_here = coeffs.shape[0]
     tile_count, links, tile, comps = curl_tiles.shape
-    group_size = lax.axis_size(GROUP)
+    chips, cores, samp = (lax.axis_size(axis) for axis in GROUP)
+    group_size = chips * cores * samp
     parts = parts_here * group_size
     table = half_table(parts)
-    pieces = jnp.asarray(bf16_pieces(table))
+    before = np.roll(np.arange(parts).reshape(chips, cores, -1), 1, axis=1).reshape(-1)
+    pieces = jnp.asarray(np.stack([bf16_pieces(table), bf16_pieces(table[:, before])]))
     own_columns = jnp.asarray(
         table.reshape(HALF, group_size, parts_here).transpose(1, 0, 2).astype(np.float32)
     )
@@ -268,7 +282,7 @@
     first_curl, columns_here, coeffs_here, pieces_here, source_here, *others = fetched
     pattern_here = others[0]
 
-    right, left = from_neighbours(coeffs, tile)
+    left, right = from_neighbours(coeffs, tile)
     block = jnp.concatenate([left, coeffs_here, right], axis=1)
     copies = jnp.broadcast_to(block[None], (group_size,) + block.shape)
     window = lax.all_to_all(copies, GROUP, 0, 0).reshape(parts, block.shape[1])
@@ -306,9 +320,9 @@
         in_hbm(curl_tiles),
     )
     if lax.axis_size("space") == 2:
-        beside = [shifted(halo, "space", 1)] * 2
+        beside = [across(halo, 0, 1)] * 2
     else:
-        beside = [shifted(halo, "space", -1), shifted(halo, "space", 1)]
+        beside = [across(halo, 0, -1), across(halo, 0, 1)]
     own = pl.pallas_call(
         sum_kernel,
         out_shape=pltpu.VMEM(source.shape, jnp.float32),
@@ -340,6 +354,14 @@
 
 
 def solution(mesh):
+    at = mesh.axis_names.index("harm")
+    harm = mesh.shape["harm"]
+    cores = 2 if harm % 2 == 0 else 1
+    sizes = mesh.devices.shape
+    split = jax.sharding.Mesh(
+        mesh.devices.reshape(sizes[:at] + (harm // cores, cores) + sizes[at + 1 :]),
+        mesh.axis_names[:at] + ("chip", "core") + mesh.axis_names[at + 1 :],
+    )
     placed = (
         P(GROUP, "space"),
         P("space", None, None, None),
@@ -350,7 +372,7 @@
     )
     return jax.shard_map(
         per_device,
-        mesh=mesh,
+        mesh=split,
         in_specs=placed,
         out_specs=P(GROUP, "space"),
         check_vma=False,

time: 26 us -> 25.7 us (0.988)
  starting transfers between devices: 4.55 us -> 4.05 us
    ppermute x2, starting transfers between devices: 4.55 us -> 4.05 us  [across(): return lax.ppermute(array, ('core', 'space'), pairs)]
where the time goes in v22:
time: 25.7 us; the launch traced here: 25.4 us
  blocking collectives  13.5 us (53%)
  Pallas kernels  7.56 us (29%)
  starting transfers between devices  4.05 us (16%)
    all_to_all x1, blocking collectives, per_device(): window = lax.all_to_all(copies, GROUP, 0, 0).reshape(parts, block.shape[1])  13.5 us
    ppermute x2, starting transfers between devices, across(): return lax.ppermute(array, ('core', 'space'), pairs)  4.05 us
    pallas_call x1, Pallas kernels, per_device(): pl.pallas_call(field_kernel, out_shape=(pltpu.VMEM((tile_count, parts_her...  2.64 us
    pallas_call x1, Pallas kernels, per_device(): pl.pallas_call(sum_kernel, out_shape=pltpu.VMEM(source.shape, jnp.float32...  2.34 us
    pallas_call x1, Pallas kernels, per_device(): pl.pallas_call(fetch_kernel, out_shape=[pltpu.VMEM(shape, o.dtype) for sh...  1.97 us
    pallas_call x1, Pallas kernels, per_device(): pl.pallas_call(halo_kernel, out_shape=jax.ShapeDtypeStruct(source.shape,...  0.62 us
  transfers between devices with their start and end apart: 2, of which 0 were waited for; matrix products, arithmetic and copies ran while one was open for 0% of the time, Pallas kernels for 17%

profile of v22, /device:TPU:0, one launch (start us, length us, event | category | flops | bytes accessed | tf_op | source)
XLA Modules:
  0.0 25.4 jit_solution(1372683830264057370)
XLA Ops:
  0.0 2.4 %collective-permute-start = (bf16[2,2048]{1,0:T(2,128)(2,1)}, bf16[2,2048]{1,0:T(2,128)(2,1)S(1)}, u32[]{:S(2)}, u32[]{:S(2)}) collective-permute-start(bf16[2,2048]{1,0:T(2,128)(2,1)} %refs_2_.1), channel_id=1, source_target_pairs={{0,12},{4,8},{8,4},{12,0},{1,13},{5,9},{9,5},{13,1},{2,14},{6,10},... | collective-permute-start | bytes 24584 | tf_op jit(solution)/shard_map/ppermute | solution.py:44
  2.4 2.0 %fetch_operands.1 = (bf16[8,4,128,384]{3,2,1,0:T(8,128)(2,1)S(1)}, f32[32,2]{1,0:T(8,128)S(1)}, bf16[2,2048]{1,0:T(2,128)(2,1)S(1)}, bf16[2,32,96]{2,1,0:T(8,128...) custom-call(bf16[16,4,128,384]{3,2,1,0:T(8,128)(2,1)} %curl_hbm.1, ...), custom_call_target="tpu_custom_call" | custom-call | bytes 6291456 | tf_op jit(solution)/shard_map/fetch_operands/pallas_call | solution.py:270
  4.4 0.0 collective-permute-done
  4.4 0.1 broadcast_in_dim.2
  4.5 13.5 %all_to_all.5 = bf16[16,2,2304]{2,1,0:T(2,128)(2,1)S(1)} all-to-all(bf16[16,2,2304]{2,1,0:T(2,128)(2,1)S(1)} %broadcast_in_dim.2), channel_id=1, replica_groups=mesh['chip'=2,'core'=2,'space'=2,'samp'=4] {'chip','core','samp'}, dimensions={0} | all-to-all | bytes 294912 | tf_op jit(solution)/shard_map/all_to_all | solution.py:288
  18.1 0.1 reshape.4.window
  18.1 2.6 %shard_fields.1 = (f32[16,2,384]{2,1,0:T(2,128)S(1)}, f32[2,256]{1,0:T(2,128)S(1)}, bf16[8,4,128,384]{3,2,1,0:T(8,128)(2,1)S(1)}) custom-call(bf16[32,2304]{1,0:T(8,128)(2,1)S(1)} %reshape.4.window, bf16[8,4,128,384]{3,2,1,0:T(8,128)(2,1)S(1)} %get-tuple-element.17.first_curl, f32[32,2]{1,0:T(8,128)S(1)} %get-tuple-element.18.table, ...), custom_call_target="tpu_custom_call" | custom-call | flops 402653184 | bytes 6291456 | tf_op jit(solution)/shard_map/shard_fields/pallas_call | solution.py:290
  20.8 1.6 %collective-permute-start.1 = (f32[2,256]{1,0:T(2,128)S(1)}, f32[2,256]{1,0:T(2,128)S(1)}, u32[]{:S(2)}, u32[]{:S(2)}) collective-permute-start(f32[2,256]{1,0:T(2,128)S(1)} %get-tuple-element.26), channel_id=1, source_target_pairs={{0,4},{4,0},{8,12},{12,8},{1,5},{5,1},{9,13},{13,9},{2,6},{6,2},{1... | collective-permute-start | bytes 6152 | tf_op jit(solution)/shard_map/ppermute | solution.py:44
  22.4 2.3 %shard_sums.1.own = f32[2,2048]{1,0:T(2,128)S(1)} custom-call(f32[16,2,384]{2,1,0:T(2,128)S(1)} %get-tuple-element.23.projected, bf16[8,4,128,384]{3,2,1,0:T(8,128)(2,1)S(1)} %get-tuple-element.17.first_curl, bf16[8,4,128,384]{3,2,1,0:T(8,128)(2,1)S(1)} %get-tuple-element.24.later_curl, f32[2,2048]{1,0:T(2,128)S(1)} %get-tuple-element.25.source, ...), custom_call_target="tpu_custom_call" | custom-call | flops 402653184 | bytes 6291456 | tf_op jit(solution)/shard_map/shard_sums/pallas_call | solution.py:326
  24.8 0.0 collective-permute-done.1.from_right.from_left
  24.8 0.6 %halo_sum.1 = f32[2,2048]{1,0:T(2,128)} custom-call(f32[2,2048]{1,0:T(2,128)S(1)} %shard_sums.1.own, f32[2,256]{1,0:T(2,128)S(1)} %collective-permute-done.1.from_right.from_left, f32[2,256]{1,0:T(2,128)S(1)} %collective-permute-done.1.from_right.from_left), custom_call_target="tpu_custom_call" | custom-call | tf_op jit(solution)/shard_map/halo_sum/pallas_call | solution.py:346
  (2 shorter events, 0.0 us)
Async XLA Ops:
  0.0 4.4 %collective-permute-start = (bf16[2,2048]{1,0:T(2,128)(2,1)}, bf16[2,2048]{1,0:T(2,128)(2,1)S(1)}, u32[]{:S(2)}, u32[]{:S(2)}) collective-permute-start(bf16[2,2048]{1,0:T(2,128)(2,1)} %refs_2_.1), channel_id=1, source_target_pairs={{0,12},{4,8},{8,4},{12,0},{1,13},{5,9},{9,5},{13,1},{2,14},{6,10},... | collective-permute-start | bytes 24584 | tf_op jit(solution)/shard_map/ppermute | solution.py:44
  20.8 4.0 %collective-permute-start.1 = (f32[2,256]{1,0:T(2,128)S(1)}, f32[2,256]{1,0:T(2,128)S(1)}, u32[]{:S(2)}, u32[]{:S(2)}) collective-permute-start(f32[2,256]{1,0:T(2,128)S(1)} %get-tuple-element.26), channel_id=1, source_target_pairs={{0,4},{4,0},{8,12},{12,8},{1,5},{5,1},{9,13},{13,9},{2,6},{6,2},{1... | collective-permute-start | bytes 6152 | tf_op jit(solution)/shard_map/ppermute | solution.py:44

commit v23 on v22

--- a/solution.py
+++ b/solution.py
@@ -15,6 +15,7 @@
 MIB = 1024 * 1024
 LISTED = 4
 CHUNK = 4
+AHEAD = 3
 
 
 def half_table(parts):
@@ -173,7 +174,7 @@
     def add_outer(turn, carry):
         for slot in range(LISTED):
             spot = turn * LISTED + slot
-            code = jnp.where(spot < count, outer[jnp.minimum(spot, count - 1)], 0)
+            code = jnp.where(spot < count, outer[jnp.minimum(spot, jnp.maximum(count - 1, 0))], 0)
             elem, link = code // links, code % links
             block = jnp.where(
                 elem < early,
@@ -185,7 +186,8 @@
             edge_sums[slot, side] += jnp.where(spot < count, contrib, 0.0)
         return carry
 
-    lax.fori_loop(0, (count + LISTED - 1) // LISTED, add_outer, 0)
+    add_outer(0, 0)
+    lax.fori_loop(1, (count + LISTED - 1) // LISTED, add_outer, 0)
     total = edge_sums[0]
     for slot in range(1, LISTED):
         total = total + edge_sums[slot]
@@ -211,10 +213,15 @@
     small.start()
     for total in sums:
         total[...] = jnp.zeros_like(total)
+
+    def contribution(elem):
+        curl = first_curl[elem] if elem < early else later_curl[elem - early]
+        return weighted(projected[elem], curl.reshape(links * tile, comps))
+
+    ahead = [contribution(elem) for elem in range(AHEAD)]
     small.wait()
     for elem in range(tile_count):
-        curl = first_curl[elem] if elem < early else later_curl[elem - early]
-        contrib = weighted(projected[elem], curl.reshape(links * tile, comps))
+        contrib = ahead[elem] if elem < AHEAD else contribution(elem)
         for link in range(links):
             sums[link][pattern[link, elem]] += contrib[:, link * tile : (link + 1) * tile]
     for w in range(tile_count):

time: 25.7 us -> 25.2 us (0.981)
  Pallas kernels: 7.56 us -> 7.22 us
    pallas_call x1, Pallas kernels: 2.34 us -> 2.06 us  [per_device(): pl.pallas_call(sum_kernel, out_shape=pltpu.VMEM(source.shape, jnp.float32...]
  transfers between devices with their start and end apart: 2 -> 2, of which waited for: 0 -> 0; matrix products, arithmetic and copies ran while one was open for 0% -> 0% of each run, Pallas kernels for 17% -> 16%
where the time goes in v23:
time: 25.2 us; the launch traced here: 25 us
  blocking collectives  13.5 us (54%)
  Pallas kernels  7.22 us (29%)
  starting transfers between devices  4.04 us (16%)
    all_to_all x1, blocking collectives, per_device(): window = lax.all_to_all(copies, GROUP, 0, 0).reshape(parts, block.shape[1])  13.5 us
    ppermute x2, starting transfers between devices, across(): return lax.ppermute(array, ('core', 'space'), pairs)  4.04 us
    pallas_call x1, Pallas kernels, per_device(): pl.pallas_call(field_kernel, out_shape=(pltpu.VMEM((tile_count, parts_her...  2.58 us
    pallas_call x1, Pallas kernels, per_device(): pl.pallas_call(sum_kernel, out_shape=pltpu.VMEM(source.shape, jnp.float32...  2.06 us
    pallas_call x1, Pallas kernels, per_device(): pl.pallas_call(fetch_kernel, out_shape=[pltpu.VMEM(shape, o.dtype) for sh...  1.97 us
    pallas_call x1, Pallas kernels, per_device(): pl.pallas_call(halo_kernel, out_shape=jax.ShapeDtypeStruct(source.shape,...  0.62 us
  transfers between devices with their start and end apart: 2, of which 0 were waited for; matrix products, arithmetic and copies ran while one was open for 0% of the time, Pallas kernels for 16%

profile of v23, /device:TPU:0, one launch (start us, length us, event | category | flops | bytes accessed | tf_op | source)
XLA Modules:
  0.0 25.0 jit_solution(16167487275161286230)
XLA Ops:
  0.0 2.4 %collective-permute-start = (bf16[2,2048]{1,0:T(2,128)(2,1)}, bf16[2,2048]{1,0:T(2,128)(2,1)S(1)}, u32[]{:S(2)}, u32[]{:S(2)}) collective-permute-start(bf16[2,2048]{1,0:T(2,128)(2,1)} %refs_2_.1), channel_id=1, source_target_pairs={{0,12},{4,8},{8,4},{12,0},{1,13},{5,9},{9,5},{13,1},{2,14},{6,10},... | collective-permute-start | bytes 24584 | tf_op jit(solution)/shard_map/ppermute | solution.py:45
  2.4 2.0 %fetch_operands.1 = (bf16[8,4,128,384]{3,2,1,0:T(8,128)(2,1)S(1)}, f32[32,2]{1,0:T(8,128)S(1)}, bf16[2,2048]{1,0:T(2,128)(2,1)S(1)}, bf16[2,32,96]{2,1,0:T(8,128...) custom-call(bf16[16,4,128,384]{3,2,1,0:T(8,128)(2,1)} %curl_hbm.1, ...), custom_call_target="tpu_custom_call" | custom-call | bytes 6291456 | tf_op jit(solution)/shard_map/fetch_operands/pallas_call | solution.py:277
  4.4 0.0 collective-permute-done
  4.4 0.1 broadcast_in_dim.2
  4.5 13.5 %all_to_all.5 = bf16[16,2,2304]{2,1,0:T(2,128)(2,1)S(1)} all-to-all(bf16[16,2,2304]{2,1,0:T(2,128)(2,1)S(1)} %broadcast_in_dim.2), channel_id=1, replica_groups=mesh['chip'=2,'core'=2,'space'=2,'samp'=4] {'chip','core','samp'}, dimensions={0} | all-to-all | bytes 294912 | tf_op jit(solution)/shard_map/all_to_all | solution.py:295
  18.1 0.1 reshape.4.window
  18.1 2.6 %shard_fields.1 = (f32[16,2,384]{2,1,0:T(2,128)S(1)}, f32[2,256]{1,0:T(2,128)S(1)}, bf16[8,4,128,384]{3,2,1,0:T(8,128)(2,1)S(1)}) custom-call(bf16[32,2304]{1,0:T(8,128)(2,1)S(1)} %reshape.4.window, bf16[8,4,128,384]{3,2,1,0:T(8,128)(2,1)S(1)} %get-tuple-element.17.first_curl, f32[32,2]{1,0:T(8,128)S(1)} %get-tuple-element.18.table, ...), custom_call_target="tpu_custom_call" | custom-call | flops 402653184 | bytes 6291456 | tf_op jit(solution)/shard_map/shard_fields/pallas_call | solution.py:297
  20.7 1.6 %collective-permute-start.1 = (f32[2,256]{1,0:T(2,128)S(1)}, f32[2,256]{1,0:T(2,128)S(1)}, u32[]{:S(2)}, u32[]{:S(2)}) collective-permute-start(f32[2,256]{1,0:T(2,128)S(1)} %get-tuple-element.26), channel_id=1, source_target_pairs={{0,4},{4,0},{8,12},{12,8},{1,5},{5,1},{9,13},{13,9},{2,6},{6,2},{1... | collective-permute-start | bytes 6152 | tf_op jit(solution)/shard_map/ppermute | solution.py:45
  22.3 2.1 %shard_sums.1.own = f32[2,2048]{1,0:T(2,128)S(1)} custom-call(f32[16,2,384]{2,1,0:T(2,128)S(1)} %get-tuple-element.23.projected, bf16[8,4,128,384]{3,2,1,0:T(8,128)(2,1)S(1)} %get-tuple-element.17.first_curl, bf16[8,4,128,384]{3,2,1,0:T(8,128)(2,1)S(1)} %get-tuple-element.24.later_curl, f32[2,2048]{1,0:T(2,128)S(1)} %get-tuple-element.25.source, ...), custom_call_target="tpu_custom_call" | custom-call | flops 402653184 | bytes 6291456 | tf_op jit(solution)/shard_map/shard_sums/pallas_call | solution.py:333
  24.4 0.0 collective-permute-done.1.from_right.from_left
  24.4 0.6 %halo_sum.1 = f32[2,2048]{1,0:T(2,128)} custom-call(f32[2,2048]{1,0:T(2,128)S(1)} %shard_sums.1.own, f32[2,256]{1,0:T(2,128)S(1)} %collective-permute-done.1.from_right.from_left, f32[2,256]{1,0:T(2,128)S(1)} %collective-permute-done.1.from_right.from_left), custom_call_target="tpu_custom_call" | custom-call | tf_op jit(solution)/shard_map/halo_sum/pallas_call | solution.py:353
  (2 shorter events, 0.0 us)
Async XLA Ops:
  0.0 4.4 %collective-permute-start = (bf16[2,2048]{1,0:T(2,128)(2,1)}, bf16[2,2048]{1,0:T(2,128)(2,1)S(1)}, u32[]{:S(2)}, u32[]{:S(2)}) collective-permute-start(bf16[2,2048]{1,0:T(2,128)(2,1)} %refs_2_.1), channel_id=1, source_target_pairs={{0,12},{4,8},{8,4},{12,0},{1,13},{5,9},{9,5},{13,1},{2,14},{6,10},... | collective-permute-start | bytes 24584 | tf_op jit(solution)/shard_map/ppermute | solution.py:45
  20.7 3.7 %collective-permute-start.1 = (f32[2,256]{1,0:T(2,128)S(1)}, f32[2,256]{1,0:T(2,128)S(1)}, u32[]{:S(2)}, u32[]{:S(2)}) collective-permute-start(f32[2,256]{1,0:T(2,128)S(1)} %get-tuple-element.26), channel_id=1, source_target_pairs={{0,4},{4,0},{8,12},{12,8},{1,5},{5,1},{9,13},{13,9},{2,6},{6,2},{1... | collective-permute-start | bytes 6152 | tf_op jit(solution)/shard_map/ppermute | solution.py:45

commit v24 on v23

--- a/solution.py
+++ b/solution.py
@@ -246,8 +246,11 @@
     group_size = chips * cores * samp
     parts = parts_here * group_size
     table = half_table(parts)
-    before = np.roll(np.arange(parts).reshape(chips, cores, -1), 1, axis=1).reshape(-1)
-    pieces = jnp.asarray(np.stack([bf16_pieces(table), bf16_pieces(table[:, before])]))
+    by_rank = np.arange(parts).reshape(chips, cores, samp, parts_here)
+    orders = [
+        by_core.transpose(2, 0, 1, 3).reshape(-1) for by_core in (by_rank, np.roll(by_rank, 1, 1))
+    ]
+    pieces = jnp.asarray(np.stack([bf16_pieces(table[:, order]) for order in orders]))
     own_columns = jnp.asarray(
         table.reshape(HALF, group_size, parts_here).transpose(1, 0, 2).astype(np.float32)
     )
@@ -292,7 +295,7 @@
     left, right = from_neighbours(coeffs, tile)
     block = jnp.concatenate([left, coeffs_here, right], axis=1)
     copies = jnp.broadcast_to(block[None], (group_size,) + block.shape)
-    window = lax.all_to_all(copies, GROUP, 0, 0).reshape(parts, block.shape[1])
+    window = lax.all_to_all(copies, ("samp", "chip", "core"), 0, 0).reshape(parts, block.shape[1])
     pattern_words = pltpu.SMEM((links, tile_count), jnp.int32)
     projected, halo, later_curl = pl.pallas_call(
         field_kernel,

time: 25.2 us -> 26.1 us (1.036)
  blocking collectives: 13.5 us -> 14.3 us
  starting transfers between devices: 4.04 us -> 4.33 us
    all_to_all x1, blocking collectives: 13.5 us -> 14.3 us  [per_device(): lax.all_to_all(copies, ('samp', 'chip', 'core'), 0, 0)]
    ppermute x2, starting transfers between devices: 4.04 us -> 4.33 us  [across(): return lax.ppermute(array, ('core', 'space'), pairs)]
  transfers between devices with their start and end apart: 2 -> 2, of which waited for: 0 -> 0; matrix products, arithmetic and copies ran while one was open for 0% -> 0% of each run, Pallas kernels for 16% -> 15%
where the time goes in v24:
time: 26.1 us; the launch traced here: 26 us
  blocking collectives  14.3 us (55%)
  Pallas kernels  7.22 us (28%)
  starting transfers between devices  4.33 us (17%)
    all_to_all x1, blocking collectives, per_device(): lax.all_to_all(copies, ('samp', 'chip', 'core'), 0, 0)  14.3 us
    ppermute x2, starting transfers between devices, across(): return lax.ppermute(array, ('core', 'space'), pairs)  4.33 us
    pallas_call x1, Pallas kernels, per_device(): pl.pallas_call(field_kernel, out_shape=(pltpu.VMEM((tile_count, parts_her...  2.57 us
    pallas_call x1, Pallas kernels, per_device(): pl.pallas_call(sum_kernel, out_shape=pltpu.VMEM(source.shape, jnp.float32...  2.06 us
    pallas_call x1, Pallas kernels, per_device(): pl.pallas_call(fetch_kernel, out_shape=[pltpu.VMEM(shape, o.dtype) for sh...  1.97 us
    pallas_call x1, Pallas kernels, per_device(): pl.pallas_call(halo_kernel, out_shape=jax.ShapeDtypeStruct(source.shape,...  0.62 us
  transfers between devices with their start and end apart: 2, of which 0 were waited for; matrix products, arithmetic and copies ran while one was open for 0% of the time, Pallas kernels for 15%

profile of v24, /device:TPU:0, one launch (start us, length us, event | category | flops | bytes accessed | tf_op | source)
XLA Modules:
  0.0 26.0 jit_solution(8651646981130202297)
XLA Ops:
  0.0 2.4 %collective-permute-start = (bf16[2,2048]{1,0:T(2,128)(2,1)}, bf16[2,2048]{1,0:T(2,128)(2,1)S(1)}, u32[]{:S(2)}, u32[]{:S(2)}) collective-permute-start(bf16[2,2048]{1,0:T(2,128)(2,1)} %refs_2_.1), channel_id=1, source_target_pairs={{0,12},{4,8},{8,4},{12,0},{1,13},{5,9},{9,5},{13,1},{2,14},{6,10},... | collective-permute-start | bytes 24584 | tf_op jit(solution)/shard_map/ppermute | solution.py:45
  2.4 2.0 %fetch_operands.1 = (bf16[8,4,128,384]{3,2,1,0:T(8,128)(2,1)S(1)}, f32[32,2]{1,0:T(8,128)S(1)}, bf16[2,2048]{1,0:T(2,128)(2,1)S(1)}, bf16[2,32,96]{2,1,0:T(8,128...) custom-call(bf16[16,4,128,384]{3,2,1,0:T(8,128)(2,1)} %curl_hbm.1, ...), custom_call_target="tpu_custom_call" | custom-call | bytes 6291456 | tf_op jit(solution)/shard_map/fetch_operands/pallas_call | solution.py:280
  4.4 0.0 collective-permute-done
  4.4 0.1 broadcast_in_dim.2
  4.5 14.3 %all_to_all.5 = bf16[16,2,2304]{2,1,0:T(2,128)(2,1)S(1)} all-to-all(bf16[16,2,2304]{2,1,0:T(2,128)(2,1)S(1)} %broadcast_in_dim.2), channel_id=1, replica_groups=mesh['chip'=2,'core'=2,'space'=2,'samp'=4] {'samp','chip','core'}, dimensions={0} | all-to-all | bytes 294912 | tf_op jit(solution)/shard_map/all_to_all | solution.py:298
  18.8 0.1 reshape.4.window
  18.8 2.6 %shard_fields.1 = (f32[16,2,384]{2,1,0:T(2,128)S(1)}, f32[2,256]{1,0:T(2,128)S(1)}, bf16[8,4,128,384]{3,2,1,0:T(8,128)(2,1)S(1)}) custom-call(bf16[32,2304]{1,0:T(8,128)(2,1)S(1)} %reshape.4.window, bf16[8,4,128,384]{3,2,1,0:T(8,128)(2,1)S(1)} %get-tuple-element.17.first_curl, f32[32,2]{1,0:T(8,128)S(1)} %get-tuple-element.18.table, ...), custom_call_target="tpu_custom_call" | custom-call | flops 402653184 | bytes 6291456 | tf_op jit(solution)/shard_map/shard_fields/pallas_call | solution.py:300
  21.4 1.9 %collective-permute-start.1 = (f32[2,256]{1,0:T(2,128)S(1)}, f32[2,256]{1,0:T(2,128)S(1)}, u32[]{:S(2)}, u32[]{:S(2)}) collective-permute-start(f32[2,256]{1,0:T(2,128)S(1)} %get-tuple-element.26), channel_id=1, source_target_pairs={{0,4},{4,0},{8,12},{12,8},{1,5},{5,1},{9,13},{13,9},{2,6},{6,2},{1... | collective-permute-start | bytes 6152 | tf_op jit(solution)/shard_map/ppermute | solution.py:45
  23.3 2.1 %shard_sums.1.own = f32[2,2048]{1,0:T(2,128)S(1)} custom-call(f32[16,2,384]{2,1,0:T(2,128)S(1)} %get-tuple-element.23.projected, bf16[8,4,128,384]{3,2,1,0:T(8,128)(2,1)S(1)} %get-tuple-element.17.first_curl, bf16[8,4,128,384]{3,2,1,0:T(8,128)(2,1)S(1)} %get-tuple-element.24.later_curl, f32[2,2048]{1,0:T(2,128)S(1)} %get-tuple-element.25.source, ...), custom_call_target="tpu_custom_call" | custom-call | flops 402653184 | bytes 6291456 | tf_op jit(solution)/shard_map/shard_sums/pallas_call | solution.py:336
  25.4 0.0 collective-permute-done.1.from_right.from_left
  25.4 0.6 %halo_sum.1 = f32[2,2048]{1,0:T(2,128)} custom-call(f32[2,2048]{1,0:T(2,128)S(1)} %shard_sums.1.own, f32[2,256]{1,0:T(2,128)S(1)} %collective-permute-done.1.from_right.from_left, f32[2,256]{1,0:T(2,128)S(1)} %collective-permute-done.1.from_right.from_left), custom_call_target="tpu_custom_call" | custom-call | tf_op jit(solution)/shard_map/halo_sum/pallas_call | solution.py:356
  (2 shorter events, 0.0 us)
Async XLA Ops:
  0.0 4.4 %collective-permute-start = (bf16[2,2048]{1,0:T(2,128)(2,1)}, bf16[2,2048]{1,0:T(2,128)(2,1)S(1)}, u32[]{:S(2)}, u32[]{:S(2)}) collective-permute-start(bf16[2,2048]{1,0:T(2,128)(2,1)} %refs_2_.1), channel_id=1, source_target_pairs={{0,12},{4,8},{8,4},{12,0},{1,13},{5,9},{9,5},{13,1},{2,14},{6,10},... | collective-permute-start | bytes 24584 | tf_op jit(solution)/shard_map/ppermute | solution.py:45
  21.4 4.0 %collective-permute-start.1 = (f32[2,256]{1,0:T(2,128)S(1)}, f32[2,256]{1,0:T(2,128)S(1)}, u32[]{:S(2)}, u32[]{:S(2)}) collective-permute-start(f32[2,256]{1,0:T(2,128)S(1)} %get-tuple-element.26), channel_id=1, source_target_pairs={{0,4},{4,0},{8,12},{12,8},{1,5},{5,1},{9,13},{13,9},{2,6},{6,2},{1... | collective-permute-start | bytes 6152 | tf_op jit(solution)/shard_map/ppermute | solution.py:45

commit v25 on v24

--- a/solution.py
+++ b/solution.py
@@ -12,6 +12,7 @@
 SAMPLES = 64
 HALF = SAMPLES // 2
 GROUP = ("chip", "core", "samp")
+ARRIVAL = ("samp", "core", "chip")
 MIB = 1024 * 1024
 LISTED = 4
 CHUNK = 4
@@ -248,7 +249,8 @@
     table = half_table(parts)
     by_rank = np.arange(parts).reshape(chips, cores, samp, parts_here)
     orders = [
-        by_core.transpose(2, 0, 1, 3).reshape(-1) for by_core in (by_rank, np.roll(by_rank, 1, 1))
+        by_core.transpose([GROUP.index(axis) for axis in ARRIVAL] + [3]).reshape(-1)
+        for by_core in (by_rank, np.roll(by_rank, 1, 1))
     ]
     pieces = jnp.asarray(np.stack([bf16_pieces(table[:, order]) for order in orders]))
     own_columns = jnp.asarray(
@@ -295,7 +297,7 @@
     left, right = from_neighbours(coeffs, tile)
     block = jnp.concatenate([left, coeffs_here, right], axis=1)
     copies = jnp.broadcast_to(block[None], (group_size,) + block.shape)
-    window = lax.all_to_all(copies, ("samp", "chip", "core"), 0, 0).reshape(parts, block.shape[1])
+    window = lax.all_to_all(copies, ARRIVAL, 0, 0).reshape(parts, block.shape[1])
     pattern_words = pltpu.SMEM((links, tile_count), jnp.int32)
     projected, halo, later_curl = pl.pallas_call(
         field_kernel,

time: 26.1 us -> 25.5 us (0.977)
  blocking collectives: 14.3 us -> 13.7 us
  starting transfers between devices: 4.33 us -> 4.05 us
    all_to_all x1, blocking collectives: 14.3 us -> 13.7 us  [per_device(): lax.all_to_all(copies, ARRIVAL, 0, 0).reshape(parts, block.shape[1])]
    ppermute x2, starting transfers between devices: 4.33 us -> 4.05 us  [across(): return lax.ppermute(array, ('core', 'space'), pairs)]
  transfers between devices with their start and end apart: 2 -> 2, of which waited for: 0 -> 0; matrix products, arithmetic and copies ran while one was open for 0% -> 0% of each run, Pallas kernels for 15% -> 16%
where the time goes in v25:
time: 25.5 us; the launch traced here: 25.2 us
  blocking collectives  13.7 us (54%)
  Pallas kernels  7.22 us (28%)
  starting transfers between devices  4.05 us (16%)
    all_to_all x1, blocking collectives, per_device(): lax.all_to_all(copies, ARRIVAL, 0, 0).reshape(parts, block.shape[1])  13.7 us
    ppermute x2, starting transfers between devices, across(): return lax.ppermute(array, ('core', 'space'), pairs)  4.05 us
    pallas_call x1, Pallas kernels, per_device(): pl.pallas_call(field_kernel, out_shape=(pltpu.VMEM((tile_count, parts_her...  2.57 us
    pallas_call x1, Pallas kernels, per_device(): pl.pallas_call(sum_kernel, out_shape=pltpu.VMEM(source.shape, jnp.float32...  2.06 us
    pallas_call x1, Pallas kernels, per_device(): pl.pallas_call(fetch_kernel, out_shape=[pltpu.VMEM(shape, o.dtype) for sh...  1.97 us
    pallas_call x1, Pallas kernels, per_device(): pl.pallas_call(halo_kernel, out_shape=jax.ShapeDtypeStruct(source.shape,...  0.62 us
  transfers between devices with their start and end apart: 2, of which 0 were waited for; matrix products, arithmetic and copies ran while one was open for 0% of the time, Pallas kernels for 16%

profile of v25, /device:TPU:0, one launch (start us, length us, event | category | flops | bytes accessed | tf_op | source)
XLA Modules:
  0.0 25.2 jit_solution(12536040891342249062)
XLA Ops:
  0.0 2.4 %collective-permute-start = (bf16[2,2048]{1,0:T(2,128)(2,1)}, bf16[2,2048]{1,0:T(2,128)(2,1)S(1)}, u32[]{:S(2)}, u32[]{:S(2)}) collective-permute-start(bf16[2,2048]{1,0:T(2,128)(2,1)} %refs_2_.1), channel_id=1, source_target_pairs={{0,12},{4,8},{8,4},{12,0},{1,13},{5,9},{9,5},{13,1},{2,14},{6,10},... | collective-permute-start | bytes 24584 | tf_op jit(solution)/shard_map/ppermute | solution.py:46
  2.4 2.0 %fetch_operands.1 = (bf16[8,4,128,384]{3,2,1,0:T(8,128)(2,1)S(1)}, f32[32,2]{1,0:T(8,128)S(1)}, bf16[2,2048]{1,0:T(2,128)(2,1)S(1)}, bf16[2,32,96]{2,1,0:T(8,128...) custom-call(bf16[16,4,128,384]{3,2,1,0:T(8,128)(2,1)} %curl_hbm.1, ...), custom_call_target="tpu_custom_call" | custom-call | bytes 6291456 | tf_op jit(solution)/shard_map/fetch_operands/pallas_call | solution.py:282
  4.4 0.0 collective-permute-done
  4.4 0.1 broadcast_in_dim.2
  4.5 13.7 %all_to_all.5 = bf16[16,2,2304]{2,1,0:T(2,128)(2,1)S(1)} all-to-all(bf16[16,2,2304]{2,1,0:T(2,128)(2,1)S(1)} %broadcast_in_dim.2), channel_id=1, replica_groups=mesh['chip'=2,'core'=2,'space'=2,'samp'=4] {'samp','core','chip'}, dimensions={0} | all-to-all | bytes 294912 | tf_op jit(solution)/shard_map/all_to_all | solution.py:300
  18.3 0.1 reshape.4.window
  18.3 2.6 %shard_fields.1 = (f32[16,2,384]{2,1,0:T(2,128)S(1)}, f32[2,256]{1,0:T(2,128)S(1)}, bf16[8,4,128,384]{3,2,1,0:T(8,128)(2,1)S(1)}) custom-call(bf16[32,2304]{1,0:T(8,128)(2,1)S(1)} %reshape.4.window, bf16[8,4,128,384]{3,2,1,0:T(8,128)(2,1)S(1)} %get-tuple-element.17.first_curl, f32[32,2]{1,0:T(8,128)S(1)} %get-tuple-element.18.table, ...), custom_call_target="tpu_custom_call" | custom-call | flops 402653184 | bytes 6291456 | tf_op jit(solution)/shard_map/shard_fields/pallas_call | solution.py:302
  20.9 1.6 %collective-permute-start.1 = (f32[2,256]{1,0:T(2,128)S(1)}, f32[2,256]{1,0:T(2,128)S(1)}, u32[]{:S(2)}, u32[]{:S(2)}) collective-permute-start(f32[2,256]{1,0:T(2,128)S(1)} %get-tuple-element.26), channel_id=1, source_target_pairs={{0,4},{4,0},{8,12},{12,8},{1,5},{5,1},{9,13},{13,9},{2,6},{6,2},{1... | collective-permute-start | bytes 6152 | tf_op jit(solution)/shard_map/ppermute | solution.py:46
  22.5 2.1 %shard_sums.1.own = f32[2,2048]{1,0:T(2,128)S(1)} custom-call(f32[16,2,384]{2,1,0:T(2,128)S(1)} %get-tuple-element.23.projected, bf16[8,4,128,384]{3,2,1,0:T(8,128)(2,1)S(1)} %get-tuple-element.17.first_curl, bf16[8,4,128,384]{3,2,1,0:T(8,128)(2,1)S(1)} %get-tuple-element.24.later_curl, f32[2,2048]{1,0:T(2,128)S(1)} %get-tuple-element.25.source, ...), custom_call_target="tpu_custom_call" | custom-call | flops 402653184 | bytes 6291456 | tf_op jit(solution)/shard_map/shard_sums/pallas_call | solution.py:338
  24.6 0.0 collective-permute-done.1.from_right.from_left
  24.6 0.6 %halo_sum.1 = f32[2,2048]{1,0:T(2,128)} custom-call(f32[2,2048]{1,0:T(2,128)S(1)} %shard_sums.1.own, f32[2,256]{1,0:T(2,128)S(1)} %collective-permute-done.1.from_right.from_left, f32[2,256]{1,0:T(2,128)S(1)} %collective-permute-done.1.from_right.from_left), custom_call_target="tpu_custom_call" | custom-call | tf_op jit(solution)/shard_map/halo_sum/pallas_call | solution.py:358
  (2 shorter events, 0.0 us)
Async XLA Ops:
  0.0 4.4 %collective-permute-start = (bf16[2,2048]{1,0:T(2,128)(2,1)}, bf16[2,2048]{1,0:T(2,128)(2,1)S(1)}, u32[]{:S(2)}, u32[]{:S(2)}) collective-permute-start(bf16[2,2048]{1,0:T(2,128)(2,1)} %refs_2_.1), channel_id=1, source_target_pairs={{0,12},{4,8},{8,4},{12,0},{1,13},{5,9},{9,5},{13,1},{2,14},{6,10},... | collective-permute-start | bytes 24584 | tf_op jit(solution)/shard_map/ppermute | solution.py:46
  20.9 3.7 %collective-permute-start.1 = (f32[2,256]{1,0:T(2,128)S(1)}, f32[2,256]{1,0:T(2,128)S(1)}, u32[]{:S(2)}, u32[]{:S(2)}) collective-permute-start(f32[2,256]{1,0:T(2,128)S(1)} %get-tuple-element.26), channel_id=1, source_target_pairs={{0,4},{4,0},{8,12},{12,8},{1,5},{5,1},{9,13},{13,9},{2,6},{6,2},{1... | collective-permute-start | bytes 6152 | tf_op jit(solution)/shard_map/ppermute | solution.py:46

commit v26 on v23

--- a/solution.py
+++ b/solution.py
@@ -55,8 +55,12 @@
 def fetch_kernel(*refs):
     count = (len(refs) - 1) // 2
     sources, targets, sems = refs[:count], refs[count : 2 * count], refs[-1]
-    rank = lax.axis_index(GROUP)
-    sources = (sources[0].at[: targets[0].shape[0]], sources[1].at[rank]) + sources[2:]
+    early = targets[0].shape[0]
+    sources = [sources[0].at[i] for i in range(early)] + [
+        sources[1].at[lax.axis_index(GROUP)],
+        *sources[2:],
+    ]
+    targets = [targets[0].at[i] for i in range(early)] + list(targets[1:])
     copies = [
         pltpu.make_async_copy(source, target, sems.at[i])
         for i, (source, target) in enumerate(zip(sources, targets))
@@ -115,11 +119,9 @@
     ]
     later = {
         elem: pltpu.make_async_copy(
-            curl_hbm.at[elem : min(elem + CHUNK, tile_count)],
-            later_curl.at[elem - early : min(elem + CHUNK, tile_count) - early],
-            curl_sems.at[(elem - early) // CHUNK],
+            curl_hbm.at[elem], later_curl.at[elem - early], curl_sems.at[elem - early]
         )
-        for elem in range(early, tile_count, CHUNK)
+        for elem in range(early, tile_count)
     }
     for copy in small + list(later.values()):
         copy.start()
@@ -165,8 +167,9 @@
 
     for turn in range(tile_count + 1):
         if turn < tile_count:
-            if turn in later:
-                later[turn].wait()
+            if turn >= early and (turn - early) % CHUNK == 0:
+                for elem in range(turn, min(turn + CHUNK, tile_count)):
+                    later[elem].wait()
             find_density(turn)
         if turn:
             project(turn - 1)
@@ -279,7 +282,7 @@
         out_shape=[pltpu.VMEM(shape, o.dtype) for shape, o in zip(shapes, operands)],
         in_specs=[hbm] * len(operands),
         out_specs=[vmem] * len(operands),
-        scratch_shapes=[pltpu.SemaphoreType.DMA((len(operands),))],
+        scratch_shapes=[pltpu.SemaphoreType.DMA((early + len(operands) - 1,))],
         compiler_params=pltpu.CompilerParams(vmem_limit_bytes=16 * MIB),
         cost_estimate=pl.CostEstimate(
             flops=0, bytes_accessed=4 * early * links * tile * comps, transcendentals=0
@@ -312,7 +315,7 @@
             pltpu.VMEM((tile_count, HALF, comps), jnp.float32),
             pltpu.VMEM((LISTED, 2, parts_here, tile), jnp.float32),
             pltpu.SemaphoreType.DMA((3,)),
-            pltpu.SemaphoreType.DMA((pl.cdiv(tile_count - early, CHUNK),)),
+            pltpu.SemaphoreType.DMA((tile_count - early,)),
         ],
         compiler_params=pltpu.CompilerParams(vmem_limit_bytes=32 * MIB),
         cost_estimate=pl.CostEstimate(

time: 25.2 us -> 25.3 us (level)
  starting transfers between devices: 4.04 us -> 4.32 us
    ppermute x2, starting transfers between devices: 4.04 us -> 4.32 us  [across(): return lax.ppermute(array, ('core', 'space'), pairs)]
where the time goes in v26:
time: 25.3 us
  blocking collectives  13.5 us (53%)
  Pallas kernels  7.21 us (28%)
  starting transfers between devices  4.32 us (17%)
    all_to_all x1, blocking collectives, per_device(): window = lax.all_to_all(copies, GROUP, 0, 0).reshape(parts, block.shape[1])  13.5 us
    ppermute x2, starting transfers between devices, across(): return lax.ppermute(array, ('core', 'space'), pairs)  4.32 us
    pallas_call x1, Pallas kernels, per_device(): pl.pallas_call(field_kernel, out_shape=(pltpu.VMEM((tile_count, parts_her...  2.57 us
    pallas_call x1, Pallas kernels, per_device(): pl.pallas_call(sum_kernel, out_shape=pltpu.VMEM(source.shape, jnp.float32...  2.06 us
    pallas_call x1, Pallas kernels, per_device(): pl.pallas_call(fetch_kernel, out_shape=[pltpu.VMEM(shape, o.dtype) for sh...  1.97 us
    pallas_call x1, Pallas kernels, per_device(): pl.pallas_call(halo_kernel, out_shape=jax.ShapeDtypeStruct(source.shape,...  0.62 us
  transfers between devices with their start and end apart: 2, of which 0 were waited for; matrix products, arithmetic and copies ran while one was open for 0% of the time, Pallas kernels for 16%

profile of v26, /device:TPU:0, one launch (start us, length us, event | category | flops | bytes accessed | tf_op | source)
XLA Modules:
  0.0 25.3 jit_solution(1092310095444244463)
XLA Ops:
  0.0 2.4 %collective-permute-start = (bf16[2,2048]{1,0:T(2,128)(2,1)}, bf16[2,2048]{1,0:T(2,128)(2,1)S(1)}, u32[]{:S(2)}, u32[]{:S(2)}) collective-permute-start(bf16[2,2048]{1,0:T(2,128)(2,1)} %refs_2_.1), channel_id=1, source_target_pairs={{0,12},{4,8},{8,4},{12,0},{1,13},{5,9},{9,5},{13,1},{2,14},{6,10},... | collective-permute-start | bytes 24584 | tf_op jit(solution)/shard_map/ppermute | solution.py:45
  2.4 2.0 %fetch_operands.1 = (bf16[8,4,128,384]{3,2,1,0:T(8,128)(2,1)S(1)}, f32[32,2]{1,0:T(8,128)S(1)}, bf16[2,2048]{1,0:T(2,128)(2,1)S(1)}, bf16[2,32,96]{2,1,0:T(8,128...) custom-call(bf16[16,4,128,384]{3,2,1,0:T(8,128)(2,1)} %curl_hbm.1, ...), custom_call_target="tpu_custom_call" | custom-call | bytes 6291456 | tf_op jit(solution)/shard_map/fetch_operands/pallas_call | solution.py:280
  4.4 0.0 collective-permute-done
  4.4 0.1 broadcast_in_dim.2
  4.5 13.5 %all_to_all.5 = bf16[16,2,2304]{2,1,0:T(2,128)(2,1)S(1)} all-to-all(bf16[16,2,2304]{2,1,0:T(2,128)(2,1)S(1)} %broadcast_in_dim.2), channel_id=1, replica_groups=mesh['chip'=2,'core'=2,'space'=2,'samp'=4] {'chip','core','samp'}, dimensions={0} | all-to-all | bytes 294912 | tf_op jit(solution)/shard_map/all_to_all | solution.py:298
  18.1 0.1 reshape.4.window
  18.1 2.6 %shard_fields.1 = (f32[16,2,384]{2,1,0:T(2,128)S(1)}, f32[2,256]{1,0:T(2,128)S(1)}, bf16[8,4,128,384]{3,2,1,0:T(8,128)(2,1)S(1)}) custom-call(bf16[32,2304]{1,0:T(8,128)(2,1)S(1)} %reshape.4.window, bf16[8,4,128,384]{3,2,1,0:T(8,128)(2,1)S(1)} %get-tuple-element.17.first_curl, f32[32,2]{1,0:T(8,128)S(1)} %get-tuple-element.18.table, ...), custom_call_target="tpu_custom_call" | custom-call | flops 402653184 | bytes 6291456 | tf_op jit(solution)/shard_map/shard_fields/pallas_call | solution.py:300
  20.7 1.9 %collective-permute-start.1 = (f32[2,256]{1,0:T(2,128)S(1)}, f32[2,256]{1,0:T(2,128)S(1)}, u32[]{:S(2)}, u32[]{:S(2)}) collective-permute-start(f32[2,256]{1,0:T(2,128)S(1)} %get-tuple-element.26), channel_id=1, source_target_pairs={{0,4},{4,0},{8,12},{12,8},{1,5},{5,1},{9,13},{13,9},{2,6},{6,2},{1... | collective-permute-start | bytes 6152 | tf_op jit(solution)/shard_map/ppermute | solution.py:45
  22.6 2.1 %shard_sums.1.own = f32[2,2048]{1,0:T(2,128)S(1)} custom-call(f32[16,2,384]{2,1,0:T(2,128)S(1)} %get-tuple-element.23.projected, bf16[8,4,128,384]{3,2,1,0:T(8,128)(2,1)S(1)} %get-tuple-element.17.first_curl, bf16[8,4,128,384]{3,2,1,0:T(8,128)(2,1)S(1)} %get-tuple-element.24.later_curl, f32[2,2048]{1,0:T(2,128)S(1)} %get-tuple-element.25.source, ...), custom_call_target="tpu_custom_call" | custom-call | flops 402653184 | bytes 6291456 | tf_op jit(solution)/shard_map/shard_sums/pallas_call | solution.py:336
  24.7 0.0 collective-permute-done.1.from_right.from_left
  24.7 0.6 %halo_sum.1 = f32[2,2048]{1,0:T(2,128)} custom-call(f32[2,2048]{1,0:T(2,128)S(1)} %shard_sums.1.own, f32[2,256]{1,0:T(2,128)S(1)} %collective-permute-done.1.from_right.from_left, f32[2,256]{1,0:T(2,128)S(1)} %collective-permute-done.1.from_right.from_left), custom_call_target="tpu_custom_call" | custom-call | tf_op jit(solution)/shard_map/halo_sum/pallas_call | solution.py:356
  (2 shorter events, 0.0 us)
Async XLA Ops:
  0.0 4.4 %collective-permute-start = (bf16[2,2048]{1,0:T(2,128)(2,1)}, bf16[2,2048]{1,0:T(2,128)(2,1)S(1)}, u32[]{:S(2)}, u32[]{:S(2)}) collective-permute-start(bf16[2,2048]{1,0:T(2,128)(2,1)} %refs_2_.1), channel_id=1, source_target_pairs={{0,12},{4,8},{8,4},{12,0},{1,13},{5,9},{9,5},{13,1},{2,14},{6,10},... | collective-permute-start | bytes 24584 | tf_op jit(solution)/shard_map/ppermute | solution.py:45
  20.7 4.0 %collective-permute-start.1 = (f32[2,256]{1,0:T(2,128)S(1)}, f32[2,256]{1,0:T(2,128)S(1)}, u32[]{:S(2)}, u32[]{:S(2)}) collective-permute-start(f32[2,256]{1,0:T(2,128)S(1)} %get-tuple-element.26), channel_id=1, source_target_pairs={{0,4},{4,0},{8,12},{12,8},{1,5},{5,1},{9,13},{13,9},{2,6},{6,2},{1... | collective-permute-start | bytes 6152 | tf_op jit(solution)/shard_map/ppermute | solution.py:45

commit v27 on v25

--- a/solution.py
+++ b/solution.py
@@ -12,7 +12,7 @@
 SAMPLES = 64
 HALF = SAMPLES // 2
 GROUP = ("chip", "core", "samp")
-ARRIVAL = ("samp", "core", "chip")
+ARRIVAL = ("core", "chip", "samp")
 MIB = 1024 * 1024
 LISTED = 4
 CHUNK = 4

time: 25.5 us -> 25.5 us (level)
  no operation moved by 1% of the time
where the time goes in v27:
time: 25.5 us; the launch traced here: 25.4 us
  blocking collectives  13.9 us (55%)
  Pallas kernels  7.23 us (28%)
  starting transfers between devices  4.04 us (16%)
    all_to_all x1, blocking collectives, per_device(): lax.all_to_all(copies, ARRIVAL, 0, 0).reshape(parts, block.shape[1])  13.9 us
    ppermute x2, starting transfers between devices, across(): return lax.ppermute(array, ('core', 'space'), pairs)  4.04 us
    pallas_call x1, Pallas kernels, per_device(): pl.pallas_call(field_kernel, out_shape=(pltpu.VMEM((tile_count, parts_her...  2.58 us
    pallas_call x1, Pallas kernels, per_device(): pl.pallas_call(sum_kernel, out_shape=pltpu.VMEM(source.shape, jnp.float32...  2.06 us
    pallas_call x1, Pallas kernels, per_device(): pl.pallas_call(fetch_kernel, out_shape=[pltpu.VMEM(shape, o.dtype) for sh...  1.97 us
    pallas_call x1, Pallas kernels, per_device(): pl.pallas_call(halo_kernel, out_shape=jax.ShapeDtypeStruct(source.shape,...  0.62 us
  transfers between devices with their start and end apart: 2, of which 0 were waited for; matrix products, arithmetic and copies ran while one was open for 0% of the time, Pallas kernels for 16%

profile of v27, /device:TPU:0, one launch (start us, length us, event | category | flops | bytes accessed | tf_op | source)
XLA Modules:
  0.0 25.4 jit_solution(11855537381585954900)
XLA Ops:
  0.0 2.4 %collective-permute-start = (bf16[2,2048]{1,0:T(2,128)(2,1)}, bf16[2,2048]{1,0:T(2,128)(2,1)S(1)}, u32[]{:S(2)}, u32[]{:S(2)}) collective-permute-start(bf16[2,2048]{1,0:T(2,128)(2,1)} %refs_2_.1), channel_id=1, source_target_pairs={{0,12},{4,8},{8,4},{12,0},{1,13},{5,9},{9,5},{13,1},{2,14},{6,10},... | collective-permute-start | bytes 24584 | tf_op jit(solution)/shard_map/ppermute | solution.py:46
  2.4 2.0 %fetch_operands.1 = (bf16[8,4,128,384]{3,2,1,0:T(8,128)(2,1)S(1)}, f32[32,2]{1,0:T(8,128)S(1)}, bf16[2,2048]{1,0:T(2,128)(2,1)S(1)}, bf16[2,32,96]{2,1,0:T(8,128...) custom-call(bf16[16,4,128,384]{3,2,1,0:T(8,128)(2,1)} %curl_hbm.1, ...), custom_call_target="tpu_custom_call" | custom-call | bytes 6291456 | tf_op jit(solution)/shard_map/fetch_operands/pallas_call | solution.py:282
  4.4 0.0 collective-permute-done
  4.4 0.1 broadcast_in_dim.2
  4.5 13.9 %all_to_all.5 = bf16[16,2,2304]{2,1,0:T(2,128)(2,1)S(1)} all-to-all(bf16[16,2,2304]{2,1,0:T(2,128)(2,1)S(1)} %broadcast_in_dim.2), channel_id=1, replica_groups=mesh['chip'=2,'core'=2,'space'=2,'samp'=4] {'core','chip','samp'}, dimensions={0} | all-to-all | bytes 294912 | tf_op jit(solution)/shard_map/all_to_all | solution.py:300
  18.4 0.1 reshape.4.window
  18.4 2.6 %shard_fields.1 = (f32[16,2,384]{2,1,0:T(2,128)S(1)}, f32[2,256]{1,0:T(2,128)S(1)}, bf16[8,4,128,384]{3,2,1,0:T(8,128)(2,1)S(1)}) custom-call(bf16[32,2304]{1,0:T(8,128)(2,1)S(1)} %reshape.4.window, bf16[8,4,128,384]{3,2,1,0:T(8,128)(2,1)S(1)} %get-tuple-element.17.first_curl, f32[32,2]{1,0:T(8,128)S(1)} %get-tuple-element.18.table, ...), custom_call_target="tpu_custom_call" | custom-call | flops 402653184 | bytes 6291456 | tf_op jit(solution)/shard_map/shard_fields/pallas_call | solution.py:302
  21.0 1.6 %collective-permute-start.1 = (f32[2,256]{1,0:T(2,128)S(1)}, f32[2,256]{1,0:T(2,128)S(1)}, u32[]{:S(2)}, u32[]{:S(2)}) collective-permute-start(f32[2,256]{1,0:T(2,128)S(1)} %get-tuple-element.26), channel_id=1, source_target_pairs={{0,4},{4,0},{8,12},{12,8},{1,5},{5,1},{9,13},{13,9},{2,6},{6,2},{1... | collective-permute-start | bytes 6152 | tf_op jit(solution)/shard_map/ppermute | solution.py:46
  22.7 2.1 %shard_sums.1.own = f32[2,2048]{1,0:T(2,128)S(1)} custom-call(f32[16,2,384]{2,1,0:T(2,128)S(1)} %get-tuple-element.23.projected, bf16[8,4,128,384]{3,2,1,0:T(8,128)(2,1)S(1)} %get-tuple-element.17.first_curl, bf16[8,4,128,384]{3,2,1,0:T(8,128)(2,1)S(1)} %get-tuple-element.24.later_curl, f32[2,2048]{1,0:T(2,128)S(1)} %get-tuple-element.25.source, ...), custom_call_target="tpu_custom_call" | custom-call | flops 402653184 | bytes 6291456 | tf_op jit(solution)/shard_map/shard_sums/pallas_call | solution.py:338
  24.7 0.0 collective-permute-done.1.from_right.from_left
  24.7 0.6 %halo_sum.1 = f32[2,2048]{1,0:T(2,128)} custom-call(f32[2,2048]{1,0:T(2,128)S(1)} %shard_sums.1.own, f32[2,256]{1,0:T(2,128)S(1)} %collective-permute-done.1.from_right.from_left, f32[2,256]{1,0:T(2,128)S(1)} %collective-permute-done.1.from_right.from_left), custom_call_target="tpu_custom_call" | custom-call | tf_op jit(solution)/shard_map/halo_sum/pallas_call | solution.py:358
  (2 shorter events, 0.0 us)
Async XLA Ops:
  0.0 4.4 %collective-permute-start = (bf16[2,2048]{1,0:T(2,128)(2,1)}, bf16[2,2048]{1,0:T(2,128)(2,1)S(1)}, u32[]{:S(2)}, u32[]{:S(2)}) collective-permute-start(bf16[2,2048]{1,0:T(2,128)(2,1)} %refs_2_.1), channel_id=1, source_target_pairs={{0,12},{4,8},{8,4},{12,0},{1,13},{5,9},{9,5},{13,1},{2,14},{6,10},... | collective-permute-start | bytes 24584 | tf_op jit(solution)/shard_map/ppermute | solution.py:46
  21.0 3.7 %collective-permute-start.1 = (f32[2,256]{1,0:T(2,128)S(1)}, f32[2,256]{1,0:T(2,128)S(1)}, u32[]{:S(2)}, u32[]{:S(2)}) collective-permute-start(f32[2,256]{1,0:T(2,128)S(1)} %get-tuple-element.26), channel_id=1, source_target_pairs={{0,4},{4,0},{8,12},{12,8},{1,5},{5,1},{9,13},{13,9},{2,6},{6,2},{1... | collective-permute-start | bytes 6152 | tf_op jit(solution)/shard_map/ppermute | solution.py:46

commit v28 on v26

--- a/solution.py
+++ b/solution.py
@@ -13,8 +13,8 @@
 HALF = SAMPLES // 2
 GROUP = ("chip", "core", "samp")
 MIB = 1024 * 1024
-LISTED = 4
-CHUNK = 4
+LISTED = 6
+CHUNK = 5
 AHEAD = 3
 
 

time: 25.3 us -> 25.3 us (level)
  starting transfers between devices: 4.32 us -> 4.05 us
    ppermute x2, starting transfers between devices: 4.32 us -> 4.05 us  [across(): return lax.ppermute(array, ('core', 'space'), pairs)]
where the time goes in v28:
time: 25.3 us; the launch traced here: 25.2 us
  blocking collectives  13.5 us (53%)
  Pallas kernels  7.35 us (29%)
  starting transfers between devices  4.05 us (16%)
    all_to_all x1, blocking collectives, per_device(): window = lax.all_to_all(copies, GROUP, 0, 0).reshape(parts, block.shape[1])  13.5 us
    ppermute x2, starting transfers between devices, across(): return lax.ppermute(array, ('core', 'space'), pairs)  4.05 us
    pallas_call x1, Pallas kernels, per_device(): pl.pallas_call(field_kernel, out_shape=(pltpu.VMEM((tile_count, parts_her...  2.71 us
    pallas_call x1, Pallas kernels, per_device(): pl.pallas_call(sum_kernel, out_shape=pltpu.VMEM(source.shape, jnp.float32...  2.06 us
    pallas_call x1, Pallas kernels, per_device(): pl.pallas_call(fetch_kernel, out_shape=[pltpu.VMEM(shape, o.dtype) for sh...  1.97 us
    pallas_call x1, Pallas kernels, per_device(): pl.pallas_call(halo_kernel, out_shape=jax.ShapeDtypeStruct(source.shape,...  0.62 us
  transfers between devices with their start and end apart: 2, of which 0 were waited for; matrix products, arithmetic and copies ran while one was open for 0% of the time, Pallas kernels for 16%

profile of v28, /device:TPU:0, one launch (start us, length us, event | category | flops | bytes accessed | tf_op | source)
XLA Modules:
  0.0 25.2 jit_solution(8221566766913347496)
XLA Ops:
  0.0 2.4 %collective-permute-start = (bf16[2,2048]{1,0:T(2,128)(2,1)}, bf16[2,2048]{1,0:T(2,128)(2,1)S(1)}, u32[]{:S(2)}, u32[]{:S(2)}) collective-permute-start(bf16[2,2048]{1,0:T(2,128)(2,1)} %refs_2_.1), channel_id=1, source_target_pairs={{0,12},{4,8},{8,4},{12,0},{1,13},{5,9},{9,5},{13,1},{2,14},{6,10},... | collective-permute-start | bytes 24584 | tf_op jit(solution)/shard_map/ppermute | solution.py:45
  2.4 2.0 %fetch_operands.1 = (bf16[8,4,128,384]{3,2,1,0:T(8,128)(2,1)S(1)}, f32[32,2]{1,0:T(8,128)S(1)}, bf16[2,2048]{1,0:T(2,128)(2,1)S(1)}, bf16[2,32,96]{2,1,0:T(8,128...) custom-call(bf16[16,4,128,384]{3,2,1,0:T(8,128)(2,1)} %curl_hbm.1, ...), custom_call_target="tpu_custom_call" | custom-call | bytes 6291456 | tf_op jit(solution)/shard_map/fetch_operands/pallas_call | solution.py:280
  4.4 0.0 collective-permute-done
  4.4 0.1 broadcast_in_dim.2
  4.5 13.5 %all_to_all.5 = bf16[16,2,2304]{2,1,0:T(2,128)(2,1)S(1)} all-to-all(bf16[16,2,2304]{2,1,0:T(2,128)(2,1)S(1)} %broadcast_in_dim.2), channel_id=1, replica_groups=mesh['chip'=2,'core'=2,'space'=2,'samp'=4] {'chip','core','samp'}, dimensions={0} | all-to-all | bytes 294912 | tf_op jit(solution)/shard_map/all_to_all | solution.py:298
  18.1 0.1 reshape.4.window
  18.1 2.7 %shard_fields.1 = (f32[16,2,384]{2,1,0:T(2,128)S(1)}, f32[2,256]{1,0:T(2,128)S(1)}, bf16[8,4,128,384]{3,2,1,0:T(8,128)(2,1)S(1)}) custom-call(bf16[32,2304]{1,0:T(8,128)(2,1)S(1)} %reshape.4.window, bf16[8,4,128,384]{3,2,1,0:T(8,128)(2,1)S(1)} %get-tuple-element.17.first_curl, f32[32,2]{1,0:T(8,128)S(1)} %get-tuple-element.18.table, ...), custom_call_target="tpu_custom_call" | custom-call | flops 402653184 | bytes 6291456 | tf_op jit(solution)/shard_map/shard_fields/pallas_call | solution.py:300
  20.8 1.6 %collective-permute-start.1 = (f32[2,256]{1,0:T(2,128)S(1)}, f32[2,256]{1,0:T(2,128)S(1)}, u32[]{:S(2)}, u32[]{:S(2)}) collective-permute-start(f32[2,256]{1,0:T(2,128)S(1)} %get-tuple-element.26), channel_id=1, source_target_pairs={{0,4},{4,0},{8,12},{12,8},{1,5},{5,1},{9,13},{13,9},{2,6},{6,2},{1... | collective-permute-start | bytes 6152 | tf_op jit(solution)/shard_map/ppermute | solution.py:45
  22.5 2.1 %shard_sums.1.own = f32[2,2048]{1,0:T(2,128)S(1)} custom-call(f32[16,2,384]{2,1,0:T(2,128)S(1)} %get-tuple-element.23.projected, bf16[8,4,128,384]{3,2,1,0:T(8,128)(2,1)S(1)} %get-tuple-element.17.first_curl, bf16[8,4,128,384]{3,2,1,0:T(8,128)(2,1)S(1)} %get-tuple-element.24.later_curl, f32[2,2048]{1,0:T(2,128)S(1)} %get-tuple-element.25.source, ...), custom_call_target="tpu_custom_call" | custom-call | flops 402653184 | bytes 6291456 | tf_op jit(solution)/shard_map/shard_sums/pallas_call | solution.py:336
  24.5 0.0 collective-permute-done.1.from_right.from_left
  24.6 0.6 %halo_sum.1 = f32[2,2048]{1,0:T(2,128)} custom-call(f32[2,2048]{1,0:T(2,128)S(1)} %shard_sums.1.own, f32[2,256]{1,0:T(2,128)S(1)} %collective-permute-done.1.from_right.from_left, f32[2,256]{1,0:T(2,128)S(1)} %collective-permute-done.1.from_right.from_left), custom_call_target="tpu_custom_call" | custom-call | tf_op jit(solution)/shard_map/halo_sum/pallas_call | solution.py:356
  (2 shorter events, 0.0 us)
Async XLA Ops:
  0.0 4.4 %collective-permute-start = (bf16[2,2048]{1,0:T(2,128)(2,1)}, bf16[2,2048]{1,0:T(2,128)(2,1)S(1)}, u32[]{:S(2)}, u32[]{:S(2)}) collective-permute-start(bf16[2,2048]{1,0:T(2,128)(2,1)} %refs_2_.1), channel_id=1, source_target_pairs={{0,12},{4,8},{8,4},{12,0},{1,13},{5,9},{9,5},{13,1},{2,14},{6,10},... | collective-permute-start | bytes 24584 | tf_op jit(solution)/shard_map/ppermute | solution.py:45
  20.8 3.7 %collective-permute-start.1 = (f32[2,256]{1,0:T(2,128)S(1)}, f32[2,256]{1,0:T(2,128)S(1)}, u32[]{:S(2)}, u32[]{:S(2)}) collective-permute-start(f32[2,256]{1,0:T(2,128)S(1)} %get-tuple-element.26), channel_id=1, source_target_pairs={{0,4},{4,0},{8,12},{12,8},{1,5},{5,1},{9,13},{13,9},{2,6},{6,2},{1... | collective-permute-start | bytes 6152 | tf_op jit(solution)/shard_map/ppermute | solution.py:45

commit v29 on v23

--- a/solution.py
+++ b/solution.py
@@ -172,18 +172,27 @@
             project(turn - 1)
 
     def add_outer(turn, carry):
+        listed, sides, rows, curls = [], [], [], []
         for slot in range(LISTED):
             spot = turn * LISTED + slot
             code = jnp.where(spot < count, outer[jnp.minimum(spot, jnp.maximum(count - 1, 0))], 0)
             elem, link = code // links, code % links
-            block = jnp.where(
-                elem < early,
-                first_curl[jnp.minimum(elem, early - 1), link],
-                later_curl[jnp.maximum(elem - early, 0), link],
+            curls.append(
+                jnp.where(
+                    elem < early,
+                    first_curl[jnp.minimum(elem, early - 1), link],
+                    later_curl[jnp.maximum(elem - early, 0), link],
+                )
             )
-            contrib = weighted(projected[elem], block)
-            side = jnp.where(pattern[link, elem] == 0, 0, 1)
-            edge_sums[slot, side] += jnp.where(spot < count, contrib, 0.0)
+            rows.append(projected[elem])
+            sides.append(jnp.where(pattern[link, elem] == 0, 0, 1))
+            listed.append(spot < count)
+        contrib = weighted(jnp.concatenate(rows, axis=0), jnp.concatenate(curls, axis=0))
+        for slot in range(LISTED):
+            block = contrib[
+                slot * parts_here : (slot + 1) * parts_here, slot * tile : (slot + 1) * tile
+            ]
+            edge_sums[slot, sides[slot]] += jnp.where(listed[slot], block, 0.0)
         return carry
 
     add_outer(0, 0)

time: 25.2 us -> 25.3 us (level)
  no operation moved by 1% of the time
where the time goes in v29:
time: 25.3 us; the launch traced here: 25 us
  blocking collectives  13.5 us (53%)
  Pallas kernels  7.17 us (28%)
  starting transfers between devices  4.05 us (16%)
    all_to_all x1, blocking collectives, per_device(): window = lax.all_to_all(copies, GROUP, 0, 0).reshape(parts, block.shape[1])  13.5 us
    ppermute x2, starting transfers between devices, across(): return lax.ppermute(array, ('core', 'space'), pairs)  4.05 us
    pallas_call x1, Pallas kernels, per_device(): pl.pallas_call(field_kernel, out_shape=(pltpu.VMEM((tile_count, parts_her...  2.52 us
    pallas_call x1, Pallas kernels, per_device(): pl.pallas_call(sum_kernel, out_shape=pltpu.VMEM(source.shape, jnp.float32...  2.06 us
    pallas_call x1, Pallas kernels, per_device(): pl.pallas_call(fetch_kernel, out_shape=[pltpu.VMEM(shape, o.dtype) for sh...  1.97 us
    pallas_call x1, Pallas kernels, per_device(): pl.pallas_call(halo_kernel, out_shape=jax.ShapeDtypeStruct(source.shape,...  0.62 us
  transfers between devices with their start and end apart: 2, of which 0 were waited for; matrix products, arithmetic and copies ran while one was open for 0% of the time, Pallas kernels for 16%

profile of v29, /device:TPU:0, one launch (start us, length us, event | category | flops | bytes accessed | tf_op | source)
XLA Modules:
  0.0 25.0 jit_solution(4994733048929720928)
XLA Ops:
  0.0 2.4 %collective-permute-start = (bf16[2,2048]{1,0:T(2,128)(2,1)}, bf16[2,2048]{1,0:T(2,128)(2,1)S(1)}, u32[]{:S(2)}, u32[]{:S(2)}) collective-permute-start(bf16[2,2048]{1,0:T(2,128)(2,1)} %refs_2_.1), channel_id=1, source_target_pairs={{0,12},{4,8},{8,4},{12,0},{1,13},{5,9},{9,5},{13,1},{2,14},{6,10},... | collective-permute-start | bytes 24584 | tf_op jit(solution)/shard_map/ppermute | solution.py:45
  2.4 2.0 %fetch_operands.1 = (bf16[8,4,128,384]{3,2,1,0:T(8,128)(2,1)S(1)}, f32[32,2]{1,0:T(8,128)S(1)}, bf16[2,2048]{1,0:T(2,128)(2,1)S(1)}, bf16[2,32,96]{2,1,0:T(8,128...) custom-call(bf16[16,4,128,384]{3,2,1,0:T(8,128)(2,1)} %curl_hbm.1, ...), custom_call_target="tpu_custom_call" | custom-call | bytes 6291456 | tf_op jit(solution)/shard_map/fetch_operands/pallas_call | solution.py:286
  4.4 0.0 collective-permute-done
  4.4 0.1 broadcast_in_dim.2
  4.5 13.5 %all_to_all.5 = bf16[16,2,2304]{2,1,0:T(2,128)(2,1)S(1)} all-to-all(bf16[16,2,2304]{2,1,0:T(2,128)(2,1)S(1)} %broadcast_in_dim.2), channel_id=1, replica_groups=mesh['chip'=2,'core'=2,'space'=2,'samp'=4] {'chip','core','samp'}, dimensions={0} | all-to-all | bytes 294912 | tf_op jit(solution)/shard_map/all_to_all | solution.py:304
  18.1 0.1 reshape.4.window
  18.1 2.5 %shard_fields.1 = (f32[16,2,384]{2,1,0:T(2,128)S(1)}, f32[2,256]{1,0:T(2,128)S(1)}, bf16[8,4,128,384]{3,2,1,0:T(8,128)(2,1)S(1)}) custom-call(bf16[32,2304]{1,0:T(8,128)(2,1)S(1)} %reshape.4.window, bf16[8,4,128,384]{3,2,1,0:T(8,128)(2,1)S(1)} %get-tuple-element.17.first_curl, f32[32,2]{1,0:T(8,128)S(1)} %get-tuple-element.18.table, ...), custom_call_target="tpu_custom_call" | custom-call | flops 402653184 | bytes 6291456 | tf_op jit(solution)/shard_map/shard_fields/pallas_call | solution.py:306
  20.6 1.6 %collective-permute-start.1 = (f32[2,256]{1,0:T(2,128)S(1)}, f32[2,256]{1,0:T(2,128)S(1)}, u32[]{:S(2)}, u32[]{:S(2)}) collective-permute-start(f32[2,256]{1,0:T(2,128)S(1)} %get-tuple-element.26), channel_id=1, source_target_pairs={{0,4},{4,0},{8,12},{12,8},{1,5},{5,1},{9,13},{13,9},{2,6},{6,2},{1... | collective-permute-start | bytes 6152 | tf_op jit(solution)/shard_map/ppermute | solution.py:45
  22.3 2.1 %shard_sums.1.own = f32[2,2048]{1,0:T(2,128)S(1)} custom-call(f32[16,2,384]{2,1,0:T(2,128)S(1)} %get-tuple-element.23.projected, bf16[8,4,128,384]{3,2,1,0:T(8,128)(2,1)S(1)} %get-tuple-element.17.first_curl, bf16[8,4,128,384]{3,2,1,0:T(8,128)(2,1)S(1)} %get-tuple-element.24.later_curl, f32[2,2048]{1,0:T(2,128)S(1)} %get-tuple-element.25.source, ...), custom_call_target="tpu_custom_call" | custom-call | flops 402653184 | bytes 6291456 | tf_op jit(solution)/shard_map/shard_sums/pallas_call | solution.py:342
  24.4 0.0 collective-permute-done.1.from_right.from_left
  24.4 0.6 %halo_sum.1 = f32[2,2048]{1,0:T(2,128)} custom-call(f32[2,2048]{1,0:T(2,128)S(1)} %shard_sums.1.own, f32[2,256]{1,0:T(2,128)S(1)} %collective-permute-done.1.from_right.from_left, f32[2,256]{1,0:T(2,128)S(1)} %collective-permute-done.1.from_right.from_left), custom_call_target="tpu_custom_call" | custom-call | tf_op jit(solution)/shard_map/halo_sum/pallas_call | solution.py:362
  (2 shorter events, 0.0 us)
Async XLA Ops:
  0.0 4.4 %collective-permute-start = (bf16[2,2048]{1,0:T(2,128)(2,1)}, bf16[2,2048]{1,0:T(2,128)(2,1)S(1)}, u32[]{:S(2)}, u32[]{:S(2)}) collective-permute-start(bf16[2,2048]{1,0:T(2,128)(2,1)} %refs_2_.1), channel_id=1, source_target_pairs={{0,12},{4,8},{8,4},{12,0},{1,13},{5,9},{9,5},{13,1},{2,14},{6,10},... | collective-permute-start | bytes 24584 | tf_op jit(solution)/shard_map/ppermute | solution.py:45
  20.6 3.7 %collective-permute-start.1 = (f32[2,256]{1,0:T(2,128)S(1)}, f32[2,256]{1,0:T(2,128)S(1)}, u32[]{:S(2)}, u32[]{:S(2)}) collective-permute-start(f32[2,256]{1,0:T(2,128)S(1)} %get-tuple-element.26), channel_id=1, source_target_pairs={{0,4},{4,0},{8,12},{12,8},{1,5},{5,1},{9,13},{13,9},{2,6},{6,2},{1... | collective-permute-start | bytes 6152 | tf_op jit(solution)/shard_map/ppermute | solution.py:45

commit v30 on v29

--- a/solution.py
+++ b/solution.py
@@ -101,7 +101,6 @@
     law,
     outer,
     timed,
-    densities,
     edge_sums,
     small_sems,
     curl_sems,
@@ -149,10 +148,9 @@
             [timed[:, pl.ds(pl.multiple_of(at * tile, tile), tile)] for at in places[elem]], axis=1
         )
         split = jnp.dot(picked, blocks(elem), preferred_element_type=jnp.float32)
-        densities[elem] = split[:HALF] + split[HALF:]
-
-    def project(elem):
-        density = densities[elem]
+        return split[:HALF] + split[HALF:]
+
+    def project(elem, density):
         comp = [density[:, c * tile : (c + 1) * tile] for c in range(comps // tile)]
         square = comp[0] * comp[0]
         for c in comp[1:]:
@@ -163,13 +161,15 @@
         rows = [jnp.sum(column * field, axis=0, keepdims=True) for column in columns]
         projected[elem] = jnp.concatenate(rows, axis=0) * (4.0 / SAMPLES)
 
+    density = None
     for turn in range(tile_count + 1):
+        last = density
         if turn < tile_count:
             if turn in later:
                 later[turn].wait()
-            find_density(turn)
+            density = find_density(turn)
         if turn:
-            project(turn - 1)
+            project(turn - 1, last)
 
     def add_outer(turn, carry):
         listed, sides, rows, curls = [], [], [], []
@@ -318,7 +318,6 @@
             pltpu.SMEM(material_law.shape, jnp.float32),
             pltpu.SMEM((links * tile_count + 1,), jnp.int32),
             pltpu.VMEM((SAMPLES, (tile_count + 2) * tile), jnp.bfloat16),
-            pltpu.VMEM((tile_count, HALF, comps), jnp.float32),
             pltpu.VMEM((LISTED, 2, parts_here, tile), jnp.float32),
             pltpu.SemaphoreType.DMA((3,)),
             pltpu.SemaphoreType.DMA((pl.cdiv(tile_count - early, CHUNK),)),

time: 25.3 us -> 25.2 us (level)
  no operation moved by 1% of the time
where the time goes in v30:
time: 25.2 us; the launch traced here: 25 us
  blocking collectives  13.5 us (54%)
  Pallas kernels  7.17 us (28%)
  starting transfers between devices  4.03 us (16%)
    all_to_all x1, blocking collectives, per_device(): window = lax.all_to_all(copies, GROUP, 0, 0).reshape(parts, block.shape[1])  13.5 us
    ppermute x2, starting transfers between devices, across(): return lax.ppermute(array, ('core', 'space'), pairs)  4.03 us
    pallas_call x1, Pallas kernels, per_device(): pl.pallas_call(field_kernel, out_shape=(pltpu.VMEM((tile_count, parts_her...  2.53 us
    pallas_call x1, Pallas kernels, per_device(): pl.pallas_call(sum_kernel, out_shape=pltpu.VMEM(source.shape, jnp.float32...  2.06 us
    pallas_call x1, Pallas kernels, per_device(): pl.pallas_call(fetch_kernel, out_shape=[pltpu.VMEM(shape, o.dtype) for sh...  1.97 us
    pallas_call x1, Pallas kernels, per_device(): pl.pallas_call(halo_kernel, out_shape=jax.ShapeDtypeStruct(source.shape,...  0.62 us
  transfers between devices with their start and end apart: 2, of which 0 were waited for; matrix products, arithmetic and copies ran while one was open for 0% of the time, Pallas kernels for 16%

profile of v30, /device:TPU:0, one launch (start us, length us, event | category | flops | bytes accessed | tf_op | source)
XLA Modules:
  0.0 25.0 jit_solution(4994733048929720928)
XLA Ops:
  0.0 2.4 %collective-permute-start = (bf16[2,2048]{1,0:T(2,128)(2,1)}, bf16[2,2048]{1,0:T(2,128)(2,1)S(1)}, u32[]{:S(2)}, u32[]{:S(2)}) collective-permute-start(bf16[2,2048]{1,0:T(2,128)(2,1)} %refs_2_.1), channel_id=1, source_target_pairs={{0,12},{4,8},{8,4},{12,0},{1,13},{5,9},{9,5},{13,1},{2,14},{6,10},... | collective-permute-start | bytes 24584 | tf_op jit(solution)/shard_map/ppermute | solution.py:45
  2.4 2.0 %fetch_operands.1 = (bf16[8,4,128,384]{3,2,1,0:T(8,128)(2,1)S(1)}, f32[32,2]{1,0:T(8,128)S(1)}, bf16[2,2048]{1,0:T(2,128)(2,1)S(1)}, bf16[2,32,96]{2,1,0:T(8,128...) custom-call(bf16[16,4,128,384]{3,2,1,0:T(8,128)(2,1)} %curl_hbm.1, ...), custom_call_target="tpu_custom_call" | custom-call | bytes 6291456 | tf_op jit(solution)/shard_map/fetch_operands/pallas_call | solution.py:286
  4.4 0.0 collective-permute-done
  4.4 0.1 broadcast_in_dim.2
  4.5 13.5 %all_to_all.5 = bf16[16,2,2304]{2,1,0:T(2,128)(2,1)S(1)} all-to-all(bf16[16,2,2304]{2,1,0:T(2,128)(2,1)S(1)} %broadcast_in_dim.2), channel_id=1, replica_groups=mesh['chip'=2,'core'=2,'space'=2,'samp'=4] {'chip','core','samp'}, dimensions={0} | all-to-all | bytes 294912 | tf_op jit(solution)/shard_map/all_to_all | solution.py:304
  18.1 0.1 reshape.4.window
  18.1 2.5 %shard_fields.1 = (f32[16,2,384]{2,1,0:T(2,128)S(1)}, f32[2,256]{1,0:T(2,128)S(1)}, bf16[8,4,128,384]{3,2,1,0:T(8,128)(2,1)S(1)}) custom-call(bf16[32,2304]{1,0:T(8,128)(2,1)S(1)} %reshape.4.window, bf16[8,4,128,384]{3,2,1,0:T(8,128)(2,1)S(1)} %get-tuple-element.17.first_curl, f32[32,2]{1,0:T(8,128)S(1)} %get-tuple-element.18.table, ...), custom_call_target="tpu_custom_call" | custom-call | flops 402653184 | bytes 6291456 | tf_op jit(solution)/shard_map/shard_fields/pallas_call | solution.py:306
  20.7 1.6 %collective-permute-start.1 = (f32[2,256]{1,0:T(2,128)S(1)}, f32[2,256]{1,0:T(2,128)S(1)}, u32[]{:S(2)}, u32[]{:S(2)}) collective-permute-start(f32[2,256]{1,0:T(2,128)S(1)} %get-tuple-element.26), channel_id=1, source_target_pairs={{0,4},{4,0},{8,12},{12,8},{1,5},{5,1},{9,13},{13,9},{2,6},{6,2},{1... | collective-permute-start | bytes 6152 | tf_op jit(solution)/shard_map/ppermute | solution.py:45
  22.3 2.1 %shard_sums.1.own = f32[2,2048]{1,0:T(2,128)S(1)} custom-call(f32[16,2,384]{2,1,0:T(2,128)S(1)} %get-tuple-element.23.projected, bf16[8,4,128,384]{3,2,1,0:T(8,128)(2,1)S(1)} %get-tuple-element.17.first_curl, bf16[8,4,128,384]{3,2,1,0:T(8,128)(2,1)S(1)} %get-tuple-element.24.later_curl, f32[2,2048]{1,0:T(2,128)S(1)} %get-tuple-element.25.source, ...), custom_call_target="tpu_custom_call" | custom-call | flops 402653184 | bytes 6291456 | tf_op jit(solution)/shard_map/shard_sums/pallas_call | solution.py:341
  24.3 0.0 collective-permute-done.1.from_right.from_left
  24.4 0.6 %halo_sum.1 = f32[2,2048]{1,0:T(2,128)} custom-call(f32[2,2048]{1,0:T(2,128)S(1)} %shard_sums.1.own, f32[2,256]{1,0:T(2,128)S(1)} %collective-permute-done.1.from_right.from_left, f32[2,256]{1,0:T(2,128)S(1)} %collective-permute-done.1.from_right.from_left), custom_call_target="tpu_custom_call" | custom-call | tf_op jit(solution)/shard_map/halo_sum/pallas_call | solution.py:361
  (2 shorter events, 0.0 us)
Async XLA Ops:
  0.0 4.4 %collective-permute-start = (bf16[2,2048]{1,0:T(2,128)(2,1)}, bf16[2,2048]{1,0:T(2,128)(2,1)S(1)}, u32[]{:S(2)}, u32[]{:S(2)}) collective-permute-start(bf16[2,2048]{1,0:T(2,128)(2,1)} %refs_2_.1), channel_id=1, source_target_pairs={{0,12},{4,8},{8,4},{12,0},{1,13},{5,9},{9,5},{13,1},{2,14},{6,10},... | collective-permute-start | bytes 24584 | tf_op jit(solution)/shard_map/ppermute | solution.py:45
  20.7 3.7 %collective-permute-start.1 = (f32[2,256]{1,0:T(2,128)S(1)}, f32[2,256]{1,0:T(2,128)S(1)}, u32[]{:S(2)}, u32[]{:S(2)}) collective-permute-start(f32[2,256]{1,0:T(2,128)S(1)} %get-tuple-element.26), channel_id=1, source_target_pairs={{0,4},{4,0},{8,12},{12,8},{1,5},{5,1},{9,13},{13,9},{2,6},{6,2},{1... | collective-permute-start | bytes 6152 | tf_op jit(solution)/shard_map/ppermute | solution.py:45

commit v31 on v30

--- a/solution.py
+++ b/solution.py
@@ -125,8 +125,11 @@
     edge_sums[...] = jnp.zeros_like(edge_sums)
     own, outer_tiles = pieces[0], pieces[1]
     timed[:, tile:-tile] = time_samples(own, window[:, tile:-tile])
-    timed[:, :tile] = time_samples(outer_tiles, window[:, :tile])
-    timed[:, -tile:] = time_samples(outer_tiles, window[:, -tile:])
+    ends = time_samples(
+        outer_tiles, jnp.concatenate([window[:, :tile], window[:, -tile:]], axis=1)
+    )
+    timed[:, :tile] = ends[:, :tile]
+    timed[:, -tile:] = ends[:, tile:]
     columns = [
         jnp.broadcast_to(table[:, part : part + 1], (HALF, comps)) for part in range(parts_here)
     ]

time: 25.2 us -> 25.2 us (level)
  no operation moved by 1% of the time
where the time goes in v31:
time: 25.2 us; the launch traced here: 25 us
  blocking collectives  13.5 us (54%)
  Pallas kernels  7.16 us (28%)
  starting transfers between devices  4.06 us (16%)
    all_to_all x1, blocking collectives, per_device(): window = lax.all_to_all(copies, GROUP, 0, 0).reshape(parts, block.shape[1])  13.5 us
    ppermute x2, starting transfers between devices, across(): return lax.ppermute(array, ('core', 'space'), pairs)  4.06 us
    pallas_call x1, Pallas kernels, per_device(): pl.pallas_call(field_kernel, out_shape=(pltpu.VMEM((tile_count, parts_her...  2.52 us
    pallas_call x1, Pallas kernels, per_device(): pl.pallas_call(sum_kernel, out_shape=pltpu.VMEM(source.shape, jnp.float32...  2.06 us
    pallas_call x1, Pallas kernels, per_device(): pl.pallas_call(fetch_kernel, out_shape=[pltpu.VMEM(shape, o.dtype) for sh...  1.97 us
    pallas_call x1, Pallas kernels, per_device(): pl.pallas_call(halo_kernel, out_shape=jax.ShapeDtypeStruct(source.shape,...  0.62 us
  transfers between devices with their start and end apart: 2, of which 0 were waited for; matrix products, arithmetic and copies ran while one was open for 0% of the time, Pallas kernels for 16%

profile of v31, /device:TPU:0, one launch (start us, length us, event | category | flops | bytes accessed | tf_op | source)
XLA Modules:
  0.0 25.0 jit_solution(4403615513332932888)
XLA Ops:
  0.0 2.4 %collective-permute-start = (bf16[2,2048]{1,0:T(2,128)(2,1)}, bf16[2,2048]{1,0:T(2,128)(2,1)S(1)}, u32[]{:S(2)}, u32[]{:S(2)}) collective-permute-start(bf16[2,2048]{1,0:T(2,128)(2,1)} %refs_2_.1), channel_id=1, source_target_pairs={{0,12},{4,8},{8,4},{12,0},{1,13},{5,9},{9,5},{13,1},{2,14},{6,10},... | collective-permute-start | bytes 24584 | tf_op jit(solution)/shard_map/ppermute | solution.py:45
  2.4 2.0 %fetch_operands.1 = (bf16[8,4,128,384]{3,2,1,0:T(8,128)(2,1)S(1)}, f32[32,2]{1,0:T(8,128)S(1)}, bf16[2,2048]{1,0:T(2,128)(2,1)S(1)}, bf16[2,32,96]{2,1,0:T(8,128...) custom-call(bf16[16,4,128,384]{3,2,1,0:T(8,128)(2,1)} %curl_hbm.1, ...), custom_call_target="tpu_custom_call" | custom-call | bytes 6291456 | tf_op jit(solution)/shard_map/fetch_operands/pallas_call | solution.py:289
  4.4 0.0 collective-permute-done
  4.4 0.1 broadcast_in_dim.2
  4.5 13.5 %all_to_all.5 = bf16[16,2,2304]{2,1,0:T(2,128)(2,1)S(1)} all-to-all(bf16[16,2,2304]{2,1,0:T(2,128)(2,1)S(1)} %broadcast_in_dim.2), channel_id=1, replica_groups=mesh['chip'=2,'core'=2,'space'=2,'samp'=4] {'chip','core','samp'}, dimensions={0} | all-to-all | bytes 294912 | tf_op jit(solution)/shard_map/all_to_all | solution.py:307
  18.1 0.1 reshape.4.window
  18.1 2.5 %shard_fields.1 = (f32[16,2,384]{2,1,0:T(2,128)S(1)}, f32[2,256]{1,0:T(2,128)S(1)}, bf16[8,4,128,384]{3,2,1,0:T(8,128)(2,1)S(1)}) custom-call(bf16[32,2304]{1,0:T(8,128)(2,1)S(1)} %reshape.4.window, bf16[8,4,128,384]{3,2,1,0:T(8,128)(2,1)S(1)} %get-tuple-element.17.first_curl, f32[32,2]{1,0:T(8,128)S(1)} %get-tuple-element.18.table, ...), custom_call_target="tpu_custom_call" | custom-call | flops 402653184 | bytes 6291456 | tf_op jit(solution)/shard_map/shard_fields/pallas_call | solution.py:309
  20.6 1.6 %collective-permute-start.1 = (f32[2,256]{1,0:T(2,128)S(1)}, f32[2,256]{1,0:T(2,128)S(1)}, u32[]{:S(2)}, u32[]{:S(2)}) collective-permute-start(f32[2,256]{1,0:T(2,128)S(1)} %get-tuple-element.26), channel_id=1, source_target_pairs={{0,4},{4,0},{8,12},{12,8},{1,5},{5,1},{9,13},{13,9},{2,6},{6,2},{1... | collective-permute-start | bytes 6152 | tf_op jit(solution)/shard_map/ppermute | solution.py:45
  22.3 2.1 %shard_sums.1.own = f32[2,2048]{1,0:T(2,128)S(1)} custom-call(f32[16,2,384]{2,1,0:T(2,128)S(1)} %get-tuple-element.23.projected, bf16[8,4,128,384]{3,2,1,0:T(8,128)(2,1)S(1)} %get-tuple-element.17.first_curl, bf16[8,4,128,384]{3,2,1,0:T(8,128)(2,1)S(1)} %get-tuple-element.24.later_curl, f32[2,2048]{1,0:T(2,128)S(1)} %get-tuple-element.25.source, ...), custom_call_target="tpu_custom_call" | custom-call | flops 402653184 | bytes 6291456 | tf_op jit(solution)/shard_map/shard_sums/pallas_call | solution.py:344
  24.4 0.0 collective-permute-done.1.from_right.from_left
  24.4 0.6 %halo_sum.1 = f32[2,2048]{1,0:T(2,128)} custom-call(f32[2,2048]{1,0:T(2,128)S(1)} %shard_sums.1.own, f32[2,256]{1,0:T(2,128)S(1)} %collective-permute-done.1.from_right.from_left, f32[2,256]{1,0:T(2,128)S(1)} %collective-permute-done.1.from_right.from_left), custom_call_target="tpu_custom_call" | custom-call | tf_op jit(solution)/shard_map/halo_sum/pallas_call | solution.py:364
  (2 shorter events, 0.0 us)
Async XLA Ops:
  0.0 4.4 %collective-permute-start = (bf16[2,2048]{1,0:T(2,128)(2,1)}, bf16[2,2048]{1,0:T(2,128)(2,1)S(1)}, u32[]{:S(2)}, u32[]{:S(2)}) collective-permute-start(bf16[2,2048]{1,0:T(2,128)(2,1)} %refs_2_.1), channel_id=1, source_target_pairs={{0,12},{4,8},{8,4},{12,0},{1,13},{5,9},{9,5},{13,1},{2,14},{6,10},... | collective-permute-start | bytes 24584 | tf_op jit(solution)/shard_map/ppermute | solution.py:45
  20.6 3.7 %collective-permute-start.1 = (f32[2,256]{1,0:T(2,128)S(1)}, f32[2,256]{1,0:T(2,128)S(1)}, u32[]{:S(2)}, u32[]{:S(2)}) collective-permute-start(f32[2,256]{1,0:T(2,128)S(1)} %get-tuple-element.26), channel_id=1, source_target_pairs={{0,4},{4,0},{8,12},{12,8},{1,5},{5,1},{9,13},{13,9},{2,6},{6,2},{1... | collective-permute-start | bytes 6152 | tf_op jit(solution)/shard_map/ppermute | solution.py:45

commit v32 on v31

--- a/solution.py
+++ b/solution.py
@@ -14,7 +14,7 @@
 GROUP = ("chip", "core", "samp")
 MIB = 1024 * 1024
 LISTED = 4
-CHUNK = 4
+CHUNK = 5
 AHEAD = 3
 
 

time: 25.2 us -> 25.3 us (level)
  no operation moved by 1% of the time
where the time goes in v32:
time: 25.3 us; the launch traced here: 25.1 us
  blocking collectives  13.5 us (53%)
  Pallas kernels  7.24 us (29%)
  starting transfers between devices  4.04 us (16%)
    all_to_all x1, blocking collectives, per_device(): window = lax.all_to_all(copies, GROUP, 0, 0).reshape(parts, block.shape[1])  13.5 us
    ppermute x2, starting transfers between devices, across(): return lax.ppermute(array, ('core', 'space'), pairs)  4.04 us
    pallas_call x1, Pallas kernels, per_device(): pl.pallas_call(field_kernel, out_shape=(pltpu.VMEM((tile_count, parts_her...  2.6 us
    pallas_call x1, Pallas kernels, per_device(): pl.pallas_call(sum_kernel, out_shape=pltpu.VMEM(source.shape, jnp.float32...  2.06 us
    pallas_call x1, Pallas kernels, per_device(): pl.pallas_call(fetch_kernel, out_shape=[pltpu.VMEM(shape, o.dtype) for sh...  1.97 us
    pallas_call x1, Pallas kernels, per_device(): pl.pallas_call(halo_kernel, out_shape=jax.ShapeDtypeStruct(source.shape,...  0.62 us
  transfers between devices with their start and end apart: 2, of which 0 were waited for; matrix products, arithmetic and copies ran while one was open for 0% of the time, Pallas kernels for 16%

profile of v32, /device:TPU:0, one launch (start us, length us, event | category | flops | bytes accessed | tf_op | source)
XLA Modules:
  0.0 25.1 jit_solution(6737678920824521254)
XLA Ops:
  0.0 2.4 %collective-permute-start = (bf16[2,2048]{1,0:T(2,128)(2,1)}, bf16[2,2048]{1,0:T(2,128)(2,1)S(1)}, u32[]{:S(2)}, u32[]{:S(2)}) collective-permute-start(bf16[2,2048]{1,0:T(2,128)(2,1)} %refs_2_.1), channel_id=1, source_target_pairs={{0,12},{4,8},{8,4},{12,0},{1,13},{5,9},{9,5},{13,1},{2,14},{6,10},... | collective-permute-start | bytes 24584 | tf_op jit(solution)/shard_map/ppermute | solution.py:45
  2.4 2.0 %fetch_operands.1 = (bf16[8,4,128,384]{3,2,1,0:T(8,128)(2,1)S(1)}, f32[32,2]{1,0:T(8,128)S(1)}, bf16[2,2048]{1,0:T(2,128)(2,1)S(1)}, bf16[2,32,96]{2,1,0:T(8,128...) custom-call(bf16[16,4,128,384]{3,2,1,0:T(8,128)(2,1)} %curl_hbm.1, ...), custom_call_target="tpu_custom_call" | custom-call | bytes 6291456 | tf_op jit(solution)/shard_map/fetch_operands/pallas_call | solution.py:289
  4.4 0.0 collective-permute-done
  4.4 0.1 broadcast_in_dim.2
  4.5 13.5 %all_to_all.5 = bf16[16,2,2304]{2,1,0:T(2,128)(2,1)S(1)} all-to-all(bf16[16,2,2304]{2,1,0:T(2,128)(2,1)S(1)} %broadcast_in_dim.2), channel_id=1, replica_groups=mesh['chip'=2,'core'=2,'space'=2,'samp'=4] {'chip','core','samp'}, dimensions={0} | all-to-all | bytes 294912 | tf_op jit(solution)/shard_map/all_to_all | solution.py:307
  18.1 0.1 reshape.4.window
  18.1 2.6 %shard_fields.1 = (f32[16,2,384]{2,1,0:T(2,128)S(1)}, f32[2,256]{1,0:T(2,128)S(1)}, bf16[8,4,128,384]{3,2,1,0:T(8,128)(2,1)S(1)}) custom-call(bf16[32,2304]{1,0:T(8,128)(2,1)S(1)} %reshape.4.window, bf16[8,4,128,384]{3,2,1,0:T(8,128)(2,1)S(1)} %get-tuple-element.17.first_curl, f32[32,2]{1,0:T(8,128)S(1)} %get-tuple-element.18.table, ...), custom_call_target="tpu_custom_call" | custom-call | flops 402653184 | bytes 6291456 | tf_op jit(solution)/shard_map/shard_fields/pallas_call | solution.py:309
  20.7 1.6 %collective-permute-start.1 = (f32[2,256]{1,0:T(2,128)S(1)}, f32[2,256]{1,0:T(2,128)S(1)}, u32[]{:S(2)}, u32[]{:S(2)}) collective-permute-start(f32[2,256]{1,0:T(2,128)S(1)} %get-tuple-element.26), channel_id=1, source_target_pairs={{0,4},{4,0},{8,12},{12,8},{1,5},{5,1},{9,13},{13,9},{2,6},{6,2},{1... | collective-permute-start | bytes 6152 | tf_op jit(solution)/shard_map/ppermute | solution.py:45
  22.4 2.1 %shard_sums.1.own = f32[2,2048]{1,0:T(2,128)S(1)} custom-call(f32[16,2,384]{2,1,0:T(2,128)S(1)} %get-tuple-element.23.projected, bf16[8,4,128,384]{3,2,1,0:T(8,128)(2,1)S(1)} %get-tuple-element.17.first_curl, bf16[8,4,128,384]{3,2,1,0:T(8,128)(2,1)S(1)} %get-tuple-element.24.later_curl, f32[2,2048]{1,0:T(2,128)S(1)} %get-tuple-element.25.source, ...), custom_call_target="tpu_custom_call" | custom-call | flops 402653184 | bytes 6291456 | tf_op jit(solution)/shard_map/shard_sums/pallas_call | solution.py:344
  24.4 0.0 collective-permute-done.1.from_right.from_left
  24.4 0.6 %halo_sum.1 = f32[2,2048]{1,0:T(2,128)} custom-call(f32[2,2048]{1,0:T(2,128)S(1)} %shard_sums.1.own, f32[2,256]{1,0:T(2,128)S(1)} %collective-permute-done.1.from_right.from_left, f32[2,256]{1,0:T(2,128)S(1)} %collective-permute-done.1.from_right.from_left), custom_call_target="tpu_custom_call" | custom-call | tf_op jit(solution)/shard_map/halo_sum/pallas_call | solution.py:364
  (2 shorter events, 0.0 us)
Async XLA Ops:
  0.0 4.4 %collective-permute-start = (bf16[2,2048]{1,0:T(2,128)(2,1)}, bf16[2,2048]{1,0:T(2,128)(2,1)S(1)}, u32[]{:S(2)}, u32[]{:S(2)}) collective-permute-start(bf16[2,2048]{1,0:T(2,128)(2,1)} %refs_2_.1), channel_id=1, source_target_pairs={{0,12},{4,8},{8,4},{12,0},{1,13},{5,9},{9,5},{13,1},{2,14},{6,10},... | collective-permute-start | bytes 24584 | tf_op jit(solution)/shard_map/ppermute | solution.py:45
  20.7 3.7 %collective-permute-start.1 = (f32[2,256]{1,0:T(2,128)S(1)}, f32[2,256]{1,0:T(2,128)S(1)}, u32[]{:S(2)}, u32[]{:S(2)}) collective-permute-start(f32[2,256]{1,0:T(2,128)S(1)} %get-tuple-element.26), channel_id=1, source_target_pairs={{0,4},{4,0},{8,12},{12,8},{1,5},{5,1},{9,13},{13,9},{2,6},{6,2},{1... | collective-permute-start | bytes 6152 | tf_op jit(solution)/shard_map/ppermute | solution.py:45

commit v33 on v29

--- a/solution.py
+++ b/solution.py
@@ -14,7 +14,7 @@
 GROUP = ("chip", "core", "samp")
 MIB = 1024 * 1024
 LISTED = 4
-CHUNK = 4
+FIRST = 3
 AHEAD = 3
 
 
@@ -113,13 +113,12 @@
     small = [
         pltpu.make_async_copy(src, dst, small_sems.at[i]) for i, (src, dst) in enumerate(fetched)
     ]
+    middle = early + FIRST
     later = {
-        elem: pltpu.make_async_copy(
-            curl_hbm.at[elem : min(elem + CHUNK, tile_count)],
-            later_curl.at[elem - early : min(elem + CHUNK, tile_count) - early],
-            curl_sems.at[(elem - early) // CHUNK],
+        at: pltpu.make_async_copy(
+            curl_hbm.at[at:end], later_curl.at[at - early : end - early], curl_sems.at[i]
         )
-        for elem in range(early, tile_count, CHUNK)
+        for i, (at, end) in enumerate([(early, middle), (middle, tile_count)])
     }
     for copy in small + list(later.values()):
         copy.start()
@@ -321,7 +320,7 @@
             pltpu.VMEM((tile_count, HALF, comps), jnp.float32),
             pltpu.VMEM((LISTED, 2, parts_here, tile), jnp.float32),
             pltpu.SemaphoreType.DMA((3,)),
-            pltpu.SemaphoreType.DMA((pl.cdiv(tile_count - early, CHUNK),)),
+            pltpu.SemaphoreType.DMA((2,)),
         ],
         compiler_params=pltpu.CompilerParams(vmem_limit_bytes=32 * MIB),
         cost_estimate=pl.CostEstimate(

time: 25.3 us -> 25.4 us (level)
  no operation moved by 1% of the time
where the time goes in v33:
time: 25.4 us; the launch traced here: 25.1 us
  blocking collectives  13.5 us (53%)
  Pallas kernels  7.27 us (29%)
  starting transfers between devices  4.05 us (16%)
    all_to_all x1, blocking collectives, per_device(): window = lax.all_to_all(copies, GROUP, 0, 0).reshape(parts, block.shape[1])  13.5 us
    ppermute x2, starting transfers between devices, across(): return lax.ppermute(array, ('core', 'space'), pairs)  4.05 us
    pallas_call x1, Pallas kernels, per_device(): pl.pallas_call(field_kernel, out_shape=(pltpu.VMEM((tile_count, parts_her...  2.62 us
    pallas_call x1, Pallas kernels, per_device(): pl.pallas_call(sum_kernel, out_shape=pltpu.VMEM(source.shape, jnp.float32...  2.06 us
    pallas_call x1, Pallas kernels, per_device(): pl.pallas_call(fetch_kernel, out_shape=[pltpu.VMEM(shape, o.dtype) for sh...  1.97 us
    pallas_call x1, Pallas kernels, per_device(): pl.pallas_call(halo_kernel, out_shape=jax.ShapeDtypeStruct(source.shape,...  0.62 us
  transfers between devices with their start and end apart: 2, of which 0 were waited for; matrix products, arithmetic and copies ran while one was open for 0% of the time, Pallas kernels for 16%

profile of v33, /device:TPU:0, one launch (start us, length us, event | category | flops | bytes accessed | tf_op | source)
XLA Modules:
  0.0 25.1 jit_solution(12712180838010761422)
XLA Ops:
  0.0 2.4 %collective-permute-start = (bf16[2,2048]{1,0:T(2,128)(2,1)}, bf16[2,2048]{1,0:T(2,128)(2,1)S(1)}, u32[]{:S(2)}, u32[]{:S(2)}) collective-permute-start(bf16[2,2048]{1,0:T(2,128)(2,1)} %refs_2_.1), channel_id=1, source_target_pairs={{0,12},{4,8},{8,4},{12,0},{1,13},{5,9},{9,5},{13,1},{2,14},{6,10},... | collective-permute-start | bytes 24584 | tf_op jit(solution)/shard_map/ppermute | solution.py:45
  2.4 2.0 %fetch_operands.1 = (bf16[8,4,128,384]{3,2,1,0:T(8,128)(2,1)S(1)}, f32[32,2]{1,0:T(8,128)S(1)}, bf16[2,2048]{1,0:T(2,128)(2,1)S(1)}, bf16[2,32,96]{2,1,0:T(8,128...) custom-call(bf16[16,4,128,384]{3,2,1,0:T(8,128)(2,1)} %curl_hbm.1, ...), custom_call_target="tpu_custom_call" | custom-call | bytes 6291456 | tf_op jit(solution)/shard_map/fetch_operands/pallas_call | solution.py:285
  4.4 0.0 collective-permute-done
  4.4 0.1 broadcast_in_dim.2
  4.5 13.5 %all_to_all.5 = bf16[16,2,2304]{2,1,0:T(2,128)(2,1)S(1)} all-to-all(bf16[16,2,2304]{2,1,0:T(2,128)(2,1)S(1)} %broadcast_in_dim.2), channel_id=1, replica_groups=mesh['chip'=2,'core'=2,'space'=2,'samp'=4] {'chip','core','samp'}, dimensions={0} | all-to-all | bytes 294912 | tf_op jit(solution)/shard_map/all_to_all | solution.py:303
  18.1 0.1 reshape.4.window
  18.1 2.6 %shard_fields.1 = (f32[16,2,384]{2,1,0:T(2,128)S(1)}, f32[2,256]{1,0:T(2,128)S(1)}, bf16[8,4,128,384]{3,2,1,0:T(8,128)(2,1)S(1)}) custom-call(bf16[32,2304]{1,0:T(8,128)(2,1)S(1)} %reshape.4.window, bf16[8,4,128,384]{3,2,1,0:T(8,128)(2,1)S(1)} %get-tuple-element.17.first_curl, f32[32,2]{1,0:T(8,128)S(1)} %get-tuple-element.18.table, ...), custom_call_target="tpu_custom_call" | custom-call | flops 402653184 | bytes 6291456 | tf_op jit(solution)/shard_map/shard_fields/pallas_call | solution.py:305
  20.7 1.6 %collective-permute-start.1 = (f32[2,256]{1,0:T(2,128)S(1)}, f32[2,256]{1,0:T(2,128)S(1)}, u32[]{:S(2)}, u32[]{:S(2)}) collective-permute-start(f32[2,256]{1,0:T(2,128)S(1)} %get-tuple-element.26), channel_id=1, source_target_pairs={{0,4},{4,0},{8,12},{12,8},{1,5},{5,1},{9,13},{13,9},{2,6},{6,2},{1... | collective-permute-start | bytes 6152 | tf_op jit(solution)/shard_map/ppermute | solution.py:45
  22.4 2.1 %shard_sums.1.own = f32[2,2048]{1,0:T(2,128)S(1)} custom-call(f32[16,2,384]{2,1,0:T(2,128)S(1)} %get-tuple-element.23.projected, bf16[8,4,128,384]{3,2,1,0:T(8,128)(2,1)S(1)} %get-tuple-element.17.first_curl, bf16[8,4,128,384]{3,2,1,0:T(8,128)(2,1)S(1)} %get-tuple-element.24.later_curl, f32[2,2048]{1,0:T(2,128)S(1)} %get-tuple-element.25.source, ...), custom_call_target="tpu_custom_call" | custom-call | flops 402653184 | bytes 6291456 | tf_op jit(solution)/shard_map/shard_sums/pallas_call | solution.py:341
  24.5 0.0 collective-permute-done.1.from_right.from_left
  24.5 0.6 %halo_sum.1 = f32[2,2048]{1,0:T(2,128)} custom-call(f32[2,2048]{1,0:T(2,128)S(1)} %shard_sums.1.own, f32[2,256]{1,0:T(2,128)S(1)} %collective-permute-done.1.from_right.from_left, f32[2,256]{1,0:T(2,128)S(1)} %collective-permute-done.1.from_right.from_left), custom_call_target="tpu_custom_call" | custom-call | tf_op jit(solution)/shard_map/halo_sum/pallas_call | solution.py:361
  (2 shorter events, 0.0 us)
Async XLA Ops:
  0.0 4.4 %collective-permute-start = (bf16[2,2048]{1,0:T(2,128)(2,1)}, bf16[2,2048]{1,0:T(2,128)(2,1)S(1)}, u32[]{:S(2)}, u32[]{:S(2)}) collective-permute-start(bf16[2,2048]{1,0:T(2,128)(2,1)} %refs_2_.1), channel_id=1, source_target_pairs={{0,12},{4,8},{8,4},{12,0},{1,13},{5,9},{9,5},{13,1},{2,14},{6,10},... | collective-permute-start | bytes 24584 | tf_op jit(solution)/shard_map/ppermute | solution.py:45
  20.7 3.7 %collective-permute-start.1 = (f32[2,256]{1,0:T(2,128)S(1)}, f32[2,256]{1,0:T(2,128)S(1)}, u32[]{:S(2)}, u32[]{:S(2)}) collective-permute-start(f32[2,256]{1,0:T(2,128)S(1)} %get-tuple-element.26), channel_id=1, source_target_pairs={{0,4},{4,0},{8,12},{12,8},{1,5},{5,1},{9,13},{13,9},{2,6},{6,2},{1... | collective-permute-start | bytes 6152 | tf_op jit(solution)/shard_map/ppermute | solution.py:45

commit v34 on v29

--- a/solution.py
+++ b/solution.py
@@ -129,7 +129,7 @@
     timed[:, :tile] = time_samples(outer_tiles, window[:, :tile])
     timed[:, -tile:] = time_samples(outer_tiles, window[:, -tile:])
     columns = [
-        jnp.broadcast_to(table[:, part : part + 1], (HALF, comps)) for part in range(parts_here)
+        jnp.broadcast_to(table[:, part : part + 1], (HALF, tile)) for part in range(parts_here)
     ]
     for copy in small:
         copy.wait()
@@ -159,8 +159,11 @@
             square = square + c * c
         region = region_ids[elem]
         reluct = law[0, region] + law[2, region] * square / (square + law[1, region])
-        field = jnp.concatenate([reluct * c for c in comp], axis=1)
-        rows = [jnp.sum(column * field, axis=0, keepdims=True) for column in columns]
+        field = [reluct * c for c in comp]
+        rows = [
+            jnp.concatenate([jnp.sum(column * f, axis=0, keepdims=True) for f in field], axis=1)
+            for column in columns
+        ]
         projected[elem] = jnp.concatenate(rows, axis=0) * (4.0 / SAMPLES)
 
     for turn in range(tile_count + 1):

time: 25.3 us -> 25.1 us (level)
  no operation moved by 1% of the time
where the time goes in v34:
time: 25.1 us; the launch traced here: 25 us
  blocking collectives  13.5 us (54%)
  Pallas kernels  7.16 us (29%)
  starting transfers between devices  4.05 us (16%)
    all_to_all x1, blocking collectives, per_device(): window = lax.all_to_all(copies, GROUP, 0, 0).reshape(parts, block.shape[1])  13.5 us
    ppermute x2, starting transfers between devices, across(): return lax.ppermute(array, ('core', 'space'), pairs)  4.05 us
    pallas_call x1, Pallas kernels, per_device(): pl.pallas_call(field_kernel, out_shape=(pltpu.VMEM((tile_count, parts_her...  2.52 us
    pallas_call x1, Pallas kernels, per_device(): pl.pallas_call(sum_kernel, out_shape=pltpu.VMEM(source.shape, jnp.float32...  2.06 us
    pallas_call x1, Pallas kernels, per_device(): pl.pallas_call(fetch_kernel, out_shape=[pltpu.VMEM(shape, o.dtype) for sh...  1.97 us
    pallas_call x1, Pallas kernels, per_device(): pl.pallas_call(halo_kernel, out_shape=jax.ShapeDtypeStruct(source.shape,...  0.62 us
  transfers between devices with their start and end apart: 2, of which 0 were waited for; matrix products, arithmetic and copies ran while one was open for 0% of the time, Pallas kernels for 16%

profile of v34, /device:TPU:0, one launch (start us, length us, event | category | flops | bytes accessed | tf_op | source)
XLA Modules:
  0.0 25.0 jit_solution(531814832909851989)
XLA Ops:
  0.0 2.4 %collective-permute-start = (bf16[2,2048]{1,0:T(2,128)(2,1)}, bf16[2,2048]{1,0:T(2,128)(2,1)S(1)}, u32[]{:S(2)}, u32[]{:S(2)}) collective-permute-start(bf16[2,2048]{1,0:T(2,128)(2,1)} %refs_2_.1), channel_id=1, source_target_pairs={{0,12},{4,8},{8,4},{12,0},{1,13},{5,9},{9,5},{13,1},{2,14},{6,10},... | collective-permute-start | bytes 24584 | tf_op jit(solution)/shard_map/ppermute | solution.py:45
  2.4 2.0 %fetch_operands.1 = (bf16[8,4,128,384]{3,2,1,0:T(8,128)(2,1)S(1)}, f32[32,2]{1,0:T(8,128)S(1)}, bf16[2,2048]{1,0:T(2,128)(2,1)S(1)}, bf16[2,32,96]{2,1,0:T(8,128...) custom-call(bf16[16,4,128,384]{3,2,1,0:T(8,128)(2,1)} %curl_hbm.1, ...), custom_call_target="tpu_custom_call" | custom-call | bytes 6291456 | tf_op jit(solution)/shard_map/fetch_operands/pallas_call | solution.py:289
  4.4 0.0 collective-permute-done
  4.4 0.1 broadcast_in_dim.2
  4.5 13.5 %all_to_all.5 = bf16[16,2,2304]{2,1,0:T(2,128)(2,1)S(1)} all-to-all(bf16[16,2,2304]{2,1,0:T(2,128)(2,1)S(1)} %broadcast_in_dim.2), channel_id=1, replica_groups=mesh['chip'=2,'core'=2,'space'=2,'samp'=4] {'chip','core','samp'}, dimensions={0} | all-to-all | bytes 294912 | tf_op jit(solution)/shard_map/all_to_all | solution.py:307
  18.1 0.1 reshape.4.window
  18.1 2.5 %shard_fields.1 = (f32[16,2,384]{2,1,0:T(2,128)S(1)}, f32[2,256]{1,0:T(2,128)S(1)}, bf16[8,4,128,384]{3,2,1,0:T(8,128)(2,1)S(1)}) custom-call(bf16[32,2304]{1,0:T(8,128)(2,1)S(1)} %reshape.4.window, bf16[8,4,128,384]{3,2,1,0:T(8,128)(2,1)S(1)} %get-tuple-element.17.first_curl, f32[32,2]{1,0:T(8,128)S(1)} %get-tuple-element.18.table, ...), custom_call_target="tpu_custom_call" | custom-call | flops 402653184 | bytes 6291456 | tf_op jit(solution)/shard_map/shard_fields/pallas_call | solution.py:309
  20.6 1.6 %collective-permute-start.1 = (f32[2,256]{1,0:T(2,128)S(1)}, f32[2,256]{1,0:T(2,128)S(1)}, u32[]{:S(2)}, u32[]{:S(2)}) collective-permute-start(f32[2,256]{1,0:T(2,128)S(1)} %get-tuple-element.26), channel_id=1, source_target_pairs={{0,4},{4,0},{8,12},{12,8},{1,5},{5,1},{9,13},{13,9},{2,6},{6,2},{1... | collective-permute-start | bytes 6152 | tf_op jit(solution)/shard_map/ppermute | solution.py:45
  22.3 2.1 %shard_sums.1.own = f32[2,2048]{1,0:T(2,128)S(1)} custom-call(f32[16,2,384]{2,1,0:T(2,128)S(1)} %get-tuple-element.23.projected, bf16[8,4,128,384]{3,2,1,0:T(8,128)(2,1)S(1)} %get-tuple-element.17.first_curl, bf16[8,4,128,384]{3,2,1,0:T(8,128)(2,1)S(1)} %get-tuple-element.24.later_curl, f32[2,2048]{1,0:T(2,128)S(1)} %get-tuple-element.25.source, ...), custom_call_target="tpu_custom_call" | custom-call | flops 402653184 | bytes 6291456 | tf_op jit(solution)/shard_map/shard_sums/pallas_call | solution.py:345
  24.4 0.0 collective-permute-done.1.from_right.from_left
  24.4 0.6 %halo_sum.1 = f32[2,2048]{1,0:T(2,128)} custom-call(f32[2,2048]{1,0:T(2,128)S(1)} %shard_sums.1.own, f32[2,256]{1,0:T(2,128)S(1)} %collective-permute-done.1.from_right.from_left, f32[2,256]{1,0:T(2,128)S(1)} %collective-permute-done.1.from_right.from_left), custom_call_target="tpu_custom_call" | custom-call | tf_op jit(solution)/shard_map/halo_sum/pallas_call | solution.py:365
  (2 shorter events, 0.0 us)
Async XLA Ops:
  0.0 4.4 %collective-permute-start = (bf16[2,2048]{1,0:T(2,128)(2,1)}, bf16[2,2048]{1,0:T(2,128)(2,1)S(1)}, u32[]{:S(2)}, u32[]{:S(2)}) collective-permute-start(bf16[2,2048]{1,0:T(2,128)(2,1)} %refs_2_.1), channel_id=1, source_target_pairs={{0,12},{4,8},{8,4},{12,0},{1,13},{5,9},{9,5},{13,1},{2,14},{6,10},... | collective-permute-start | bytes 24584 | tf_op jit(solution)/shard_map/ppermute | solution.py:45
  20.6 3.7 %collective-permute-start.1 = (f32[2,256]{1,0:T(2,128)S(1)}, f32[2,256]{1,0:T(2,128)S(1)}, u32[]{:S(2)}, u32[]{:S(2)}) collective-permute-start(f32[2,256]{1,0:T(2,128)S(1)} %get-tuple-element.26), channel_id=1, source_target_pairs={{0,4},{4,0},{8,12},{12,8},{1,5},{5,1},{9,13},{13,9},{2,6},{6,2},{1... | collective-permute-start | bytes 6152 | tf_op jit(solution)/shard_map/ppermute | solution.py:45

commit v35 on v34

--- a/solution.py
+++ b/solution.py
@@ -135,10 +135,6 @@
         copy.wait()
     places = [[pattern[link, elem] for link in range(links)] for elem in range(tile_count)]
     count = jnp.int32(0)
-    for elem in range(tile_count):
-        for link, at in enumerate(places[elem]):
-            outer[count] = elem * links + link
-            count += jnp.where((at == 0) | (at == tile_count + 1), 1, 0)
 
     def blocks(elem):
         curl = first_curl[elem] if elem < early else later_curl[elem - early]
@@ -171,6 +167,9 @@
             if turn in later:
                 later[turn].wait()
             find_density(turn)
+            for link, at in enumerate(places[turn]):
+                outer[count] = turn * links + link
+                count += jnp.where((at == 0) | (at == tile_count + 1), 1, 0)
         if turn:
             project(turn - 1)
 

time: 25.1 us -> 25.3 us (level)
  no operation moved by 1% of the time
where the time goes in v35:
time: 25.3 us; the launch traced here: 25 us
  blocking collectives  13.5 us (53%)
  Pallas kernels  7.17 us (28%)
  starting transfers between devices  4.05 us (16%)
    all_to_all x1, blocking collectives, per_device(): window = lax.all_to_all(copies, GROUP, 0, 0).reshape(parts, block.shape[1])  13.5 us
    ppermute x2, starting transfers between devices, across(): return lax.ppermute(array, ('core', 'space'), pairs)  4.05 us
    pallas_call x1, Pallas kernels, per_device(): pl.pallas_call(field_kernel, out_shape=(pltpu.VMEM((tile_count, parts_her...  2.53 us
    pallas_call x1, Pallas kernels, per_device(): pl.pallas_call(sum_kernel, out_shape=pltpu.VMEM(source.shape, jnp.float32...  2.06 us
    pallas_call x1, Pallas kernels, per_device(): pl.pallas_call(fetch_kernel, out_shape=[pltpu.VMEM(shape, o.dtype) for sh...  1.97 us
    pallas_call x1, Pallas kernels, per_device(): pl.pallas_call(halo_kernel, out_shape=jax.ShapeDtypeStruct(source.shape,...  0.62 us
  transfers between devices with their start and end apart: 2, of which 0 were waited for; matrix products, arithmetic and copies ran while one was open for 0% of the time, Pallas kernels for 16%

profile of v35, /device:TPU:0, one launch (start us, length us, event | category | flops | bytes accessed | tf_op | source)
XLA Modules:
  0.0 25.0 jit_solution(4771047093659743564)
XLA Ops:
  0.0 2.4 %collective-permute-start = (bf16[2,2048]{1,0:T(2,128)(2,1)}, bf16[2,2048]{1,0:T(2,128)(2,1)S(1)}, u32[]{:S(2)}, u32[]{:S(2)}) collective-permute-start(bf16[2,2048]{1,0:T(2,128)(2,1)} %refs_2_.1), channel_id=1, source_target_pairs={{0,12},{4,8},{8,4},{12,0},{1,13},{5,9},{9,5},{13,1},{2,14},{6,10},... | collective-permute-start | bytes 24584 | tf_op jit(solution)/shard_map/ppermute | solution.py:45
  2.4 2.0 %fetch_operands.1 = (bf16[8,4,128,384]{3,2,1,0:T(8,128)(2,1)S(1)}, f32[32,2]{1,0:T(8,128)S(1)}, bf16[2,2048]{1,0:T(2,128)(2,1)S(1)}, bf16[2,32,96]{2,1,0:T(8,128...) custom-call(bf16[16,4,128,384]{3,2,1,0:T(8,128)(2,1)} %curl_hbm.1, ...), custom_call_target="tpu_custom_call" | custom-call | bytes 6291456 | tf_op jit(solution)/shard_map/fetch_operands/pallas_call | solution.py:288
  4.4 0.0 collective-permute-done
  4.4 0.1 broadcast_in_dim.2
  4.5 13.5 %all_to_all.5 = bf16[16,2,2304]{2,1,0:T(2,128)(2,1)S(1)} all-to-all(bf16[16,2,2304]{2,1,0:T(2,128)(2,1)S(1)} %broadcast_in_dim.2), channel_id=1, replica_groups=mesh['chip'=2,'core'=2,'space'=2,'samp'=4] {'chip','core','samp'}, dimensions={0} | all-to-all | bytes 294912 | tf_op jit(solution)/shard_map/all_to_all | solution.py:306
  18.1 0.1 reshape.4.window
  18.1 2.5 %shard_fields.1 = (f32[16,2,384]{2,1,0:T(2,128)S(1)}, f32[2,256]{1,0:T(2,128)S(1)}, bf16[8,4,128,384]{3,2,1,0:T(8,128)(2,1)S(1)}) custom-call(bf16[32,2304]{1,0:T(8,128)(2,1)S(1)} %reshape.4.window, bf16[8,4,128,384]{3,2,1,0:T(8,128)(2,1)S(1)} %get-tuple-element.17.first_curl, f32[32,2]{1,0:T(8,128)S(1)} %get-tuple-element.18.table, ...), custom_call_target="tpu_custom_call" | custom-call | flops 402653184 | bytes 6291456 | tf_op jit(solution)/shard_map/shard_fields/pallas_call | solution.py:308
  20.7 1.6 %collective-permute-start.1 = (f32[2,256]{1,0:T(2,128)S(1)}, f32[2,256]{1,0:T(2,128)S(1)}, u32[]{:S(2)}, u32[]{:S(2)}) collective-permute-start(f32[2,256]{1,0:T(2,128)S(1)} %get-tuple-element.26), channel_id=1, source_target_pairs={{0,4},{4,0},{8,12},{12,8},{1,5},{5,1},{9,13},{13,9},{2,6},{6,2},{1... | collective-permute-start | bytes 6152 | tf_op jit(solution)/shard_map/ppermute | solution.py:45
  22.3 2.1 %shard_sums.1.own = f32[2,2048]{1,0:T(2,128)S(1)} custom-call(f32[16,2,384]{2,1,0:T(2,128)S(1)} %get-tuple-element.23.projected, bf16[8,4,128,384]{3,2,1,0:T(8,128)(2,1)S(1)} %get-tuple-element.17.first_curl, bf16[8,4,128,384]{3,2,1,0:T(8,128)(2,1)S(1)} %get-tuple-element.24.later_curl, f32[2,2048]{1,0:T(2,128)S(1)} %get-tuple-element.25.source, ...), custom_call_target="tpu_custom_call" | custom-call | flops 402653184 | bytes 6291456 | tf_op jit(solution)/shard_map/shard_sums/pallas_call | solution.py:344
  24.4 0.0 collective-permute-done.1.from_right.from_left
  24.4 0.6 %halo_sum.1 = f32[2,2048]{1,0:T(2,128)} custom-call(f32[2,2048]{1,0:T(2,128)S(1)} %shard_sums.1.own, f32[2,256]{1,0:T(2,128)S(1)} %collective-permute-done.1.from_right.from_left, f32[2,256]{1,0:T(2,128)S(1)} %collective-permute-done.1.from_right.from_left), custom_call_target="tpu_custom_call" | custom-call | tf_op jit(solution)/shard_map/halo_sum/pallas_call | solution.py:364
  (2 shorter events, 0.0 us)
Async XLA Ops:
  0.0 4.4 %collective-permute-start = (bf16[2,2048]{1,0:T(2,128)(2,1)}, bf16[2,2048]{1,0:T(2,128)(2,1)S(1)}, u32[]{:S(2)}, u32[]{:S(2)}) collective-permute-start(bf16[2,2048]{1,0:T(2,128)(2,1)} %refs_2_.1), channel_id=1, source_target_pairs={{0,12},{4,8},{8,4},{12,0},{1,13},{5,9},{9,5},{13,1},{2,14},{6,10},... | collective-permute-start | bytes 24584 | tf_op jit(solution)/shard_map/ppermute | solution.py:45
  20.7 3.7 %collective-permute-start.1 = (f32[2,256]{1,0:T(2,128)S(1)}, f32[2,256]{1,0:T(2,128)S(1)}, u32[]{:S(2)}, u32[]{:S(2)}) collective-permute-start(f32[2,256]{1,0:T(2,128)S(1)} %get-tuple-element.26), channel_id=1, source_target_pairs={{0,4},{4,0},{8,12},{12,8},{1,5},{5,1},{9,13},{13,9},{2,6},{6,2},{1... | collective-permute-start | bytes 6152 | tf_op jit(solution)/shard_map/ppermute | solution.py:45

commit v36 on v35

--- a/solution.py
+++ b/solution.py
@@ -28,7 +28,7 @@
 def bf16_pieces(table):
     rest = table
     pieces = []
-    for _ in range(3):
+    for _ in range(2):
         piece = rest.astype(ml_dtypes.bfloat16)
         pieces.append(piece)
         rest = rest - piece.astype(np.float64)
@@ -68,7 +68,7 @@
 
 
 def time_samples(pieces, rows):
-    stacked = jnp.concatenate([rows] * 3, axis=0)
+    stacked = jnp.concatenate([rows] * 2, axis=0)
     samples = jnp.dot(pieces, stacked, preferred_element_type=jnp.float32)
     high = samples.astype(jnp.bfloat16)
     low = (samples - high.astype(jnp.float32)).astype(jnp.bfloat16)

time: 25.3 us -> 25.2 us (level); the launches traced: 25 us -> 25.2 us
  transfers between devices with their start and end apart: 2 -> 2, of which waited for: 0 -> 1; matrix products, arithmetic and copies ran while one was open for 0% -> 0% of each run, Pallas kernels for 16% -> 16%
where the time goes in v36:
time: 25.2 us
  blocking collectives  13.5 us (54%)
  Pallas kernels  7.41 us (29%)
  starting transfers between devices  3.82 us (15%)
    all_to_all x1, blocking collectives, per_device(): window = lax.all_to_all(copies, GROUP, 0, 0).reshape(parts, block.shape[1])  13.5 us
    ppermute x2, starting transfers between devices, across(): return lax.ppermute(array, ('core', 'space'), pairs)  3.82 us
    pallas_call x1, Pallas kernels, per_device(): pl.pallas_call(field_kernel, out_shape=(pltpu.VMEM((tile_count, parts_her...  2.77 us
    pallas_call x1, Pallas kernels, per_device(): pl.pallas_call(sum_kernel, out_shape=pltpu.VMEM(source.shape, jnp.float32...  2.06 us
    pallas_call x1, Pallas kernels, per_device(): pl.pallas_call(fetch_kernel, out_shape=[pltpu.VMEM(shape, o.dtype) for sh...  1.97 us
    pallas_call x1, Pallas kernels, per_device(): pl.pallas_call(halo_kernel, out_shape=jax.ShapeDtypeStruct(source.shape,...  0.61 us
  transfers between devices with their start and end apart: 2, of which 1 were waited for; matrix products, arithmetic and copies ran while one was open for 0% of the time, Pallas kernels for 16%

profile of v36, /device:TPU:0, one launch (start us, length us, event | category | flops | bytes accessed | tf_op | source)
XLA Modules:
  0.0 25.2 jit_solution(11141559772965833457)
XLA Ops:
  0.0 2.4 %collective-permute-start = (bf16[2,2048]{1,0:T(2,128)(2,1)}, bf16[2,2048]{1,0:T(2,128)(2,1)S(1)}, u32[]{:S(2)}, u32[]{:S(2)}) collective-permute-start(bf16[2,2048]{1,0:T(2,128)(2,1)} %refs_2_.1), channel_id=1, source_target_pairs={{0,12},{4,8},{8,4},{12,0},{1,13},{5,9},{9,5},{13,1},{2,14},{6,10},... | collective-permute-start | bytes 24584 | tf_op jit(solution)/shard_map/ppermute | solution.py:45
  2.4 2.0 %fetch_operands.1 = (bf16[8,4,128,384]{3,2,1,0:T(8,128)(2,1)S(1)}, f32[32,2]{1,0:T(8,128)S(1)}, bf16[2,2048]{1,0:T(2,128)(2,1)S(1)}, bf16[2,32,64]{2,1,0:T(8,128...) custom-call(bf16[16,4,128,384]{3,2,1,0:T(8,128)(2,1)} %curl_hbm.1, ...), custom_call_target="tpu_custom_call" | custom-call | bytes 6291456 | tf_op jit(solution)/shard_map/fetch_operands/pallas_call | solution.py:288
  4.4 0.0 collective-permute-done
  4.4 0.1 broadcast_in_dim.2
  4.5 13.5 %all_to_all.5 = bf16[16,2,2304]{2,1,0:T(2,128)(2,1)S(1)} all-to-all(bf16[16,2,2304]{2,1,0:T(2,128)(2,1)S(1)} %broadcast_in_dim.2), channel_id=1, replica_groups=mesh['chip'=2,'core'=2,'space'=2,'samp'=4] {'chip','core','samp'}, dimensions={0} | all-to-all | bytes 294912 | tf_op jit(solution)/shard_map/all_to_all | solution.py:306
  18.1 0.1 reshape.4.window
  18.1 2.8 %shard_fields.1 = (f32[16,2,384]{2,1,0:T(2,128)S(1)}, f32[2,256]{1,0:T(2,128)S(1)}, bf16[8,4,128,384]{3,2,1,0:T(8,128)(2,1)S(1)}) custom-call(bf16[32,2304]{1,0:T(8,128)(2,1)S(1)} %reshape.4.window, bf16[8,4,128,384]{3,2,1,0:T(8,128)(2,1)S(1)} %get-tuple-element.17.first_curl, f32[32,2]{1,0:T(8,128)S(1)} %get-tuple-element.18.table, ...), custom_call_target="tpu_custom_call" | custom-call | flops 402653184 | bytes 6291456 | tf_op jit(solution)/shard_map/shard_fields/pallas_call | solution.py:308
  20.9 1.4 %collective-permute-start.1 = (f32[2,256]{1,0:T(2,128)S(1)}, f32[2,256]{1,0:T(2,128)S(1)}, u32[]{:S(2)}, u32[]{:S(2)}) collective-permute-start(f32[2,256]{1,0:T(2,128)S(1)} %get-tuple-element.26), channel_id=1, source_target_pairs={{0,4},{4,0},{8,12},{12,8},{1,5},{5,1},{9,13},{13,9},{2,6},{6,2},{1... | collective-permute-start | bytes 6152 | tf_op jit(solution)/shard_map/ppermute | solution.py:45
  22.3 2.1 %shard_sums.1.own = f32[2,2048]{1,0:T(2,128)S(1)} custom-call(f32[16,2,384]{2,1,0:T(2,128)S(1)} %get-tuple-element.23.projected, bf16[8,4,128,384]{3,2,1,0:T(8,128)(2,1)S(1)} %get-tuple-element.17.first_curl, bf16[8,4,128,384]{3,2,1,0:T(8,128)(2,1)S(1)} %get-tuple-element.24.later_curl, f32[2,2048]{1,0:T(2,128)S(1)} %get-tuple-element.25.source, ...), custom_call_target="tpu_custom_call" | custom-call | flops 402653184 | bytes 6291456 | tf_op jit(solution)/shard_map/shard_sums/pallas_call | solution.py:344
  24.4 0.2 collective-permute-done.1.from_right.from_left
  24.5 0.6 %halo_sum.1 = f32[2,2048]{1,0:T(2,128)} custom-call(f32[2,2048]{1,0:T(2,128)S(1)} %shard_sums.1.own, f32[2,256]{1,0:T(2,128)S(1)} %collective-permute-done.1.from_right.from_left, f32[2,256]{1,0:T(2,128)S(1)} %collective-permute-done.1.from_right.from_left), custom_call_target="tpu_custom_call" | custom-call | tf_op jit(solution)/shard_map/halo_sum/pallas_call | solution.py:364
  (2 shorter events, 0.0 us)
Async XLA Ops:
  0.0 4.4 %collective-permute-start = (bf16[2,2048]{1,0:T(2,128)(2,1)}, bf16[2,2048]{1,0:T(2,128)(2,1)S(1)}, u32[]{:S(2)}, u32[]{:S(2)}) collective-permute-start(bf16[2,2048]{1,0:T(2,128)(2,1)} %refs_2_.1), channel_id=1, source_target_pairs={{0,12},{4,8},{8,4},{12,0},{1,13},{5,9},{9,5},{13,1},{2,14},{6,10},... | collective-permute-start | bytes 24584 | tf_op jit(solution)/shard_map/ppermute | solution.py:45
  20.9 3.7 %collective-permute-start.1 = (f32[2,256]{1,0:T(2,128)S(1)}, f32[2,256]{1,0:T(2,128)S(1)}, u32[]{:S(2)}, u32[]{:S(2)}) collective-permute-start(f32[2,256]{1,0:T(2,128)S(1)} %get-tuple-element.26), channel_id=1, source_target_pairs={{0,4},{4,0},{8,12},{12,8},{1,5},{5,1},{9,13},{13,9},{2,6},{6,2},{1... | collective-permute-start | bytes 6152 | tf_op jit(solution)/shard_map/ppermute | solution.py:45

commit v37 on v35

--- a/solution.py
+++ b/solution.py
@@ -15,7 +15,7 @@
 MIB = 1024 * 1024
 LISTED = 4
 CHUNK = 4
-AHEAD = 3
+AHEAD = 6
 
 
 def half_table(parts):

time: 25.3 us -> 25.1 us (level)
  transfers between devices with their start and end apart: 2 -> 2, of which waited for: 0 -> 1; matrix products, arithmetic and copies ran while one was open for 0% -> 0% of each run, Pallas kernels for 16% -> 16%
where the time goes in v37:
time: 25.1 us; the launch traced here: 24.9 us
  blocking collectives  13.5 us (54%)
  Pallas kernels  7.01 us (28%)
  starting transfers between devices  4.06 us (16%)
    all_to_all x1, blocking collectives, per_device(): window = lax.all_to_all(copies, GROUP, 0, 0).reshape(parts, block.shape[1])  13.5 us
    ppermute x2, starting transfers between devices, across(): return lax.ppermute(array, ('core', 'space'), pairs)  4.06 us
    pallas_call x1, Pallas kernels, per_device(): pl.pallas_call(field_kernel, out_shape=(pltpu.VMEM((tile_count, parts_her...  2.53 us
    pallas_call x1, Pallas kernels, per_device(): pl.pallas_call(fetch_kernel, out_shape=[pltpu.VMEM(shape, o.dtype) for sh...  1.97 us
    pallas_call x1, Pallas kernels, per_device(): pl.pallas_call(sum_kernel, out_shape=pltpu.VMEM(source.shape, jnp.float32...  1.9 us
    pallas_call x1, Pallas kernels, per_device(): pl.pallas_call(halo_kernel, out_shape=jax.ShapeDtypeStruct(source.shape,...  0.61 us
  transfers between devices with their start and end apart: 2, of which 1 were waited for; matrix products, arithmetic and copies ran while one was open for 0% of the time, Pallas kernels for 16%

profile of v37, /device:TPU:0, one launch (start us, length us, event | category | flops | bytes accessed | tf_op | source)
XLA Modules:
  0.0 24.9 jit_solution(10209717923739044085)
XLA Ops:
  0.0 2.4 %collective-permute-start = (bf16[2,2048]{1,0:T(2,128)(2,1)}, bf16[2,2048]{1,0:T(2,128)(2,1)S(1)}, u32[]{:S(2)}, u32[]{:S(2)}) collective-permute-start(bf16[2,2048]{1,0:T(2,128)(2,1)} %refs_2_.1), channel_id=1, source_target_pairs={{0,12},{4,8},{8,4},{12,0},{1,13},{5,9},{9,5},{13,1},{2,14},{6,10},... | collective-permute-start | bytes 24584 | tf_op jit(solution)/shard_map/ppermute | solution.py:45
  2.4 2.0 %fetch_operands.1 = (bf16[8,4,128,384]{3,2,1,0:T(8,128)(2,1)S(1)}, f32[32,2]{1,0:T(8,128)S(1)}, bf16[2,2048]{1,0:T(2,128)(2,1)S(1)}, bf16[2,32,96]{2,1,0:T(8,128...) custom-call(bf16[16,4,128,384]{3,2,1,0:T(8,128)(2,1)} %curl_hbm.1, ...), custom_call_target="tpu_custom_call" | custom-call | bytes 6291456 | tf_op jit(solution)/shard_map/fetch_operands/pallas_call | solution.py:288
  4.4 0.0 collective-permute-done
  4.4 0.1 broadcast_in_dim.2
  4.5 13.5 %all_to_all.5 = bf16[16,2,2304]{2,1,0:T(2,128)(2,1)S(1)} all-to-all(bf16[16,2,2304]{2,1,0:T(2,128)(2,1)S(1)} %broadcast_in_dim.2), channel_id=1, replica_groups=mesh['chip'=2,'core'=2,'space'=2,'samp'=4] {'chip','core','samp'}, dimensions={0} | all-to-all | bytes 294912 | tf_op jit(solution)/shard_map/all_to_all | solution.py:306
  18.1 0.1 reshape.4.window
  18.1 2.5 %shard_fields.1 = (f32[16,2,384]{2,1,0:T(2,128)S(1)}, f32[2,256]{1,0:T(2,128)S(1)}, bf16[8,4,128,384]{3,2,1,0:T(8,128)(2,1)S(1)}) custom-call(bf16[32,2304]{1,0:T(8,128)(2,1)S(1)} %reshape.4.window, bf16[8,4,128,384]{3,2,1,0:T(8,128)(2,1)S(1)} %get-tuple-element.17.first_curl, f32[32,2]{1,0:T(8,128)S(1)} %get-tuple-element.18.table, ...), custom_call_target="tpu_custom_call" | custom-call | flops 402653184 | bytes 6291456 | tf_op jit(solution)/shard_map/shard_fields/pallas_call | solution.py:308
  20.7 1.6 %collective-permute-start.1 = (f32[2,256]{1,0:T(2,128)S(1)}, f32[2,256]{1,0:T(2,128)S(1)}, u32[]{:S(2)}, u32[]{:S(2)}) collective-permute-start(f32[2,256]{1,0:T(2,128)S(1)} %get-tuple-element.26), channel_id=1, source_target_pairs={{0,4},{4,0},{8,12},{12,8},{1,5},{5,1},{9,13},{13,9},{2,6},{6,2},{1... | collective-permute-start | bytes 6152 | tf_op jit(solution)/shard_map/ppermute | solution.py:45
  22.3 1.9 %shard_sums.1.own = f32[2,2048]{1,0:T(2,128)S(1)} custom-call(f32[16,2,384]{2,1,0:T(2,128)S(1)} %get-tuple-element.23.projected, bf16[8,4,128,384]{3,2,1,0:T(8,128)(2,1)S(1)} %get-tuple-element.17.first_curl, bf16[8,4,128,384]{3,2,1,0:T(8,128)(2,1)S(1)} %get-tuple-element.24.later_curl, f32[2,2048]{1,0:T(2,128)S(1)} %get-tuple-element.25.source, ...), custom_call_target="tpu_custom_call" | custom-call | flops 402653184 | bytes 6291456 | tf_op jit(solution)/shard_map/shard_sums/pallas_call | solution.py:344
  24.2 0.1 collective-permute-done.1.from_right.from_left
  24.3 0.6 %halo_sum.1 = f32[2,2048]{1,0:T(2,128)} custom-call(f32[2,2048]{1,0:T(2,128)S(1)} %shard_sums.1.own, f32[2,256]{1,0:T(2,128)S(1)} %collective-permute-done.1.from_right.from_left, f32[2,256]{1,0:T(2,128)S(1)} %collective-permute-done.1.from_right.from_left), custom_call_target="tpu_custom_call" | custom-call | tf_op jit(solution)/shard_map/halo_sum/pallas_call | solution.py:364
  (2 shorter events, 0.0 us)
Async XLA Ops:
  0.0 4.4 %collective-permute-start = (bf16[2,2048]{1,0:T(2,128)(2,1)}, bf16[2,2048]{1,0:T(2,128)(2,1)S(1)}, u32[]{:S(2)}, u32[]{:S(2)}) collective-permute-start(bf16[2,2048]{1,0:T(2,128)(2,1)} %refs_2_.1), channel_id=1, source_target_pairs={{0,12},{4,8},{8,4},{12,0},{1,13},{5,9},{9,5},{13,1},{2,14},{6,10},... | collective-permute-start | bytes 24584 | tf_op jit(solution)/shard_map/ppermute | solution.py:45
  20.7 3.7 %collective-permute-start.1 = (f32[2,256]{1,0:T(2,128)S(1)}, f32[2,256]{1,0:T(2,128)S(1)}, u32[]{:S(2)}, u32[]{:S(2)}) collective-permute-start(f32[2,256]{1,0:T(2,128)S(1)} %get-tuple-element.26), channel_id=1, source_target_pairs={{0,4},{4,0},{8,12},{12,8},{1,5},{5,1},{9,13},{13,9},{2,6},{6,2},{1... | collective-permute-start | bytes 6152 | tf_op jit(solution)/shard_map/ppermute | solution.py:45

commit v38 on v37

--- a/solution.py
+++ b/solution.py
@@ -13,7 +13,7 @@
 HALF = SAMPLES // 2
 GROUP = ("chip", "core", "samp")
 MIB = 1024 * 1024
-LISTED = 4
+LISTED = 6
 CHUNK = 4
 AHEAD = 6
 

time: 25.1 us -> 25.2 us (level)
  transfers between devices with their start and end apart: 2 -> 2, of which waited for: 1 -> 1; matrix products, arithmetic and copies ran while one was open for 0% -> 0% of each run, Pallas kernels for 16% -> 15%
where the time goes in v38:
time: 25.2 us; the launch traced here: 25 us
  blocking collectives  13.5 us (54%)
  Pallas kernels  7.12 us (28%)
  starting transfers between devices  4.05 us (16%)
    all_to_all x1, blocking collectives, per_device(): window = lax.all_to_all(copies, GROUP, 0, 0).reshape(parts, block.shape[1])  13.5 us
    ppermute x2, starting transfers between devices, across(): return lax.ppermute(array, ('core', 'space'), pairs)  4.05 us
    pallas_call x1, Pallas kernels, per_device(): pl.pallas_call(field_kernel, out_shape=(pltpu.VMEM((tile_count, parts_her...  2.63 us
    pallas_call x1, Pallas kernels, per_device(): pl.pallas_call(fetch_kernel, out_shape=[pltpu.VMEM(shape, o.dtype) for sh...  1.97 us
    pallas_call x1, Pallas kernels, per_device(): pl.pallas_call(sum_kernel, out_shape=pltpu.VMEM(source.shape, jnp.float32...  1.9 us
    pallas_call x1, Pallas kernels, per_device(): pl.pallas_call(halo_kernel, out_shape=jax.ShapeDtypeStruct(source.shape,...  0.61 us
  transfers between devices with their start and end apart: 2, of which 1 were waited for; matrix products, arithmetic and copies ran while one was open for 0% of the time, Pallas kernels for 15%

profile of v38, /device:TPU:0, one launch (start us, length us, event | category | flops | bytes accessed | tf_op | source)
XLA Modules:
  0.0 25.0 jit_solution(15150204815493988835)
XLA Ops:
  0.0 2.4 %collective-permute-start = (bf16[2,2048]{1,0:T(2,128)(2,1)}, bf16[2,2048]{1,0:T(2,128)(2,1)S(1)}, u32[]{:S(2)}, u32[]{:S(2)}) collective-permute-start(bf16[2,2048]{1,0:T(2,128)(2,1)} %refs_2_.1), channel_id=1, source_target_pairs={{0,12},{4,8},{8,4},{12,0},{1,13},{5,9},{9,5},{13,1},{2,14},{6,10},... | collective-permute-start | bytes 24584 | tf_op jit(solution)/shard_map/ppermute | solution.py:45
  2.4 2.0 %fetch_operands.1 = (bf16[8,4,128,384]{3,2,1,0:T(8,128)(2,1)S(1)}, f32[32,2]{1,0:T(8,128)S(1)}, bf16[2,2048]{1,0:T(2,128)(2,1)S(1)}, bf16[2,32,96]{2,1,0:T(8,128...) custom-call(bf16[16,4,128,384]{3,2,1,0:T(8,128)(2,1)} %curl_hbm.1, ...), custom_call_target="tpu_custom_call" | custom-call | bytes 6291456 | tf_op jit(solution)/shard_map/fetch_operands/pallas_call | solution.py:288
  4.4 0.0 collective-permute-done
  4.4 0.1 broadcast_in_dim.2
  4.5 13.5 %all_to_all.5 = bf16[16,2,2304]{2,1,0:T(2,128)(2,1)S(1)} all-to-all(bf16[16,2,2304]{2,1,0:T(2,128)(2,1)S(1)} %broadcast_in_dim.2), channel_id=1, replica_groups=mesh['chip'=2,'core'=2,'space'=2,'samp'=4] {'chip','core','samp'}, dimensions={0} | all-to-all | bytes 294912 | tf_op jit(solution)/shard_map/all_to_all | solution.py:306
  18.1 0.1 reshape.4.window
  18.1 2.6 %shard_fields.1 = (f32[16,2,384]{2,1,0:T(2,128)S(1)}, f32[2,256]{1,0:T(2,128)S(1)}, bf16[8,4,128,384]{3,2,1,0:T(8,128)(2,1)S(1)}) custom-call(bf16[32,2304]{1,0:T(8,128)(2,1)S(1)} %reshape.4.window, bf16[8,4,128,384]{3,2,1,0:T(8,128)(2,1)S(1)} %get-tuple-element.17.first_curl, f32[32,2]{1,0:T(8,128)S(1)} %get-tuple-element.18.table, ...), custom_call_target="tpu_custom_call" | custom-call | flops 402653184 | bytes 6291456 | tf_op jit(solution)/shard_map/shard_fields/pallas_call | solution.py:308
  20.8 1.6 %collective-permute-start.1 = (f32[2,256]{1,0:T(2,128)S(1)}, f32[2,256]{1,0:T(2,128)S(1)}, u32[]{:S(2)}, u32[]{:S(2)}) collective-permute-start(f32[2,256]{1,0:T(2,128)S(1)} %get-tuple-element.26), channel_id=1, source_target_pairs={{0,4},{4,0},{8,12},{12,8},{1,5},{5,1},{9,13},{13,9},{2,6},{6,2},{1... | collective-permute-start | bytes 6152 | tf_op jit(solution)/shard_map/ppermute | solution.py:45
  22.4 1.9 %shard_sums.1.own = f32[2,2048]{1,0:T(2,128)S(1)} custom-call(f32[16,2,384]{2,1,0:T(2,128)S(1)} %get-tuple-element.23.projected, bf16[8,4,128,384]{3,2,1,0:T(8,128)(2,1)S(1)} %get-tuple-element.17.first_curl, bf16[8,4,128,384]{3,2,1,0:T(8,128)(2,1)S(1)} %get-tuple-element.24.later_curl, f32[2,2048]{1,0:T(2,128)S(1)} %get-tuple-element.25.source, ...), custom_call_target="tpu_custom_call" | custom-call | flops 402653184 | bytes 6291456 | tf_op jit(solution)/shard_map/shard_sums/pallas_call | solution.py:344
  24.3 0.1 collective-permute-done.1.from_right.from_left
  24.4 0.6 %halo_sum.1 = f32[2,2048]{1,0:T(2,128)} custom-call(f32[2,2048]{1,0:T(2,128)S(1)} %shard_sums.1.own, f32[2,256]{1,0:T(2,128)S(1)} %collective-permute-done.1.from_right.from_left, f32[2,256]{1,0:T(2,128)S(1)} %collective-permute-done.1.from_right.from_left), custom_call_target="tpu_custom_call" | custom-call | tf_op jit(solution)/shard_map/halo_sum/pallas_call | solution.py:364
  (2 shorter events, 0.0 us)
Async XLA Ops:
  0.0 4.4 %collective-permute-start = (bf16[2,2048]{1,0:T(2,128)(2,1)}, bf16[2,2048]{1,0:T(2,128)(2,1)S(1)}, u32[]{:S(2)}, u32[]{:S(2)}) collective-permute-start(bf16[2,2048]{1,0:T(2,128)(2,1)} %refs_2_.1), channel_id=1, source_target_pairs={{0,12},{4,8},{8,4},{12,0},{1,13},{5,9},{9,5},{13,1},{2,14},{6,10},... | collective-permute-start | bytes 24584 | tf_op jit(solution)/shard_map/ppermute | solution.py:45
  20.8 3.7 %collective-permute-start.1 = (f32[2,256]{1,0:T(2,128)S(1)}, f32[2,256]{1,0:T(2,128)S(1)}, u32[]{:S(2)}, u32[]{:S(2)}) collective-permute-start(f32[2,256]{1,0:T(2,128)S(1)} %get-tuple-element.26), channel_id=1, source_target_pairs={{0,4},{4,0},{8,12},{12,8},{1,5},{5,1},{9,13},{13,9},{2,6},{6,2},{1... | collective-permute-start | bytes 6152 | tf_op jit(solution)/shard_map/ppermute | solution.py:45
